TPU v7x, 32 devices: a whole 2x2x4 slice. The times are simulated.
32 devices in a mesh: dp: 8 (over y, x, core), tensor: 4 (over z).
Axes of the slice: x: 2, y: 2, z: 4, core: 2. Of those that a mesh axis runs over, the one named last changes fastest.
Arguments:
- tokens: bfloat16 [8, 1024, 2048], P('dp', 'tensor'), may hold values from -6 to 6
- cotangent: bfloat16 [8, 1024, 2048], P('dp', 'tensor'), may hold values from -6 to 6
- adapter_ids: int32 [8, 1], P('dp'), may hold values from 0 to 7
- segments: int32 [8, 1024], P('dp'), may hold values from 0 to 5, never falling along the last dimension, each value on 1 to 800 neighbouring positions
- norm_attn: float32 [2048], replicated, may hold values from 0.1 to 1.9
- norm_mlp: float32 [2048], replicated, may hold values from 0.1 to 1.9
- weight_query: bfloat16 [2048, 2048], P('dp', 'tensor'), may hold values from -0.125 to 0.125
- weight_key: bfloat16 [2048, 2048], P('dp', 'tensor'), may hold values from -0.125 to 0.125
- weight_value: bfloat16 [2048, 4096], P('dp', 'tensor'), may hold values from -0.125 to 0.125
- weight_gate: bfloat16 [2048, 4096], P('dp', 'tensor'), may hold values from -0.125 to 0.125
- weight_out: bfloat16 [4096, 2048], P('tensor', 'dp'), may hold values from -0.1875 to 0.1875
- weight_mlp_gate: bfloat16 [2048, 4096], P('dp', 'tensor'), may hold values from -0.125 to 0.125
- weight_mlp_up: bfloat16 [2048, 4096], P('dp', 'tensor'), may hold values from -0.125 to 0.125
- weight_mlp_down: bfloat16 [4096, 2048], P('tensor', 'dp'), may hold values from -0.1875 to 0.1875
- adapt_attn_in: bfloat16 [8, 2048, 64], replicated, may hold values from -0.125 to 0.125
- adapt_query_key: bfloat16 [8, 2, 16, 2048], P(None, None, None, 'tensor'), may hold values from -1.5 to 1.5
- adapt_value_gate: bfloat16 [8, 2, 16, 4096], P(None, None, None, 'tensor'), may hold values from -1.5 to 1.5
- adapt_out_in: bfloat16 [8, 4096, 16], P(None, 'tensor'), may hold values from -0.09375 to 0.09375
- adapt_out_back: bfloat16 [8, 16, 2048], replicated, may hold values from -1.5 to 1.5
- adapt_mlp_in: bfloat16 [8, 2048, 32], replicated, may hold values from -0.125 to 0.125
- adapt_mlp_hidden: bfloat16 [8, 2, 16, 4096], P(None, None, None, 'tensor'), may hold values from -1.5 to 1.5
- adapt_down_in: bfloat16 [8, 4096, 16], P(None, 'tensor'), may hold values from -0.09375 to 0.09375
- adapt_down_back: bfloat16 [8, 16, 2048], replicated, may hold values from -1.5 to 1.5
Outputs:
- output: bfloat16 [8, 1024, 2048], P('dp', 'tensor')
- input_grad: float32 [8, 1024, 2048], P('dp', 'tensor')
- grad_attn_in: float32 [8, 2048, 64], replicated
- grad_query_key: float32 [8, 2, 16, 2048], P(None, None, None, 'tensor')
- grad_value_gate: float32 [8, 2, 16, 4096], P(None, None, None, 'tensor')
- grad_out_in: float32 [8, 4096, 16], P(None, 'tensor')
- grad_out_back: float32 [8, 16, 2048], replicated
- grad_mlp_in: float32 [8, 2048, 32], replicated
- grad_mlp_hidden: float32 [8, 2, 16, 4096], P(None, None, None, 'tensor')
- grad_down_in: float32 [8, 4096, 16], P(None, 'tensor')
- grad_down_back: float32 [8, 16, 2048], replicated
Inputs may be any that keep to these rules, and one draw needn't show every extreme that they name: `adapter_ids`: every one of the 8 adapters is chosen by at least one sequence. `segments`: along a sequence the document numbers never fall; a document has at most 800 tokens, and some document has exactly 800.
All inputs are finite; a program needn't handle non-finite values.
Results may differ from a plain program's by a relative error of at most 0.023.
Values may be sent and summed in bfloat16 or wider, within the bound.
No kernel may reach another device: no remote copies, remote signals or barrier semaphores. Data moves between devices by JAX's collectives and lax.ppermute only.
A program may use at most 192 MiB of HBM per device.

v0:
```python
from functools import partial

import jax
import jax.numpy as jnp
from jax import lax
from jax.sharding import PartitionSpec as P

KEY_DIM = 256
VALUE_DIM = 512
RANK = 16
ROW_BLOCK = 512


highest = lax.Precision.HIGHEST
rms_epsilon = 1e-06
group_floor = 1.0


def matmul(left_side, right_side):
    return jnp.dot(left_side, right_side, preferred_element_type=jnp.float32)


def matmul_exact(left_side, right_side):
    return jnp.dot(left_side, right_side, precision=highest, preferred_element_type=jnp.float32)


def choose_table(selector, adapter_table):
    picked = jnp.einsum(
        "e,e...->...",
        selector.astype(adapter_table.dtype),
        adapter_table,
        preferred_element_type=jnp.float32,
    )
    return picked.astype(adapter_table.dtype)


def rms_forward(rows_in):
    inverse = lax.rsqrt(jnp.mean(rows_in * rows_in, axis=-1, keepdims=True) + rms_epsilon)
    return (rows_in * inverse, inverse)


def rms_backward(grad_rows, normed, inverse, gain_row):
    scaled = grad_rows * gain_row
    return inverse * (scaled - normed * jnp.mean(scaled * normed, axis=-1, keepdims=True))


def rotation_tables(seq_length, half_dim):
    positions = jnp.arange(seq_length, dtype=jnp.float32)
    frequency = jnp.exp(-jnp.log(10000.0) * jnp.arange(half_dim, dtype=jnp.float32) / half_dim)
    angles = positions[:, None] * frequency[None, :]
    return (jnp.cos(angles)[:, None, :], jnp.sin(angles)[:, None, :])


def rotate(values, cosine, sine_table):
    middle = values.shape[-1] // 2
    first_half = values[..., :middle]
    second = values[..., middle:]
    return jnp.concatenate(
        [first_half * cosine - second * sine_table, second * cosine + first_half * sine_table],
        axis=-1,
    )


def unrotate(values, cosine, sine_table):
    middle = values.shape[-1] // 2
    first_half = values[..., :middle]
    second = values[..., middle:]
    return jnp.concatenate(
        [first_half * cosine + second * sine_table, second * cosine - first_half * sine_table],
        axis=-1,
    )


def decay_block(head_ids, first_row, block_rows, seg_all):
    key_pos = jnp.arange(seg_all.shape[0], dtype=jnp.int32)
    query_pos = first_row + jnp.arange(block_rows, dtype=jnp.int32)
    distance = query_pos[:, None] - key_pos[None, :]
    seg_query = lax.dynamic_slice_in_dim(seg_all, first_row, block_rows, 0)
    alive_mask = (distance >= 0) & (seg_query[:, None] == seg_all[None, :])
    decay_rate = jnp.log(1.0 - jnp.exp2(-5.0 - head_ids))
    weight_table = jnp.exp(
        jnp.maximum(distance, 0).astype(head_ids.dtype)[None, :, :] * decay_rate[:, None, None]
    )
    return jnp.where(alive_mask[None, :, :], weight_table, jnp.zeros_like(weight_table))


def row_slice(matrix, first_row, block_rows):
    return lax.dynamic_slice_in_dim(matrix, first_row, block_rows, 0)


def shards(
    tokens,
    cotangent,
    adapter_ids,
    segments,
    norm_attn,
    norm_mlp,
    weight_query,
    weight_key,
    weight_value,
    weight_gate,
    weight_out,
    weight_mlp_gate,
    weight_mlp_up,
    weight_mlp_down,
    adapt_attn_in,
    adapt_query_key,
    adapt_value_gate,
    adapt_out_in,
    adapt_out_back,
    adapt_mlp_in,
    adapt_mlp_hidden,
    adapt_down_in,
    adapt_down_back,
):
    local_rows = tokens[0].astype(jnp.float32)
    shard_rows = local_rows.shape[0]
    seg_all = segments[0]
    seq_length = seg_all.shape[0]
    key_scale = 1.0 / KEY_DIM**0.5
    selector = (jnp.arange(adapt_attn_in.shape[0], dtype=jnp.int32) == adapter_ids[0, 0]).astype(
        jnp.float32
    )
    attn_in = choose_table(selector, adapt_attn_in)
    query_key = choose_table(selector, adapt_query_key)
    value_gate = choose_table(selector, adapt_value_gate)
    out_in = choose_table(selector, adapt_out_in)
    out_back = choose_table(selector, adapt_out_back)
    mlp_in = choose_table(selector, adapt_mlp_in)
    mlp_hidden = choose_table(selector, adapt_mlp_hidden)
    down_in = choose_table(selector, adapt_down_in)
    down_back = choose_table(selector, adapt_down_back)
    frozen = (
        lax.all_gather(weight_query, "dp", axis=0, tiled=True),
        lax.all_gather(weight_key, "dp", axis=0, tiled=True),
        lax.all_gather(weight_value, "dp", axis=0, tiled=True),
        lax.all_gather(weight_gate, "dp", axis=0, tiled=True),
        lax.all_gather(weight_out, "dp", axis=1, tiled=True),
        lax.all_gather(weight_mlp_gate, "dp", axis=0, tiled=True),
        lax.all_gather(weight_mlp_up, "dp", axis=0, tiled=True),
        lax.all_gather(weight_mlp_down, "dp", axis=1, tiled=True),
    )
    (
        query_full,
        key_full,
        value_full,
        gate_full,
        out_full,
        mlp_gate_full,
        mlp_up_full,
        mlp_down_full,
    ) = frozen
    heads_local = query_full.shape[1] // KEY_DIM
    head_ids = (
        lax.axis_index("tensor") * heads_local + jnp.arange(heads_local, dtype=jnp.int32)
    ).astype(jnp.float32)
    cosine, sine_table = rotation_tables(seq_length, KEY_DIM // 2)
    starts = jnp.arange(seq_length // ROW_BLOCK, dtype=jnp.int32) * ROW_BLOCK
    normed_attn, inverse_attn = rms_forward(local_rows)
    attn_rows = lax.all_gather(
        (normed_attn * norm_attn).astype(jnp.bfloat16), "tensor", axis=0, tiled=True
    )
    attn_low = matmul(attn_rows, attn_in).astype(jnp.bfloat16)
    proj_query = matmul(attn_rows, query_full) + matmul(attn_low[:, :RANK], query_key[0])
    proj_key = matmul(attn_rows, key_full) + matmul(attn_low[:, RANK : 2 * RANK], query_key[1])
    proj_value = matmul(attn_rows, value_full) + matmul(
        attn_low[:, 2 * RANK : 3 * RANK], value_gate[0]
    )
    proj_gate = matmul(attn_rows, gate_full) + matmul(attn_low[:, 3 * RANK :], value_gate[1])
    queries = rotate(
        proj_query.reshape(seq_length, heads_local, KEY_DIM), cosine, sine_table
    ).astype(jnp.bfloat16)
    keys_all = (
        key_scale * rotate(proj_key.reshape(seq_length, heads_local, KEY_DIM), cosine, sine_table)
    ).astype(jnp.bfloat16)
    values_all = proj_value.reshape(seq_length, heads_local, VALUE_DIM).astype(jnp.bfloat16)

    def forward_block(first_row):
        query_block = row_slice(queries, first_row, ROW_BLOCK)
        scores = jnp.einsum(
            "qhd,khd->hqk", query_block, keys_all, preferred_element_type=jnp.float32
        )
        mixed_low = (scores * decay_block(head_ids, first_row, ROW_BLOCK, seg_all)).astype(
            jnp.bfloat16
        )
        return jnp.einsum("hqk,khd->qhd", mixed_low, values_all, preferred_element_type=jnp.float32)

    retained = lax.map(forward_block, starts).reshape(seq_length, heads_local, VALUE_DIM)
    centered = retained - jnp.mean(retained, axis=-1, keepdims=True)
    inverse_group = lax.rsqrt(jnp.mean(centered * centered, axis=-1, keepdims=True) + group_floor)
    grouped_heads = centered * inverse_group
    grouped = grouped_heads.reshape(seq_length, heads_local * VALUE_DIM)
    swished, swish_pullback = jax.vjp(jax.nn.silu, proj_gate)
    gated_low = (swished * grouped).astype(jnp.bfloat16)
    out_low = matmul(gated_low, out_in)
    out_back_wide = out_back.astype(jnp.float32)
    first_row = jnp.int32(0)
    middle_rows = local_rows + lax.psum_scatter(
        matmul(row_slice(gated_low, first_row, shard_rows * lax.axis_size("tensor")), out_full)
        + matmul_exact(
            row_slice(out_low, first_row, shard_rows * lax.axis_size("tensor")), out_back_wide
        ),
        "tensor",
        scatter_dimension=0,
        tiled=True,
    )
    normed_mlp, inverse_mlp = rms_forward(middle_rows)
    mlp_rows = lax.all_gather(
        (normed_mlp * norm_mlp).astype(jnp.bfloat16), "tensor", axis=0, tiled=True
    )
    mlp_low = matmul(mlp_rows, mlp_in).astype(jnp.bfloat16)
    proj_mlp_gate = matmul(mlp_rows, mlp_gate_full) + matmul(mlp_low[:, :RANK], mlp_hidden[0])
    proj_mlp_up = matmul(mlp_rows, mlp_up_full) + matmul(mlp_low[:, RANK:], mlp_hidden[1])
    activated, gelu_pullback = jax.vjp(partial(jax.nn.gelu, approximate=False), proj_mlp_gate)
    hidden = (activated * proj_mlp_up).astype(jnp.bfloat16)
    down_low = matmul(hidden, down_in)
    down_back_wide = down_back.astype(jnp.float32)
    first_row = jnp.int32(0)
    output_rows = middle_rows + lax.psum_scatter(
        (
            matmul(
                row_slice(hidden, first_row, lax.axis_size("tensor") * shard_rows), mlp_down_full
            )
            + matmul_exact(
                row_slice(down_low, first_row, lax.axis_size("tensor") * shard_rows), down_back_wide
            )
        ).astype(jnp.bfloat16),
        "tensor",
        scatter_dimension=0,
        tiled=True,
    ).astype(jnp.float32)
    frozen_back = (
        lax.all_gather(weight_query, "dp", axis=0, tiled=True),
        lax.all_gather(weight_key, "dp", axis=0, tiled=True),
        lax.all_gather(weight_value, "dp", axis=0, tiled=True),
        lax.all_gather(weight_gate, "dp", axis=0, tiled=True),
        lax.all_gather(weight_out, "dp", axis=1, tiled=True),
        lax.all_gather(weight_mlp_gate, "dp", axis=0, tiled=True),
        lax.all_gather(weight_mlp_up, "dp", axis=0, tiled=True),
        lax.all_gather(weight_mlp_down, "dp", axis=1, tiled=True),
    )
    (
        query_back,
        key_back,
        value_back,
        gate_back,
        out_full_back,
        mlp_gate_back,
        mlp_up_back,
        mlp_down_back,
    ) = frozen_back
    grad_output = cotangent[0].astype(jnp.float32)
    grad_mlp_out = lax.all_gather(grad_output.astype(jnp.bfloat16), "tensor", axis=0, tiled=True)
    grad_down_low = matmul(grad_mlp_out, down_back.T).astype(jnp.bfloat16)
    grad_down_back_local = matmul_exact(down_low.T, grad_mlp_out)
    grad_down_in_local = matmul(hidden.T, grad_down_low)
    grad_hidden = matmul(grad_mlp_out, mlp_down_back.T) + matmul(grad_down_low, down_in.T)
    grad_mlp_gate = gelu_pullback(grad_hidden * proj_mlp_up)[0].astype(jnp.bfloat16)
    grad_mlp_up = (grad_hidden * activated).astype(jnp.bfloat16)
    grad_mlp_low = jnp.concatenate(
        [matmul(grad_mlp_gate, mlp_hidden[0].T), matmul(grad_mlp_up, mlp_hidden[1].T)], axis=1
    )
    grad_mlp_hidden_local = jnp.stack(
        [matmul(mlp_low[:, :RANK].T, grad_mlp_gate), matmul(mlp_low[:, RANK:].T, grad_mlp_up)]
    )
    grad_mlp_in_local = matmul_exact(mlp_rows.T, grad_mlp_low)
    mlp_in_wide = mlp_in.astype(jnp.float32)
    first_row = jnp.int32(0)
    grad_middle = grad_output + rms_backward(
        lax.psum_scatter(
            (
                matmul(
                    row_slice(grad_mlp_gate, first_row, lax.axis_size("tensor") * shard_rows),
                    mlp_gate_back.T,
                )
                + matmul(
                    row_slice(grad_mlp_up, first_row, lax.axis_size("tensor") * shard_rows),
                    mlp_up_back.T,
                )
                + matmul_exact(
                    row_slice(grad_mlp_low, first_row, lax.axis_size("tensor") * shard_rows),
                    mlp_in_wide.T,
                )
            ).astype(jnp.bfloat16),
            "tensor",
            scatter_dimension=0,
            tiled=True,
        ).astype(jnp.float32),
        normed_mlp,
        inverse_mlp,
        norm_mlp,
    )
    grad_attn_out = lax.all_gather(grad_middle.astype(jnp.bfloat16), "tensor", axis=0, tiled=True)
    grad_out_low = matmul(grad_attn_out, out_back.T).astype(jnp.bfloat16)
    grad_out_back_local = matmul_exact(out_low.T, grad_attn_out)
    grad_out_in_local = matmul(gated_low.T, grad_out_low)
    grad_gated = matmul(grad_attn_out, out_full_back.T) + matmul(grad_out_low, out_in.T)
    grad_gate = swish_pullback(grad_gated * grouped)[0].astype(jnp.bfloat16)
    grad_grouped = (grad_gated * swished).reshape(seq_length, heads_local, VALUE_DIM)
    grad_retained = (
        inverse_group
        * (
            grad_grouped
            - jnp.mean(grad_grouped, axis=-1, keepdims=True)
            - grouped_heads * jnp.mean(grad_grouped * grouped_heads, axis=-1, keepdims=True)
        )
    ).astype(jnp.bfloat16)

    def backward_block(running, first_row):
        grad_keys, grad_values = running
        query_block = row_slice(queries, first_row, ROW_BLOCK)
        grad_block = row_slice(grad_retained, first_row, ROW_BLOCK)
        decay_mask = decay_block(head_ids, first_row, ROW_BLOCK, seg_all)
        scores = jnp.einsum(
            "qhd,khd->hqk", query_block, keys_all, preferred_element_type=jnp.float32
        )
        mixed_low = (scores * decay_mask).astype(jnp.bfloat16)
        grad_mixed = jnp.einsum(
            "qhd,khd->hqk", grad_block, values_all, preferred_element_type=jnp.float32
        )
        grad_scores = (grad_mixed * decay_mask).astype(jnp.bfloat16)
        grad_query_block = jnp.einsum(
            "hqk,khd->qhd", grad_scores, keys_all, preferred_element_type=jnp.float32
        )
        grad_keys = grad_keys + jnp.einsum(
            "hqk,qhd->khd", grad_scores, query_block, preferred_element_type=jnp.float32
        )
        grad_values = grad_values + jnp.einsum(
            "hqk,qhd->khd", mixed_low, grad_block, preferred_element_type=jnp.float32
        )
        return ((grad_keys, grad_values), grad_query_block)

    empty_keys = jnp.zeros((seq_length, heads_local, KEY_DIM), jnp.float32)
    empty_values = jnp.zeros((seq_length, heads_local, VALUE_DIM), jnp.float32)
    (grad_keys, grad_values), grad_queries = lax.scan(
        backward_block, (empty_keys, empty_values), starts
    )
    grad_query = (
        unrotate(grad_queries.reshape(seq_length, heads_local, KEY_DIM), cosine, sine_table)
        .reshape(seq_length, heads_local * KEY_DIM)
        .astype(jnp.bfloat16)
    )
    grad_key = (
        (key_scale * unrotate(grad_keys, cosine, sine_table))
        .reshape(seq_length, heads_local * KEY_DIM)
        .astype(jnp.bfloat16)
    )
    grad_value = grad_values.reshape(seq_length, heads_local * VALUE_DIM).astype(jnp.bfloat16)
    grad_attn_low = jnp.concatenate(
        [
            matmul(grad_query, query_key[0].T),
            matmul(grad_key, query_key[1].T),
            matmul(grad_value, value_gate[0].T),
            matmul(grad_gate, value_gate[1].T),
        ],
        axis=1,
    )
    grad_query_key_local = jnp.stack(
        [matmul(attn_low[:, :RANK].T, grad_query), matmul(attn_low[:, RANK : 2 * RANK].T, grad_key)]
    )
    grad_value_gate_local = jnp.stack(
        [
            matmul(attn_low[:, 2 * RANK : 3 * RANK].T, grad_value),
            matmul(attn_low[:, 3 * RANK :].T, grad_gate),
        ]
    )
    grad_attn_in_local = matmul_exact(attn_rows.T, grad_attn_low)
    attn_in_wide = attn_in.astype(jnp.float32)
    first_row = jnp.int32(0)
    block_rows = lax.axis_size("tensor") * shard_rows
    grad_input = grad_middle + rms_backward(
        lax.psum_scatter(
            (
                matmul(row_slice(grad_query, first_row, block_rows), query_back.T)
                + matmul(row_slice(grad_key, first_row, block_rows), key_back.T)
                + matmul(row_slice(grad_value, first_row, block_rows), value_back.T)
                + matmul(row_slice(grad_gate, first_row, block_rows), gate_back.T)
                + matmul_exact(row_slice(grad_attn_low, first_row, block_rows), attn_in_wide.T)
            ).astype(jnp.bfloat16),
            "tensor",
            scatter_dimension=0,
            tiled=True,
        ).astype(jnp.float32),
        normed_attn,
        inverse_attn,
        norm_attn,
    )

    def spread(grad_local):
        return selector.reshape((selector.shape[0],) + (1,) * grad_local.ndim) * grad_local[None]

    shared = lax.psum(
        (
            spread(grad_attn_in_local),
            spread(grad_out_back_local),
            spread(grad_mlp_in_local),
            spread(grad_down_back_local),
        ),
        ("dp", "tensor"),
    )
    split_sums = (
        lax.psum(spread(grad_query_key_local).astype(jnp.bfloat16), "dp").astype(jnp.float32),
        lax.psum(spread(grad_value_gate_local).astype(jnp.bfloat16), "dp").astype(jnp.float32),
        lax.psum(spread(grad_out_in_local).astype(jnp.bfloat16), "dp").astype(jnp.float32),
        lax.psum(spread(grad_mlp_hidden_local).astype(jnp.bfloat16), "dp").astype(jnp.float32),
        lax.psum(spread(grad_down_in_local).astype(jnp.bfloat16), "dp").astype(jnp.float32),
    )
    return (
        output_rows.astype(jnp.bfloat16)[None],
        grad_input[None],
        shared[0],
        split_sums[0],
        split_sums[1],
        split_sums[2],
        shared[1],
        shared[2],
        split_sums[3],
        split_sums[4],
        shared[3],
    )


def solution(mesh):
    in_specs = (
        P("dp", "tensor", None),
        P("dp", "tensor", None),
        P("dp", None),
        P("dp", None),
        P(),
        P(),
        P("dp", "tensor"),
        P("dp", "tensor"),
        P("dp", "tensor"),
        P("dp", "tensor"),
        P("tensor", "dp"),
        P("dp", "tensor"),
        P("dp", "tensor"),
        P("tensor", "dp"),
        P(),
        P(None, None, None, "tensor"),
        P(None, None, None, "tensor"),
        P(None, "tensor", None),
        P(),
        P(),
        P(None, None, None, "tensor"),
        P(None, "tensor", None),
        P(),
    )
    out_specs = (
        P("dp", "tensor", None),
        P("dp", "tensor", None),
        P(),
        P(None, None, None, "tensor"),
        P(None, None, None, "tensor"),
        P(None, "tensor", None),
        P(),
        P(),
        P(None, None, None, "tensor"),
        P(None, "tensor", None),
        P(),
    )
    return jax.shard_map(shards, mesh=mesh, in_specs=in_specs, out_specs=out_specs, check_vma=False)
```

profile of v0, /device:TPU:1, one launch (start us, length us, event | category | flops | bytes accessed | tf_op | source)
XLA Modules:
  0.0 1413.4 jit_solution(13757482282538517458)
XLA Ops:
  25.5 14.8 %all-gather.20.cloned.1.call-done = bf16[2048,512]{1,0:T(8,128)(2,1)} async-done(((bf16[256,512]{1,0:T(8,128)(2,1)}), bf16[2048,512]{1,0:T(8,128)(2,1)}) %all-gather.20.cloned.1.call-update) | async-done | bytes 2097168 | tf_op jit(solution)/shard_map/all_gather | solution.py:135
  40.4 82.5 %all-gather.14.cloned.1.call-done = bf16[1024,2048]{1,0:T(8,128)(2,1)} async-done(((bf16[256,2048]{1,0:T(8,128)(2,1)}), bf16[1024,2048]{1,0:T(8,128)(2,1)}) %all-gather.14.cloned.1.call-update) | async-done | bytes 4194320 | tf_op jit(solution)/shard_map/all_gather | solution.py:160
  122.9 5.4 fusion.137
  131.5 20.1 %all-gather.18.cloned.1.call-done = bf16[2048,512]{1,0:T(8,128)(2,1)} async-done(((bf16[256,512]{1,0:T(8,128)(2,1)}), bf16[2048,512]{1,0:T(8,128)(2,1)}) %all-gather.18.cloned.1.call-update) | async-done | bytes 2097168 | tf_op jit(solution)/shard_map/all_gather | solution.py:134
  151.7 5.2 fusion.136
  175.7 14.4 %all-gather.22.cloned.1.call-done = bf16[2048,1024]{1,0:T(8,128)(2,1)} async-done(((bf16[256,1024]{1,0:T(8,128)(2,1)}), bf16[2048,1024]{1,0:T(8,128)(2,1)}) %all-gather.22.cloned.1.call-update) | async-done | bytes 4194320 | tf_op jit(solution)/shard_map/all_gather | solution.py:136
  190.1 7.8 fusion.138
  201.3 21.2 %while.26 = (s32[]{:T(128)}, f32[2,512,2,512]{3,1,2,0:T(8,128)}, s32[2]{0:T(128)S(1)}, bf16[1024,2,256]{2,0,1:T(8,128)(2,1)}, bf16[1024,2,256]{2,0,1:T(8,128)(2,...) while((s32[]{:T(128)}, f32[2,512,2,512]{3,1,2,0:T(8,128)}, ...), condition=%wide.region_2.3_spmd.clone, body=%wide.region_1.2_spmd.clone.sunk | while | flops 1618477568 | bytes 11026639 | solution.py:188
  206.4 5.5 bitcast_dynamic-update-slice_fusion.2
  217.0 5.5 bitcast_dynamic-update-slice_fusion.2
  222.5 7.7 copy.84
  230.2 5.2 copy.149
  241.2 8.2 fusion.135
  253.5 14.4 %all-gather.24.cloned.1.call-done = bf16[1024,2048]{1,0:T(8,128)(2,1)} async-done(((bf16[1024,256]{1,0:T(8,128)(2,1)}), bf16[1024,2048]{1,0:T(8,128)(2,1)}) %all-gather.24.cloned.1.call-update) | async-done | bytes 4194320 | tf_op jit(solution)/shard_map/all_gather | solution.py:138
  267.8 6.4 fusion.139
  274.3 5.8 convolution_add_fusion
  281.6 142.5 %reduce-scatter.5.cloned.1.call-done = f32[256,2048]{1,0:T(8,128)} async-done(((f32[1024,2048]{1,0:T(8,128)}), f32[256,2048]{1,0:T(8,128)}) %reduce-scatter.5.cloned.1.call-update) | async-done | bytes 2097168 | tf_op jit(solution)/shard_map/reduce_scatter | solution.py:198
  433.9 73.5 %all-gather.36.cloned.1.call-done = bf16[1,1024,2048]{2,1,0:T(8,128)(2,1)} async-done(((bf16[1,256,2048]{2,1,0:T(8,128)(2,1)}), bf16[1,1024,2048]{2,1,0:T(8,128)(2,1)}) %all-gather.36.cloned.1.call-update) | async-done | bytes 4194320 | tf_op jit(solution)/shard_map/all_gather | solution.py:253
  510.7 34.9 %all-gather.32.cloned.1.call-done = bf16[1024,2048]{1,0:T(8,128)(2,1)} async-done(((bf16[1024,256]{1,0:T(8,128)(2,1)}), bf16[1024,2048]{1,0:T(8,128)(2,1)}) %all-gather.32.cloned.1.call-update) | async-done | bytes 4194320 | tf_op jit(solution)/shard_map/all_gather | solution.py:141
  545.6 10.0 fusion.41
  555.7 72.4 %all-gather.26.cloned.1.call-done = bf16[1024,2048]{1,0:T(8,128)(2,1)} async-done(((bf16[256,2048]{1,0:T(8,128)(2,1)}), bf16[1024,2048]{1,0:T(8,128)(2,1)}) %all-gather.26.cloned.1.call-update) | async-done | bytes 4194320 | tf_op jit(solution)/shard_map/all_gather | solution.py:208
  631.5 34.1 %all-gather.28.cloned.1.call-done = bf16[2048,1024]{1,0:T(8,128)(2,1)} async-done(((bf16[256,1024]{1,0:T(8,128)(2,1)}), bf16[2048,1024]{1,0:T(8,128)(2,1)}) %all-gather.28.cloned.1.call-update) | async-done | bytes 4194320 | tf_op jit(solution)/shard_map/all_gather | solution.py:139
  665.6 7.8 fusion.140
  675.9 10.8 multiply_convert_fusion.4
  688.5 15.6 %all-gather.30.cloned.1.call-done = bf16[2048,1024]{1,0:T(8,128)(2,1)} async-done(((bf16[256,1024]{1,0:T(8,128)(2,1)}), bf16[2048,1024]{1,0:T(8,128)(2,1)}) %all-gather.30.cloned.1.call-update) | async-done | bytes 4194320 | tf_op jit(solution)/shard_map/all_gather | solution.py:140
  704.1 7.7 fusion.141
  716.4 4.6 fusion.143
  725.5 5.3 add_convert_fusion.1
  731.1 76.3 %reduce-scatter.9.cloned.1.call-done = bf16[256,2048]{1,0:T(8,128)(2,1)} async-done(((bf16[1024,2048]{1,0:T(8,128)(2,1)}), bf16[256,2048]{1,0:T(8,128)(2,1)}) %reduce-scatter.9.cloned.1.call-update) | async-done | bytes 1048592 | tf_op jit(solution)/shard_map/reduce_scatter | solution.py:270
  814.1 4.8 copy.94
  822.2 72.7 %all-gather.34.cloned.1.call-done = bf16[1024,2048]{1,0:T(8,128)(2,1)} async-done(((bf16[256,2048]{1,0:T(8,128)(2,1)}), bf16[1024,2048]{1,0:T(8,128)(2,1)}) %all-gather.34.cloned.1.call-update) | async-done | bytes 4194320 | tf_op jit(solution)/shard_map/all_gather | solution.py:293
  894.9 8.0 fusion.145
  911.6 5.4 copy.93
  925.6 46.5 %while.27 = (s32[]{:T(128)}, f32[1024,2,256]{0,2,1:T(8,128)}, f32[1024,2,512]{0,2,1:T(8,128)}, f32[2,512,2,256]{3,1,0,2:T(8,128)}, s32[2]{0:T(128)S(1)}, /*index...) while((s32[]{:T(128)}, f32[1024,2,256]{0,2,1:T(8,128)}, ...), condition=%wide.region_13.14_spmd.clone, body=%wide.region_12.13_spmd.clone.sunk | while | flops 3773301248 | bytes 37242648 | solution.py:335
  939.6 6.6 bitcast_add_fusion.5
  962.4 7.9 bitcast_add_fusion.5
  993.4 10.9 fusion.149
  1004.3 6.8 fusion.148
  1011.1 5.7 fusion.146
  1016.9 5.6 fusion.147
  1022.5 15.4 %add_convert_fusion = bf16[1024,2048]{1,0:T(8,128)(2,1)} fusion(f32[1024,2048]{1,0:T(8,128)} %fusion.149, f32[1024,2048]{1,0:T(8,128)} %fusion.148, f32[1024,2048]{1,0:T(8,128)} %fusion.146, f32[1024,2048]{1,0:T(8,128)} %fusion.147, bf16[1,2048,64]{2,1,0:T(8,128)(2,1)S(1)} %copy-done.41, f32[1024,16]{0,1:T(8,128)S(1)} %copy-done.61, ...), kind=kOutput, calls=%fused_computation.42 | convolution fusion | flops 1621295104 | bytes 38273024 | tf_op jit(solution)/shard_map/dot_general | solution.py:24
  1040.0 6.7 fusion.142
  1046.7 5.6 add_convert_fusion.2
  1077.5 54.0 %reduce-scatter.11.cloned.1.call-done = bf16[256,2048]{1,0:T(8,128)(2,1)} async-done(((bf16[1024,2048]{1,0:T(8,128)(2,1)}), bf16[256,2048]{1,0:T(8,128)(2,1)}) %reduce-scatter.11.cloned.1.call-update) | async-done | bytes 1048592 | tf_op jit(solution)/shard_map/reduce_scatter | solution.py:372
  1133.3 77.8 %reduce-scatter.7.cloned.1.call-done = bf16[256,2048]{1,0:T(8,128)(2,1)} async-done(((bf16[1024,2048]{1,0:T(8,128)(2,1)}), bf16[256,2048]{1,0:T(8,128)(2,1)}) %reduce-scatter.7.cloned.1.call-update) | async-done | bytes 1048592 | tf_op jit(solution)/shard_map/reduce_scatter | solution.py:219
  1211.1 5.4 fusion.57
  1216.6 181.7 %all-reduce.5.cloned.1.call-done = (f32[8,2048,64]{1,2,0:T(8,128)}, f32[8,16,2048]{2,1,0:T(8,128)}, f32[8,2048,32]{1,2,0:T(8,128)}, f32[8,16,2048]{2,1,0:T(8,128)}) async-done(((f32[8,2048,64]{1,2,0:T(8,128)}, f32[8,16,2048]{2,1,0:T(8,128)}, f32[8,2048,32]{1,2,0:T(8,128)}, f32[8,16,2048]{2,1,0:T(8,128)}), (f32[8,2048,64]{1,2,0:T(8,128)}, f32[8,16,2048]{2,1,0:T(8,128)}, f32[8,2048,32]{1,2,0:T(8,128)}, ...) | async-done | bytes 8388624 | tf_op jit(solution)/shard_map/psum | solution.py:392
  1398.3 4.8 copy.210
  (382 shorter events, 198.5 us)
Async XLA Ops:
  7.2 8.7 copy-start
  7.2 33.2 %all-gather.20.cloned.1.call-start = ((), (), s32[]{:S(2)}) async-start(), calls=%async_computation.7 | async-start | bytes 2359296 | tf_op jit(solution)/shard_map/all_gather | solution.py:135
  7.9 114.9 %all-gather.14.cloned.1.call-start = ((), (), s32[]{:S(2)}) async-start(), calls=%async_computation.4 | async-start | bytes 5242880 | tf_op jit(solution)/shard_map/all_gather | solution.py:160
  12.6 10.3 copy-start.77
  12.7 139.0 %all-gather.18.cloned.1.call-start = ((), (), s32[]{:S(2)}) async-start(), calls=%async_computation.6 | async-start | bytes 2359296 | tf_op jit(solution)/shard_map/all_gather | solution.py:134
  13.4 176.7 %all-gather.22.cloned.1.call-start = ((), (), s32[]{:S(2)}) async-start(), calls=%async_computation.8 | async-start | bytes 4718592 | tf_op jit(solution)/shard_map/all_gather | solution.py:136
  14.0 227.2 %all-gather.16.cloned.1.call-start = ((), (), s32[]{:S(2)}) async-start(), calls=%async_computation.5 | async-start | bytes 4718592 | tf_op jit(solution)/shard_map/all_gather | solution.py:137
  14.6 253.3 %all-gather.24.cloned.1.call-start = ((), (), s32[]{:S(2)}) async-start(), calls=%async_computation.9 | async-start | bytes 4718592 | tf_op jit(solution)/shard_map/all_gather | solution.py:138
  15.1 409.0 %reduce-scatter.5.cloned.1.call-start = ((), (), s32[]{:S(2)}) async-start(), calls=%async_computation.10 | async-start | bytes 10485760 | tf_op jit(solution)/shard_map/reduce_scatter | solution.py:198
  18.2 110.1 %copy-start.40 = (bf16[1,2048,64]{2,1,0:T(8,128)(2,1)}, bf16[1,2048,64]{2,1,0:T(8,128)(2,1)S(1)}, u32[]{:S(2)}) copy-start(bf16[1,2048,64]{2,1,0:T(8,128)(2,1)S(1)} %copy.106) | copy-start | bytes 786436
  18.5 111.2 %copy-start.71 = (bf16[1,2,16,512]{3,2,1,0:T(8,128)(2,1)}, bf16[1,2,16,512]{3,2,1,0:T(8,128)(2,1)S(1)}, u32[]{:S(2)}) copy-start(bf16[1,2,16,512]{3,2,1,0:T(8,128)(2,1)S(1)} %copy.179) | copy-start | bytes 98308
  20.4 151.3 %copy-start.34 = (f32[1024,128]{1,0:T(8,128)}, f32[1024,128]{1,0:T(8,128)S(1)}, u32[]{:S(2)}) copy-start(f32[1024,128]{1,0:T(8,128)S(1)} %get-tuple-element.331) | copy-start | bytes 1572868
  20.5 151.3 %copy-start.37 = (f32[1024,128]{1,0:T(8,128)}, f32[1024,128]{1,0:T(8,128)S(1)}, u32[]{:S(2)}) copy-start(f32[1024,128]{1,0:T(8,128)S(1)} %get-tuple-element.332) | copy-start | bytes 1572868
  129.7 119.7 %copy-start.46 = (bf16[1024,64]{0,1:T(8,128)(2,1)}, bf16[1024,64]{0,1:T(8,128)(2,1)S(1)}, u32[]{:S(2)}) copy-start(bf16[1024,64]{0,1:T(8,128)(2,1)S(1)} %convolution_convert_fusion) | copy-start | bytes 393220
  253.0 21.2 %copy-start.17 = (bf16[1024,1024]{0,1:T(8,128)(2,1)}, bf16[1024,1024]{0,1:T(8,128)(2,1)S(1)}, u32[]{:S(2)}) copy-start(bf16[1024,1024]{0,1:T(8,128)(2,1)S(1)} %get-tuple-element.333) | copy-start | bytes 6291460
  253.5 20.8 %copy-start.58 = (f32[1024,16]{0,1:T(8,128)}, f32[1024,16]{0,1:T(8,128)S(1)}, u32[]{:S(2)}) copy-start(f32[1024,16]{0,1:T(8,128)S(1)} %fusion.87) | copy-start | bytes 196612
  253.5 20.8 %copy-start.67 = (bf16[1,16,2048]{2,0,1:T(2,128)(2,1)S(1)}, bf16[1,16,2048]{2,0,1:T(2,128)(2,1)}, u32[]{:S(2)}) copy-start(bf16[1,16,2048]{2,0,1:T(2,128)(2,1)} %fusion.74) | copy-start | bytes 196612
  280.0 144.1 %copy-start.2 = (bf16[1,256,2048]{2,1,0:T(8,128)(2,1)S(1)}, bf16[1,256,2048]{2,1,0:T(8,128)(2,1)}, u32[]{:S(2)}) copy-start(bf16[1,256,2048]{2,1,0:T(8,128)(2,1)} %param.27) | copy-start | bytes 3145732
  280.1 146.2 %copy-start.78 = (f32[2048]{0:T(1024)S(1)}, f32[2048]{0:T(1024)}, u32[]{:S(2)}) copy-start(f32[2048]{0:T(1024)} %param.32) | copy-start | bytes 24580
  280.1 227.3 %all-gather.36.cloned.1.call-start = ((), (), s32[]{:S(2)}) async-start(), calls=%async_computation.19 | async-start | bytes 5242880 | tf_op jit(solution)/shard_map/all_gather | solution.py:253
  280.8 264.8 %all-gather.32.cloned.1.call-start = ((), (), s32[]{:S(2)}) async-start(), calls=%async_computation.14 | async-start | bytes 4718592 | tf_op jit(solution)/shard_map/all_gather | solution.py:141
  281.6 147.7 %copy-start.66 = (bf16[8,2,16,1024]{3,2,1,0:T(8,128)(2,1)S(1)}, bf16[8,2,16,1024]{3,2,1,0:T(8,128)(2,1)}, u32[]{:S(2)}) copy-start(bf16[8,2,16,1024]{3,2,1,0:T(8,128)(2,1)} %param.47) | copy-start | bytes 1572868
  281.6 346.5 %all-gather.26.cloned.1.call-start = ((), (), s32[]{:S(2)}) async-start(), calls=%async_computation.11 | async-start | bytes 5242880 | tf_op jit(solution)/shard_map/all_gather | solution.py:208
  427.7 237.9 %all-gather.28.cloned.1.call-start = ((), (), s32[]{:S(2)}) async-start(), calls=%async_computation.12 | async-start | bytes 4718592 | tf_op jit(solution)/shard_map/all_gather | solution.py:139
  428.4 275.7 %all-gather.30.cloned.1.call-start = ((), (), s32[]{:S(2)}) async-start(), calls=%async_computation.13 | async-start | bytes 4718592 | tf_op jit(solution)/shard_map/all_gather | solution.py:140
  429.0 378.4 %reduce-scatter.9.cloned.1.call-start = ((), (), s32[]{:S(2)}) async-start(), calls=%async_computation.16 | async-start | bytes 5242880 | tf_op jit(solution)/shard_map/reduce_scatter | solution.py:270
  432.2 242.0 %copy-start.48 = (bf16[1,1024,16]{2,1,0:T(8,128)(2,1)}, bf16[1,1024,16]{2,1,0:T(8,128)(2,1)S(1)}, u32[]{:S(2)}) copy-start(bf16[1,1024,16]{2,1,0:T(8,128)(2,1)S(1)} %copy.127) | copy-start | bytes 98308
  433.9 121.8 %copy-start.63 = (bf16[1,16,2048]{2,0,1:T(2,128)(2,1)}, bf16[1,16,2048]{2,0,1:T(2,128)(2,1)S(1)}, u32[]{:S(2)}) copy-start(bf16[1,16,2048]{2,0,1:T(2,128)(2,1)S(1)} %fusion.70) | copy-start | bytes 196612
  675.9 10.8 copy-start.43
  730.9 76.6 %copy-start.79 = (f32[2048]{0:T(1024)S(1)}, f32[2048]{0:T(1024)}, u32[]{:S(2)}) copy-start(f32[2048]{0:T(1024)} %param.32) | copy-start | bytes 24580
  730.9 76.6 %copy-start.84 = (f32[256]{0:T(256)S(1)}, f32[256]{0:T(256)}, u32[]{:S(2)}) copy-start(f32[256]{0:T(256)} %copy-done.83) | copy-start | bytes 3076
  730.9 79.2 %copy-start.21 = (bf16[1,256,2048]{2,1,0:T(8,128)(2,1)S(1)}, bf16[1,256,2048]{2,1,0:T(8,128)(2,1)}, u32[]{:S(2)}) copy-start(bf16[1,256,2048]{2,1,0:T(8,128)(2,1)} %param.28) | copy-start | bytes 3145732
  730.9 164.0 %all-gather.34.cloned.1.call-start = ((), (), s32[]{:S(2)}) async-start(), calls=%async_computation.17 | async-start | bytes 5242880 | tf_op jit(solution)/shard_map/all_gather | solution.py:293
  813.4 255.2 %all-reduce.7.cloned.1.call-start = ((), (), s32[]{:S(2)}) async-start(), calls=%async_computation.21 | async-start | bytes 3670016 | tf_op jit(solution)/shard_map/psum | solution.py:402
  822.2 80.7 %copy-start.68 = (bf16[1,16,2048]{2,0,1:T(2,128)(2,1)S(1)}, bf16[1,16,2048]{2,0,1:T(2,128)(2,1)}, u32[]{:S(2)}) copy-start(bf16[1,16,2048]{2,0,1:T(2,128)(2,1)} %fusion.74) | copy-start | bytes 196612
  894.9 9.2 copy-start.11
  992.9 138.6 %reduce-scatter.11.cloned.1.call-start = ((), (), s32[]{:S(2)}) async-start(), calls=%async_computation.18 | async-start | bytes 5242880 | tf_op jit(solution)/shard_map/reduce_scatter | solution.py:372
  993.4 10.9 copy-start.91
  1038.0 173.2 %reduce-scatter.7.cloned.1.call-start = ((), (), s32[]{:S(2)}) async-start(), calls=%async_computation.15 | async-start | bytes 5242880 | tf_op jit(solution)/shard_map/reduce_scatter | solution.py:219
  1052.3 345.9 %all-reduce.5.cloned.1.call-start = ((), (), s32[]{:S(2)}) async-start(), calls=%async_computation.20 | async-start | bytes 16777216 | tf_op jit(solution)/shard_map/psum | solution.py:392
  1068.5 63.0 %copy-start.3 = (bf16[1,256,2048]{2,1,0:T(8,128)(2,1)S(1)}, bf16[1,256,2048]{2,1,0:T(8,128)(2,1)}, u32[]{:S(2)}) copy-start(bf16[1,256,2048]{2,1,0:T(8,128)(2,1)} %param.27) | copy-start | bytes 3145732
  1068.5 63.0 %copy-start.82 = (f32[2048]{0:T(1024)S(1)}, f32[2048]{0:T(1024)}, u32[]{:S(2)}) copy-start(f32[2048]{0:T(1024)} %param.31) | copy-start | bytes 24580
  1068.6 63.0 %copy-start.88 = (f32[256]{0:T(256)S(1)}, f32[256]{0:T(256)}, u32[]{:S(2)}) copy-start(f32[256]{0:T(256)} %copy-done.87) | copy-start | bytes 3076
  1068.6 142.5 %copy-start.22 = (bf16[1,256,2048]{2,1,0:T(8,128)(2,1)S(1)}, bf16[1,256,2048]{2,1,0:T(8,128)(2,1)}, u32[]{:S(2)}) copy-start(bf16[1,256,2048]{2,1,0:T(8,128)(2,1)} %param.28) | copy-start | bytes 3145732
  1068.6 142.5 %copy-start.25 = (bf16[256,2048]{1,0:T(8,128)(2,1)S(1)}, bf16[256,2048]{1,0:T(8,128)(2,1)}, u32[]{:S(2)}) copy-start(bf16[256,2048]{1,0:T(8,128)(2,1)} %reduce-scatter.9.cloned.1.call-done) | copy-start | bytes 3145732
  1068.6 142.5 %copy-start.80 = (f32[2048]{0:T(1024)S(1)}, f32[2048]{0:T(1024)}, u32[]{:S(2)}) copy-start(f32[2048]{0:T(1024)} %param.32) | copy-start | bytes 24580
  1068.6 142.5 %copy-start.85 = (f32[256]{0:T(256)S(1)}, f32[256]{0:T(256)}, u32[]{:S(2)}) copy-start(f32[256]{0:T(256)} %copy-done.83) | copy-start | bytes 3076
  1068.6 142.5 %copy-start.90 = (f32[256]{0:T(256)S(1)}, f32[256]{0:T(256)}, u32[]{:S(2)}) copy-start(f32[256]{0:T(256)} %copy-done.89) | copy-start | bytes 3076
  (72 other events, 316.0 us)
Sparse Core Ops, SparseCore 0:
  9.9 30.3 all-gather.19
  42.5 80.3 all-gather.13
  124.8 26.8 all-gather.17
  153.4 36.7 all-gather.21
  191.9 36.7 all-gather.15
  230.4 37.4 all-gather.23
  280.2 143.8 reduce-scatter.4
  425.7 81.6 all-gather.35
  509.2 36.3 all-gather.31
  547.6 80.3 all-gather.25
  629.9 35.6 all-gather.27
  667.4 36.7 all-gather.29
  731.0 76.3 reduce-scatter.8
  813.6 81.2 all-gather.33
  993.0 58.7 all-reduce.6
  1054.5 76.9 reduce-scatter.10
  1133.8 77.2 reduce-scatter.6
  1218.2 180.0 all-reduce.4
where the time goes:
time: 1420 us; the launch traced here: 1410 us
  waiting for transfers between devices  987 us (70%)
  matrix products  257 us (18%)
  other arithmetic  75.6 us (5%)
  local copies, waits for them, and re-layouts  67.7 us (5%)
  between operations  16.3 us (1%)
    psum x1, waiting for transfers between devices, shards(): lax.psum((spread(grad_attn_in_local), spread(grad_out_back_local), spread...  182 us
    dot_general x44, matrix products, matmul(): return jnp.dot(left_side, right_side, preferred_element_type=jnp.float32)  160 us
    reduce_scatter x1, waiting for transfers between devices, shards(): lax.psum_scatter(matmul(row_slice(gated_low, first_row, shard_rows * lax....  142 us
    all_gather x1, waiting for transfers between devices, shards(): lax.all_gather((normed_attn * norm_attn).astype(jnp.bfloat16), 'tensor',...  82.5 us
    reduce_scatter x1, waiting for transfers between devices, shards(): lax.psum_scatter((matmul(row_slice(hidden, first_row, lax.axis_size('tens...  77.8 us
    reduce_scatter x1, waiting for transfers between devices, shards(): lax.psum_scatter((matmul(row_slice(grad_mlp_gate, first_row, lax.axis_siz...  76.3 us
    all_gather x1, waiting for transfers between devices, shards(): lax.all_gather(grad_output.astype(jnp.bfloat16), 'tensor', axis=0, tiled=...  73.5 us
    all_gather x1, waiting for transfers between devices, shards(): lax.all_gather(grad_middle.astype(jnp.bfloat16), 'tensor', axis=0, tiled=...  72.7 us
  transfers between devices with their start and end apart: 18, of which 16 were waited for; matrix products, arithmetic and copies ran while one was open for 17% of the time, Pallas kernels for 0%

commit v1 on v0

v1 whole, which is shorter than its diff:
```python
from functools import partial

import jax
import jax.numpy as jnp
from jax import lax
from jax.experimental import pallas as pl
from jax.experimental.pallas import tpu as pltpu
from jax.sharding import PartitionSpec as P

KEY_DIM = 256
VALUE_DIM = 512
RANK = 16
HALF = KEY_DIM // 2

rms_epsilon = 1e-06
group_floor = 1.0
BF = jnp.bfloat16
F32 = jnp.float32


def dot(a, b):
    return jnp.dot(a, b, preferred_element_type=F32)


def dot_nt(a, b):
    return lax.dot_general(a, b, (((1,), (1,)), ((), ())), preferred_element_type=F32)


def dot_tn(a, b):
    return lax.dot_general(a, b, (((0,), (0,)), ((), ())), preferred_element_type=F32)


def aligned(start, size):
    return pl.ds(pl.multiple_of(start, size), size)


def params(mib):
    return pltpu.CompilerParams(
        vmem_limit_bytes=mib << 20, dimension_semantics=("arbitrary",)
    )


def estimate(flops, moved):
    return pl.CostEstimate(flops=1, bytes_accessed=1, transcendentals=0)


def full(shape):
    return pl.BlockSpec(shape, lambda *_: (0,) * len(shape))


def in_hbm(*arrays):
    return [pltpu.with_memory_space_constraint(array, pltpu.HBM) for array in arrays]


def smem():
    return pl.BlockSpec(memory_space=pltpu.SMEM)


def columns(refs, ids):
    count = ids.shape[0]
    width = refs[0].shape[1] // count
    if count == 1:
        return all_rows(refs)
    return jnp.concatenate(
        [
            jnp.concatenate([ref[:, aligned(ids[i] * width, width)] for i in range(count)], axis=1)
            for ref in refs
        ],
        axis=0,
    )


def all_rows(refs):
    return refs[0][...] if len(refs) == 1 else jnp.concatenate([ref[...] for ref in refs], axis=0)


def low_rows(low_in, refs):
    return jnp.concatenate([dot_nt(low_in, ref[...]) for ref in refs], axis=1)


def whole(arrays):
    return [full(array.shape) for array in arrays]


def row_count(arrays):
    return sum(array.shape[0] for array in arrays)


def stacked(refs):
    return jnp.concatenate([w[s] for w in refs for s in range(w.shape[0])], axis=0)


def rotated(values, cosine, sine_table):
    first = values[:, :HALF]
    second = values[:, HALF:]
    return jnp.concatenate(
        [first * cosine - second * sine_table, second * cosine + first * sine_table], axis=1
    )


def unrotated(values, cosine, sine_table):
    first = values[:, :HALF]
    second = values[:, HALF:]
    return jnp.concatenate(
        [first * cosine + second * sine_table, second * cosine - first * sine_table], axis=1
    )


def norm_kernel(x, gain, out):
    rows = x[...].astype(F32)
    inverse = lax.rsqrt(jnp.mean(rows * rows, axis=1, keepdims=True) + rms_epsilon)
    out[...] = (rows * inverse * gain[...]).astype(BF)


def norm_rows(x, gain):
    return pl.pallas_call(
        norm_kernel,
        out_shape=jax.ShapeDtypeStruct(x.shape, BF),
        compiler_params=pltpu.CompilerParams(vmem_limit_bytes=24 << 20),
        name="norm_rows",
    )(x, gain)


def query_key_kernel(parts, ids, chunks, low_in, low_out, cosine, sine_table, *refs):
    act, pieces, (out, low) = refs[:parts], refs[parts:-2], refs[-2:]
    n = pl.program_id(0)

    @pl.when(n == 0)
    def _():
        low[...] = low_rows(low_in[...], act).astype(BF)

    product = dot(columns(act, ids), stacked(pieces)) + dot_tn(low[...], low_out[...])
    scale = jnp.where(n >= pl.num_programs(0) // 2, 1.0 / KEY_DIM**0.5, 1.0)
    size = out.shape[0] // chunks.shape[0]
    for j in range(chunks.shape[0]):
        at = aligned(chunks[j] * size, size)
        rows = slice(j * size, (j + 1) * size)
        out[rows, :] = (scale * rotated(product[rows], cosine[at, :], sine_table[at, :])).astype(BF)


def piece_specs(pieces, width):
    return [
        pl.BlockSpec((w.shape[0], w.shape[1], width), lambda n: (0, 0, n)) for w in pieces
    ]


def project_query_key(ids, chunks, act, low_in, low_out, cosine, sine_table, pieces):
    rows, depth = row_count(act), act[0].shape[1]
    width = pieces[0].shape[2]
    block = KEY_DIM
    return pl.pallas_call(
        partial(query_key_kernel, len(act)),
        grid=(width // block,),
        in_specs=[smem(), smem(), full(low_in.shape),
                  pl.BlockSpec((low_out.shape[0], block), lambda n: (0, n)),
                  full(cosine.shape), full(cosine.shape)] + whole(act)
        + piece_specs(pieces, block),
        out_specs=[pl.BlockSpec((rows, block), lambda n: (0, n)),
                   full((low_in.shape[0], rows))],
        out_shape=[jax.ShapeDtypeStruct((rows, width), BF),
                   jax.ShapeDtypeStruct((low_in.shape[0], rows), BF)],
        compiler_params=params(40),
        cost_estimate=estimate(2 * rows * depth * width, 2 * depth * width + 8 * rows * depth),
        name="project_query_key",
    )(ids, chunks, low_in, low_out, cosine, sine_table, *act, *pieces)


def project_kernel(parts, ids, low, low_out, *refs):
    act, pieces, out = refs[:parts], refs[parts:-1], refs[-1]
    product = dot(columns(act, ids), stacked(pieces)) + dot_tn(low[...], low_out[...])
    out[...] = product.astype(out.dtype)


def project(ids, act, low, low_out, pieces, kind):
    rows, depth = row_count(act), act[0].shape[1]
    width = pieces[0].shape[2]
    block = 256
    return pl.pallas_call(
        partial(project_kernel, len(act)),
        grid=(width // block,),
        in_specs=[smem(), full(low.shape),
                  pl.BlockSpec((low_out.shape[0], block), lambda n: (0, n))]
        + whole(act) + piece_specs(pieces, block),
        out_specs=pl.BlockSpec((rows, block), lambda n: (0, n)),
        out_shape=jax.ShapeDtypeStruct((rows, width), kind),
        compiler_params=params(40),
        cost_estimate=estimate(2 * rows * depth * width, 2 * depth * width + 8 * rows * depth),
        name="project",
    )(ids, low, low_out, *act, *pieces)


def decay_factors(rate, size):
    down = lax.broadcasted_iota(jnp.int32, (size, 1), 0).astype(F32)
    across = lax.broadcasted_iota(jnp.int32, (1, size), 1).astype(F32)
    return down, across


def retention_kernel(spots, rates, seg_col, seg_row, q, k, v, gate, out, nrm, inverse):
    rate = rates[pl.program_id(0)]
    count = spots.shape[0]
    size = q.shape[0] // count
    down, across = decay_factors(rate, size)
    row_factor = jnp.exp(rate * down)
    for i in range(count):
        here = aligned(spots[i] * size, size)
        query = q[here, :]
        seg_here = seg_col[i * size:(i + 1) * size, :]
        total = jnp.zeros((size, v.shape[1]), F32)
        for j in range(i + 1):
            there = aligned(spots[j] * size, size)
            column_factor = jnp.exp(rate * ((i - j) * size - across))
            alive = seg_here == seg_row[:, j * size:(j + 1) * size]
            if i == j:
                alive = alive & (down >= across)
            scores = dot_nt(query, k[there, :])
            mixed = jnp.where(alive, scores * row_factor * column_factor, 0.0).astype(BF)
            total = total + dot(mixed, v[there, :])
        centered = total - jnp.mean(total, axis=1, keepdims=True)
        scale = lax.rsqrt(jnp.mean(centered * centered, axis=1, keepdims=True) + group_floor)
        normed = centered * scale
        level = gate[here, :]
        out[here, :] = (level / (1.0 + jnp.exp(-level)) * normed).astype(BF)
        nrm[here, :] = normed.astype(nrm.dtype)
        inverse[0, here, :] = jnp.broadcast_to(scale, (size, 128))


def retention(spots, rates, seg_col, seg_row, qk, v, gate):
    rows = qk.shape[0]
    heads = v.shape[1] // VALUE_DIM
    return pl.pallas_call(
        retention_kernel,
        grid=(heads,),
        in_specs=[smem(), smem(), full(seg_col.shape), full(seg_row.shape),
                  pl.BlockSpec((rows, KEY_DIM), lambda h: (0, h)),
                  pl.BlockSpec((rows, KEY_DIM), lambda h: (0, h + heads)),
                  pl.BlockSpec((rows, VALUE_DIM), lambda h: (0, h)),
                  pl.BlockSpec((rows, VALUE_DIM), lambda h: (0, h))],
        out_specs=[pl.BlockSpec((rows, VALUE_DIM), lambda h: (0, h)),
                   pl.BlockSpec((rows, VALUE_DIM), lambda h: (0, h)),
                   pl.BlockSpec((1, rows, 128), lambda h: (h, 0, 0))],
        out_shape=[jax.ShapeDtypeStruct(v.shape, BF), jax.ShapeDtypeStruct(v.shape, F32),
                   jax.ShapeDtypeStruct((heads, rows, 128), F32)],
        compiler_params=params(40),
        cost_estimate=estimate(2 * rows * rows * 768 * heads, 30 << 20),
        name="retention",
    )(spots, rates, seg_col, seg_row, qk, qk, v, gate)


def fold_kernel(ids, act, low_in, low_out, *refs):
    pieces, (outs, low) = refs[:-5], (refs[-5:-1], refs[-1])
    step = pl.program_id(0)
    subs = pl.num_programs(0)
    width = pieces[0].shape[2]
    size = outs[0].shape[0]

    @pl.when(step == 0)
    def _():
        low[...] = dot_nt(low_in[...], act[...])

    extra = low[...].astype(BF)
    rows = act[...]
    for i, piece in enumerate(pieces):
        at = aligned(ids[i * subs + step] * width, width)
        product = (dot(rows, piece[0]) + dot_tn(extra, low_out[:, at])).astype(BF)
        for j, out in enumerate(outs):
            out[:, at] = product[j * size:(j + 1) * size]


def fold(ids, act, low_in, low_out, pieces):
    rows, depth = act.shape
    subs = pieces[0].shape[0]
    width = low_out.shape[1]
    return pl.pallas_call(
        fold_kernel,
        grid=(subs,),
        in_specs=[smem(), full(act.shape), full(low_in.shape), full(low_out.shape)]
        + [pl.BlockSpec((1,) + w.shape[1:], lambda s: (s, 0, 0)) for w in pieces],
        out_specs=[full((rows // 4, width))] * 4 + [full((low_in.shape[0], rows))],
        out_shape=[jax.ShapeDtypeStruct((rows // 4, width), BF)] * 4
        + [jax.ShapeDtypeStruct((low_in.shape[0], rows), F32)],
        compiler_params=params(48),
        cost_estimate=estimate(2 * rows * depth * width, 2 * depth * width + 4 * rows * depth),
        name="fold",
    )(ids, act, low_in, low_out, *pieces)


def join_kernel(x, part0, part1, part2, gain, middle, normed):
    rows = x[...].astype(F32) + (
        part0[...].astype(F32) + part1[...].astype(F32) + part2[...].astype(F32)
    )
    inverse = lax.rsqrt(jnp.mean(rows * rows, axis=1, keepdims=True) + rms_epsilon)
    middle[...] = rows
    normed[...] = (rows * inverse * gain[...]).astype(BF)


def join_rows(x, parts, gain):
    return pl.pallas_call(
        join_kernel,
        out_shape=[jax.ShapeDtypeStruct(x.shape, F32), jax.ShapeDtypeStruct(x.shape, BF)],
        compiler_params=pltpu.CompilerParams(vmem_limit_bytes=24 << 20),
        name="join_rows",
    )(x, *parts, gain)


def rms_back_kernel(rows_in, grad_in, part0, part1, part2, gain, out, out_low):
    rows = rows_in[...].astype(F32)
    inverse = lax.rsqrt(jnp.mean(rows * rows, axis=1, keepdims=True) + rms_epsilon)
    normed = rows * inverse
    scaled = gain[...] * (
        part0[...].astype(F32) + part1[...].astype(F32) + part2[...].astype(F32)
    )
    result = grad_in[...].astype(F32) + inverse * (
        scaled - normed * jnp.mean(scaled * normed, axis=1, keepdims=True)
    )
    out[...] = result
    out_low[...] = result.astype(BF)


def rms_back(rows_in, grad_in, parts, gain, begin, count):
    width = rows_in.shape[1]
    size = 128
    block = lambda skip: pl.BlockSpec((size, width), lambda i: (i + skip // size, 0))
    skips = (begin,) * 4 + (0,)
    return pl.pallas_call(
        rms_back_kernel,
        grid=(count // size,),
        in_specs=[block(skip) for skip in skips] + [full(gain.shape)],
        out_specs=[block(0)] * 2,
        out_shape=[jax.ShapeDtypeStruct((count, width), F32),
                   jax.ShapeDtypeStruct((count, width), BF)],
        compiler_params=params(24),
        name="rms_back",
    )(rows_in, grad_in, *parts, gain)


def hidden_grad_kernel(parts, ids, low_back, low_in, *refs):
    act, pieces, (out, low) = refs[:parts], refs[parts:-2], refs[-2:]

    @pl.when(pl.program_id(0) == 0)
    def _():
        low[...] = low_rows(low_back[...], act).astype(BF)

    weights = jnp.concatenate([w[s] for w in pieces for s in range(w.shape[0])], axis=1)
    out[...] = dot_nt(columns(act, ids), weights) + dot_tn(low[...], low_in[...])


def hidden_grad(ids, act, low_back, low_in, pieces):
    rows, depth = row_count(act), act[0].shape[1]
    width = pieces[0].shape[1]
    block = 256
    return pl.pallas_call(
        partial(hidden_grad_kernel, len(act)),
        grid=(width // block,),
        in_specs=[smem(), full(low_back.shape),
                  pl.BlockSpec((low_in.shape[0], block), lambda n: (0, n))]
        + whole(act) + [pl.BlockSpec((w.shape[0], block, w.shape[2]), lambda n: (0, n, 0)) for w in pieces],
        out_specs=[pl.BlockSpec((rows, block), lambda n: (0, n)),
                   full((low_back.shape[0], rows))],
        out_shape=[jax.ShapeDtypeStruct((rows, width), F32),
                   jax.ShapeDtypeStruct((low_back.shape[0], rows), BF)],
        compiler_params=params(40),
        cost_estimate=estimate(2 * rows * depth * width, 2 * depth * width + 8 * rows * depth),
        name="hidden_grad",
    )(ids, low_back, low_in, *act, *pieces)


def mlp_kernel(parts, count, ids, low_in, gate_out, up_out, down_in, grad, grad_low, *refs):
    act, refs = refs[:parts], refs[parts:]
    gate_pieces, up_pieces = refs[:count], refs[count:2 * count]
    hid, dgate, dup, low, lows, grad_hidden, grad_down = refs[2 * count:]

    @pl.when(pl.program_id(0) == 0)
    def _():
        low[...] = low_rows(low_in[...], act).astype(BF)
        lows[...] = jnp.zeros(lows.shape, F32)

    rows = columns(act, ids)
    extra = low[...]
    gate = dot(rows, stacked(gate_pieces)) + dot_tn(extra, gate_out[...])
    up = dot(rows, stacked(up_pieces)) + dot_tn(extra, up_out[...])
    chance = 0.5 * (1.0 + lax.erf(gate * (0.5**0.5)))
    active = gate * chance
    slope = chance + gate * (jnp.exp(-0.5 * gate * gate) * 0.3989422804014327)
    hidden = (active * up).astype(BF)
    back = grad[...]
    back_gate = (back * up * slope).astype(BF)
    back_up = (back * active).astype(BF)
    hid[...] = hidden
    dgate[...] = back_gate
    dup[...] = back_up
    lows[:RANK, :] += dot_nt(down_in[...], hidden)
    lows[RANK:, :] += dot_nt(gate_out[...], back_gate) + dot_nt(up_out[...], back_up)
    grad_hidden[:RANK, :] = dot(extra[:RANK], back_gate).astype(BF)
    grad_hidden[RANK:, :] = dot(extra[RANK:], back_up).astype(BF)
    grad_down[...] = dot(grad_low[...], hidden).astype(BF)


def mlp(ids, act, low_in, gate_out, up_out, down_in, grad, grad_low, gate_pieces, up_pieces):
    rows, depth = row_count(act), act[0].shape[1]
    width = gate_pieces[0].shape[2]
    block = 256
    ranks = low_in.shape[0]
    column = lambda height: pl.BlockSpec((height, block), lambda n: (0, n))
    return pl.pallas_call(
        partial(mlp_kernel, len(act), len(gate_pieces)),
        grid=(width // block,),
        in_specs=[smem(), full(low_in.shape), column(ranks), column(ranks),
                  column(down_in.shape[0]), column(rows), full(grad_low.shape)]
        + whole(act) + piece_specs(gate_pieces, block) + piece_specs(up_pieces, block),
        out_specs=[column(rows), column(rows), column(rows), full((ranks, rows)),
                   full((ranks + RANK, rows)), column(ranks), column(grad_low.shape[0])],
        out_shape=[jax.ShapeDtypeStruct((rows, width), BF)] * 3
        + [jax.ShapeDtypeStruct((ranks, rows), BF),
           jax.ShapeDtypeStruct((ranks + RANK, rows), F32),
           jax.ShapeDtypeStruct((ranks, width), BF),
           jax.ShapeDtypeStruct((grad_low.shape[0], width), BF)],
        compiler_params=params(48),
        cost_estimate=estimate(4 * rows * depth * width, 4 * depth * width + 8 * rows * depth),
        name="mlp",
    )(ids, low_in, gate_out, up_out, down_in, grad, grad_low, *act, *gate_pieces, *up_pieces)


def unfold_kernel(layout, ids, low_in, *refs):
    blocks, count, weights = layout
    lows, refs = refs[:blocks], refs[blocks:]
    acts, pieces, outs = refs[:blocks * count], refs[blocks * count:-blocks], refs[-blocks:]
    size = outs[0].shape[0]
    step = pl.program_id(0)
    subs = pl.num_programs(0)
    width = pieces[0].shape[1]
    extra = jnp.concatenate([low[...] for low in lows], axis=1).astype(BF)
    per = len(pieces) // weights
    rows = jnp.concatenate(
        [jnp.concatenate([act[...] for act in acts[i * count:(i + 1) * count]], axis=1)
         for i in range(blocks)], axis=0
    )
    for i in range(per):
        at = aligned(ids[i * subs + step] * width, width)
        weight = jnp.concatenate([pieces[k * per + i][0] for k in range(weights)], axis=1)
        product = (dot_nt(rows, weight) + dot_tn(extra, low_in[:, at])).astype(BF)
        for j, out in enumerate(outs):
            out[:, at] = product[j * size:(j + 1) * size]


def unfold(ids, acts, low, low_in, weights, size, blocks):
    subs = weights[0][0].shape[0]
    width = low_in.shape[1]
    pieces = [piece for weight in weights for piece in weight]
    depth = sum(act.shape[1] for act in acts)
    count = len(blocks)
    return pl.pallas_call(
        partial(unfold_kernel, (count, len(acts), len(weights))),
        grid=(subs,),
        in_specs=[smem(), full(low_in.shape)]
        + [pl.BlockSpec((low.shape[0], size), lambda s, at=at: (0, at)) for at in blocks]
        + [pl.BlockSpec((size, act.shape[1]), lambda s, at=at: (at, 0))
           for at in blocks for act in acts]
        + [pl.BlockSpec((1,) + w.shape[1:], lambda s: (s, 0, 0)) for w in pieces],
        out_specs=[full((size, width))] * count,
        out_shape=[jax.ShapeDtypeStruct((size, width), BF)] * count,
        compiler_params=params(48),
        cost_estimate=estimate(
            2 * count * size * depth * width, 2 * depth * width + 4 * count * size * depth
        ),
        name="unfold",
    )(ids, low_in, *[low] * count, *list(acts) * count, *pieces)


def gate_back_kernel(parts, ids, low_back, low_in, gate, nrm, inverse, hold, low_gate, low_out,
                     *refs):
    act, pieces = refs[:parts], refs[parts:-6]
    dgate, dret, low, dlow, grad_in, grad_gate = refs[-6:]

    @pl.when(pl.program_id(0) == 0)
    def _():
        low[...] = low_rows(low_back[...], act).astype(BF)
        dlow[...] = jnp.zeros(dlow.shape, F32)

    weights = jnp.concatenate([w[s] for w in pieces for s in range(w.shape[0])], axis=1)
    back = dot_nt(columns(act, ids), weights) + dot_tn(low[...], low_in[...])
    level = gate[...]
    normed = nrm[...]
    chance = 1.0 / (1.0 + jnp.exp(-level))
    slope = chance * (1.0 + level * (1.0 - chance))
    back_gate = (back * normed * slope).astype(BF)
    grad = back * (level * chance)
    mean = jnp.mean(grad, axis=1, keepdims=True)
    along = jnp.mean(grad * normed, axis=1, keepdims=True)
    dgate[...] = back_gate
    dret[...] = (inverse[0, :, :1] * (grad - mean - normed * along)).astype(BF)
    grad_in[...] = dot(low[...], hold[...]).astype(BF)
    grad_gate[...] = dot(low_gate[...], back_gate).astype(BF)
    dlow[...] += dot_nt(low_out[...], back_gate)


def gate_back(ids, act, low_back, low_in, gate, nrm, inverse, hold, low_gate, low_out, pieces):
    rows, depth = row_count(act), act[0].shape[1]
    width = gate.shape[1]
    block = VALUE_DIM
    ranks = low_back.shape[0]
    column = lambda height: pl.BlockSpec((height, block), lambda n: (0, n))
    return pl.pallas_call(
        partial(gate_back_kernel, len(act)),
        grid=(width // block,),
        in_specs=[smem(), full(low_back.shape), column(ranks), column(rows),
                  column(rows), pl.BlockSpec((1, rows, 128), lambda n: (n, 0, 0)), column(rows),
                  full(low_gate.shape), column(low_out.shape[0])]
        + whole(act) + [pl.BlockSpec((w.shape[0], block, w.shape[2]), lambda n: (0, n, 0)) for w in pieces],
        out_specs=[column(rows), column(rows), full((ranks, rows)),
                   full((low_out.shape[0], rows)), column(ranks), column(ranks)],
        out_shape=[jax.ShapeDtypeStruct((rows, width), BF)] * 2
        + [jax.ShapeDtypeStruct((ranks, rows), BF),
           jax.ShapeDtypeStruct((low_out.shape[0], rows), F32),
           jax.ShapeDtypeStruct((ranks, width), BF), jax.ShapeDtypeStruct((ranks, width), BF)],
        compiler_params=params(56),
        cost_estimate=estimate(2 * rows * depth * width, 2 * depth * width + 16 * rows * width),
        name="gate_back",
    )(ids, low_back, low_in, gate, nrm, inverse, hold, low_gate, low_out, *act, *pieces)


def retention_back_kernel(spots, rates, seg_col, seg_row, cosine, sine_table, low, begin, q_out,
                          k_out, v_out, q, k, v, dret, dq, dk, dv, dlow, grad_q, grad_k, grad_v,
                          sums):
    head = pl.program_id(0)
    rate = rates[head]
    count = spots.shape[0]
    size = q.shape[0] // count
    down, across = decay_factors(rate, size)
    column_factor = jnp.exp(rate * across)
    key_scale = 1.0 / KEY_DIM**0.5

    @pl.when(head == 0)
    def _():
        dlow[...] = begin[...]

    sums[...] = jnp.zeros(sums.shape, F32)
    for j in range(count):
        there = aligned(spots[j] * size, size)
        place = slice(j * size, (j + 1) * size)
        key, value = k[there, :], v[there, :]
        seg_there = seg_col[place, :]
        key_sum = jnp.zeros((size, KEY_DIM), F32)
        value_sum = jnp.zeros((size, VALUE_DIM), F32)
        for i in range(j, count):
            here = aligned(spots[i] * size, size)
            query, back = q[here, :], dret[here, :]
            row_factor = jnp.exp(rate * ((i - j) * size - down))
            alive = seg_there == seg_row[:, i * size:(i + 1) * size]
            if i == j:
                alive = alive & (across >= down)
            weight = jnp.where(alive, row_factor * column_factor, 0.0)
            mixed = (dot_nt(key, query) * weight).astype(BF)
            grad = (dot_nt(value, back) * weight).astype(BF)
            value_sum = value_sum + dot(mixed, back)
            key_sum = key_sum + dot(grad, query)
            sums[i * size:(i + 1) * size, :] += dot_tn(grad, key)
        dk[there, :] = (
            key_scale * unrotated(key_sum, cosine[place, :], sine_table[place, :])
        ).astype(BF)
        dv[there, :] = value_sum.astype(BF)
    for i in range(count):
        place = slice(i * size, (i + 1) * size)
        dq[aligned(spots[i] * size, size), :] = unrotated(
            sums[place, :], cosine[place, :], sine_table[place, :]
        ).astype(BF)
    back_q, back_k, back_v = dq[...], dk[...], dv[...]
    dlow[...] += (
        dot_nt(q_out[...], back_q) + dot_nt(k_out[...], back_k) + dot_nt(v_out[...], back_v)
    )
    grad_q[...] = dot(low[:RANK, :], back_q).astype(BF)
    grad_k[...] = dot(low[RANK:2 * RANK, :], back_k).astype(BF)
    grad_v[...] = dot(low[2 * RANK:3 * RANK, :], back_v).astype(BF)


def retention_back(spots, rates, seg_col, seg_row, cosine, sine_table, low, begin, qk_out, v_out,
                   qk, v, dret):
    rows = qk.shape[0]
    heads = v.shape[1] // VALUE_DIM
    ranks = low.shape[0]
    key = lambda height: pl.BlockSpec((height, KEY_DIM), lambda h: (0, h))
    later = lambda height: pl.BlockSpec((height, KEY_DIM), lambda h: (0, h + heads))
    value = lambda height: pl.BlockSpec((height, VALUE_DIM), lambda h: (0, h))
    keys = heads * KEY_DIM
    return pl.pallas_call(
        retention_back_kernel,
        grid=(heads,),
        in_specs=[smem(), smem(), full(seg_col.shape), full(seg_row.shape), full(cosine.shape),
                  full(cosine.shape), full(low.shape), full(begin.shape), key(ranks),
                  later(ranks), value(ranks),
                  key(rows), later(rows), value(rows), value(rows)],
        out_specs=[key(rows), key(rows), value(rows), full((ranks, rows)), key(RANK), key(RANK),
                   value(RANK)],
        out_shape=[jax.ShapeDtypeStruct((rows, keys), BF), jax.ShapeDtypeStruct((rows, keys), BF),
                   jax.ShapeDtypeStruct(v.shape, BF), jax.ShapeDtypeStruct((ranks, rows), F32),
                   jax.ShapeDtypeStruct((RANK, keys), BF), jax.ShapeDtypeStruct((RANK, keys), BF),
                   jax.ShapeDtypeStruct((RANK, v.shape[1]), BF)],
        scratch_shapes=[pltpu.VMEM((rows, KEY_DIM), F32)],
        compiler_params=params(48),
        cost_estimate=estimate(2 * rows * rows * 1792 * heads, 30 << 20),
        name="retention_back",
    )(spots, rates, seg_col, seg_row, cosine, sine_table, low, begin, qk_out, qk_out, v_out, qk, qk,
      v, dret)


def share_kernel(heights, rank, low, *refs):
    out = refs[-1]
    at, first = 0, 0
    for height, parts in heights:
        total = jnp.zeros((height, out.shape[1]), F32)
        begin = 0
        for ref in refs[first:first + parts]:
            end = begin + ref.shape[0]
            total = total + dot(low[at:at + height, begin:end], ref[...])
            begin = end
        out[at:at + height, :] = total.astype(BF)
        at, first = at + height, first + parts


def share(rank, low, span, items):
    acts = [array for _, act in items for array in act]
    heights = tuple((height, len(act)) for height, act in items)
    return pl.pallas_call(
        partial(share_kernel, heights),
        grid_spec=pltpu.PrefetchScalarGridSpec(
            num_scalar_prefetch=1,
            grid=(1,),
            in_specs=[pl.BlockSpec(low.shape, lambda i, r: (0, 0))]
            + [pl.BlockSpec((act.shape[0], span), lambda i, r: (0, r[0])) for act in acts],
            out_specs=pl.BlockSpec((low.shape[0], span), lambda i, r: (0, 0)),
        ),
        out_shape=jax.ShapeDtypeStruct((low.shape[0], span), BF),
        compiler_params=params(24),
        cost_estimate=estimate(2 * low.shape[0] * low.shape[1] * span, 4 << 20),
        name="share",
    )(rank.reshape(1), low, *in_hbm(*acts))


def place_kernel(layout, order, places, pack, *outs):
    span = pack.shape[2]
    count = places.shape[0]
    for (begin, height, kind, stride), out in zip(layout, outs):
        if kind == "shares":
            for j in range(count):
                rows = pack[0, begin + stride * j:begin + stride * j + height, :]
                out[0, :, aligned(places[j] * span, span)] = rows.astype(F32)
        elif kind == "halves":
            for j in range(2):
                rows = pack[0, begin + stride * j:begin + stride * j + height, :]
                out[0, :, j * span:(j + 1) * span] = rows.astype(F32)
        else:
            for j in range(2):
                rows = pack[0, begin + stride * j:begin + stride * j + height, :]
                out[0, j] = rows.astype(F32)


def place(order, places, pack, layout):
    entries = order.shape[0]
    span, count = pack.shape[2], places.shape[0]
    shapes = []
    for _, height, kind, _ in layout:
        shapes.append({"shares": (height, count * span), "halves": (height, 2 * span)}.get(
            kind, (2, height, span)))
    return pl.pallas_call(
        partial(place_kernel, layout),
        grid_spec=pltpu.PrefetchScalarGridSpec(
            num_scalar_prefetch=2,
            grid=(entries,),
            in_specs=[pl.BlockSpec((1,) + pack.shape[1:], lambda e, o, p: (o[e], 0, 0))],
            out_specs=[
                pl.BlockSpec((1,) + shape, lambda e, o, p, n=len(shape): (e,) + (0,) * n)
                for shape in shapes
            ],
        ),
        out_shape=[jax.ShapeDtypeStruct((entries,) + shape, F32) for shape in shapes],
        compiler_params=params(32),
        cost_estimate=estimate(0, 10 << 20),
        name="place",
    )(order, places, pack)


def after(x, *others):
    return lax.optimization_barrier((x,) + others)[0]


class PlainLinks:
    def __init__(self, ndp, nt):
        self.ndp, self.nt = ndp, nt
        self.rank = lax.axis_index("tensor")
        self.chunks = jnp.arange(nt, dtype=jnp.int32)
        self.spots = self.chunks
        self.row_ids = jnp.zeros((1,), jnp.int32)

    def exchange(self, x):
        return x

    def mine(self, own, other):
        return own

    def gather(self, x):
        return [lax.all_gather(x, "tensor", axis=0, tiled=True)]

    def scatter(self, rows):
        total = lax.psum_scatter(
            jnp.concatenate(rows, axis=0), "tensor", scatter_dimension=0, tiled=True
        )
        zero = jnp.zeros_like(total)
        return (total, zero, zero)

    def forward(self, shards, tokens, cotangent, line, steps):
        blocks = [
            [lax.all_gather(shard, "dp", axis=int(shard.shape[1] * self.ndp == tokens.shape[1]),
                            tiled=True)[None]]
            for shard in shards
        ]
        steps.ready(line, steps.tables(line, line)[0])
        a = self.gather(steps.norm(tokens))
        dy = self.gather(cotangent)
        qkv = steps.query_key_value(a, blocks[0], blocks[1])
        mixed = steps.gate_and_mix(a, *qkv, blocks[2])
        *rows, low = steps.fold(mixed[0], blocks[3])
        middle, b = steps.join(tokens, self.scatter(rows))
        dhid = steps.hidden_grad(dy, blocks[4])
        return (blocks, tokens, a, cotangent, dy, qkv, mixed, low, middle, self.gather(b), dhid)

    def group_sum(self, x):
        return lax.psum(x.astype(BF), "tensor")

    def all_shares(self, x, height):
        first = lax.all_gather(x[:height], "tensor", tiled=True)
        every = lax.all_gather(jnp.concatenate([first, x[height:]]), "dp")
        return every, jnp.arange(self.ndp, dtype=jnp.int32), self.chunks

    def backward(self, steps):
        steps.mlp()
        dz = self.gather(steps.dz(self.scatter(steps.unfold_mlp(256, (0, 1, 2, 3)))))
        output = steps.output(self.scatter(steps.fold_down(steps.hid)))
        lows = self.group_sum(steps.early_lows())
        steps.gate_back(dz)
        early = self.all_shares(steps.early(lows, dz), steps.early_height)
        steps.retention_back(steps.dret)
        late = self.all_shares(steps.late(self.group_sum(steps.dlow)), steps.late_height)
        parts = self.scatter(steps.unfold_attn(256, (0, 1, 2, 3)))
        dx, _ = steps.dx(parts, 0, parts[0].shape[0])
        return output, dx, early, late


class PairedLinks:
    def __init__(self, ndp, nt):
        self.ndp, self.nt = ndp, nt
        d, t = lax.axis_index("dp"), lax.axis_index("tensor")
        c, p, m = d % 2, t // 2, t % 2
        self.home = c == p
        self.rank = 2 * c + m
        flips = jnp.array([0, 2, 1, 3], jnp.int32)
        self.chunks = self.rank ^ flips
        order = jnp.arange(4, dtype=jnp.int32) ^ self.rank
        self.spots = (order % 2) * 2 + order // 2
        g = d // 2
        self.row_ids = ((2 * (g ^ jnp.arange(4, dtype=jnp.int32))[:, None]
                         + jnp.arange(2, dtype=jnp.int32)[None, :]) ^ c).reshape(-1)
        self.last = {}
        self.last_round = ()
        self.slow = ()

    def pairs(self, place):
        listed = []
        for d in range(self.ndp):
            for t in range(self.nt):
                to = place(d, t)
                if to is not None:
                    listed.append((d * self.nt + t, to[0] * self.nt + to[1]))
        return listed

    def move(self, x, place, chain=None):
        if chain in self.last:
            x = after(x, *self.last[chain])
        moved = lax.ppermute(x, ("dp", "tensor"), self.pairs(place))
        if chain is not None:
            self.last[chain] = (moved,)
        return moved

    def send(self, moves):
        return [lax.ppermute(x, ("dp", "tensor"), self.pairs(place)) for x, place in moves]

    def round(self, moves, work=None, inputs=(), later=(), slow=()):
        every = list(moves) + list(slow)
        values = [x for x, _ in every]
        flat, form = jax.tree.flatten((values, inputs))
        last, _ = jax.tree.flatten(self.last_round)
        if last:
            flat = lax.optimization_barrier((*flat, *last))[:len(flat)]
        values, inputs = jax.tree.unflatten(form, flat)
        moved = self.send([(x, place) for x, (_, place) in zip(values, every)])
        moved, slowly = moved[:len(moves)], moved[len(moves):]
        second = []
        if later:
            count, make = later
            moves = make(moved[:count])
            values = [x for x, _ in moves]
            values = lax.optimization_barrier((*values, *moved[:count]))[:len(values)]
            second = self.send([(x, place) for x, (_, place) in zip(values, moves)])
        made = work(*inputs) if work is not None else ()
        self.last_round = (moved, second, made, self.slow)
        self.slow = slowly
        return moved + slowly, second, made

    def core(self, x):
        return self.move(x, lambda d, t: (d ^ 1, t))

    def pair(self, x):
        return self.move(x, lambda d, t: (d, t ^ 1), "pair")

    def mine(self, own, other):
        return jnp.where(self.home, own, other)

    def exchange(self, x):
        moved = self.move(
            x, lambda d, t: (d ^ 1, t ^ 2) if d % 2 != t // 2 else None, "middle"
        )
        return jnp.where(self.home, x, moved)

    def gather(self, x):
        across = self.pair(x)
        return [x, self.core(x), across, self.core(across)]

    def forward(self, shards, tokens, cotangent, line, steps):
        by_one = lambda d, t: (d ^ 2, t)
        by_two = lambda d, t: (d ^ 4, t)
        core = lambda d, t: (d ^ 1, t)
        pair = lambda d, t: (d, t ^ 1)
        swap = lambda d, t: (d ^ 1, t ^ 2) if d % 2 != t // 2 else None
        seat = lambda d, t: (d, t ^ 2) if d % 2 == t // 2 else None
        blocks = [[None] * 4 for _ in shards]
        doubled = [jnp.stack([shards[0], self.core(shards[0])])]

        def over(i):
            return (doubled[i], seat)

        def arrived(i, moved):
            blocks[i][0] = self.mine(doubled[i], moved)

        hops = {
            "x": lambda i: (blocks[i][0], by_one),
            "y": lambda i: (blocks[i][0], by_two),
            "xy": lambda i: (blocks[i][1], by_two),
            "yx": lambda i: (blocks[i][2], by_one),
        }
        place_of = {"x": 1, "y": 2, "xy": 3, "yx": 3}

        def go(first, second, others, work=None, inputs=()):
            def later(moved):
                for (i, way), block in zip(first, moved):
                    blocks[i][place_of[way]] = block
                return [hops[way](i) for i, way in second]

            moved, seconds, made = self.round(
                [hops[way](i) for i, way in first] + list(others), work, inputs,
                (len(first), later)
            )
            for (i, way), block in zip(second, seconds):
                blocks[i][place_of[way]] = block
            return moved[len(first):], made

        def double(rest):
            return [jnp.stack([shard, self.core(shard)]) for shard in rest]

        def whole_rows(own, across):
            return [own, self.core(own), across, self.core(across)]

        other = self.core(line)
        (moved,), made = go([], [], [over(0)], double, (shards[1:],))
        doubled += made
        arrived(0, moved)
        (moved,), (home_table, sent_table) = go(
            [(0, "x"), (0, "y")], [], [over(1)], steps.tables, (line, other)
        )
        arrived(1, moved)
        (one, two), _ = go([(1, "x"), (0, "xy")], [(1, "y")], [over(2), over(3)])
        arrived(2, one)
        arrived(3, two)
        (x, table, moved), _ = go([(2, "x"), (2, "y")], [(1, "yx"), (2, "xy")],
                                  [(tokens, swap), (sent_table, seat), over(4)])
        arrived(4, moved)
        x = self.mine(tokens, x)
        steps.ready(other, self.mine(home_table, table))
        a = steps.norm(x)
        (moved, grad, across), _ = go([(3, "x"), (3, "y")], [(4, "x"), (3, "xy")],
                                      [over(5), (cotangent, swap), (a, pair)])
        arrived(5, moved)
        grad = self.mine(cotangent, grad)

        def attend(own, across, *weights):
            a = whole_rows(own, across)
            return a, steps.query_key_value(a, *weights)

        (moved,), (a, qkv) = go([(5, "x"), (4, "y")], [], [over(6)], attend,
                                (a, across, blocks[0], blocks[1]))
        arrived(6, moved)

        def mix(a, qk, low, v, w_g, w_o):
            mixed = steps.gate_and_mix(a, qk, low, v, w_g)
            return mixed, steps.fold(mixed[0], w_o)

        (across,), (mixed, folded) = go([(4, "yx"), (5, "y")], [], [(grad, pair)], mix,
                                        (a, *qkv, blocks[2], blocks[3]))
        own, near, far, beyond, low = folded
        near, beyond = self.send([(near, core), (beyond, core)])
        far = (far.astype(F32) + beyond.astype(F32)).astype(BF)

        def grad_rows(grad, across, w_d):
            dy = whole_rows(grad, across)
            return dy, steps.hidden_grad(dy, w_d)

        (far,), (dy, dhid) = go([(6, "x"), (6, "y")], [], [(far, pair)], grad_rows,
                                (grad, across, blocks[4]))
        parts = (own, near)
        middle, b = steps.join(x, (*parts, far))
        (across,), _ = go([(5, "yx"), (6, "xy")], [], [(b, pair)])
        b = whole_rows(b, across)
        return blocks, x, a, grad, dy, qkv, mixed, low, middle, b, dhid

    def core_sum(self, x, other):
        size = x.shape[1] // 4
        other = other.astype(F32)
        return (x + jnp.concatenate(
            [other[:, i * size:(i + 1) * size] for i in (1, 0, 3, 2)], axis=1
        )).astype(BF)

    def pair_sum(self, x, other):
        size = x.shape[1] // 2
        other = jnp.concatenate([other[:, size:], other[:, :size]], axis=1)
        return (x.astype(F32) + other.astype(F32)).astype(BF)

    def backward(self, steps):
        pair = lambda d, t: (d, t ^ 1)
        swap = lambda d, t: (d ^ 1, t ^ 2) if d % 2 != t // 2 else None
        over = lambda d, t: (d, t ^ 2)
        by_one = lambda d, t: (d ^ 2, t)
        by_two = lambda d, t: (d ^ 4, t)
        core = lambda d, t: (d ^ 1, t)

        def add(one, two):
            return (one.astype(F32) + two.astype(F32)).astype(BF)

        steps.mlp()
        near, beyond = steps.unfold_mlp(256, (1, 3))
        far, = steps.unfold_mlp(256, (2,))
        near, beyond, lows = self.send([(near, core), (beyond, core), (steps.lows_low(), core)])
        far = add(far, beyond)
        lows = self.core_sum(steps.early_lows(), lows)
        self.last_round = ()
        (far, other), _, (own, folded) = self.round(
            [(far, pair), (lows, pair)],
            lambda hid: (steps.unfold_mlp(256, (0,))[0], steps.fold_down(hid)), (steps.hid,)
        )
        lows = self.pair_sum(lows, other)
        dz = steps.dz((own, near, far))
        own_out, near_out, far_out, beyond_out = folded
        (across, dz_near, near_out, beyond_out), _, _ = self.round(
            [(dz, pair), (dz, core), (near_out, core), (beyond_out, core)]
        )
        (dz_beyond, far_out), _, _ = self.round(
            [(across, core)], slow=[(add(far_out, beyond_out), pair)]
        )
        dz = [dz, dz_near, across, dz_beyond]
        _, _, (early, dret) = self.round([], steps.middle_back, (lows, dz))
        (moved,), _, dpv = self.round([(early, swap)], steps.retention_back, (dret,))
        early = self.mine(early, moved)
        first = early[:steps.early_height]
        output = steps.output((own_out, near_out, far_out))

        (moved, dlow), _, (near, beyond) = self.round(
            [(first, pair), (steps.dlow.astype(BF), core)],
            lambda dpv: steps.unfold_attn(256, (1, 3), dpv), (dpv,)
        )
        dlow = self.core_sum(steps.dlow, dlow)
        first = jnp.concatenate([first, moved])
        (moved, near, beyond, other), _, (far,) = self.round(
            [(first, over), (near, core), (beyond, core), (dlow, pair)],
            lambda dpv: steps.unfold_attn(256, (2,), dpv), (dpv,)
        )
        early = jnp.concatenate([first, moved, early[steps.early_height:]])
        far = add(far, beyond)
        half = far.shape[0] // 2
        late = steps.late(self.pair_sum(dlow, other))
        (moved, far0, far1), _, (own,) = self.round(
            [(late, swap)], lambda dpv: steps.unfold_attn(256, (0,), dpv), (dpv,),
            slow=[(far[:half], pair), (far[half:], pair)]
        )
        early = lax.all_gather(early, "dp")
        late = self.mine(late, moved)
        moved_out, = self.send([(output, swap)])
        rows = []
        for i, part in enumerate((far0, far1)):
            dx, low = steps.dx((own, near, part), i * half, half)
            moved, = self.send([(low, swap)])
            rows.append(self.mine(dx, moved.astype(F32)))
        first = late[:steps.late_height]
        first = jnp.concatenate([first, *self.send([(first, pair)])])
        first = jnp.concatenate([first, *self.send([(first, over)])])
        late = jnp.concatenate([first, late[steps.late_height:]])[None]
        for place in (by_one, by_two, core):
            late = jnp.concatenate([late, *self.send([(late, place)])])
        places = jnp.arange(self.nt, dtype=jnp.int32) ^ lax.axis_index("tensor")
        at = jnp.arange(self.ndp, dtype=jnp.int32)
        apart = at ^ lax.axis_index("dp")
        return (self.mine(output, moved_out), jnp.concatenate(rows), (early, at, places),
                (late, apart // 2 + 4 * (apart % 2), places))


def rotation_tables(seq_length, half_dim):
    positions = jnp.arange(seq_length, dtype=jnp.float32)
    frequency = jnp.exp(-jnp.log(10000.0) * jnp.arange(half_dim, dtype=jnp.float32) / half_dim)
    angles = positions[:, None] * frequency[None, :]
    return (jnp.cos(angles), jnp.sin(angles))


def shards(
    ndp,
    nt,
    tokens,
    cotangent,
    adapter_ids,
    segments,
    norm_attn,
    norm_mlp,
    weight_query,
    weight_key,
    weight_value,
    weight_gate,
    weight_out,
    weight_mlp_gate,
    weight_mlp_up,
    weight_mlp_down,
    adapt_attn_in,
    adapt_query_key,
    adapt_value_gate,
    adapt_out_in,
    adapt_out_back,
    adapt_mlp_in,
    adapt_mlp_hidden,
    adapt_down_in,
    adapt_down_back,
):
    links = PairedLinks(ndp, nt) if (ndp, nt) == (8, 4) else PlainLinks(ndp, nt)
    rank, chunks, spots, ids = links.rank, links.chunks, links.spots, links.row_ids
    adapters = adapt_attn_in.shape[0]
    depth = tokens.shape[2]
    seq_length = segments.shape[1]
    gain_attn, gain_mlp = norm_attn[None], norm_mlp[None]

    def pick(table, which):
        return lax.dynamic_index_in_dim(table, which, 0, keepdims=False)

    def packed(which):
        qk, vg = pick(adapt_query_key, which), pick(adapt_value_gate, which)
        return jnp.concatenate(
            [jnp.concatenate([qk[0], qk[1]], axis=1), vg[0], vg[1],
             pick(adapt_mlp_hidden, which).reshape(2 * RANK, -1),
             pick(adapt_out_in, which).T, pick(adapt_down_in, which).T], axis=0
        )

    own_id = adapter_ids[0, 0]
    own_line = jnp.concatenate([segments, jnp.broadcast_to(adapter_ids, (1, 128))], axis=1)
    wide = weight_gate.shape[1]
    keys = adapt_query_key.shape[3]
    heads_local = wide // VALUE_DIM
    head_ids = (rank * heads_local + jnp.arange(heads_local, dtype=jnp.int32)).astype(F32)
    rates = jnp.log(1.0 - jnp.exp2(-5.0 - head_ids))
    cosine, sine_table = rotation_tables(seq_length, HALF)

    class Steps:
        def tables(self, line, other):
            return packed(line[0, seq_length]), packed(other[0, seq_length])

        def ready(self, other, table):
            line = links.mine(own_line, other)
            self.work_id = work_id = line[0, seq_length]
            self.seg_row = line[:, :seq_length]
            self.seg_col = self.seg_row.reshape(seq_length, 1)
            blank = jnp.zeros((RANK, wide), BF)
            left = jnp.arange(wide)[None, :] < keys
            zero = jnp.zeros((), BF)
            self.qk_out = jnp.concatenate([jnp.where(left, table[:RANK], zero),
                                           jnp.where(left, zero, table[:RANK]), blank, blank])
            self.v_out = jnp.concatenate([blank, blank, table[RANK:2 * RANK], blank])
            self.g_out = jnp.concatenate([blank, blank, blank, table[2 * RANK:3 * RANK]])
            self.mg_out = jnp.concatenate([table[3 * RANK:4 * RANK], blank])
            self.mu_out = jnp.concatenate([blank, table[4 * RANK:5 * RANK]])
            self.out_in = table[5 * RANK:6 * RANK]
            self.down_in = table[6 * RANK:7 * RANK]
            self.attn_in = pick(adapt_attn_in, work_id).T
            self.out_back = pick(adapt_out_back, work_id)
            self.mlp_in = pick(adapt_mlp_in, work_id).T
            self.down_back = pick(adapt_down_back, work_id)

        def norm(self, x):
            return norm_rows(x, gain_attn)

        def query_key_value(self, a, w_qk, w_v):
            qk, low = project_query_key(
                ids, chunks, a, self.attn_in, self.qk_out, cosine, sine_table, w_qk
            )
            return qk, low, project(ids, a, low, self.v_out, w_v, BF)

        def gate_and_mix(self, a, qk, low, v, w_g):
            gate = project(ids, a, low, self.g_out, w_g, F32)
            return (*retention(spots, rates, self.seg_col, self.seg_row, qk, v, gate), gate)

        def fold(self, o, w_o):
            return fold(ids, o, self.out_in, self.out_back, w_o)

        def join(self, x, parts):
            return join_rows(x, parts, gain_mlp)

        def hidden_grad(self, dy, w_d):
            return hidden_grad(ids, dy, self.down_back, self.down_in, w_d)

    steps = Steps()
    ((w_qk, w_v, w_g, w_o, w_d, w_mg, w_mu), x, a, grad, dy, (qk, low_a, v),
     (o, nrm, inverse, gate), low_o, middle, b, (dhid, low_dy)) = links.forward(
        [jnp.concatenate([weight_query, weight_key], axis=1), weight_value, weight_gate,
         weight_out, weight_mlp_down, weight_mlp_gate, weight_mlp_up],
        tokens[0], cotangent[0], own_line, steps,
    )
    seg_row, seg_col, work_id = steps.seg_row, steps.seg_col, steps.work_id
    qk_out, v_out, g_out, mg_out, mu_out = (
        steps.qk_out, steps.v_out, steps.g_out, steps.mg_out, steps.mu_out
    )
    attn_in, out_in, out_back = steps.attn_in, steps.out_in, steps.out_back
    mlp_in, down_in, down_back = steps.mlp_in, steps.down_in, steps.down_back

    span = depth // nt
    halves = lambda y: jnp.concatenate([y[:, :wide // 2], y[:, wide // 2:]])

    class Back:
        early_height = 4 * RANK
        late_height = 4 * RANK

        def mlp(self):
            (self.hid, self.dgate, self.dup, _, self.lows, self.grad_hidden,
             self.grad_down) = mlp(
                ids, b, mlp_in, mg_out, mu_out, down_in, dhid, low_dy, w_mg, w_mu
            )

        def unfold_mlp(self, size, blocks):
            return unfold(ids, (self.dgate, self.dup), self.lows[RANK:], mlp_in, (w_mg, w_mu),
                          size, blocks)

        def dz(self, parts):
            self.dmid, low = rms_back(middle, grad, parts, gain_mlp, 0, middle.shape[0])
            return low

        def fold_down(self, hid):
            return fold(ids, hid, down_in, down_back, w_d)[:4]

        def output(self, parts):
            return (middle + (
                parts[0].astype(F32) + parts[1].astype(F32) + parts[2].astype(F32)
            )).astype(BF)

        def early_lows(self):
            return jnp.concatenate([self.lows, low_o])

        def lows_low(self):
            return self.early_lows().astype(BF)

        def early(self, lows, dz):
            mark = jnp.full((RANK, span), work_id, F32).astype(BF)
            return jnp.concatenate(
                [share(rank, lows, span, ((RANK, dy), (2 * RANK, b), (RANK, dz))),
                 halves(jnp.concatenate([self.grad_hidden, self.grad_down, self.grad_out_in,
                                         self.grad_gate])), mark]
            )

        def gate_back(self, dz):
            (self.dpg, self.dret, _, self.dlow, self.grad_out_in, self.grad_gate) = gate_back(
                ids, dz, out_back, out_in, gate, nrm, inverse, o, low_a[3 * RANK:], g_out, w_o
            )

        def middle_back(self, lows, dz):
            self.gate_back(dz)
            return self.early(lows, dz), self.dret

        def retention_back(self, dret):
            (self.dpq, self.dpk, self.dpv, self.dlow, self.grad_q, self.grad_k,
             self.grad_v) = retention_back(
                spots, rates, seg_col, seg_row, cosine, sine_table, low_a, self.dlow, qk_out,
                v_out, qk, v, dret
            )
            self.dpqk = jnp.concatenate([self.dpq, self.dpk], axis=1)
            return self.dpv

        def late(self, lows):
            return jnp.concatenate(
                [share(rank, lows, span, ((4 * RANK, a),)),
                 halves(jnp.concatenate(
                     [jnp.concatenate([self.grad_q, self.grad_k], axis=1), self.grad_v]
                 ))]
            )

        def unfold_attn(self, size, blocks, dpv=None):
            dpv = self.dpv if dpv is None else dpv
            return unfold(ids, (self.dpqk, dpv, self.dpg), self.dlow, attn_in,
                          (w_qk, w_v, w_g), size, blocks)

        def dx(self, parts, begin, count):
            return rms_back(x, self.dmid, parts, gain_attn, begin, count)

    output, input_grad, early, late = links.backward(Back())
    early, early_at, early_places = early
    late, late_at, late_places = late
    shares = nt * Back.early_height
    all_ids = early[:, shares + 10 * RANK, 0].astype(jnp.int32)
    chosen = jnp.arange(adapters, dtype=jnp.int32)[:, None] == all_ids[None, :]
    if all_ids.shape[0] == adapters:
        order = jnp.sum(
            jnp.where(chosen, jnp.arange(adapters, dtype=jnp.int32)[None, :], 0), axis=1
        )
    else:
        total = lambda y: jnp.einsum(
            "es,sij->eij", chosen.astype(BF), y, preferred_element_type=F32
        )
        early, late = total(early), total(late)
        order = jnp.arange(adapters, dtype=jnp.int32)
        early_at = late_at = order
    pitch = Back.early_height
    down_back_out, mlp_out, out_back_out, hidden_out, down_out, out_out, gate_out = place(
        early_at[order], early_places, early,
        ((0, RANK, "shares", pitch), (RANK, 2 * RANK, "shares", pitch),
         (3 * RANK, RANK, "shares", pitch), (shares, 2 * RANK, "halves", 5 * RANK),
         (shares + 2 * RANK, RANK, "halves", 5 * RANK),
         (shares + 3 * RANK, RANK, "halves", 5 * RANK),
         (shares + 4 * RANK, RANK, "halves", 5 * RANK))
    )
    pitch = Back.late_height
    shares = nt * pitch
    attn_out, qk_grads, value_out = place(
        late_at[order], late_places, late,
        ((0, 4 * RANK, "shares", pitch), (shares, RANK, "apart", 2 * RANK),
         (shares + RANK, RANK, "halves", 2 * RANK))
    )
    return (
        output[None],
        input_grad[None],
        jnp.swapaxes(attn_out, 1, 2),
        qk_grads,
        jnp.stack([value_out, gate_out], axis=1),
        jnp.swapaxes(out_out, 1, 2),
        out_back_out,
        jnp.swapaxes(mlp_out, 1, 2),
        hidden_out.reshape(adapters, 2, RANK, wide),
        jnp.swapaxes(down_out, 1, 2),
        down_back_out,
    )


def solution(mesh):
    in_specs = (
        P("dp", "tensor", None),
        P("dp", "tensor", None),
        P("dp", None),
        P("dp", None),
        P(),
        P(),
        P("dp", "tensor"),
        P("dp", "tensor"),
        P("dp", "tensor"),
        P("dp", "tensor"),
        P("tensor", "dp"),
        P("dp", "tensor"),
        P("dp", "tensor"),
        P("tensor", "dp"),
        P(),
        P(None, None, None, "tensor"),
        P(None, None, None, "tensor"),
        P(None, "tensor", None),
        P(),
        P(),
        P(None, None, None, "tensor"),
        P(None, "tensor", None),
        P(),
    )
    out_specs = (
        P("dp", "tensor", None),
        P("dp", "tensor", None),
        P(),
        P(None, None, None, "tensor"),
        P(None, None, None, "tensor"),
        P(None, "tensor", None),
        P(),
        P(),
        P(None, None, None, "tensor"),
        P(None, "tensor", None),
        P(),
    )
    local = partial(shards, mesh.shape["dp"], mesh.shape["tensor"])
    return jax.shard_map(local, mesh=mesh, in_specs=in_specs, out_specs=out_specs, check_vma=False)
```

time: 1420 us -> 680 us (0.48)
  waiting for transfers between devices: 987 us -> 294 us
  matrix products: 257 us -> 0 us
  Pallas kernels: 0 us -> 173 us
  starting transfers between devices: 1.52 us -> 86.4 us
  other arithmetic: 75.6 us -> 46.8 us
  local copies, waits for them, and re-layouts: 67.7 us -> 48.9 us
    all_gather x12 -> x1, waiting for transfers between devices: 450 us -> 0.01 us  [backward(): early = lax.all_gather(early, 'dp')]
    reduce_scatter x4 -> x0, waiting for transfers between devices: 351 us -> none  [the longest x1 142 us: shards(): lax.psum_scatter(matmul(row_slice(gated_low, first_row, shard_rows * lax....]
    ppermute x0 -> x80, waiting for transfers between devices: none -> 294 us  [the longest x66 292 us: send(): lax.ppermute(x, ('dp', 'tensor'), self.pairs(place))]
    dot_general x71 -> x0, matrix products: 257 us -> none  [the longest x44 160 us: matmul(): return jnp.dot(left_side, right_side, preferred_element_type=jnp.float32)]
    psum x2 -> x0, waiting for transfers between devices: 182 us -> none  [the longest x1 182 us: shards(): lax.psum((spread(grad_attn_in_local), spread(grad_out_back_local), spread...]
    pallas_call x0 -> x25, Pallas kernels: none -> 173 us  [the longest x6 45.6 us: unfold(): pl.pallas_call(partial(unfold_kernel, (count, len(acts), len(weights))),...]
    ppermute x0 -> x80, starting transfers between devices: none -> 86.4 us  [the longest x66 70.9 us: send(): lax.ppermute(x, ('dp', 'tensor'), self.pairs(place))]
    convert_element_type x21 -> x12, other arithmetic: 27.9 us -> 6.7 us  [the longest x3 4.48 us: add(): return (one.astype(F32) + two.astype(F32)).astype(BF)]
  transfers between devices with their start and end apart: 18 -> 81, of which waited for: 16 -> 39; matrix products, arithmetic and copies ran while one was open for 17% -> 9% of each run, Pallas kernels for 0% -> 17%
where the time goes in v1:
time: 680 us; the launch traced here: 673 us
  waiting for transfers between devices  294 us (43%)
  Pallas kernels  173 us (25%)
  starting transfers between devices  86.4 us (13%)
  local copies, waits for them, and re-layouts  48.9 us (7%)
  other arithmetic  46.8 us (7%)
  between operations  23.4 us (3%)
    ppermute x66, waiting for transfers between devices, send(): lax.ppermute(x, ('dp', 'tensor'), self.pairs(place))  292 us
    ppermute x66, starting transfers between devices, send(): lax.ppermute(x, ('dp', 'tensor'), self.pairs(place))  70.9 us
    pallas_call x6, Pallas kernels, unfold(): pl.pallas_call(partial(unfold_kernel, (count, len(acts), len(weights))),...  45.6 us
    unnamed x249, local copies, waits for them, and re-layouts  33.8 us
    pallas_call x2, Pallas kernels, fold(): pl.pallas_call(fold_kernel, grid=(subs,), in_specs=[smem(), full(act.shap...  19.1 us
    pallas_call x1, Pallas kernels, mlp(): pl.pallas_call(partial(mlp_kernel, len(act), len(gate_pieces)), grid=(wid...  18.6 us
    select_n x15, other arithmetic, mine(): return jnp.where(self.home, own, other)  17 us
    pallas_call x2, Pallas kernels, project(): pl.pallas_call(partial(project_kernel, len(act)), grid=(width // block,),...  16.7 us
  transfers between devices with their start and end apart: 81, of which 39 were waited for; matrix products, arithmetic and copies ran while one was open for 9% of the time, Pallas kernels for 17%

profile of v1, /device:TPU:1, one launch (start us, length us, event | category | flops | bytes accessed | tf_op | source)
XLA Modules:
  0.0 672.5 jit_solution(16471192881850231341)
XLA Ops:
  14.5 5.7 collective-permute-start.6
  32.6 9.0 %collective-permute-done.3 = bf16[2,256,1024]{2,1,0:T(8,128)(2,1)} collective-permute-done((bf16[2,256,1024]{2,1,0:T(8,128)(2,1)}, bf16[2,256,1024]{2,1,0:T(8,128)(2,1)}, u32[]{:S(2)}, u32[]{:S(2)}) %collective-permute-start.3) | collective-permute-done | bytes 1048608 | tf_op jit(solution)/shard_map/ppermute | solution.py:783
  58.9 30.2 %collective-permute-done.9 = bf16[2,256,1024]{2,1,0:T(8,128)(2,1)} collective-permute-done((bf16[2,256,1024]{2,1,0:T(8,128)(2,1)}, bf16[2,256,1024]{2,1,0:T(8,128)(2,1)}, u32[]{:S(2)}, u32[]{:S(2)}) %collective-permute-start.9) | collective-permute-done | bytes 1048608 | tf_op jit(solution)/shard_map/ppermute | solution.py:783
  95.9 9.4 %collective-permute-done.13.refs_5_.refs_13_.refs_9_ = bf16[2,256,1024]{2,1,0:T(8,128)(2,1)S(1)} collective-permute-done((bf16[2,256,1024]{2,1,0:T(8,128)(2,1)S(1)}, bf16[2,256,1024]{2,1,0:T(8,128)(2,1)S(1)}, u32[]{:S(2)}, u32[]{:S(2)}) %collective-permute-start.13) | collective-permute-done | bytes 1048608 | tf_op jit(solution)/shard_map/ppermute | solution.py:783
  106.3 4.9 collective-permute-done.14.refs_7_.refs_11_
  116.6 4.4 collective-permute-done.15
  121.0 9.8 %collective-permute-done.16.refs_6_.refs_14_.refs_10_ = bf16[2,256,1024]{2,1,0:T(8,128)(2,1)S(1)} collective-permute-done((bf16[2,256,1024]{2,1,0:T(8,128)(2,1)S(1)}, bf16[2,256,1024]{2,1,0:T(8,128)(2,1)S(1)}, u32[]{:S(2)}, u32[]{:S(2)}) %collective-permute-start.16) | collective-permute-done | bytes 1048608 | tf_op jit(solution)/shard_map/ppermute | solution.py:783
  137.0 9.7 %collective-permute-done.18.refs_5_.refs_17_.refs_13_ = bf16[2,256,1024]{2,1,0:T(8,128)(2,1)} collective-permute-done((bf16[2,256,1024]{2,1,0:T(8,128)(2,1)}, bf16[2,256,1024]{2,1,0:T(8,128)(2,1)}, u32[]{:S(2)}, u32[]{:S(2)}) %collective-permute-start.18) | collective-permute-done | bytes 1048608 | tf_op jit(solution)/shard_map/ppermute | solution.py:783
  153.5 25.6 %collective-permute-done.17 = bf16[256,2048]{1,0:T(8,128)(2,1)} collective-permute-done((bf16[256,2048]{1,0:T(8,128)(2,1)}, bf16[256,2048]{1,0:T(8,128)(2,1)}, u32[]{:S(2)}, u32[]{:S(2)}) %collective-permute-start.17) | collective-permute-done | bytes 1048608 | tf_op jit(solution)/shard_map/ppermute | solution.py:783
  189.4 4.7 collective-permute-start.28
  203.5 18.8 %collective-permute-done.24 = bf16[2,256,1024]{2,1,0:T(8,128)(2,1)} collective-permute-done((bf16[2,256,1024]{2,1,0:T(8,128)(2,1)}, bf16[2,256,1024]{2,1,0:T(8,128)(2,1)}, u32[]{:S(2)}, u32[]{:S(2)}) %collective-permute-start.24) | collective-permute-done | bytes 1048608 | tf_op jit(solution)/shard_map/ppermute | solution.py:783
  224.0 11.0 %collective-permute-done.25.refs_2_ = bf16[256,2048]{1,0:T(8,128)(2,1)} collective-permute-done((bf16[256,2048]{1,0:T(8,128)(2,1)}, bf16[256,2048]{1,0:T(8,128)(2,1)}, u32[]{:S(2)}, u32[]{:S(2)}) %collective-permute-start.25) | collective-permute-done | bytes 1048608 | tf_op jit(solution)/shard_map/ppermute | solution.py:783
  236.3 3.1 collective-permute-start.32
  246.1 10.6 %project_query_key.1 = (bf16[1024,1024]{1,0:T(8,128)(2,1)S(1)}, bf16[64,1024]{1,0:T(8,128)(2,1)S(1)}) custom-call(s32[8]{0:T(128)S(1)} %xor.46.ids, s32[4]{0:T(128)S(1)} %broadcast_xor_fusion.chunks, bf16[64,2048]{1,0:T(8,128)(2,1)S(1)} %dynamic-slice_bitcast_fusion.low_in, bf16[64,1024]{1,0:T(8,128)(2,1)S(1)} %get-tuple-element.383.low_out.q_out.k_out, ...), custom_call_target="tpu_custom_call" | custom-call | flops 1 | bytes 1 | tf_op jit(solution)/shard_map/project_query_key/pallas_call | solution.py:151
  256.8 8.6 %project.2.v = bf16[1024,1024]{1,0:T(8,128)(2,1)S(1)} custom-call(s32[8]{0:T(128)S(1)} %xor.46.ids, bf16[64,1024]{1,0:T(8,128)(2,1)S(1)} %get-tuple-element.200.low, bf16[64,1024]{1,0:T(8,128)(2,1)S(1)} %get-tuple-element.382.low_out.v_out, bf16[256,2048]{1,0:T(8,128)(2,1)} %norm_rows.1.refs_0_, bf16[256,2048]{1,0:T(8,128)(2,1)S(1)} %collective-permute-done.32.refs_1_, ...), custom_call_target="tpu_custom_call" | custom-call | flops 1 | bytes 1 | tf_op jit(solution)/shard_map/project/pallas_call | solution.py:178
  270.3 8.1 %project.3.gate = f32[1024,1024]{1,0:T(8,128)S(1)} custom-call(s32[8]{0:T(128)S(1)} %xor.46.ids, bf16[64,1024]{1,0:T(8,128)(2,1)S(1)} %copy-done.54, bf16[64,1024]{1,0:T(8,128)(2,1)S(1)} %concatenate.104.low_out, bf16[256,2048]{1,0:T(8,128)(2,1)} %norm_rows.1.refs_0_, bf16[256,2048]{1,0:T(8,128)(2,1)S(1)} %collective-permute-done.32.refs_1_, ...), custom_call_target="tpu_custom_call" | custom-call | flops 1 | bytes 1 | tf_op jit(solution)/shard_map/project/pallas_call | solution.py:178
  280.4 7.3 %retention.1 = (bf16[1024,1024]{1,0:T(8,128)(2,1)S(1)}, f32[1024,1024]{1,0:T(8,128)S(1)}, f32[2,1024,128]{2,1,0:T(8,128)S(1)}) custom-call(s32[4]{0:T(128)S(1)} %fusion.6.spots, f32[2]{0:T(128)S(1)} %subtract_log_fusion.rates, s32[1024,1]{1,0:T(8,128)S(1)} %copy-done.38, s32[1,1024]{1,0:T(1,128)S(1)} %get-tuple-element.384.seg_row, ...), custom_call_target="tpu_custom_call" | custom-call | flops 1 | bytes 1 | tf_op jit(solution)/shard_map/retention/pallas_call | solution.py:230
  291.1 9.4 %fold.2 = (bf16[256,2048]{1,0:T(8,128)(2,1)S(1)}, bf16[256,2048]{1,0:T(8,128)(2,1)S(1)}, bf16[256,2048]{1,0:T(8,128)(2,1)S(1)}, bf16[256,2048]{1,0:T(8,128)(2,1)S(1)}, f32[16,1024]{1,0:T(8,128)S(1)}) custom-call(s32[8]{0:T(128)S(1)} %xor.46.ids, bf16[1024,1024]{1,0:T(8,128)(2,1)} %copy-done.26, bf16[16,1024]{1,0:T(8,128)(2,1)S(1)} %copy-done.65, ...), custom_call_target="tpu_custom_call" | custom-call | flops 1 | bytes 1 | tf_op jit(solution)/shard_map/fold/pallas_call | solution.py:273
  301.1 4.5 collective-permute-start.38
  307.4 21.8 %collective-permute-done.38.refs_2_ = bf16[256,2048]{1,0:T(8,128)(2,1)S(1)} collective-permute-done((bf16[256,2048]{1,0:T(8,128)(2,1)S(1)}, bf16[256,2048]{1,0:T(8,128)(2,1)S(1)}, u32[]{:S(2)}, u32[]{:S(2)}) %collective-permute-start.38) | collective-permute-done | bytes 1048608 | tf_op jit(solution)/shard_map/ppermute | solution.py:783
  335.1 9.1 %hidden_grad.1 = (f32[1024,1024]{1,0:T(8,128)S(1)}, bf16[16,1024]{1,0:T(8,128)(2,1)S(1)}) custom-call(s32[8]{0:T(128)S(1)} %xor.46.ids, bf16[16,2048]{1,0:T(8,128)(2,1)S(1)} %dynamic-slice_bitcast_fusion.2.low_back.low_out, bf16[16,1024]{1,0:T(8,128)(2,1)S(1)} %get-tuple-element.356.low_in.down_in, ...), custom_call_target="tpu_custom_call" | custom-call | flops 1 | bytes 1 | tf_op jit(solution)/shard_map/hidden_grad/pallas_call | solution.py:351
  344.3 12.5 %collective-permute-done.41.part2 = bf16[256,2048]{1,0:T(8,128)(2,1)S(1)} collective-permute-done((bf16[256,2048]{1,0:T(8,128)(2,1)S(1)}, bf16[256,2048]{1,0:T(8,128)(2,1)S(1)}, u32[]{:S(2)}, u32[]{:S(2)}) %collective-permute-start.41) | collective-permute-done | bytes 1048608 | tf_op jit(solution)/shard_map/ppermute | solution.py:783
  362.3 20.3 %collective-permute-done.47.refs_2_.refs_6_ = bf16[256,2048]{1,0:T(8,128)(2,1)S(1)} collective-permute-done((bf16[256,2048]{1,0:T(8,128)(2,1)S(1)}, bf16[256,2048]{1,0:T(8,128)(2,1)S(1)}, u32[]{:S(2)}, u32[]{:S(2)}) %collective-permute-start.47) | collective-permute-done | bytes 1048608 | tf_op jit(solution)/shard_map/ppermute | solution.py:783
  388.1 18.6 %mlp.1 = (bf16[1024,1024]{1,0:T(8,128)(2,1)}, bf16[1024,1024]{1,0:T(8,128)(2,1)}, bf16[1024,1024]{1,0:T(8,128)(2,1)}, bf16[32,1024]{1,0:T(8,128)(2,1)}, f32[48,1...) custom-call(s32[8]{0:T(128)S(1)} %xor.46.ids, ...), custom_call_target="tpu_custom_call" | custom-call | flops 1 | bytes 1 | tf_op jit(solution)/shard_map/mlp/pallas_call | solution.py:404
  409.8 8.9 %unfold.7 = (bf16[256,2048]{1,0:T(8,128)(2,1)}, bf16[256,2048]{1,0:T(8,128)(2,1)S(1)}) custom-call(s32[8]{0:T(128)S(1)} %xor.46.ids, bf16[32,2048]{1,0:T(8,128)(2,1)S(1)} %dynamic-slice_bitcast_fusion.1.low_in, f32[32,1024]{1,0:T(8,128)S(1)} %slice.162.refs_0_.refs_1_, f32[32,1024]{1,0:T(8,128)S(1)} %slice.162.refs_0_.refs_1_, ...), custom_call_target="tpu_custom_call" | custom-call | flops 1 | bytes 1 | tf_op jit(solution)/shard_map/unfold/pallas_call | solution.py:451
  419.6 4.9 unfold.8
  429.3 4.9 unfold.6.part0
  434.3 9.7 %fold.3 = (bf16[256,2048]{1,0:T(8,128)(2,1)S(1)}, bf16[256,2048]{1,0:T(8,128)(2,1)S(1)}, bf16[256,2048]{1,0:T(8,128)(2,1)S(1)}, bf16[256,2048]{1,0:T(8,128)(2,1)S(1)}, f32[16,1024]{1,0:T(8,128)}) custom-call(s32[8]{0:T(128)S(1)} %xor.46.ids, bf16[1024,1024]{1,0:T(8,128)(2,1)} %get-tuple-element.240.act, ...), custom_call_target="tpu_custom_call" | custom-call | flops 1 | bytes 1 | tf_op jit(solution)/shard_map/fold/pallas_call | solution.py:273
  444.1 6.3 collective-permute-done.53.part2
  461.2 21.2 %collective-permute-done.57.refs_2_.refs_10_ = bf16[256,2048]{1,0:T(8,128)(2,1)} collective-permute-done((bf16[256,2048]{1,0:T(8,128)(2,1)S(1)}, bf16[256,2048]{1,0:T(8,128)(2,1)}, u32[]{:S(2)}, u32[]{:S(2)}) %collective-permute-start.57) | collective-permute-done | bytes 1048608 | tf_op jit(solution)/shard_map/ppermute | solution.py:783
  488.8 15.4 %gate_back.1 = (bf16[1024,1024]{1,0:T(8,128)(2,1)}, bf16[1024,1024]{1,0:T(8,128)(2,1)}, bf16[16,1024]{1,0:T(8,128)(2,1)}, f32[64,1024]{1,0:T(8,128)}, bf16[16,10...) custom-call(s32[8]{0:T(128)} %copy-done.67, bf16[16,2048]{1,0:T(8,128)(2,1)} %dynamic-slice_bitcast_fusion.3.low_out.low_back, ...), custom_call_target="tpu_custom_call" | custom-call | flops 1 | bytes 1 | tf_op jit(solution)/shard_map/gate_back/pallas_call | solution.py:502
  507.0 4.4 collective-permute-done.60
  513.4 12.0 %retention_back.1 = (bf16[1024,512]{1,0:T(8,128)(2,1)S(1)}, bf16[1024,512]{1,0:T(8,128)(2,1)S(1)}, bf16[1024,1024]{1,0:T(8,128)(2,1)}, f32[64,1024]{1,0:T(8,128)...) custom-call(s32[4]{0:T(128)S(1)} %copy-done.74, f32[2]{0:T(128)S(1)} %copy-done.76, ...), custom_call_target="tpu_custom_call" | custom-call | flops 1 | bytes 1 | tf_op jit(solution)/shard_map/retention_back/pallas_call | solution.py:584
  528.8 12.1 %unfold.9 = (bf16[256,2048]{1,0:T(8,128)(2,1)S(1)}, bf16[256,2048]{1,0:T(8,128)(2,1)}) custom-call(s32[8]{0:T(128)S(1)} %copy-done.68, bf16[64,2048]{1,0:T(8,128)(2,1)S(1)} %copy-done.32, f32[64,1024]{1,0:T(8,128)S(1)} %get-tuple-element.270.refs_0_.refs_1_, f32[64,1024]{1,0:T(8,128)S(1)} %get-tuple-element.270.refs_0_.refs_1_, ...), custom_call_target="tpu_custom_call" | custom-call | flops 1 | bytes 1 | tf_op jit(solution)/shard_map/unfold/pallas_call | solution.py:451
  545.2 5.2 collective-permute-done.68
  555.2 7.2 %unfold.10 = bf16[256,2048]{1,0:T(8,128)(2,1)S(1)} custom-call(s32[8]{0:T(128)S(1)} %copy-done.68, bf16[64,2048]{1,0:T(8,128)(2,1)S(1)} %copy-done.33, f32[64,1024]{1,0:T(8,128)S(1)} %get-tuple-element.270.refs_0_.refs_1_, bf16[1024,1024]{1,0:T(8,128)(2,1)} %copy-done.78, bf16[1024,1024]{1,0:T(8,128)(2,1)} %get-tuple-element.289.refs_3_.refs_6_.refs_2_, ...), custom_call_target="tpu_custom_call" | custom-call | flops 1 | bytes 1 | tf_op jit(solution)/shard_map/unfold/pallas_call | solution.py:451
  568.0 5.4 collective-permute-done.74
  573.5 3.5 collective-permute-done.75
  577.1 8.5 %collective-permute-done.76 = bf16[128,512]{1,0:T(8,128)(2,1)S(1)} collective-permute-done((bf16[128,512]{1,0:T(8,128)(2,1)S(1)}, bf16[128,512]{1,0:T(8,128)(2,1)S(1)}, u32[]{:S(2)}, u32[]{:S(2)}) %collective-permute-start.76) | collective-permute-done | bytes 131104 | tf_op jit(solution)/shard_map/ppermute | solution.py:783
  588.3 6.3 collective-permute-done.77
  596.4 7.5 %unfold.11.part0 = bf16[256,2048]{1,0:T(8,128)(2,1)S(1)} custom-call(s32[8]{0:T(128)S(1)} %copy-done.68, bf16[64,2048]{1,0:T(8,128)(2,1)S(1)} %copy-done.33, f32[64,1024]{1,0:T(8,128)S(1)} %get-tuple-element.270.refs_0_.refs_1_, bf16[1024,1024]{1,0:T(8,128)(2,1)} %copy-done.78, bf16[1024,1024]{1,0:T(8,128)(2,1)} %get-tuple-element.289.refs_3_.refs_6_.refs_2_, ...), custom_call_target="tpu_custom_call" | custom-call | flops 1 | bytes 1 | tf_op jit(solution)/shard_map/unfold/pallas_call | solution.py:451
  603.9 15.1 %collective-permute-done.72.part2 = bf16[128,2048]{1,0:T(8,128)(2,1)S(1)} collective-permute-done((bf16[128,2048]{1,0:T(8,128)(2,1)S(1)}, bf16[128,2048]{1,0:T(8,128)(2,1)S(1)}, u32[]{:S(2)}, u32[]{:S(2)}) %collective-permute-start.72) | collective-permute-done | bytes 524320 | tf_op jit(solution)/shard_map/ppermute | solution.py:783
  619.8 3.5 collective-permute-start.73
  623.3 7.0 %collective-permute-done.70.part2 = bf16[128,2048]{1,0:T(8,128)(2,1)S(1)} collective-permute-done((bf16[128,2048]{1,0:T(8,128)(2,1)S(1)}, bf16[128,2048]{1,0:T(8,128)(2,1)S(1)}, u32[]{:S(2)}, u32[]{:S(2)}) %collective-permute-start.70) | collective-permute-done | bytes 524320 | tf_op jit(solution)/shard_map/ppermute | solution.py:783
  635.7 6.5 collective-permute-done.73
  642.3 5.5 collective-permute-done.71
  654.7 4.4 place.3
  659.1 4.1 place.2
  (492 shorter events, 182.5 us)
Async XLA Ops:
  7.2 642.3 %all-gather.3.cloned.1.call-start = ((), (), s32[]{:S(2)}) async-start(), calls=%async_computation | async-start | bytes 3981312 | tf_op jit(solution)/shard_map/all_gather | solution.py:990
  10.0 15.8 %collective-permute-start.5 = (bf16[1024,256]{1,0:T(8,128)(2,1)}, bf16[1024,256]{1,0:T(8,128)(2,1)}, u32[]{:S(2)}, u32[]{:S(2)}) collective-permute-start(bf16[1024,256]{1,0:T(8,128)(2,1)} %param.34), channel_id=1, source_target_pairs={{0,4},{1,5},{2,6},{3,7},{4,0},{5,1},{6,2},{7,3},{8,12},{9,13},{10,... | collective-permute-start | bytes 1572872 | tf_op jit(solution)/shard_map/ppermute | solution.py:777
  13.2 28.4 %collective-permute-start.3 = (bf16[2,256,1024]{2,1,0:T(8,128)(2,1)}, bf16[2,256,1024]{2,1,0:T(8,128)(2,1)}, u32[]{:S(2)}, u32[]{:S(2)}) collective-permute-start(bf16[2,256,1024]{2,1,0:T(8,128)(2,1)} %pad_maximum_fusion.4), channel_id=1, source_target_pairs={{0,2},{1,3},{6,4},{7,5},{8,10},{9,11},{14,12},{15,13},{16,18},{17,... | collective-permute-start | bytes 3145736 | tf_op jit(solution)/shard_map/ppermute | solution.py:783
  25.9 17.2 %collective-permute-start.4 = (s32[1,1152]{1,0:T(1,128)S(1)}, s32[1,1152]{1,0:T(1,128)S(1)}, u32[]{:S(2)}, u32[]{:S(2)}) collective-permute-start(s32[1,1152]{1,0:T(1,128)S(1)} %concatenate.97), channel_id=1, source_target_pairs={{0,4},{1,5},{2,6},{3,7},{4,0},{5,1},{6,2},{7,3},{8,12},{9,13},{10,... | collective-permute-start | bytes 13832 | tf_op jit(solution)/shard_map/ppermute | solution.py:777
  46.7 42.5 %collective-permute-start.9 = (bf16[2,256,1024]{2,1,0:T(8,128)(2,1)}, bf16[2,256,1024]{2,1,0:T(8,128)(2,1)}, u32[]{:S(2)}, u32[]{:S(2)}) collective-permute-start(bf16[2,256,1024]{2,1,0:T(8,128)(2,1)} %pad_maximum_fusion.3), channel_id=1, source_target_pairs={{0,2},{1,3},{6,4},{7,5},{8,10},{9,11},{14,12},{15,13},{16,18},{17,... | collective-permute-start | bytes 3145736 | tf_op jit(solution)/shard_map/ppermute | solution.py:783
  48.0 42.8 %collective-permute-start.10 = (bf16[2,256,1024]{2,1,0:T(8,128)(2,1)S(1)}, bf16[2,256,1024]{2,1,0:T(8,128)(2,1)}, u32[]{:S(2)}, u32[]{:S(2)}) collective-permute-start(bf16[2,256,1024]{2,1,0:T(8,128)(2,1)S(1)} %broadcast_select_fusion.6.refs_4_.refs_8_), channel_id=1, source_target_pairs={{0,8},{1,9},{2,10},{3,11},{4,12},{5,13},{6,14},{7,15},{8,0},{9,1},... | collective-permute-start | bytes 3145736 | tf_op jit(solution)/shard_map/ppermute | solution.py:783
  49.9 40.9 %collective-permute-start.11 = (bf16[2,256,1024]{2,1,0:T(8,128)(2,1)S(1)}, bf16[2,256,1024]{2,1,0:T(8,128)(2,1)}, u32[]{:S(2)}, u32[]{:S(2)}) collective-permute-start(bf16[2,256,1024]{2,1,0:T(8,128)(2,1)S(1)} %broadcast_select_fusion.6.refs_4_.refs_8_), channel_id=1, source_target_pairs={{0,16},{1,17},{2,18},{3,19},{4,20},{5,21},{6,22},{7,23},{8,24},{9,... | collective-permute-start | bytes 3145736 | tf_op jit(solution)/shard_map/ppermute | solution.py:783
  92.1 19.1 %collective-permute-start.14 = (bf16[2,256,1024]{2,1,0:T(8,128)(2,1)}, bf16[2,256,1024]{2,1,0:T(8,128)(2,1)S(1)}, u32[]{:S(2)}, u32[]{:S(2)}) collective-permute-start(bf16[2,256,1024]{2,1,0:T(8,128)(2,1)} %collective-permute-done.10.refs_5_.refs_9_), channel_id=1, source_target_pairs={{0,16},{1,17},{2,18},{3,19},{4,20},{5,21},{6,22},{7,23},{8,24},{9,... | collective-permute-start | bytes 3145736 | tf_op jit(solution)/shard_map/ppermute | solution.py:783
  93.3 21.1 %collective-permute-start.12 = (bf16[2,256,1024]{2,1,0:T(8,128)(2,1)S(1)}, bf16[2,256,1024]{2,1,0:T(8,128)(2,1)S(1)}, u32[]{:S(2)}, u32[]{:S(2)}) collective-permute-start(bf16[2,256,1024]{2,1,0:T(8,128)(2,1)S(1)} %copy-done.98), channel_id=1, source_target_pairs={{0,2},{1,3},{6,4},{7,5},{8,10},{9,11},{14,12},{15,13},{16,18},{17,... | collective-permute-start | bytes 3145736 | tf_op jit(solution)/shard_map/ppermute | solution.py:783
  94.6 26.4 %collective-permute-start.15 = (bf16[2,1024,256]{2,1,0:T(8,128)(2,1)S(1)}, bf16[2,1024,256]{2,1,0:T(8,128)(2,1)S(1)}, u32[]{:S(2)}, u32[]{:S(2)}) collective-permute-start(bf16[2,1024,256]{2,1,0:T(8,128)(2,1)S(1)} %copy-done.99), channel_id=1, source_target_pairs={{0,2},{1,3},{6,4},{7,5},{8,10},{9,11},{14,12},{15,13},{16,18},{17,... | collective-permute-start | bytes 3145736 | tf_op jit(solution)/shard_map/ppermute | solution.py:783
  112.2 18.6 %collective-permute-start.16 = (bf16[2,256,1024]{2,1,0:T(8,128)(2,1)S(1)}, bf16[2,256,1024]{2,1,0:T(8,128)(2,1)S(1)}, u32[]{:S(2)}, u32[]{:S(2)}) collective-permute-start(bf16[2,256,1024]{2,1,0:T(8,128)(2,1)S(1)} %broadcast_select_fusion.5.refs_4_.refs_12_.refs_8_), channel_id=1, source_target_pairs={{0,16},{1,17},{2,18},{3,19},{4,20},{5,21},{6,22},{7,23},{8,24},{9,... | collective-permute-start | bytes 3145736 | tf_op jit(solution)/shard_map/ppermute | solution.py:783
  133.8 45.3 %collective-permute-start.17 = (bf16[256,2048]{1,0:T(8,128)(2,1)}, bf16[256,2048]{1,0:T(8,128)(2,1)}, u32[]{:S(2)}, u32[]{:S(2)}) collective-permute-start(bf16[256,2048]{1,0:T(8,128)(2,1)} %bitcast), channel_id=1, source_target_pairs={{2,4},{3,5},{4,2},{5,3},{10,12},{11,13},{12,10},{13,11},{18,20},{1... | collective-permute-start | bytes 3145736 | tf_op jit(solution)/shard_map/ppermute | solution.py:783
  135.7 46.4 %collective-permute-start.21 = (bf16[2,1024,256]{2,1,0:T(8,128)(2,1)}, bf16[2,1024,256]{2,1,0:T(8,128)(2,1)}, u32[]{:S(2)}, u32[]{:S(2)}) collective-permute-start(bf16[2,1024,256]{2,1,0:T(8,128)(2,1)} %pad_maximum_fusion.6), channel_id=1, source_target_pairs={{0,2},{1,3},{6,4},{7,5},{8,10},{9,11},{14,12},{15,13},{16,18},{17,... | collective-permute-start | bytes 3145736 | tf_op jit(solution)/shard_map/ppermute | solution.py:783
  147.5 34.7 %collective-permute-start.22 = (bf16[2,256,1024]{2,1,0:T(8,128)(2,1)}, bf16[2,256,1024]{2,1,0:T(8,128)(2,1)}, u32[]{:S(2)}, u32[]{:S(2)}) collective-permute-start(bf16[2,256,1024]{2,1,0:T(8,128)(2,1)} %copy-done.15), channel_id=1, source_target_pairs={{0,8},{1,9},{2,10},{3,11},{4,12},{5,13},{6,14},{7,15},{8,0},{9,1},... | collective-permute-start | bytes 3145736 | tf_op jit(solution)/shard_map/ppermute | solution.py:783
  148.0 34.2 %collective-permute-start.23 = (bf16[2,256,1024]{2,1,0:T(8,128)(2,1)}, bf16[2,256,1024]{2,1,0:T(8,128)(2,1)}, u32[]{:S(2)}, u32[]{:S(2)}) collective-permute-start(bf16[2,256,1024]{2,1,0:T(8,128)(2,1)} %collective-permute-done.18.refs_5_.refs_17_.refs_13_), channel_id=1, source_target_pairs={{0,16},{1,17},{2,18},{3,19},{4,20},{5,21},{6,22},{7,23},{8,24},{9,... | collective-permute-start | bytes 3145736 | tf_op jit(solution)/shard_map/ppermute | solution.py:783
  152.1 30.1 %collective-permute-start.20 = (bf16[112,1024]{1,0:T(8,128)(2,1)S(1)}, bf16[112,1024]{1,0:T(8,128)(2,1)S(1)}, u32[]{:S(2)}, u32[]{:S(2)}) collective-permute-start(bf16[112,1024]{1,0:T(8,128)(2,1)S(1)} %get-tuple-element.172), channel_id=1, source_target_pairs={{0,2},{1,3},{6,4},{7,5},{8,10},{9,11},{14,12},{15,13},{16,18},{17,... | collective-permute-start | bytes 688136 | tf_op jit(solution)/shard_map/ppermute | solution.py:783
  188.0 34.3 %collective-permute-start.24 = (bf16[2,256,1024]{2,1,0:T(8,128)(2,1)}, bf16[2,256,1024]{2,1,0:T(8,128)(2,1)}, u32[]{:S(2)}, u32[]{:S(2)}) collective-permute-start(bf16[2,256,1024]{2,1,0:T(8,128)(2,1)} %pad_maximum_fusion.7), channel_id=1, source_target_pairs={{0,2},{1,3},{6,4},{7,5},{8,10},{9,11},{14,12},{15,13},{16,18},{17,... | collective-permute-start | bytes 3145736 | tf_op jit(solution)/shard_map/ppermute | solution.py:783
  189.3 45.6 %collective-permute-start.25 = (bf16[256,2048]{1,0:T(8,128)(2,1)}, bf16[256,2048]{1,0:T(8,128)(2,1)}, u32[]{:S(2)}, u32[]{:S(2)}) collective-permute-start(bf16[256,2048]{1,0:T(8,128)(2,1)} %norm_rows.1.refs_0_), channel_id=1, source_target_pairs={{0,1},{1,0},{2,3},{3,2},{4,5},{5,4},{6,7},{7,6},{8,9},{9,8},{10,11... | collective-permute-start | bytes 3145736 | tf_op jit(solution)/shard_map/ppermute | solution.py:783
  189.4 45.6 %collective-permute-start.28 = (bf16[256,2048]{1,0:T(8,128)(2,1)}, bf16[256,2048]{1,0:T(8,128)(2,1)}, u32[]{:S(2)}, u32[]{:S(2)}) collective-permute-start(bf16[256,2048]{1,0:T(8,128)(2,1)} %bitcast.37), channel_id=1, source_target_pairs={{2,4},{3,5},{4,2},{5,3},{10,12},{11,13},{12,10},{13,11},{18,20},{1... | collective-permute-start | bytes 3145736 | tf_op jit(solution)/shard_map/ppermute | solution.py:783
  197.3 37.6 %collective-permute-start.29 = (bf16[2,1024,256]{2,1,0:T(8,128)(2,1)}, bf16[2,1024,256]{2,1,0:T(8,128)(2,1)}, u32[]{:S(2)}, u32[]{:S(2)}) collective-permute-start(bf16[2,1024,256]{2,1,0:T(8,128)(2,1)} %broadcast_select_fusion.refs_4_.refs_0_), channel_id=1, source_target_pairs={{0,8},{1,9},{2,10},{3,11},{4,12},{5,13},{6,14},{7,15},{8,0},{9,1},... | collective-permute-start | bytes 3145736 | tf_op jit(solution)/shard_map/ppermute | solution.py:783
  198.7 36.3 %collective-permute-start.30 = (bf16[2,1024,256]{2,1,0:T(8,128)(2,1)}, bf16[2,1024,256]{2,1,0:T(8,128)(2,1)}, u32[]{:S(2)}, u32[]{:S(2)}) collective-permute-start(bf16[2,1024,256]{2,1,0:T(8,128)(2,1)} %collective-permute-done.26.refs_1_.refs_5_), channel_id=1, source_target_pairs={{0,16},{1,17},{2,18},{3,19},{4,20},{5,21},{6,22},{7,23},{8,24},{9,... | collective-permute-start | bytes 3145736 | tf_op jit(solution)/shard_map/ppermute | solution.py:783
  235.0 30.5 %collective-permute-start.31 = (bf16[2,1024,256]{2,1,0:T(8,128)(2,1)}, bf16[2,1024,256]{2,1,0:T(8,128)(2,1)S(1)}, u32[]{:S(2)}, u32[]{:S(2)}) collective-permute-start(bf16[2,1024,256]{2,1,0:T(8,128)(2,1)} %broadcast_select_fusion.refs_4_.refs_0_), channel_id=1, source_target_pairs={{0,16},{1,17},{2,18},{3,19},{4,20},{5,21},{6,22},{7,23},{8,24},{9,... | collective-permute-start | bytes 3145736 | tf_op jit(solution)/shard_map/ppermute | solution.py:783
  239.3 26.1 %collective-permute-start.34 = (bf16[2,256,1024]{2,1,0:T(8,128)(2,1)S(1)}, bf16[2,256,1024]{2,1,0:T(8,128)(2,1)S(1)}, u32[]{:S(2)}, u32[]{:S(2)}) collective-permute-start(bf16[2,256,1024]{2,1,0:T(8,128)(2,1)S(1)} %broadcast_select_fusion.3.refs_4_.refs_3_.refs_6_), channel_id=1, source_target_pairs={{0,8},{1,9},{2,10},{3,11},{4,12},{5,13},{6,14},{7,15},{8,0},{9,1},... | collective-permute-start | bytes 3145736 | tf_op jit(solution)/shard_map/ppermute | solution.py:783
  240.7 27.7 %collective-permute-start.35 = (bf16[2,256,1024]{2,1,0:T(8,128)(2,1)S(1)}, bf16[2,256,1024]{2,1,0:T(8,128)(2,1)S(1)}, u32[]{:S(2)}, u32[]{:S(2)}) collective-permute-start(bf16[2,256,1024]{2,1,0:T(8,128)(2,1)S(1)} %copy-done.97), channel_id=1, source_target_pairs={{0,2},{1,3},{6,4},{7,5},{8,10},{9,11},{14,12},{15,13},{16,18},{17,... | collective-permute-start | bytes 3145736 | tf_op jit(solution)/shard_map/ppermute | solution.py:783
  301.1 28.2 %collective-permute-start.38 = (bf16[256,2048]{1,0:T(8,128)(2,1)S(1)}, bf16[256,2048]{1,0:T(8,128)(2,1)S(1)}, u32[]{:S(2)}, u32[]{:S(2)}) collective-permute-start(bf16[256,2048]{1,0:T(8,128)(2,1)S(1)} %broadcast_select_fusion.7.refs_0_.grad_in), channel_id=1, source_target_pairs={{0,1},{1,0},{2,3},{3,2},{4,5},{5,4},{6,7},{7,6},{8,9},{9,8},{10,11... | collective-permute-start | bytes 3145736 | tf_op jit(solution)/shard_map/ppermute | solution.py:783
  305.6 24.6 %collective-permute-start.39 = (bf16[2,1024,256]{2,1,0:T(8,128)(2,1)S(1)}, bf16[2,1024,256]{2,1,0:T(8,128)(2,1)S(1)}, u32[]{:S(2)}, u32[]{:S(2)}) collective-permute-start(bf16[2,1024,256]{2,1,0:T(8,128)(2,1)S(1)} %collective-permute-done.31.refs_6_.refs_2_), channel_id=1, source_target_pairs={{0,8},{1,9},{2,10},{3,11},{4,12},{5,13},{6,14},{7,15},{8,0},{9,1},... | collective-permute-start | bytes 3145736 | tf_op jit(solution)/shard_map/ppermute | solution.py:783
  305.6 24.6 %collective-permute-start.40 = (bf16[2,256,1024]{2,1,0:T(8,128)(2,1)S(1)}, bf16[2,256,1024]{2,1,0:T(8,128)(2,1)}, u32[]{:S(2)}, u32[]{:S(2)}) collective-permute-start(bf16[2,256,1024]{2,1,0:T(8,128)(2,1)S(1)} %broadcast_select_fusion.3.refs_4_.refs_3_.refs_6_), channel_id=1, source_target_pairs={{0,16},{1,17},{2,18},{3,19},{4,20},{5,21},{6,22},{7,23},{8,24},{9,... | collective-permute-start | bytes 3145736 | tf_op jit(solution)/shard_map/ppermute | solution.py:783
  331.8 24.9 %collective-permute-start.41 = (bf16[256,2048]{1,0:T(8,128)(2,1)S(1)}, bf16[256,2048]{1,0:T(8,128)(2,1)S(1)}, u32[]{:S(2)}, u32[]{:S(2)}) collective-permute-start(bf16[256,2048]{1,0:T(8,128)(2,1)S(1)} %add_convert_fusion.4), channel_id=1, source_target_pairs={{0,1},{1,0},{2,3},{3,2},{4,5},{5,4},{6,7},{7,6},{8,9},{9,8},{10,11... | collective-permute-start | bytes 3145736 | tf_op jit(solution)/shard_map/ppermute | solution.py:783
  331.8 26.0 %collective-permute-start.45 = (bf16[2,256,1024]{2,1,0:T(8,128)(2,1)}, bf16[2,256,1024]{2,1,0:T(8,128)(2,1)}, u32[]{:S(2)}, u32[]{:S(2)}) collective-permute-start(bf16[2,256,1024]{2,1,0:T(8,128)(2,1)} %broadcast_select_fusion.2.refs_8_.refs_7_.refs_10_), channel_id=1, source_target_pairs={{0,8},{1,9},{2,10},{3,11},{4,12},{5,13},{6,14},{7,15},{8,0},{9,1},... | collective-permute-start | bytes 3145736 | tf_op jit(solution)/shard_map/ppermute | solution.py:783
  333.6 24.6 %collective-permute-start.46 = (bf16[2,256,1024]{2,1,0:T(8,128)(2,1)}, bf16[2,256,1024]{2,1,0:T(8,128)(2,1)S(1)}, u32[]{:S(2)}, u32[]{:S(2)}) collective-permute-start(bf16[2,256,1024]{2,1,0:T(8,128)(2,1)} %broadcast_select_fusion.2.refs_8_.refs_7_.refs_10_), channel_id=1, source_target_pairs={{0,16},{1,17},{2,18},{3,19},{4,20},{5,21},{6,22},{7,23},{8,24},{9,... | collective-permute-start | bytes 3145736 | tf_op jit(solution)/shard_map/ppermute | solution.py:783
  359.2 23.5 %collective-permute-start.47 = (bf16[256,2048]{1,0:T(8,128)(2,1)S(1)}, bf16[256,2048]{1,0:T(8,128)(2,1)S(1)}, u32[]{:S(2)}, u32[]{:S(2)}) collective-permute-start(bf16[256,2048]{1,0:T(8,128)(2,1)S(1)} %get-tuple-element.237.refs_0_.refs_4_), channel_id=1, source_target_pairs={{0,1},{1,0},{2,3},{3,2},{4,5},{5,4},{6,7},{7,6},{8,9},{9,8},{10,11... | collective-permute-start | bytes 3145736 | tf_op jit(solution)/shard_map/ppermute | solution.py:783
  360.1 25.6 %collective-permute-start.44 = (bf16[256,2048]{1,0:T(8,128)(2,1)S(1)}, bf16[256,2048]{1,0:T(8,128)(2,1)S(1)}, u32[]{:S(2)}, u32[]{:S(2)}) collective-permute-start(bf16[256,2048]{1,0:T(8,128)(2,1)S(1)} %get-tuple-element.237.refs_0_.refs_4_), channel_id=1, source_target_pairs={{0,4},{1,5},{2,6},{3,7},{4,0},{5,1},{6,2},{7,3},{8,12},{9,13},{10,... | collective-permute-start | bytes 3145736 | tf_op jit(solution)/shard_map/ppermute | solution.py:777
  361.8 25.0 %collective-permute-start.49 = (bf16[2,256,1024]{2,1,0:T(8,128)(2,1)}, bf16[2,256,1024]{2,1,0:T(8,128)(2,1)S(1)}, u32[]{:S(2)}, u32[]{:S(2)}) collective-permute-start(bf16[2,256,1024]{2,1,0:T(8,128)(2,1)} %collective-permute-done.40.refs_6_.refs_5_.refs_8_), channel_id=1, source_target_pairs={{0,8},{1,9},{2,10},{3,11},{4,12},{5,13},{6,14},{7,15},{8,0},{9,1},... | collective-permute-start | bytes 3145736 | tf_op jit(solution)/shard_map/ppermute | solution.py:783
  362.1 24.7 %collective-permute-start.50 = (bf16[2,256,1024]{2,1,0:T(8,128)(2,1)}, bf16[2,256,1024]{2,1,0:T(8,128)(2,1)S(1)}, u32[]{:S(2)}, u32[]{:S(2)}) collective-permute-start(bf16[2,256,1024]{2,1,0:T(8,128)(2,1)} %collective-permute-done.45.refs_9_.refs_8_.refs_11_), channel_id=1, source_target_pairs={{0,16},{1,17},{2,18},{3,19},{4,20},{5,21},{6,22},{7,23},{8,24},{9,... | collective-permute-start | bytes 3145736 | tf_op jit(solution)/shard_map/ppermute | solution.py:783
  419.5 24.6 %collective-permute-start.51 = (bf16[256,2048]{1,0:T(8,128)(2,1)}, bf16[256,2048]{1,0:T(8,128)(2,1)S(1)}, u32[]{:S(2)}, u32[]{:S(2)}) collective-permute-start(bf16[256,2048]{1,0:T(8,128)(2,1)} %get-tuple-element.245), channel_id=1, source_target_pairs={{0,4},{1,5},{2,6},{3,7},{4,0},{5,1},{6,2},{7,3},{8,12},{9,13},{10,... | collective-permute-start | bytes 3145736 | tf_op jit(solution)/shard_map/ppermute | solution.py:783
  425.9 24.5 %collective-permute-start.53 = (bf16[256,2048]{1,0:T(8,128)(2,1)}, bf16[256,2048]{1,0:T(8,128)(2,1)S(1)}, u32[]{:S(2)}, u32[]{:S(2)}) collective-permute-start(bf16[256,2048]{1,0:T(8,128)(2,1)} %add_convert_fusion.3), channel_id=1, source_target_pairs={{0,1},{1,0},{2,3},{3,2},{4,5},{5,4},{6,7},{7,6},{8,9},{9,8},{10,11... | collective-permute-start | bytes 3145736 | tf_op jit(solution)/shard_map/ppermute | solution.py:783
  429.2 25.5 %collective-permute-start.55 = (bf16[64,1024]{1,0:T(8,128)(2,1)S(1)}, bf16[64,1024]{1,0:T(8,128)(2,1)S(1)}, u32[]{:S(2)}, u32[]{:S(2)}) collective-permute-start(bf16[64,1024]{1,0:T(8,128)(2,1)S(1)} %fusion.2), channel_id=1, source_target_pairs={{0,1},{1,0},{2,3},{3,2},{4,5},{5,4},{6,7},{7,6},{8,9},{9,8},{10,11... | collective-permute-start | bytes 393224 | tf_op jit(solution)/shard_map/ppermute | solution.py:783
  457.6 24.9 %collective-permute-start.57 = (bf16[256,2048]{1,0:T(8,128)(2,1)S(1)}, bf16[256,2048]{1,0:T(8,128)(2,1)}, u32[]{:S(2)}, u32[]{:S(2)}) collective-permute-start(bf16[256,2048]{1,0:T(8,128)(2,1)S(1)} %get-tuple-element.258.refs_0_.refs_8_), channel_id=1, source_target_pairs={{0,1},{1,0},{2,3},{3,2},{4,5},{5,4},{6,7},{7,6},{8,9},{9,8},{10,11... | collective-permute-start | bytes 3145736 | tf_op jit(solution)/shard_map/ppermute | solution.py:783
  459.0 23.5 %collective-permute-start.59 = (bf16[256,2048]{1,0:T(8,128)(2,1)S(1)}, bf16[256,2048]{1,0:T(8,128)(2,1)S(1)}, u32[]{:S(2)}, u32[]{:S(2)}) collective-permute-start(bf16[256,2048]{1,0:T(8,128)(2,1)S(1)} %get-tuple-element.258.refs_0_.refs_8_), channel_id=1, source_target_pairs={{0,4},{1,5},{2,6},{3,7},{4,0},{5,1},{6,2},{7,3},{8,12},{9,13},{10,... | collective-permute-start | bytes 3145736 | tf_op jit(solution)/shard_map/ppermute | solution.py:783
  459.3 23.2 %collective-permute-start.56 = (bf16[256,2048]{1,0:T(8,128)(2,1)S(1)}, bf16[256,2048]{1,0:T(8,128)(2,1)S(1)}, u32[]{:S(2)}, u32[]{:S(2)}) collective-permute-start(bf16[256,2048]{1,0:T(8,128)(2,1)S(1)} %get-tuple-element.251), channel_id=1, source_target_pairs={{0,4},{1,5},{2,6},{3,7},{4,0},{5,1},{6,2},{7,3},{8,12},{9,13},{10,... | collective-permute-start | bytes 3145736 | tf_op jit(solution)/shard_map/ppermute | solution.py:783
  486.3 25.1 %collective-permute-start.60 = (bf16[256,2048]{1,0:T(8,128)(2,1)}, bf16[256,2048]{1,0:T(8,128)(2,1)S(1)}, u32[]{:S(2)}, u32[]{:S(2)}) collective-permute-start(bf16[256,2048]{1,0:T(8,128)(2,1)} %add_convert_fusion.2), channel_id=1, source_target_pairs={{0,1},{1,0},{2,3},{3,2},{4,5},{5,4},{6,7},{7,6},{8,9},{9,8},{10,11... | collective-permute-start | bytes 3145736 | tf_op jit(solution)/shard_map/ppermute | solution.py:783
  543.8 20.1 %collective-permute-start.67 = (bf16[256,2048]{1,0:T(8,128)(2,1)}, bf16[256,2048]{1,0:T(8,128)(2,1)}, u32[]{:S(2)}, u32[]{:S(2)}) collective-permute-start(bf16[256,2048]{1,0:T(8,128)(2,1)} %get-tuple-element.286), channel_id=1, source_target_pairs={{0,4},{1,5},{2,6},{3,7},{4,0},{5,1},{6,2},{7,3},{8,12},{9,13},{10,... | collective-permute-start | bytes 3145736 | tf_op jit(solution)/shard_map/ppermute | solution.py:783
  586.4 47.0 %collective-permute-start.61 = (bf16[256,2048]{1,0:T(8,128)(2,1)S(1)}, bf16[256,2048]{1,0:T(8,128)(2,1)}, u32[]{:S(2)}, u32[]{:S(2)}) collective-permute-start(bf16[256,2048]{1,0:T(8,128)(2,1)S(1)} %add_convert_fusion.1), channel_id=1, source_target_pairs={{2,4},{3,5},{4,2},{5,3},{10,12},{11,13},{12,10},{13,11},{18,20},{1... | collective-permute-start | bytes 3145736 | tf_op jit(solution)/shard_map/ppermute | solution.py:783
  594.6 38.4 %collective-permute-start.78 = (bf16[2,320,512]{2,1,0:T(8,128)(2,1)S(1)}, bf16[2,320,512]{2,1,0:T(8,128)(2,1)S(1)}, u32[]{:S(2)}, u32[]{:S(2)}) collective-permute-start(bf16[2,320,512]{2,1,0:T(8,128)(2,1)S(1)} %pad_maximum_fusion.10), channel_id=1, source_target_pairs={{0,16},{1,17},{2,18},{3,19},{4,20},{5,21},{6,22},{7,23},{8,24},{9,... | collective-permute-start | bytes 1966088 | tf_op jit(solution)/shard_map/ppermute | solution.py:783
  594.9 24.0 %collective-permute-start.72 = (bf16[128,2048]{1,0:T(8,128)(2,1)S(1)}, bf16[128,2048]{1,0:T(8,128)(2,1)S(1)}, u32[]{:S(2)}, u32[]{:S(2)}) collective-permute-start(bf16[128,2048]{1,0:T(8,128)(2,1)S(1)} %get-tuple-element.293), channel_id=1, source_target_pairs={{0,1},{1,0},{2,3},{3,2},{4,5},{5,4},{6,7},{7,6},{8,9},{9,8},{10,11... | collective-permute-start | bytes 1572872 | tf_op jit(solution)/shard_map/ppermute | solution.py:783
  594.9 35.4 %collective-permute-start.70 = (bf16[128,2048]{1,0:T(8,128)(2,1)S(1)}, bf16[128,2048]{1,0:T(8,128)(2,1)S(1)}, u32[]{:S(2)}, u32[]{:S(2)}) collective-permute-start(bf16[128,2048]{1,0:T(8,128)(2,1)S(1)} %get-tuple-element.290), channel_id=1, source_target_pairs={{0,1},{1,0},{2,3},{3,2},{4,5},{5,4},{6,7},{7,6},{8,9},{9,8},{10,11... | collective-permute-start | bytes 1572872 | tf_op jit(solution)/shard_map/ppermute | solution.py:783
  619.8 22.4 %collective-permute-start.73 = (bf16[128,2048]{1,0:T(8,128)(2,1)S(1)}, bf16[128,2048]{1,0:T(8,128)(2,1)S(1)}, u32[]{:S(2)}, u32[]{:S(2)}) collective-permute-start(bf16[128,2048]{1,0:T(8,128)(2,1)S(1)} %get-tuple-element.295), channel_id=1, source_target_pairs={{2,4},{3,5},{4,2},{5,3},{10,12},{11,13},{12,10},{13,11},{18,20},{1... | collective-permute-start | bytes 1572872 | tf_op jit(solution)/shard_map/ppermute | solution.py:783
  631.1 16.7 %collective-permute-start.71 = (bf16[128,2048]{1,0:T(8,128)(2,1)S(1)}, bf16[128,2048]{1,0:T(8,128)(2,1)S(1)}, u32[]{:S(2)}, u32[]{:S(2)}) collective-permute-start(bf16[128,2048]{1,0:T(8,128)(2,1)S(1)} %get-tuple-element.292), channel_id=1, source_target_pairs={{2,4},{3,5},{4,2},{5,3},{10,12},{11,13},{12,10},{13,11},{18,20},{1... | collective-permute-start | bytes 1572872 | tf_op jit(solution)/shard_map/ppermute | solution.py:783
  (151 other events, 2544.9 us)
Sparse Core Ops, SparseCore 0:
  551.3 33.4 all-gather.2

commit v2 on v1

--- a/solution.py
+++ b/solution.py
@@ -50,6 +50,10 @@
 
 def in_hbm(*arrays):
     return [pltpu.with_memory_space_constraint(array, pltpu.HBM) for array in arrays]
+
+
+def far(shape, kind):
+    return pltpu.HBM(shape, kind)
 
 
 def smem():
@@ -115,27 +119,10 @@
 def norm_rows(x, gain):
     return pl.pallas_call(
         norm_kernel,
-        out_shape=jax.ShapeDtypeStruct(x.shape, BF),
+        out_shape=far(x.shape, BF),
         compiler_params=pltpu.CompilerParams(vmem_limit_bytes=24 << 20),
         name="norm_rows",
     )(x, gain)
-
-
-def query_key_kernel(parts, ids, chunks, low_in, low_out, cosine, sine_table, *refs):
-    act, pieces, (out, low) = refs[:parts], refs[parts:-2], refs[-2:]
-    n = pl.program_id(0)
-
-    @pl.when(n == 0)
-    def _():
-        low[...] = low_rows(low_in[...], act).astype(BF)
-
-    product = dot(columns(act, ids), stacked(pieces)) + dot_tn(low[...], low_out[...])
-    scale = jnp.where(n >= pl.num_programs(0) // 2, 1.0 / KEY_DIM**0.5, 1.0)
-    size = out.shape[0] // chunks.shape[0]
-    for j in range(chunks.shape[0]):
-        at = aligned(chunks[j] * size, size)
-        rows = slice(j * size, (j + 1) * size)
-        out[rows, :] = (scale * rotated(product[rows], cosine[at, :], sine_table[at, :])).astype(BF)
 
 
 def piece_specs(pieces, width):
@@ -144,49 +131,74 @@
     ]
 
 
-def project_query_key(ids, chunks, act, low_in, low_out, cosine, sine_table, pieces):
+def project_kernel(layout, ids, chunks, low_in, low_out, *refs):
+    parts, count, lengths, turn = layout
+    if turn:
+        (cosine, sine_table), refs = refs[:2], refs[2:]
+    act, refs = refs[:parts], refs[parts:]
+    groups = len(lengths)
+    pieces, outs = refs[:groups * count], refs[groups * count:]
+    if turn:
+        low = outs[-1]
+
+        @pl.when(pl.program_id(0) == 0)
+        def _():
+            low[...] = low_rows(low_in[...], act).astype(BF)
+    else:
+        low = low_in
+    n = pl.program_id(0)
+    begin = 0
+    for i, length in enumerate(lengths):
+
+        @pl.when((n >= begin) & (n < begin + length))
+        def _(i=i, length=length):
+            made = dot(columns(act, ids), stacked(pieces[i * count:(i + 1) * count]))
+            made = made + dot_tn(low[...], low_out[...])
+            if i > 0 or not turn:
+                outs[i][...] = made.astype(BF)
+                return
+            scale = jnp.where(n >= length // 2, 1.0 / KEY_DIM**0.5, 1.0)
+            size = made.shape[0] // chunks.shape[0]
+            for j in range(chunks.shape[0]):
+                at = aligned(chunks[j] * size, size)
+                rows = slice(j * size, (j + 1) * size)
+                turned = rotated(made[rows], cosine[at, :], sine_table[at, :])
+                outs[i][rows, :] = (scale * turned).astype(BF)
+
+        begin += length
+
+
+def project(ids, chunks, act, low_in, low_out, weights, turn):
     rows, depth = row_count(act), act[0].shape[1]
-    width = pieces[0].shape[2]
     block = KEY_DIM
+    lengths = tuple(w[0].shape[2] // block for w in weights)
+    begins = [sum(lengths[:i]) for i in range(len(lengths))]
+
+    def at(group):
+        return lambda n: jnp.clip(n - begins[group], 0, lengths[group] - 1)
+
+    pieces = [
+        pl.BlockSpec((w.shape[0], w.shape[1], block), lambda n, at=at(i): (0, 0, at(n)))
+        for i, weight in enumerate(weights) for w in weight
+    ]
+    outs = [pl.BlockSpec((rows, block), lambda n, at=at(i): (0, at(n))) for i in range(len(weights))]
+    shapes = [far((rows, length * block), BF) for length in lengths]
+    ranks = low_in.shape[0]
+    if turn:
+        outs.append(full((ranks, rows)))
+        shapes.append(jax.ShapeDtypeStruct((ranks, rows), BF))
     return pl.pallas_call(
-        partial(query_key_kernel, len(act)),
-        grid=(width // block,),
+        partial(project_kernel, (len(act), len(weights[0]), lengths, bool(turn))),
+        grid=(sum(lengths),),
         in_specs=[smem(), smem(), full(low_in.shape),
-                  pl.BlockSpec((low_out.shape[0], block), lambda n: (0, n)),
-                  full(cosine.shape), full(cosine.shape)] + whole(act)
-        + piece_specs(pieces, block),
-        out_specs=[pl.BlockSpec((rows, block), lambda n: (0, n)),
-                   full((low_in.shape[0], rows))],
-        out_shape=[jax.ShapeDtypeStruct((rows, width), BF),
-                   jax.ShapeDtypeStruct((low_in.shape[0], rows), BF)],
-        compiler_params=params(40),
-        cost_estimate=estimate(2 * rows * depth * width, 2 * depth * width + 8 * rows * depth),
-        name="project_query_key",
-    )(ids, chunks, low_in, low_out, cosine, sine_table, *act, *pieces)
-
-
-def project_kernel(parts, ids, low, low_out, *refs):
-    act, pieces, out = refs[:parts], refs[parts:-1], refs[-1]
-    product = dot(columns(act, ids), stacked(pieces)) + dot_tn(low[...], low_out[...])
-    out[...] = product.astype(out.dtype)
-
-
-def project(ids, act, low, low_out, pieces, kind):
-    rows, depth = row_count(act), act[0].shape[1]
-    width = pieces[0].shape[2]
-    block = 256
-    return pl.pallas_call(
-        partial(project_kernel, len(act)),
-        grid=(width // block,),
-        in_specs=[smem(), full(low.shape),
-                  pl.BlockSpec((low_out.shape[0], block), lambda n: (0, n))]
-        + whole(act) + piece_specs(pieces, block),
-        out_specs=pl.BlockSpec((rows, block), lambda n: (0, n)),
-        out_shape=jax.ShapeDtypeStruct((rows, width), kind),
-        compiler_params=params(40),
-        cost_estimate=estimate(2 * rows * depth * width, 2 * depth * width + 8 * rows * depth),
+                  pl.BlockSpec((ranks, block), lambda n: (0, n))]
+        + whole(turn) + whole(act) + pieces,
+        out_specs=outs,
+        out_shape=shapes,
+        compiler_params=params(48),
+        cost_estimate=estimate(0, 0),
         name="project",
-    )(ids, low, low_out, *act, *pieces)
+    )(ids, chunks, low_in, low_out, *turn, *in_hbm(*act, *[w for x in weights for w in x]))
 
 
 def decay_factors(rate, size):
@@ -218,7 +230,7 @@
         centered = total - jnp.mean(total, axis=1, keepdims=True)
         scale = lax.rsqrt(jnp.mean(centered * centered, axis=1, keepdims=True) + group_floor)
         normed = centered * scale
-        level = gate[here, :]
+        level = gate[here, :].astype(F32)
         out[here, :] = (level / (1.0 + jnp.exp(-level)) * normed).astype(BF)
         nrm[here, :] = normed.astype(nrm.dtype)
         inverse[0, here, :] = jnp.broadcast_to(scale, (size, 128))
@@ -238,12 +250,12 @@
         out_specs=[pl.BlockSpec((rows, VALUE_DIM), lambda h: (0, h)),
                    pl.BlockSpec((rows, VALUE_DIM), lambda h: (0, h)),
                    pl.BlockSpec((1, rows, 128), lambda h: (h, 0, 0))],
-        out_shape=[jax.ShapeDtypeStruct(v.shape, BF), jax.ShapeDtypeStruct(v.shape, F32),
-                   jax.ShapeDtypeStruct((heads, rows, 128), F32)],
+        out_shape=[far(v.shape, BF), far(v.shape, BF),
+                   far((heads, rows, 128), F32)],
         compiler_params=params(40),
         cost_estimate=estimate(2 * rows * rows * 768 * heads, 30 << 20),
         name="retention",
-    )(spots, rates, seg_col, seg_row, qk, qk, v, gate)
+    )(spots, rates, seg_col, seg_row, qk, qk, *in_hbm(v, gate))
 
 
 def fold_kernel(ids, act, low_in, low_out, *refs):
@@ -276,7 +288,7 @@
         in_specs=[smem(), full(act.shape), full(low_in.shape), full(low_out.shape)]
         + [pl.BlockSpec((1,) + w.shape[1:], lambda s: (s, 0, 0)) for w in pieces],
         out_specs=[full((rows // 4, width))] * 4 + [full((low_in.shape[0], rows))],
-        out_shape=[jax.ShapeDtypeStruct((rows // 4, width), BF)] * 4
+        out_shape=[far((rows // 4, width), BF)] * 4
         + [jax.ShapeDtypeStruct((low_in.shape[0], rows), F32)],
         compiler_params=params(48),
         cost_estimate=estimate(2 * rows * depth * width, 2 * depth * width + 4 * rows * depth),
@@ -289,20 +301,20 @@
         part0[...].astype(F32) + part1[...].astype(F32) + part2[...].astype(F32)
     )
     inverse = lax.rsqrt(jnp.mean(rows * rows, axis=1, keepdims=True) + rms_epsilon)
-    middle[...] = rows
+    middle[...] = rows.astype(BF)
     normed[...] = (rows * inverse * gain[...]).astype(BF)
 
 
 def join_rows(x, parts, gain):
     return pl.pallas_call(
         join_kernel,
-        out_shape=[jax.ShapeDtypeStruct(x.shape, F32), jax.ShapeDtypeStruct(x.shape, BF)],
+        out_shape=[jax.ShapeDtypeStruct(x.shape, BF), jax.ShapeDtypeStruct(x.shape, BF)],
         compiler_params=pltpu.CompilerParams(vmem_limit_bytes=24 << 20),
         name="join_rows",
     )(x, *parts, gain)
 
 
-def rms_back_kernel(rows_in, grad_in, part0, part1, part2, gain, out, out_low):
+def rms_back_kernel(rows_in, grad_in, part0, part1, part2, gain, *outs):
     rows = rows_in[...].astype(F32)
     inverse = lax.rsqrt(jnp.mean(rows * rows, axis=1, keepdims=True) + rms_epsilon)
     normed = rows * inverse
@@ -312,22 +324,19 @@
     result = grad_in[...].astype(F32) + inverse * (
         scaled - normed * jnp.mean(scaled * normed, axis=1, keepdims=True)
     )
-    out[...] = result
-    out_low[...] = result.astype(BF)
-
-
-def rms_back(rows_in, grad_in, parts, gain, begin, count):
-    width = rows_in.shape[1]
-    size = 128
-    block = lambda skip: pl.BlockSpec((size, width), lambda i: (i + skip // size, 0))
-    skips = (begin,) * 4 + (0,)
+    for out in outs:
+        out[...] = result.astype(out.dtype)
+
+
+def rms_back(rows_in, grad_in, parts, gain, kinds):
+    count, width = rows_in.shape
+    block = pl.BlockSpec((count // 2, width), lambda i: (i, 0))
     return pl.pallas_call(
         rms_back_kernel,
-        grid=(count // size,),
-        in_specs=[block(skip) for skip in skips] + [full(gain.shape)],
-        out_specs=[block(0)] * 2,
-        out_shape=[jax.ShapeDtypeStruct((count, width), F32),
-                   jax.ShapeDtypeStruct((count, width), BF)],
+        grid=(2,),
+        in_specs=[block] * 5 + [full(gain.shape)],
+        out_specs=[block] * len(kinds),
+        out_shape=[far((count, width), kind) for kind in kinds],
         compiler_params=params(24),
         name="rms_back",
     )(rows_in, grad_in, *parts, gain)
@@ -428,7 +437,7 @@
     step = pl.program_id(0)
     subs = pl.num_programs(0)
     width = pieces[0].shape[1]
-    extra = jnp.concatenate([low[...] for low in lows], axis=1).astype(BF)
+    extra = jnp.concatenate([low[...] for low in lows], axis=1).T.astype(BF)
     per = len(pieces) // weights
     rows = jnp.concatenate(
         [jnp.concatenate([act[...] for act in acts[i * count:(i + 1) * count]], axis=1)
@@ -437,7 +446,7 @@
     for i in range(per):
         at = aligned(ids[i * subs + step] * width, width)
         weight = jnp.concatenate([pieces[k * per + i][0] for k in range(weights)], axis=1)
-        product = (dot_nt(rows, weight) + dot_tn(extra, low_in[:, at])).astype(BF)
+        product = (dot_nt(rows, weight) + dot(extra, low_in[:, at])).astype(BF)
         for j, out in enumerate(outs):
             out[:, at] = product[j * size:(j + 1) * size]
 
@@ -457,13 +466,13 @@
            for at in blocks for act in acts]
         + [pl.BlockSpec((1,) + w.shape[1:], lambda s: (s, 0, 0)) for w in pieces],
         out_specs=[full((size, width))] * count,
-        out_shape=[jax.ShapeDtypeStruct((size, width), BF)] * count,
+        out_shape=[far((size, width), BF)] * count,
         compiler_params=params(48),
         cost_estimate=estimate(
             2 * count * size * depth * width, 2 * depth * width + 4 * count * size * depth
         ),
         name="unfold",
-    )(ids, low_in, *[low] * count, *list(acts) * count, *pieces)
+    )(ids, low_in, *[low] * count, *in_hbm(*list(acts) * count, *pieces))
 
 
 def gate_back_kernel(parts, ids, low_back, low_in, gate, nrm, inverse, hold, low_gate, low_out,
@@ -478,8 +487,8 @@
 
     weights = jnp.concatenate([w[s] for w in pieces for s in range(w.shape[0])], axis=1)
     back = dot_nt(columns(act, ids), weights) + dot_tn(low[...], low_in[...])
-    level = gate[...]
-    normed = nrm[...]
+    level = gate[...].astype(F32)
+    normed = nrm[...].astype(F32)
     chance = 1.0 / (1.0 + jnp.exp(-level))
     slope = chance * (1.0 + level * (1.0 - chance))
     back_gate = (back * normed * slope).astype(BF)
@@ -504,7 +513,8 @@
         grid=(width // block,),
         in_specs=[smem(), full(low_back.shape), column(ranks), column(rows),
                   column(rows), pl.BlockSpec((1, rows, 128), lambda n: (n, 0, 0)), column(rows),
-                  full(low_gate.shape), column(low_out.shape[0])]
+                  pl.BlockSpec((ranks, rows), lambda n: (low_gate.shape[0] // ranks - 1, 0)),
+                  column(low_out.shape[0])]
         + whole(act) + [pl.BlockSpec((w.shape[0], block, w.shape[2]), lambda n: (0, n, 0)) for w in pieces],
         out_specs=[column(rows), column(rows), full((ranks, rows)),
                    full((low_out.shape[0], rows)), column(ranks), column(ranks)],
@@ -515,7 +525,7 @@
         compiler_params=params(56),
         cost_estimate=estimate(2 * rows * depth * width, 2 * depth * width + 16 * rows * width),
         name="gate_back",
-    )(ids, low_back, low_in, gate, nrm, inverse, hold, low_gate, low_out, *act, *pieces)
+    )(ids, low_back, low_in, *in_hbm(gate, nrm, inverse, hold), low_gate, low_out, *act, *pieces)
 
 
 def retention_back_kernel(spots, rates, seg_col, seg_row, cosine, sine_table, low, begin, q_out,
@@ -598,76 +608,85 @@
         compiler_params=params(48),
         cost_estimate=estimate(2 * rows * rows * 1792 * heads, 30 << 20),
         name="retention_back",
-    )(spots, rates, seg_col, seg_row, cosine, sine_table, low, begin, qk_out, qk_out, v_out, qk, qk,
-      v, dret)
-
-
-def share_kernel(heights, rank, low, *refs):
+    )(spots, rates, seg_col, seg_row,
+      cosine, sine_table, low, begin, qk_out, qk_out, v_out, qk, qk, v, dret)
+
+
+def share_kernel(heights, low, *refs):
     out = refs[-1]
     at, first = 0, 0
     for height, parts in heights:
-        total = jnp.zeros((height, out.shape[1]), F32)
+        total = jnp.zeros((height, out.shape[2]), F32)
         begin = 0
         for ref in refs[first:first + parts]:
             end = begin + ref.shape[0]
             total = total + dot(low[at:at + height, begin:end], ref[...])
             begin = end
-        out[at:at + height, :] = total.astype(BF)
+        out[0, at:at + height, :] = total.astype(BF)
         at, first = at + height, first + parts
 
 
-def share(rank, low, span, items):
+def share(low, span, items):
     acts = [array for _, act in items for array in act]
     heights = tuple((height, len(act)) for height, act in items)
+    count = acts[0].shape[1] // span
+    made = pl.pallas_call(
+        partial(share_kernel, heights),
+        grid=(count,),
+        in_specs=[full(low.shape)]
+        + [pl.BlockSpec((act.shape[0], span), lambda i: (0, i)) for act in acts],
+        out_specs=pl.BlockSpec((1, low.shape[0], span), lambda i: (i, 0, 0)),
+        out_shape=jax.ShapeDtypeStruct((count, low.shape[0], span), BF),
+        compiler_params=params(32),
+        cost_estimate=estimate(0, 0),
+        name="share",
+    )(low, *in_hbm(*acts))
+    return made.reshape(count * low.shape[0], span)
+
+
+def place_kernel(layout, arrays, order, *refs):
+    packs, outs = refs[:arrays], refs[arrays:]
+    pack = packs[0][0]
+    if arrays == 2:
+        which = order[pl.program_id(0)] >= order[pl.num_programs(0)]
+        pack = jnp.where(which, packs[1][0], pack)
+    span = pack.shape[1]
+    for (begin, height, kind, stride), out in zip(layout, outs):
+        if kind == "shares":
+            for j in range(out.shape[2] // span):
+                rows = pack[begin + stride * j:begin + stride * j + height]
+                out[0, :, j * span:(j + 1) * span] = rows.astype(F32)
+            continue
+        for j in range(2):
+            rows = pack[begin + stride * j:begin + stride * j + height].astype(F32)
+            if kind == "halves":
+                out[0, :, j * span:(j + 1) * span] = rows
+            else:
+                out[0, j] = rows
+
+
+def place(order, arrays, layout, shares):
+    entries = order.shape[0]
+    size, _, span = arrays[0].shape
+    shapes = []
+    for _, height, kind, _ in layout:
+        shapes.append({"shares": (height, shares * span),
+                       "halves": (height, 2 * span)}.get(kind, (2, height, span)))
+
+    def spec(number):
+        def index(e, o):
+            return (jnp.clip(o[e] - number * size, 0, size - 1), 0, 0)
+        return pl.BlockSpec((1,) + arrays[0].shape[1:], index)
+
+    order = jnp.concatenate([order, jnp.full((1,), size, jnp.int32)])
     return pl.pallas_call(
-        partial(share_kernel, heights),
+        partial(place_kernel, layout, len(arrays)),
         grid_spec=pltpu.PrefetchScalarGridSpec(
             num_scalar_prefetch=1,
-            grid=(1,),
-            in_specs=[pl.BlockSpec(low.shape, lambda i, r: (0, 0))]
-            + [pl.BlockSpec((act.shape[0], span), lambda i, r: (0, r[0])) for act in acts],
-            out_specs=pl.BlockSpec((low.shape[0], span), lambda i, r: (0, 0)),
-        ),
-        out_shape=jax.ShapeDtypeStruct((low.shape[0], span), BF),
-        compiler_params=params(24),
-        cost_estimate=estimate(2 * low.shape[0] * low.shape[1] * span, 4 << 20),
-        name="share",
-    )(rank.reshape(1), low, *in_hbm(*acts))
-
-
-def place_kernel(layout, order, places, pack, *outs):
-    span = pack.shape[2]
-    count = places.shape[0]
-    for (begin, height, kind, stride), out in zip(layout, outs):
-        if kind == "shares":
-            for j in range(count):
-                rows = pack[0, begin + stride * j:begin + stride * j + height, :]
-                out[0, :, aligned(places[j] * span, span)] = rows.astype(F32)
-        elif kind == "halves":
-            for j in range(2):
-                rows = pack[0, begin + stride * j:begin + stride * j + height, :]
-                out[0, :, j * span:(j + 1) * span] = rows.astype(F32)
-        else:
-            for j in range(2):
-                rows = pack[0, begin + stride * j:begin + stride * j + height, :]
-                out[0, j] = rows.astype(F32)
-
-
-def place(order, places, pack, layout):
-    entries = order.shape[0]
-    span, count = pack.shape[2], places.shape[0]
-    shapes = []
-    for _, height, kind, _ in layout:
-        shapes.append({"shares": (height, count * span), "halves": (height, 2 * span)}.get(
-            kind, (2, height, span)))
-    return pl.pallas_call(
-        partial(place_kernel, layout),
-        grid_spec=pltpu.PrefetchScalarGridSpec(
-            num_scalar_prefetch=2,
             grid=(entries,),
-            in_specs=[pl.BlockSpec((1,) + pack.shape[1:], lambda e, o, p: (o[e], 0, 0))],
+            in_specs=[spec(number) for number in range(len(arrays))],
             out_specs=[
-                pl.BlockSpec((1,) + shape, lambda e, o, p, n=len(shape): (e,) + (0,) * n)
+                pl.BlockSpec((1,) + shape, lambda e, o, n=len(shape): (e,) + (0,) * n)
                 for shape in shapes
             ],
         ),
@@ -675,7 +694,7 @@
         compiler_params=params(32),
         cost_estimate=estimate(0, 10 << 20),
         name="place",
-    )(order, places, pack)
+    )(order, *in_hbm(*arrays))
 
 
 def after(x, *others):
@@ -715,32 +734,29 @@
         steps.ready(line, steps.tables(line, line)[0])
         a = self.gather(steps.norm(tokens))
         dy = self.gather(cotangent)
-        qkv = steps.query_key_value(a, blocks[0], blocks[1])
-        mixed = steps.gate_and_mix(a, *qkv, blocks[2])
+        projected = steps.project(a, *blocks[:2])
+        mixed = steps.mix(a, *projected, blocks[2])
         *rows, low = steps.fold(mixed[0], blocks[3])
         middle, b = steps.join(tokens, self.scatter(rows))
         dhid = steps.hidden_grad(dy, blocks[4])
-        return (blocks, tokens, a, cotangent, dy, qkv, mixed, low, middle, self.gather(b), dhid)
+        return (blocks, tokens, a, cotangent, dy, projected, mixed, low, middle,
+                self.gather(b), dhid)
 
     def group_sum(self, x):
         return lax.psum(x.astype(BF), "tensor")
-
-    def all_shares(self, x, height):
-        first = lax.all_gather(x[:height], "tensor", tiled=True)
-        every = lax.all_gather(jnp.concatenate([first, x[height:]]), "dp")
-        return every, jnp.arange(self.ndp, dtype=jnp.int32), self.chunks
 
     def backward(self, steps):
         steps.mlp()
         dz = self.gather(steps.dz(self.scatter(steps.unfold_mlp(256, (0, 1, 2, 3)))))
         output = steps.output(self.scatter(steps.fold_down(steps.hid)))
-        lows = self.group_sum(steps.early_lows())
+        early = lax.all_gather(steps.early(self.group_sum(steps.lows)), "dp")
+        early = steps.place_early(early)
         steps.gate_back(dz)
-        early = self.all_shares(steps.early(lows, dz), steps.early_height)
         steps.retention_back(steps.dret)
-        late = self.all_shares(steps.late(self.group_sum(steps.dlow)), steps.late_height)
+        late = lax.all_gather(steps.late(self.group_sum(steps.late_lows()), dz), "dp")
+        late = steps.place_late([late], jnp.arange(self.ndp, dtype=jnp.int32))
         parts = self.scatter(steps.unfold_attn(256, (0, 1, 2, 3)))
-        dx, _ = steps.dx(parts, 0, parts[0].shape[0])
+        dx, _ = steps.dx(parts)
         return output, dx, early, late
 
 
@@ -782,7 +798,7 @@
     def send(self, moves):
         return [lax.ppermute(x, ("dp", "tensor"), self.pairs(place)) for x, place in moves]
 
-    def round(self, moves, work=None, inputs=(), later=(), slow=()):
+    def round(self, moves, work=None, inputs=(), later=(), slow=(), feed=0):
         every = list(moves) + list(slow)
         values = [x for x, _ in every]
         flat, form = jax.tree.flatten((values, inputs))
@@ -799,7 +815,7 @@
             values = [x for x, _ in moves]
             values = lax.optimization_barrier((*values, *moved[:count]))[:len(values)]
             second = self.send([(x, place) for x, (_, place) in zip(values, moves)])
-        made = work(*inputs) if work is not None else ()
+        made = work(*moved[:feed], *inputs) if work is not None else ()
         self.last_round = (moved, second, made, self.slow)
         self.slow = slowly
         return moved + slowly, second, made
@@ -864,9 +880,6 @@
         def double(rest):
             return [jnp.stack([shard, self.core(shard)]) for shard in rest]
 
-        def whole_rows(own, across):
-            return [own, self.core(own), across, self.core(across)]
-
         other = self.core(line)
         (moved,), made = go([], [], [over(0)], double, (shards[1:],))
         doubled += made
@@ -875,49 +888,55 @@
             [(0, "x"), (0, "y")], [], [over(1)], steps.tables, (line, other)
         )
         arrived(1, moved)
-        (one, two), _ = go([(1, "x"), (0, "xy")], [(1, "y")], [over(2), over(3)])
-        arrived(2, one)
-        arrived(3, two)
-        (x, table, moved), _ = go([(2, "x"), (2, "y")], [(1, "yx"), (2, "xy")],
-                                  [(tokens, swap), (sent_table, seat), over(4)])
-        arrived(4, moved)
+        (x, table, moved), _ = go([(1, "x"), (0, "xy")], [(1, "y")],
+                                  [(tokens, swap), (sent_table, seat), over(2)])
+        arrived(2, moved)
         x = self.mine(tokens, x)
         steps.ready(other, self.mine(home_table, table))
         a = steps.norm(x)
-        (moved, grad, across), _ = go([(3, "x"), (3, "y")], [(4, "x"), (3, "xy")],
-                                      [over(5), (cotangent, swap), (a, pair)])
+        (across, moved, grad), _ = go([(2, "x"), (2, "y")], [(1, "yx"), (2, "xy")],
+                                      [(a, pair), over(3), (cotangent, swap)])
+        arrived(3, moved)
+        grad = self.mine(cotangent, grad)
+        def attend(near, beyond, own, across, *weights):
+            a = [own, near, across, beyond]
+            return a, steps.project(a, *weights)
+
+        moves = [(a, core), (across, core), hops["x"](3), hops["y"](3), over(4)]
+        moved, _, (a, projected) = self.round(
+            moves, attend, (a, across, *blocks[:2]), feed=2
+        )
+        _, _, blocks[3][1], blocks[3][2], moved = moved
+        arrived(4, moved)
+        half = grad.shape[0] // 2
+        (moved, across0), mixed = go(
+            [(4, "x"), (3, "xy")], [], [over(5), (grad[:half], pair)], steps.mix,
+            (a, *projected, blocks[2])
+        )
         arrived(5, moved)
-        grad = self.mine(cotangent, grad)
-
-        def attend(own, across, *weights):
-            a = whole_rows(own, across)
-            return a, steps.query_key_value(a, *weights)
-
-        (moved,), (a, qkv) = go([(5, "x"), (4, "y")], [], [over(6)], attend,
-                                (a, across, blocks[0], blocks[1]))
+        (moved, across1), folded = go(
+            [(5, "x"), (4, "y")], [], [over(6), (grad[half:], pair)], steps.fold,
+            (mixed[0], blocks[3])
+        )
+        across = jnp.concatenate([across0, across1])
         arrived(6, moved)
-
-        def mix(a, qk, low, v, w_g, w_o):
-            mixed = steps.gate_and_mix(a, qk, low, v, w_g)
-            return mixed, steps.fold(mixed[0], w_o)
-
-        (across,), (mixed, folded) = go([(4, "yx"), (5, "y")], [], [(grad, pair)], mix,
-                                        (a, *qkv, blocks[2], blocks[3]))
         own, near, far, beyond, low = folded
-        near, beyond = self.send([(near, core), (beyond, core)])
-        far = (far.astype(F32) + beyond.astype(F32)).astype(BF)
-
-        def grad_rows(grad, across, w_d):
-            dy = whole_rows(grad, across)
-            return dy, steps.hidden_grad(dy, w_d)
-
-        (far,), (dy, dhid) = go([(6, "x"), (6, "y")], [], [(far, pair)], grad_rows,
-                                (grad, across, blocks[4]))
-        parts = (own, near)
-        middle, b = steps.join(x, (*parts, far))
-        (across,), _ = go([(5, "yx"), (6, "xy")], [], [(b, pair)])
-        b = whole_rows(b, across)
-        return blocks, x, a, grad, dy, qkv, mixed, low, middle, b, dhid
+        moves = [(near, core), (beyond, core), hops["yx"](4), hops["y"](5)]
+        moved, (far,), _ = self.round(
+            moves, later=(2, lambda moved: [(self.add(far, moved[1]), pair)])
+        )
+        near, _, blocks[4][3], blocks[5][2] = moved
+        middle, b = steps.join(x, (own, near, far))
+        (far, near_grad, beyond_grad), _ = go([(6, "x"), (6, "y")], [],
+                                              [(b, pair), (grad, core), (across, core)])
+        dy = [grad, near_grad, across, beyond_grad]
+        (near, beyond), dhid = go([(5, "yx"), (6, "xy")], [], [(b, core), (far, core)],
+                                  steps.hidden_grad, (dy, blocks[4]))
+        b = [b, near, far, beyond]
+        return blocks, x, a, grad, dy, projected, mixed, low, middle, b, dhid
+
+    def add(self, one, two):
+        return (one.astype(F32) + two.astype(F32)).astype(BF)
 
     def core_sum(self, x, other):
         size = x.shape[1] // 4
@@ -934,78 +953,86 @@
     def backward(self, steps):
         pair = lambda d, t: (d, t ^ 1)
         swap = lambda d, t: (d ^ 1, t ^ 2) if d % 2 != t // 2 else None
-        over = lambda d, t: (d, t ^ 2)
         by_one = lambda d, t: (d ^ 2, t)
         by_two = lambda d, t: (d ^ 4, t)
         core = lambda d, t: (d ^ 1, t)
 
-        def add(one, two):
-            return (one.astype(F32) + two.astype(F32)).astype(BF)
-
+        self.last_round = ()
         steps.mlp()
-        near, beyond = steps.unfold_mlp(256, (1, 3))
-        far, = steps.unfold_mlp(256, (2,))
-        near, beyond, lows = self.send([(near, core), (beyond, core), (steps.lows_low(), core)])
-        far = add(far, beyond)
-        lows = self.core_sum(steps.early_lows(), lows)
-        self.last_round = ()
-        (far, other), _, (own, folded) = self.round(
-            [(far, pair), (lows, pair)],
-            lambda hid: (steps.unfold_mlp(256, (0,))[0], steps.fold_down(hid)), (steps.hid,)
-        )
+        (lows,), _, (near, far, beyond) = self.round(
+            [(steps.lows.astype(BF), core)],
+            lambda dup: steps.unfold_mlp(256, (1, 2, 3), dup), (steps.dup,)
+        )
+        lows = self.core_sum(steps.lows, lows)
+        (beyond, near, other), _, _ = self.round([(beyond, core), (near, core), (lows, pair)])
+        far = self.add(far, beyond)
+        half = far.shape[0] // 2
         lows = self.pair_sum(lows, other)
+        (far,), _, ((own,), folded, early) = self.round(
+            [(far, pair)],
+            lambda dup, hid, lows: (steps.unfold_mlp(256, (0,), dup), steps.fold_down(hid),
+                                    steps.early(lows)),
+            (steps.dup, steps.hid, lows)
+        )
+        own_out, near_out, far_out, beyond_out = folded
         dz = steps.dz((own, near, far))
-        own_out, near_out, far_out, beyond_out = folded
-        (across, dz_near, near_out, beyond_out), _, _ = self.round(
-            [(dz, pair), (dz, core), (near_out, core), (beyond_out, core)]
-        )
-        (dz_beyond, far_out), _, _ = self.round(
-            [(across, core)], slow=[(add(far_out, beyond_out), pair)]
-        )
+
+        (_, across, moved, dz_near, near_out), _, far_out = self.round(
+            [(beyond_out, core), (dz, pair), (early, swap), (dz, core), (near_out, core)],
+            self.add, (far_out,), feed=1
+        )
+        early = lax.all_gather(self.mine(early, moved), "dp")
+        (dz_beyond,), _, _ = self.round([(across, core)])
         dz = [dz, dz_near, across, dz_beyond]
-        _, _, (early, dret) = self.round([], steps.middle_back, (lows, dz))
-        (moved,), _, dpv = self.round([(early, swap)], steps.retention_back, (dret,))
-        early = self.mine(early, moved)
-        first = early[:steps.early_height]
+        (far_out,), _, dret = self.round([], steps.gate_back, (dz,), slow=[(far_out, pair)])
+        _, _, dpv = self.round([], steps.retention_back, (dret,))
         output = steps.output((own_out, near_out, far_out))
 
-        (moved, dlow), _, (near, beyond) = self.round(
-            [(first, pair), (steps.dlow.astype(BF), core)],
-            lambda dpv: steps.unfold_attn(256, (1, 3), dpv), (dpv,)
-        )
-        dlow = self.core_sum(steps.dlow, dlow)
-        first = jnp.concatenate([first, moved])
-        (moved, near, beyond, other), _, (far,) = self.round(
-            [(first, over), (near, core), (beyond, core), (dlow, pair)],
-            lambda dpv: steps.unfold_attn(256, (2,), dpv), (dpv,)
-        )
-        early = jnp.concatenate([first, moved, early[steps.early_height:]])
-        far = add(far, beyond)
-        half = far.shape[0] // 2
-        late = steps.late(self.pair_sum(dlow, other))
-        (moved, far0, far1), _, (own,) = self.round(
-            [(late, swap)], lambda dpv: steps.unfold_attn(256, (0,), dpv), (dpv,),
-            slow=[(far[:half], pair), (far[half:], pair)]
-        )
-        early = lax.all_gather(early, "dp")
+        (dlow, out0), _, (far, beyond) = self.round(
+            [(steps.late_lows().astype(BF), core), (output[:half], swap)],
+            lambda dpv: steps.unfold_attn(256, (2, 3), dpv), (dpv,)
+        )
+        dlow = self.core_sum(steps.late_lows(), dlow)
+        def beside(other, dpv, dlow):
+            near, = steps.unfold_attn(256, (1,), dpv)
+            return near, steps.late(self.pair_sum(dlow, other), dz)
+
+        (_, beyond, out1), _, (near, late) = self.round(
+            [(dlow, pair), (beyond, core), (output[half:], swap)], beside, (dpv, dlow), feed=1
+        )
+        far = self.add(far, beyond)
+        (far0, near, moved), _, (own,) = self.round(
+            [(far[:half], pair), (near, core), (late, swap)],
+            lambda dpv: steps.unfold_attn(256, (0,), dpv), (dpv,)
+        )
         late = self.mine(late, moved)
-        moved_out, = self.send([(output, swap)])
-        rows = []
-        for i, part in enumerate((far0, far1)):
-            dx, low = steps.dx((own, near, part), i * half, half)
-            moved, = self.send([(low, swap)])
-            rows.append(self.mine(dx, moved.astype(F32)))
-        first = late[:steps.late_height]
-        first = jnp.concatenate([first, *self.send([(first, pair)])])
-        first = jnp.concatenate([first, *self.send([(first, over)])])
-        late = jnp.concatenate([first, late[steps.late_height:]])[None]
-        for place in (by_one, by_two, core):
-            late = jnp.concatenate([late, *self.send([(late, place)])])
-        places = jnp.arange(self.nt, dtype=jnp.int32) ^ lax.axis_index("tensor")
-        at = jnp.arange(self.ndp, dtype=jnp.int32)
-        apart = at ^ lax.axis_index("dp")
-        return (self.mine(output, moved_out), jnp.concatenate(rows), (early, at, places),
-                (late, apart // 2 + 4 * (apart % 2), places))
+        size = late.shape[0] // 2
+        late = [late[:size][None], late[size:][None]]
+        three = half + half // 2
+        (one, two, far1), _, _ = self.round(
+            [(late[0], by_one), (late[1], by_two), (far[half:three], pair)]
+        )
+        late = [jnp.concatenate([late[0], one]), jnp.concatenate([late[1], two])]
+        (one, two, far2), _, _ = self.round(
+            [(late[0], by_two), (late[1], by_one), (far[three:], pair)]
+        )
+        dx, low = steps.dx((own, near, jnp.concatenate([far0, far1, far2])))
+        late = jnp.concatenate(
+            [jnp.concatenate([late[0], one]),
+             jnp.concatenate([late[1][:1], two[:1], late[1][1:], two[1:]])], axis=1
+        )
+        apart = jnp.arange(self.ndp, dtype=jnp.int32) ^ lax.axis_index("dp")
+
+        def put(other, late, early):
+            early = steps.place_early(early)
+            return early, steps.place_late([late, other], apart // 2 + 4 * (apart % 2))
+
+        (_, moved), _, (early, late) = self.round(
+            [(late, core), (low, swap)], put, (late, early), feed=1
+        )
+        moved, early, late = lax.optimization_barrier((moved, early, late))
+        return (self.mine(output, jnp.concatenate([out0, out1])),
+                self.mine(dx, moved.astype(F32)), early, late)
 
 
 def rotation_tables(seq_length, half_dim):
@@ -1097,14 +1124,14 @@
         def norm(self, x):
             return norm_rows(x, gain_attn)
 
-        def query_key_value(self, a, w_qk, w_v):
-            qk, low = project_query_key(
-                ids, chunks, a, self.attn_in, self.qk_out, cosine, sine_table, w_qk
+        def project(self, a, w_qk, w_v):
+            return project(
+                ids, chunks, a, self.attn_in, jnp.concatenate([self.qk_out, self.v_out], axis=1),
+                (w_qk, w_v), (cosine, sine_table)
             )
-            return qk, low, project(ids, a, low, self.v_out, w_v, BF)
-
-        def gate_and_mix(self, a, qk, low, v, w_g):
-            gate = project(ids, a, low, self.g_out, w_g, F32)
+
+        def mix(self, a, qk, v, low, w_g):
+            gate, = project(ids, chunks, a, low, self.g_out, (w_g,), ())
             return (*retention(spots, rates, self.seg_col, self.seg_row, qk, v, gate), gate)
 
         def fold(self, o, w_o):
@@ -1117,7 +1144,7 @@
             return hidden_grad(ids, dy, self.down_back, self.down_in, w_d)
 
     steps = Steps()
-    ((w_qk, w_v, w_g, w_o, w_d, w_mg, w_mu), x, a, grad, dy, (qk, low_a, v),
+    ((w_qk, w_v, w_g, w_o, w_d, w_mg, w_mu), x, a, grad, dy, (qk, v, low_a),
      (o, nrm, inverse, gate), low_o, middle, b, (dhid, low_dy)) = links.forward(
         [jnp.concatenate([weight_query, weight_key], axis=1), weight_value, weight_gate,
          weight_out, weight_mlp_down, weight_mlp_gate, weight_mlp_up],
@@ -1134,8 +1161,8 @@
     halves = lambda y: jnp.concatenate([y[:, :wide // 2], y[:, wide // 2:]])
 
     class Back:
-        early_height = 4 * RANK
-        late_height = 4 * RANK
+        early_height = 3 * RANK
+        late_height = 5 * RANK
 
         def mlp(self):
             (self.hid, self.dgate, self.dup, _, self.lows, self.grad_hidden,
@@ -1143,44 +1170,38 @@
                 ids, b, mlp_in, mg_out, mu_out, down_in, dhid, low_dy, w_mg, w_mu
             )
 
-        def unfold_mlp(self, size, blocks):
-            return unfold(ids, (self.dgate, self.dup), self.lows[RANK:], mlp_in, (w_mg, w_mu),
+        def unfold_mlp(self, size, blocks, dup=None):
+            dup = self.dup if dup is None else dup
+            return unfold(ids, (self.dgate, dup), self.lows[RANK:], mlp_in, (w_mg, w_mu),
                           size, blocks)
 
         def dz(self, parts):
-            self.dmid, low = rms_back(middle, grad, parts, gain_mlp, 0, middle.shape[0])
-            return low
+            self.dmid, = rms_back(middle, grad, parts, gain_mlp, (BF,))
+            return self.dmid
 
         def fold_down(self, hid):
             return fold(ids, hid, down_in, down_back, w_d)[:4]
 
         def output(self, parts):
-            return (middle + (
+            return (middle.astype(F32) + (
                 parts[0].astype(F32) + parts[1].astype(F32) + parts[2].astype(F32)
             )).astype(BF)
 
-        def early_lows(self):
-            return jnp.concatenate([self.lows, low_o])
-
-        def lows_low(self):
-            return self.early_lows().astype(BF)
-
-        def early(self, lows, dz):
+        def early(self, lows):
             mark = jnp.full((RANK, span), work_id, F32).astype(BF)
             return jnp.concatenate(
-                [share(rank, lows, span, ((RANK, dy), (2 * RANK, b), (RANK, dz))),
-                 halves(jnp.concatenate([self.grad_hidden, self.grad_down, self.grad_out_in,
-                                         self.grad_gate])), mark]
+                [share(lows, span, ((RANK, dy), (2 * RANK, b))),
+                 halves(jnp.concatenate([self.grad_hidden, self.grad_down])), mark]
             )
 
         def gate_back(self, dz):
             (self.dpg, self.dret, _, self.dlow, self.grad_out_in, self.grad_gate) = gate_back(
-                ids, dz, out_back, out_in, gate, nrm, inverse, o, low_a[3 * RANK:], g_out, w_o
+                ids, dz, out_back, out_in, gate, nrm, inverse, o, low_a, g_out, w_o
             )
-
-        def middle_back(self, lows, dz):
-            self.gate_back(dz)
-            return self.early(lows, dz), self.dret
+            return self.dret
+
+        def late_lows(self):
+            return jnp.concatenate([self.dlow, low_o])
 
         def retention_back(self, dret):
             (self.dpq, self.dpk, self.dpv, self.dlow, self.grad_q, self.grad_k,
@@ -1188,64 +1209,69 @@
                 spots, rates, seg_col, seg_row, cosine, sine_table, low_a, self.dlow, qk_out,
                 v_out, qk, v, dret
             )
-            self.dpqk = jnp.concatenate([self.dpq, self.dpk], axis=1)
             return self.dpv
 
-        def late(self, lows):
+        def late(self, lows, dz):
             return jnp.concatenate(
-                [share(rank, lows, span, ((4 * RANK, a),)),
+                [share(lows, span, ((4 * RANK, a), (RANK, dz))),
                  halves(jnp.concatenate(
-                     [jnp.concatenate([self.grad_q, self.grad_k], axis=1), self.grad_v]
+                     [jnp.concatenate([self.grad_q, self.grad_k], axis=1), self.grad_v,
+                      self.grad_gate, self.grad_out_in]
                  ))]
             )
 
         def unfold_attn(self, size, blocks, dpv=None):
             dpv = self.dpv if dpv is None else dpv
-            return unfold(ids, (self.dpqk, dpv, self.dpg), self.dlow, attn_in,
+            return unfold(ids, (self.dpq, self.dpk, dpv, self.dpg), self.dlow, attn_in,
                           (w_qk, w_v, w_g), size, blocks)
 
-        def dx(self, parts, begin, count):
-            return rms_back(x, self.dmid, parts, gain_attn, begin, count)
+        def dx(self, parts):
+            return rms_back(x, self.dmid, parts, gain_attn, (F32, BF))
+
+        def place_early(self, early):
+            sequences = early.shape[0]
+            shares = nt * self.early_height
+            all_ids = early[:, shares + 6 * RANK, 0].astype(jnp.int32)
+            numbers = jnp.arange(adapters, dtype=jnp.int32)
+            chosen = numbers[:, None] == all_ids[None, :]
+            if sequences == adapters:
+                self.order = jnp.sum(jnp.where(chosen, numbers[None, :], 0), axis=1)
+                self.total = lambda y: y
+            else:
+                self.order = numbers
+                self.total = lambda y: jnp.einsum(
+                    "es,sij->eij", chosen.astype(BF), y, preferred_element_type=F32
+                )
+            pitch = self.early_height
+            return place(
+                self.order, [self.total(early)],
+                ((0, RANK, "shares", pitch), (RANK, 2 * RANK, "shares", pitch),
+                 (shares, 2 * RANK, "halves", 3 * RANK),
+                 (shares + 2 * RANK, RANK, "halves", 3 * RANK)), nt
+            )
+
+        def place_late(self, arrays, at):
+            if arrays[0].shape[0] * len(arrays) != adapters:
+                arrays = [self.total(arrays[0])]
+                at = self.order
+            pitch = self.late_height
+            shares = nt * pitch
+            return place(
+                at[self.order], arrays,
+                ((0, 4 * RANK, "shares", pitch), (4 * RANK, RANK, "shares", pitch),
+                 (shares, RANK, "two", 4 * RANK), (shares + RANK, 2 * RANK, "halves", 4 * RANK),
+                 (shares + 3 * RANK, RANK, "halves", 4 * RANK)), nt
+            )
 
     output, input_grad, early, late = links.backward(Back())
-    early, early_at, early_places = early
-    late, late_at, late_places = late
-    shares = nt * Back.early_height
-    all_ids = early[:, shares + 10 * RANK, 0].astype(jnp.int32)
-    chosen = jnp.arange(adapters, dtype=jnp.int32)[:, None] == all_ids[None, :]
-    if all_ids.shape[0] == adapters:
-        order = jnp.sum(
-            jnp.where(chosen, jnp.arange(adapters, dtype=jnp.int32)[None, :], 0), axis=1
-        )
-    else:
-        total = lambda y: jnp.einsum(
-            "es,sij->eij", chosen.astype(BF), y, preferred_element_type=F32
-        )
-        early, late = total(early), total(late)
-        order = jnp.arange(adapters, dtype=jnp.int32)
-        early_at = late_at = order
-    pitch = Back.early_height
-    down_back_out, mlp_out, out_back_out, hidden_out, down_out, out_out, gate_out = place(
-        early_at[order], early_places, early,
-        ((0, RANK, "shares", pitch), (RANK, 2 * RANK, "shares", pitch),
-         (3 * RANK, RANK, "shares", pitch), (shares, 2 * RANK, "halves", 5 * RANK),
-         (shares + 2 * RANK, RANK, "halves", 5 * RANK),
-         (shares + 3 * RANK, RANK, "halves", 5 * RANK),
-         (shares + 4 * RANK, RANK, "halves", 5 * RANK))
-    )
-    pitch = Back.late_height
-    shares = nt * pitch
-    attn_out, qk_grads, value_out = place(
-        late_at[order], late_places, late,
-        ((0, 4 * RANK, "shares", pitch), (shares, RANK, "apart", 2 * RANK),
-         (shares + RANK, RANK, "halves", 2 * RANK))
-    )
+    down_back_out, mlp_out, hidden_out, down_out = early
+    attn_out, out_back_out, qk_grads, vg_grads, out_out = late
     return (
         output[None],
         input_grad[None],
         jnp.swapaxes(attn_out, 1, 2),
         qk_grads,
-        jnp.stack([value_out, gate_out], axis=1),
+        vg_grads.reshape(adapters, 2, RANK, wide),
         jnp.swapaxes(out_out, 1, 2),
         out_back_out,
         jnp.swapaxes(mlp_out, 1, 2),

time: 680 us -> 623 us (0.916)
  waiting for transfers between devices: 294 us -> 243 us
  local copies, waits for them, and re-layouts: 48.9 us -> 27.2 us
  Pallas kernels: 173 us -> 192 us
    ppermute x66 -> x72, waiting for transfers between devices: 292 us -> 242 us  [send(): lax.ppermute(x, ('dp', 'tensor'), self.pairs(place))]
    unnamed x249 -> x272, local copies, waits for them, and re-layouts: 33.8 us -> 15.2 us
    pallas_call x12 -> x10, Pallas kernels: 45.6 us -> 60 us  [the longest x2 27.2 us: project(): pl.pallas_call(partial(project_kernel, (len(act), len(weights[0]), length...]
    ppermute x14 -> x8, starting transfers between devices: 15.4 us -> 7.36 us  [move(): moved = lax.ppermute(x, ('dp', 'tensor'), self.pairs(place))]
    ppermute x66 -> x72, starting transfers between devices: 70.9 us -> 75.1 us  [send(): lax.ppermute(x, ('dp', 'tensor'), self.pairs(place))]
    select_n x15 -> x13, other arithmetic: 17 us -> 13.4 us  [mine(): return jnp.where(self.home, own, other)]
    pallas_call x6 -> x5, Pallas kernels: 45.6 us -> 49 us  [unfold(): pl.pallas_call(partial(unfold_kernel, (count, len(acts), len(weights))),...]
  transfers between devices with their start and end apart: 81 -> 81, of which waited for: 39 -> 42; matrix products, arithmetic and copies ran while one was open for 9% -> 9% of each run, Pallas kernels for 17% -> 28%
where the time goes in v2:
time: 623 us; the launch traced here: 614 us
  waiting for transfers between devices  243 us (39%)
  Pallas kernels  192 us (31%)
  starting transfers between devices  82.5 us (13%)
  other arithmetic  44.5 us (7%)
  local copies, waits for them, and re-layouts  27.2 us (4%)
  between operations  23.9 us (4%)
    ppermute x72, waiting for transfers between devices, send(): lax.ppermute(x, ('dp', 'tensor'), self.pairs(place))  242 us
    ppermute x72, starting transfers between devices, send(): lax.ppermute(x, ('dp', 'tensor'), self.pairs(place))  75.1 us
    pallas_call x5, Pallas kernels, unfold(): pl.pallas_call(partial(unfold_kernel, (count, len(acts), len(weights))),...  49 us
    pallas_call x2, Pallas kernels, project(): pl.pallas_call(partial(project_kernel, (len(act), len(weights[0]), length...  27.2 us
    pallas_call x2, Pallas kernels, fold(): pl.pallas_call(fold_kernel, grid=(subs,), in_specs=[smem(), full(act.shap...  21 us
    pallas_call x1, Pallas kernels, mlp(): pl.pallas_call(partial(mlp_kernel, len(act), len(gate_pieces)), grid=(wid...  18.3 us
    pallas_call x1, Pallas kernels, gate_back(): pl.pallas_call(partial(gate_back_kernel, len(act)), grid=(width // block,...  15.3 us
    unnamed x272, local copies, waits for them, and re-layouts  15.2 us
  transfers between devices with their start and end apart: 81, of which 42 were waited for; matrix products, arithmetic and copies ran while one was open for 9% of the time, Pallas kernels for 28%

profile of v2, /device:TPU:1, one launch (start us, length us, event | category | flops | bytes accessed | tf_op | source)
XLA Modules:
  0.0 613.9 jit_solution(106122461420106785)
XLA Ops:
  13.8 5.7 collective-permute-start.7
  31.8 9.2 %collective-permute-done.2 = bf16[2,256,1024]{2,1,0:T(8,128)(2,1)} collective-permute-done((bf16[2,256,1024]{2,1,0:T(8,128)(2,1)}, bf16[2,256,1024]{2,1,0:T(8,128)(2,1)}, u32[]{:S(2)}, u32[]{:S(2)}) %collective-permute-start.2) | collective-permute-done | bytes 1048608 | tf_op jit(solution)/shard_map/ppermute | solution.py:799
  58.2 7.6 %collective-permute-done.9 = bf16[2,256,1024]{2,1,0:T(8,128)(2,1)} collective-permute-done((bf16[2,256,1024]{2,1,0:T(8,128)(2,1)}, bf16[2,256,1024]{2,1,0:T(8,128)(2,1)}, u32[]{:S(2)}, u32[]{:S(2)}) %collective-permute-start.9) | collective-permute-done | bytes 1048608 | tf_op jit(solution)/shard_map/ppermute | solution.py:799
  74.5 16.2 %collective-permute-done.14.refs_11_.refs_15_.refs_10_ = bf16[2,256,1024]{2,1,0:T(8,128)(2,1)S(1)} collective-permute-done((bf16[2,256,1024]{2,1,0:T(8,128)(2,1)S(1)}, bf16[2,256,1024]{2,1,0:T(8,128)(2,1)S(1)}, u32[]{:S(2)}, u32[]{:S(2)}) %collective-permute-start.14) | collective-permute-done | bytes 1048608 | tf_op jit(solution)/shard_map/ppermute | solution.py:799
  94.4 28.6 %collective-permute-done.12 = bf16[256,2048]{1,0:T(8,128)(2,1)S(1)} collective-permute-done((bf16[256,2048]{1,0:T(8,128)(2,1)S(1)}, bf16[256,2048]{1,0:T(8,128)(2,1)S(1)}, u32[]{:S(2)}, u32[]{:S(2)}) %collective-permute-start.12) | collective-permute-done | bytes 1048608 | tf_op jit(solution)/shard_map/ppermute | solution.py:799
  133.9 4.2 collective-permute-start.23
  138.1 3.9 collective-permute-done.20.refs_5_.refs_19_.refs_14_
  148.3 29.9 %collective-permute-done.19 = bf16[2,1024,256]{2,1,0:T(8,128)(2,1)} collective-permute-done((bf16[2,1024,256]{2,1,0:T(8,128)(2,1)}, bf16[2,1024,256]{2,1,0:T(8,128)(2,1)}, u32[]{:S(2)}, u32[]{:S(2)}) %collective-permute-start.19) | collective-permute-done | bytes 1048608 | tf_op jit(solution)/shard_map/ppermute | solution.py:799
  189.2 17.8 %project.2 = (bf16[1024,1024]{1,0:T(8,128)(2,1)}, bf16[1024,1024]{1,0:T(8,128)(2,1)}, bf16[64,1024]{1,0:T(8,128)(2,1)S(1)}) custom-call(s32[8]{0:T(128)S(1)} %xor.40.ids, s32[4]{0:T(128)S(1)} %broadcast_xor_fusion.chunks, bf16[64,2048]{1,0:T(8,128)(2,1)S(1)} %dynamic-slice_bitcast_fusion.low_in, bf16[64,2048]{1,0:T(8,128)(2,1)S(1)} %maximum_maximum_fusion.2.low_out, ...), custom_call_target="tpu_custom_call" | custom-call | flops 1 | bytes 1 | tf_op jit(solution)/shard_map/project/pallas_call | solution.py:190
  206.9 3.1 collective-permute-done.25
  218.2 9.5 %project.3.gate = bf16[1024,1024]{1,0:T(8,128)(2,1)} custom-call(s32[8]{0:T(128)S(1)} %xor.40.ids, s32[4]{0:T(128)S(1)} %broadcast_xor_fusion.chunks, bf16[64,1024]{1,0:T(8,128)(2,1)S(1)} %get-tuple-element.233.low_in.low_gate.low, bf16[64,1024]{1,0:T(8,128)(2,1)S(1)} %concatenate.108.low_out, bf16[256,2048]{1,0:T(8,128)(2,1)} %norm_rows.1.refs_2_.refs_0_, ...), custom_call_target="tpu_custom_call" | custom-call | flops 1 | bytes 1 | tf_op jit(solution)/shard_map/project/pallas_call | solution.py:190
  227.7 8.4 %retention.1 = (bf16[1024,1024]{1,0:T(8,128)(2,1)}, bf16[1024,1024]{1,0:T(8,128)(2,1)}, f32[2,1024,128]{2,1,0:T(8,128)}) custom-call(s32[4]{0:T(128)S(1)} %fusion.6.spots, f32[2]{0:T(128)S(1)} %copy-done.59, s32[1024,1]{1,0:T(8,128)S(1)} %copy-done.18, s32[1,1024]{1,0:T(1,128)S(1)} %get-tuple-element.427.seg_row, bf16[1024,1024]{1,0:T(8,128)(2,1)S(1)} %copy-done.2, ...), custom_call_target="tpu_custom_call" | custom-call | flops 1 | bytes 1 | tf_op jit(solution)/shard_map/retention/pallas_call | solution.py:242
  236.2 2.9 collective-permute-done.30
  245.2 10.4 %fold.2 = (bf16[256,2048]{1,0:T(8,128)(2,1)}, bf16[256,2048]{1,0:T(8,128)(2,1)}, bf16[256,2048]{1,0:T(8,128)(2,1)}, bf16[256,2048]{1,0:T(8,128)(2,1)}, f32[16,1024]{1,0:T(8,128)S(1)}) custom-call(s32[8]{0:T(128)S(1)} %xor.40.ids, bf16[1024,1024]{1,0:T(8,128)(2,1)} %get-tuple-element.248.act.hold, bf16[16,1024]{1,0:T(8,128)(2,1)S(1)} %copy-done.48, ...), custom_call_target="tpu_custom_call" | custom-call | flops 1 | bytes 1 | tf_op jit(solution)/shard_map/fold/pallas_call | solution.py:285
  255.7 4.7 collective-permute-done.37
  260.4 4.4 collective-permute-done.34.refs_6_.refs_2_
  264.8 5.8 collective-permute-done.36
  280.3 20.4 %collective-permute-done.40.part2 = bf16[256,2048]{1,0:T(8,128)(2,1)S(1)} collective-permute-done((bf16[256,2048]{1,0:T(8,128)(2,1)S(1)}, bf16[256,2048]{1,0:T(8,128)(2,1)S(1)}, u32[]{:S(2)}, u32[]{:S(2)}) %collective-permute-start.40) | collective-permute-done | bytes 1048608 | tf_op jit(solution)/shard_map/ppermute | solution.py:799
  307.2 19.1 %collective-permute-done.43.refs_9_.refs_14_.refs_8_ = bf16[2,256,1024]{2,1,0:T(8,128)(2,1)S(1)} collective-permute-done((bf16[2,256,1024]{2,1,0:T(8,128)(2,1)S(1)}, bf16[2,256,1024]{2,1,0:T(8,128)(2,1)S(1)}, u32[]{:S(2)}, u32[]{:S(2)}) %collective-permute-start.43) | collective-permute-done | bytes 1048608 | tf_op jit(solution)/shard_map/ppermute | solution.py:799
  326.8 3.8 collective-permute-done.47.refs_10_.refs_15_.refs_9_
  335.7 8.4 %hidden_grad.1 = (f32[1024,1024]{1,0:T(8,128)S(1)}, bf16[16,1024]{1,0:T(8,128)(2,1)S(1)}) custom-call(s32[8]{0:T(128)S(1)} %xor.40.ids, bf16[16,2048]{1,0:T(8,128)(2,1)S(1)} %dynamic-slice_bitcast_fusion.2.low_back.low_out, bf16[16,1024]{1,0:T(8,128)(2,1)S(1)} %copy-done.46, bf16[256,2048]{1,0:T(8,128)(2,1)S(1)} %broadcast_select_fusion.7.refs_0_.grad_in, ...), custom_call_target="tpu_custom_call" | custom-call | flops 1 | bytes 1 | tf_op jit(solution)/shard_map/hidden_grad/pallas_call | solution.py:360
  346.2 10.0 %collective-permute-done.50.refs_7_.refs_12_.refs_6_ = bf16[2,256,1024]{2,1,0:T(8,128)(2,1)S(1)} collective-permute-done((bf16[2,256,1024]{2,1,0:T(8,128)(2,1)S(1)}, bf16[2,256,1024]{2,1,0:T(8,128)(2,1)S(1)}, u32[]{:S(2)}, u32[]{:S(2)}) %collective-permute-start.50) | collective-permute-done | bytes 1048608 | tf_op jit(solution)/shard_map/ppermute | solution.py:799
  357.2 18.3 %mlp.1 = (bf16[1024,1024]{1,0:T(8,128)(2,1)}, bf16[1024,1024]{1,0:T(8,128)(2,1)}, bf16[1024,1024]{1,0:T(8,128)(2,1)}, bf16[32,1024]{1,0:T(8,128)(2,1)}, f32[48,1...) custom-call(s32[8]{0:T(128)S(1)} %xor.40.ids, ...), custom_call_target="tpu_custom_call" | custom-call | flops 1 | bytes 1 | tf_op jit(solution)/shard_map/mlp/pallas_call | solution.py:413
  377.0 12.8 %unfold.5 = (bf16[256,2048]{1,0:T(8,128)(2,1)}, bf16[256,2048]{1,0:T(8,128)(2,1)}, bf16[256,2048]{1,0:T(8,128)(2,1)}) custom-call(s32[8]{0:T(128)S(1)} %xor.40.ids, bf16[32,2048]{1,0:T(8,128)(2,1)S(1)} %dynamic-slice_bitcast_fusion.1.low_in, f32[32,1024]{1,0:T(8,128)S(1)} %slice.175.refs_0_.refs_1_.refs_2_, f32[32,1024]{1,0:T(8,128)S(1)} %slice.175.refs_0_.refs_1_.refs_2_, ...), custom_call_target="tpu_custom_call" | custom-call | flops 1 | bytes 1 | tf_op jit(solution)/shard_map/unfold/pallas_call | solution.py:460
  391.1 2.9 collective-permute-done.54
  396.7 4.7 share.2
  401.4 6.6 %unfold.6.part0 = bf16[256,2048]{1,0:T(8,128)(2,1)} custom-call(s32[8]{0:T(128)S(1)} %xor.40.ids, bf16[32,2048]{1,0:T(8,128)(2,1)S(1)} %dynamic-slice_bitcast_fusion.1.low_in, f32[32,1024]{1,0:T(8,128)S(1)} %slice.175.refs_0_.refs_1_.refs_2_, bf16[1024,1024]{1,0:T(8,128)(2,1)} %get-tuple-element.289.refs_3_.refs_5_.refs_7_.refs_1_, ...), custom_call_target="tpu_custom_call" | custom-call | flops 1 | bytes 1 | tf_op jit(solution)/shard_map/unfold/pallas_call | solution.py:460
  408.1 10.6 %fold.3 = (bf16[256,2048]{1,0:T(8,128)(2,1)}, bf16[256,2048]{1,0:T(8,128)(2,1)}, bf16[256,2048]{1,0:T(8,128)(2,1)}, bf16[256,2048]{1,0:T(8,128)(2,1)}, f32[16,1024]{1,0:T(8,128)}) custom-call(s32[8]{0:T(128)S(1)} %xor.40.ids, bf16[1024,1024]{1,0:T(8,128)(2,1)} %get-tuple-element.298.act, bf16[16,1024]{1,0:T(8,128)(2,1)S(1)} %copy-done.47, ...), custom_call_target="tpu_custom_call" | custom-call | flops 1 | bytes 1 | tf_op jit(solution)/shard_map/fold/pallas_call | solution.py:285
  419.3 3.7 rms_back.2.refs_0_.refs_4_.grad_in
  426.0 5.2 collective-permute-start.61
  432.7 19.9 %collective-permute-done.61 = bf16[304,512]{1,0:T(8,128)(2,1)S(1)} collective-permute-done((bf16[304,512]{1,0:T(8,128)(2,1)S(1)}, bf16[304,512]{1,0:T(8,128)(2,1)S(1)}, u32[]{:S(2)}, u32[]{:S(2)}) %collective-permute-start.61) | collective-permute-done | bytes 311328 | tf_op jit(solution)/shard_map/ppermute | solution.py:799
  457.1 2.9 collective-permute-start.63
  460.2 15.3 %gate_back.1 = (bf16[1024,1024]{1,0:T(8,128)(2,1)}, bf16[1024,1024]{1,0:T(8,128)(2,1)}, bf16[16,1024]{1,0:T(8,128)(2,1)}, f32[64,1024]{1,0:T(8,128)}, bf16[16,10...) custom-call(s32[8]{0:T(128)} %copy-done.50, bf16[16,2048]{1,0:T(8,128)(2,1)} %copy-done.43, ...), custom_call_target="tpu_custom_call" | custom-call | flops 1 | bytes 1 | tf_op jit(solution)/shard_map/gate_back/pallas_call | solution.py:511
  476.5 11.9 %retention_back.1 = (bf16[1024,512]{1,0:T(8,128)(2,1)S(1)}, bf16[1024,512]{1,0:T(8,128)(2,1)S(1)}, bf16[1024,1024]{1,0:T(8,128)(2,1)}, f32[64,1024]{1,0:T(8,128)...) custom-call(s32[4]{0:T(128)S(1)} %copy-done.58, f32[2]{0:T(128)S(1)} %copy-done.60, ...), custom_call_target="tpu_custom_call" | custom-call | flops 1 | bytes 1 | tf_op jit(solution)/shard_map/retention_back/pallas_call | solution.py:594
  496.2 12.8 %unfold.7 = (bf16[256,2048]{1,0:T(8,128)(2,1)}, bf16[256,2048]{1,0:T(8,128)(2,1)}) custom-call(s32[8]{0:T(128)S(1)} %copy-done.51, bf16[64,2048]{1,0:T(8,128)(2,1)S(1)} %dynamic-slice_bitcast_fusion.low_in, f32[64,1024]{1,0:T(8,128)S(1)} %get-tuple-element.322.refs_0_.refs_1_, f32[64,1024]{1,0:T(8,128)S(1)} %get-tuple-element.322.refs_0_.refs_1_, ...), custom_call_target="tpu_custom_call" | custom-call | flops 1 | bytes 1 | tf_op jit(solution)/shard_map/unfold/pallas_call | solution.py:460
  510.2 3.9 collective-permute-start.66
  515.5 8.6 %unfold.8 = bf16[256,2048]{1,0:T(8,128)(2,1)} custom-call(s32[8]{0:T(128)S(1)} %copy-done.51, bf16[64,2048]{1,0:T(8,128)(2,1)S(1)} %dynamic-slice_bitcast_fusion.low_in, f32[64,1024]{1,0:T(8,128)S(1)} %get-tuple-element.322.refs_0_.refs_1_, bf16[1024,512]{1,0:T(8,128)(2,1)} %copy-done.5, bf16[1024,512]{1,0:T(8,128)(2,1)} %copy-done.6, ...), custom_call_target="tpu_custom_call" | custom-call | flops 1 | bytes 1 | tf_op jit(solution)/shard_map/unfold/pallas_call | solution.py:460
  524.1 4.8 share.3
  531.5 3.0 collective-permute-start.71
  535.2 8.3 %unfold.9.part0 = bf16[256,2048]{1,0:T(8,128)(2,1)} custom-call(s32[8]{0:T(128)S(1)} %copy-done.51, bf16[64,2048]{1,0:T(8,128)(2,1)S(1)} %dynamic-slice_bitcast_fusion.low_in, f32[64,1024]{1,0:T(8,128)S(1)} %get-tuple-element.322.refs_0_.refs_1_, bf16[1024,512]{1,0:T(8,128)(2,1)} %copy-done.5, bf16[1024,512]{1,0:T(8,128)(2,1)} %copy-done.6, ...), custom_call_target="tpu_custom_call" | custom-call | flops 1 | bytes 1 | tf_op jit(solution)/shard_map/unfold/pallas_call | solution.py:460
  543.5 3.6 collective-permute-done.71
  547.3 4.0 collective-permute-done.70
  553.1 5.0 collective-permute-done.74
  562.1 6.4 %collective-permute-done.75 = bf16[64,2048]{1,0:T(8,128)(2,1)S(1)} collective-permute-done((bf16[64,2048]{1,0:T(8,128)(2,1)S(1)}, bf16[64,2048]{1,0:T(8,128)(2,1)S(1)}, u32[]{:S(2)}, u32[]{:S(2)}) %collective-permute-start.75) | collective-permute-done | bytes 262176 | tf_op jit(solution)/shard_map/ppermute | solution.py:799
  580.6 6.7 %place.2 = (f32[8,16,2048]{2,1,0:T(8,128)}, f32[8,32,2048]{2,1,0:T(8,128)}, f32[8,32,1024]{2,1,0:T(8,128)}, f32[8,16,1024]{2,1,0:T(8,128)}) custom-call(s32[9]{0:T(128)S(1)} %pad_add_fusion.order, bf16[8,304,512]{2,1,0:T(8,128)(2,1)} %bitcast.114), custom_call_target="tpu_custom_call" | custom-call | flops 1 | bytes 1 | tf_op jit(solution)/shard_map/place/pallas_call | solution.py:682
  588.1 7.7 %place.3 = (f32[8,64,2048]{2,1,0:T(8,128)}, f32[8,16,2048]{2,1,0:T(8,128)}, f32[8,2,16,512]{3,2,1,0:T(8,128)}, f32[8,32,1024]{2,1,0:T(8,128)}, f32[8,16,1024]{2,1,0:T(8,128)}) custom-call(s32[9]{0:T(128)S(1)} %pad_add_fusion.1.order, bf16[4,448,512]{2,1,0:T(8,128)(2,1)} %copy-done.76, bf16[4,448,512]{2,1,0:T(8,128)(2,1)} %collective-permute-done.79.refs_1_), custom_call_target="tpu_custom_call" | custom-call | flops 1 | bytes 1 | tf_op jit(solution)/shard_map/place/pallas_call | solution.py:682
  595.7 7.8 %collective-permute-done.78 = bf16[256,2048]{1,0:T(8,128)(2,1)} collective-permute-done((bf16[256,2048]{1,0:T(8,128)(2,1)}, bf16[256,2048]{1,0:T(8,128)(2,1)}, u32[]{:S(2)}, u32[]{:S(2)}) %collective-permute-start.78) | collective-permute-done | bytes 1048608 | tf_op jit(solution)/shard_map/ppermute | solution.py:799
  603.6 3.1 select_bitcast_fusion
  (507 shorter events, 155.4 us)
Async XLA Ops:
  7.2 566.1 %all-gather.3.cloned.1.call-start = ((), (), s32[]{:S(2)}) async-start(), calls=%async_computation | async-start | bytes 2801664 | tf_op jit(solution)/shard_map/all_gather | solution.py:984
  12.5 28.4 %collective-permute-start.2 = (bf16[2,256,1024]{2,1,0:T(8,128)(2,1)}, bf16[2,256,1024]{2,1,0:T(8,128)(2,1)}, u32[]{:S(2)}, u32[]{:S(2)}) collective-permute-start(bf16[2,256,1024]{2,1,0:T(8,128)(2,1)} %pad_maximum_fusion.1), channel_id=1, source_target_pairs={{0,2},{1,3},{6,4},{7,5},{8,10},{9,11},{14,12},{15,13},{16,18},{17,... | collective-permute-start | bytes 3145736 | tf_op jit(solution)/shard_map/ppermute | solution.py:799
  25.1 17.3 %collective-permute-start.3 = (s32[1,1152]{1,0:T(1,128)S(1)}, s32[1,1152]{1,0:T(1,128)S(1)}, u32[]{:S(2)}, u32[]{:S(2)}) collective-permute-start(s32[1,1152]{1,0:T(1,128)S(1)} %concatenate.100), channel_id=1, source_target_pairs={{0,4},{1,5},{2,6},{3,7},{4,0},{5,1},{6,2},{7,3},{8,12},{9,13},{10,... | collective-permute-start | bytes 13832 | tf_op jit(solution)/shard_map/ppermute | solution.py:793
  46.0 19.9 %collective-permute-start.9 = (bf16[2,256,1024]{2,1,0:T(8,128)(2,1)}, bf16[2,256,1024]{2,1,0:T(8,128)(2,1)}, u32[]{:S(2)}, u32[]{:S(2)}) collective-permute-start(bf16[2,256,1024]{2,1,0:T(8,128)(2,1)} %pad_maximum_fusion), channel_id=1, source_target_pairs={{0,2},{1,3},{6,4},{7,5},{8,10},{9,11},{14,12},{15,13},{16,18},{17,... | collective-permute-start | bytes 3145736 | tf_op jit(solution)/shard_map/ppermute | solution.py:799
  47.3 20.7 %collective-permute-start.10 = (bf16[2,256,1024]{2,1,0:T(8,128)(2,1)S(1)}, bf16[2,256,1024]{2,1,0:T(8,128)(2,1)}, u32[]{:S(2)}, u32[]{:S(2)}) collective-permute-start(bf16[2,256,1024]{2,1,0:T(8,128)(2,1)S(1)} %broadcast_select_fusion.6.refs_6_.refs_10_.refs_5_), channel_id=1, source_target_pairs={{0,8},{1,9},{2,10},{3,11},{4,12},{5,13},{6,14},{7,15},{8,0},{9,1},... | collective-permute-start | bytes 3145736 | tf_op jit(solution)/shard_map/ppermute | solution.py:799
  49.3 20.6 %collective-permute-start.11 = (bf16[2,256,1024]{2,1,0:T(8,128)(2,1)S(1)}, bf16[2,256,1024]{2,1,0:T(8,128)(2,1)}, u32[]{:S(2)}, u32[]{:S(2)}) collective-permute-start(bf16[2,256,1024]{2,1,0:T(8,128)(2,1)S(1)} %broadcast_select_fusion.6.refs_6_.refs_10_.refs_5_), channel_id=1, source_target_pairs={{0,16},{1,17},{2,18},{3,19},{4,20},{5,21},{6,22},{7,23},{8,24},{9,... | collective-permute-start | bytes 3145736 | tf_op jit(solution)/shard_map/ppermute | solution.py:799
  69.9 20.8 %collective-permute-start.14 = (bf16[2,256,1024]{2,1,0:T(8,128)(2,1)S(1)}, bf16[2,256,1024]{2,1,0:T(8,128)(2,1)S(1)}, u32[]{:S(2)}, u32[]{:S(2)}) collective-permute-start(bf16[2,256,1024]{2,1,0:T(8,128)(2,1)S(1)} %broadcast_select_fusion.5.refs_10_.refs_14_.refs_9_), channel_id=1, source_target_pairs={{0,8},{1,9},{2,10},{3,11},{4,12},{5,13},{6,14},{7,15},{8,0},{9,1},... | collective-permute-start | bytes 3145736 | tf_op jit(solution)/shard_map/ppermute | solution.py:799
  69.9 21.9 %collective-permute-start.15 = (bf16[2,256,1024]{2,1,0:T(8,128)(2,1)}, bf16[2,256,1024]{2,1,0:T(8,128)(2,1)S(1)}, u32[]{:S(2)}, u32[]{:S(2)}) collective-permute-start(bf16[2,256,1024]{2,1,0:T(8,128)(2,1)} %collective-permute-done.10.refs_7_.refs_11_.refs_6_), channel_id=1, source_target_pairs={{0,16},{1,17},{2,18},{3,19},{4,20},{5,21},{6,22},{7,23},{8,24},{9,... | collective-permute-start | bytes 3145736 | tf_op jit(solution)/shard_map/ppermute | solution.py:799
  71.3 51.8 %collective-permute-start.12 = (bf16[256,2048]{1,0:T(8,128)(2,1)S(1)}, bf16[256,2048]{1,0:T(8,128)(2,1)S(1)}, u32[]{:S(2)}, u32[]{:S(2)}) collective-permute-start(bf16[256,2048]{1,0:T(8,128)(2,1)S(1)} %bitcast.131), channel_id=1, source_target_pairs={{2,4},{3,5},{4,2},{5,3},{10,12},{11,13},{12,10},{13,11},{18,20},{1... | collective-permute-start | bytes 3145736 | tf_op jit(solution)/shard_map/ppermute | solution.py:799
  73.2 51.3 %collective-permute-start.13 = (bf16[2,256,1024]{2,1,0:T(8,128)(2,1)S(1)}, bf16[2,256,1024]{2,1,0:T(8,128)(2,1)S(1)}, u32[]{:S(2)}, u32[]{:S(2)}) collective-permute-start(bf16[2,256,1024]{2,1,0:T(8,128)(2,1)S(1)} %copy-done.107), channel_id=1, source_target_pairs={{0,2},{1,3},{6,4},{7,5},{8,10},{9,11},{14,12},{15,13},{16,18},{17,... | collective-permute-start | bytes 3145736 | tf_op jit(solution)/shard_map/ppermute | solution.py:799
  91.8 35.1 %collective-permute-start.17 = (bf16[2,256,1024]{2,1,0:T(8,128)(2,1)S(1)}, bf16[2,256,1024]{2,1,0:T(8,128)(2,1)S(1)}, u32[]{:S(2)}, u32[]{:S(2)}) collective-permute-start(bf16[2,256,1024]{2,1,0:T(8,128)(2,1)S(1)} %broadcast_select_fusion.5.refs_10_.refs_14_.refs_9_), channel_id=1, source_target_pairs={{0,16},{1,17},{2,18},{3,19},{4,20},{5,21},{6,22},{7,23},{8,24},{9,... | collective-permute-start | bytes 3145736 | tf_op jit(solution)/shard_map/ppermute | solution.py:799
  93.1 33.8 %collective-permute-start.16 = (bf16[112,1024]{1,0:T(8,128)(2,1)S(1)}, bf16[112,1024]{1,0:T(8,128)(2,1)S(1)}, u32[]{:S(2)}, u32[]{:S(2)}) collective-permute-start(bf16[112,1024]{1,0:T(8,128)(2,1)S(1)} %get-tuple-element.203), channel_id=1, source_target_pairs={{0,2},{1,3},{6,4},{7,5},{8,10},{9,11},{14,12},{15,13},{16,18},{17,... | collective-permute-start | bytes 688136 | tf_op jit(solution)/shard_map/ppermute | solution.py:799
  132.5 45.7 %collective-permute-start.19 = (bf16[2,1024,256]{2,1,0:T(8,128)(2,1)}, bf16[2,1024,256]{2,1,0:T(8,128)(2,1)}, u32[]{:S(2)}, u32[]{:S(2)}) collective-permute-start(bf16[2,1024,256]{2,1,0:T(8,128)(2,1)} %pad_maximum_fusion.3), channel_id=1, source_target_pairs={{0,2},{1,3},{6,4},{7,5},{8,10},{9,11},{14,12},{15,13},{16,18},{17,... | collective-permute-start | bytes 3145736 | tf_op jit(solution)/shard_map/ppermute | solution.py:799
  133.8 46.0 %collective-permute-start.18 = (bf16[256,2048]{1,0:T(8,128)(2,1)}, bf16[256,2048]{1,0:T(8,128)(2,1)}, u32[]{:S(2)}, u32[]{:S(2)}) collective-permute-start(bf16[256,2048]{1,0:T(8,128)(2,1)} %norm_rows.1.refs_2_.refs_0_), channel_id=1, source_target_pairs={{0,1},{1,0},{2,3},{3,2},{4,5},{5,4},{6,7},{7,6},{8,9},{9,8},{10,11... | collective-permute-start | bytes 3145736 | tf_op jit(solution)/shard_map/ppermute | solution.py:799
  133.9 47.4 %collective-permute-start.23 = (bf16[256,2048]{1,0:T(8,128)(2,1)}, bf16[256,2048]{1,0:T(8,128)(2,1)}, u32[]{:S(2)}, u32[]{:S(2)}) collective-permute-start(bf16[256,2048]{1,0:T(8,128)(2,1)} %bitcast.132), channel_id=1, source_target_pairs={{2,4},{3,5},{4,2},{5,3},{10,12},{11,13},{12,10},{13,11},{18,20},{1... | collective-permute-start | bytes 3145736 | tf_op jit(solution)/shard_map/ppermute | solution.py:799
  143.5 37.8 %collective-permute-start.22 = (bf16[2,256,1024]{2,1,0:T(8,128)(2,1)}, bf16[2,256,1024]{2,1,0:T(8,128)(2,1)}, u32[]{:S(2)}, u32[]{:S(2)}) collective-permute-start(bf16[2,256,1024]{2,1,0:T(8,128)(2,1)} %copy-done.66), channel_id=1, source_target_pairs={{0,8},{1,9},{2,10},{3,11},{4,12},{5,13},{6,14},{7,15},{8,0},{9,1},... | collective-permute-start | bytes 3145736 | tf_op jit(solution)/shard_map/ppermute | solution.py:799
  143.5 37.8 %collective-permute-start.24 = (bf16[2,256,1024]{2,1,0:T(8,128)(2,1)}, bf16[2,256,1024]{2,1,0:T(8,128)(2,1)}, u32[]{:S(2)}, u32[]{:S(2)}) collective-permute-start(bf16[2,256,1024]{2,1,0:T(8,128)(2,1)} %collective-permute-done.20.refs_5_.refs_19_.refs_14_), channel_id=1, source_target_pairs={{0,16},{1,17},{2,18},{3,19},{4,20},{5,21},{6,22},{7,23},{8,24},{9,... | collective-permute-start | bytes 3145736 | tf_op jit(solution)/shard_map/ppermute | solution.py:799
  182.4 27.7 %collective-permute-start.25 = (bf16[2,1024,256]{2,1,0:T(8,128)(2,1)S(1)}, bf16[2,1024,256]{2,1,0:T(8,128)(2,1)S(1)}, u32[]{:S(2)}, u32[]{:S(2)}) collective-permute-start(bf16[2,1024,256]{2,1,0:T(8,128)(2,1)S(1)} %copy-done.106), channel_id=1, source_target_pairs={{0,2},{1,3},{6,4},{7,5},{8,10},{9,11},{14,12},{15,13},{16,18},{17,... | collective-permute-start | bytes 3145736 | tf_op jit(solution)/shard_map/ppermute | solution.py:799
  183.8 28.4 %collective-permute-start.26 = (bf16[2,1024,256]{2,1,0:T(8,128)(2,1)S(1)}, bf16[2,1024,256]{2,1,0:T(8,128)(2,1)}, u32[]{:S(2)}, u32[]{:S(2)}) collective-permute-start(bf16[2,1024,256]{2,1,0:T(8,128)(2,1)S(1)} %broadcast_select_fusion.1.refs_0_.refs_4_), channel_id=1, source_target_pairs={{0,8},{1,9},{2,10},{3,11},{4,12},{5,13},{6,14},{7,15},{8,0},{9,1},... | collective-permute-start | bytes 3145736 | tf_op jit(solution)/shard_map/ppermute | solution.py:799
  184.0 28.2 %collective-permute-start.29 = (bf16[2,1024,256]{2,1,0:T(8,128)(2,1)S(1)}, bf16[2,1024,256]{2,1,0:T(8,128)(2,1)S(1)}, u32[]{:S(2)}, u32[]{:S(2)}) collective-permute-start(bf16[2,1024,256]{2,1,0:T(8,128)(2,1)S(1)} %broadcast_select_fusion.1.refs_0_.refs_4_), channel_id=1, source_target_pairs={{0,16},{1,17},{2,18},{3,19},{4,20},{5,21},{6,22},{7,23},{8,24},{9,... | collective-permute-start | bytes 3145736 | tf_op jit(solution)/shard_map/ppermute | solution.py:799
  213.2 25.9 %collective-permute-start.30 = (bf16[2,256,1024]{2,1,0:T(8,128)(2,1)}, bf16[2,256,1024]{2,1,0:T(8,128)(2,1)}, u32[]{:S(2)}, u32[]{:S(2)}) collective-permute-start(bf16[2,256,1024]{2,1,0:T(8,128)(2,1)} %pad_maximum_fusion.5), channel_id=1, source_target_pairs={{0,2},{1,3},{6,4},{7,5},{8,10},{9,11},{14,12},{15,13},{16,18},{17,... | collective-permute-start | bytes 3145736 | tf_op jit(solution)/shard_map/ppermute | solution.py:799
  215.0 25.8 %collective-permute-start.31 = (bf16[2,1024,256]{2,1,0:T(8,128)(2,1)}, bf16[2,1024,256]{2,1,0:T(8,128)(2,1)}, u32[]{:S(2)}, u32[]{:S(2)}) collective-permute-start(bf16[2,1024,256]{2,1,0:T(8,128)(2,1)} %collective-permute-done.26.refs_1_.refs_5_), channel_id=1, source_target_pairs={{0,16},{1,17},{2,18},{3,19},{4,20},{5,21},{6,22},{7,23},{8,24},{9,... | collective-permute-start | bytes 3145736 | tf_op jit(solution)/shard_map/ppermute | solution.py:799
  216.4 25.4 %collective-permute-start.32 = (bf16[2,1024,256]{2,1,0:T(8,128)(2,1)}, bf16[2,1024,256]{2,1,0:T(8,128)(2,1)}, u32[]{:S(2)}, u32[]{:S(2)}) collective-permute-start(bf16[2,1024,256]{2,1,0:T(8,128)(2,1)} %broadcast_select_fusion.refs_4_.refs_0_), channel_id=1, source_target_pairs={{0,8},{1,9},{2,10},{3,11},{4,12},{5,13},{6,14},{7,15},{8,0},{9,1},... | collective-permute-start | bytes 3145736 | tf_op jit(solution)/shard_map/ppermute | solution.py:799
  216.5 24.3 %collective-permute-start.33 = (bf16[128,2048]{1,0:T(8,128)(2,1)}, bf16[128,2048]{1,0:T(8,128)(2,1)}, u32[]{:S(2)}, u32[]{:S(2)}) collective-permute-start(bf16[128,2048]{1,0:T(8,128)(2,1)} %get-tuple-element.245), channel_id=1, source_target_pairs={{0,1},{1,0},{2,3},{3,2},{4,5},{5,4},{6,7},{7,6},{8,9},{9,8},{10,11... | collective-permute-start | bytes 1572872 | tf_op jit(solution)/shard_map/ppermute | solution.py:799
  241.9 22.9 %collective-permute-start.34 = (bf16[2,1024,256]{2,1,0:T(8,128)(2,1)}, bf16[2,1024,256]{2,1,0:T(8,128)(2,1)S(1)}, u32[]{:S(2)}, u32[]{:S(2)}) collective-permute-start(bf16[2,1024,256]{2,1,0:T(8,128)(2,1)} %broadcast_select_fusion.refs_4_.refs_0_), channel_id=1, source_target_pairs={{0,16},{1,17},{2,18},{3,19},{4,20},{5,21},{6,22},{7,23},{8,24},{9,... | collective-permute-start | bytes 3145736 | tf_op jit(solution)/shard_map/ppermute | solution.py:799
  242.0 22.9 %collective-permute-start.35 = (bf16[2,256,1024]{2,1,0:T(8,128)(2,1)S(1)}, bf16[2,256,1024]{2,1,0:T(8,128)(2,1)S(1)}, u32[]{:S(2)}, u32[]{:S(2)}) collective-permute-start(bf16[2,256,1024]{2,1,0:T(8,128)(2,1)S(1)} %broadcast_select_fusion.3.refs_4_.refs_9_.refs_3_), channel_id=1, source_target_pairs={{0,8},{1,9},{2,10},{3,11},{4,12},{5,13},{6,14},{7,15},{8,0},{9,1},... | collective-permute-start | bytes 3145736 | tf_op jit(solution)/shard_map/ppermute | solution.py:799
  243.0 27.7 %collective-permute-start.36 = (bf16[2,256,1024]{2,1,0:T(8,128)(2,1)S(1)}, bf16[2,256,1024]{2,1,0:T(8,128)(2,1)S(1)}, u32[]{:S(2)}, u32[]{:S(2)}) collective-permute-start(bf16[2,256,1024]{2,1,0:T(8,128)(2,1)S(1)} %copy-done.105), channel_id=1, source_target_pairs={{0,2},{1,3},{6,4},{7,5},{8,10},{9,11},{14,12},{15,13},{16,18},{17,... | collective-permute-start | bytes 3145736 | tf_op jit(solution)/shard_map/ppermute | solution.py:799
  275.2 25.5 %collective-permute-start.40 = (bf16[256,2048]{1,0:T(8,128)(2,1)S(1)}, bf16[256,2048]{1,0:T(8,128)(2,1)S(1)}, u32[]{:S(2)}, u32[]{:S(2)}) collective-permute-start(bf16[256,2048]{1,0:T(8,128)(2,1)S(1)} %add_convert_fusion.4), channel_id=1, source_target_pairs={{0,1},{1,0},{2,3},{3,2},{4,5},{5,4},{6,7},{7,6},{8,9},{9,8},{10,11... | collective-permute-start | bytes 3145736 | tf_op jit(solution)/shard_map/ppermute | solution.py:799
  277.5 25.3 %collective-permute-start.41 = (bf16[2,256,1024]{2,1,0:T(8,128)(2,1)S(1)}, bf16[2,256,1024]{2,1,0:T(8,128)(2,1)S(1)}, u32[]{:S(2)}, u32[]{:S(2)}) collective-permute-start(bf16[2,256,1024]{2,1,0:T(8,128)(2,1)S(1)} %broadcast_select_fusion.3.refs_4_.refs_9_.refs_3_), channel_id=1, source_target_pairs={{0,16},{1,17},{2,18},{3,19},{4,20},{5,21},{6,22},{7,23},{8,24},{9,... | collective-permute-start | bytes 3145736 | tf_op jit(solution)/shard_map/ppermute | solution.py:799
  278.5 24.3 %collective-permute-start.42 = (bf16[2,1024,256]{2,1,0:T(8,128)(2,1)S(1)}, bf16[2,1024,256]{2,1,0:T(8,128)(2,1)S(1)}, u32[]{:S(2)}, u32[]{:S(2)}) collective-permute-start(bf16[2,1024,256]{2,1,0:T(8,128)(2,1)S(1)} %collective-permute-done.34.refs_6_.refs_2_), channel_id=1, source_target_pairs={{0,8},{1,9},{2,10},{3,11},{4,12},{5,13},{6,14},{7,15},{8,0},{9,1},... | collective-permute-start | bytes 3145736 | tf_op jit(solution)/shard_map/ppermute | solution.py:799
  302.8 23.5 %collective-permute-start.43 = (bf16[2,256,1024]{2,1,0:T(8,128)(2,1)S(1)}, bf16[2,256,1024]{2,1,0:T(8,128)(2,1)S(1)}, u32[]{:S(2)}, u32[]{:S(2)}) collective-permute-start(bf16[2,256,1024]{2,1,0:T(8,128)(2,1)S(1)} %broadcast_select_fusion.2.refs_8_.refs_13_.refs_7_), channel_id=1, source_target_pairs={{0,8},{1,9},{2,10},{3,11},{4,12},{5,13},{6,14},{7,15},{8,0},{9,1},... | collective-permute-start | bytes 3145736 | tf_op jit(solution)/shard_map/ppermute | solution.py:799
  303.5 23.3 %collective-permute-start.44 = (bf16[256,2048]{1,0:T(8,128)(2,1)S(1)}, bf16[256,2048]{1,0:T(8,128)(2,1)S(1)}, u32[]{:S(2)}, u32[]{:S(2)}) collective-permute-start(bf16[256,2048]{1,0:T(8,128)(2,1)S(1)} %get-tuple-element.284.refs_0_.refs_4_), channel_id=1, source_target_pairs={{0,1},{1,0},{2,3},{3,2},{4,5},{5,4},{6,7},{7,6},{8,9},{9,8},{10,11... | collective-permute-start | bytes 3145736 | tf_op jit(solution)/shard_map/ppermute | solution.py:799
  304.6 22.2 %collective-permute-start.45 = (bf16[256,2048]{1,0:T(8,128)(2,1)S(1)}, bf16[256,2048]{1,0:T(8,128)(2,1)S(1)}, u32[]{:S(2)}, u32[]{:S(2)}) collective-permute-start(bf16[256,2048]{1,0:T(8,128)(2,1)S(1)} %broadcast_select_fusion.7.refs_0_.grad_in), channel_id=1, source_target_pairs={{0,4},{1,5},{2,6},{3,7},{4,0},{5,1},{6,2},{7,3},{8,12},{9,13},{10,... | collective-permute-start | bytes 3145736 | tf_op jit(solution)/shard_map/ppermute | solution.py:799
  306.4 20.4 %collective-permute-start.46 = (bf16[256,2048]{1,0:T(8,128)(2,1)S(1)}, bf16[256,2048]{1,0:T(8,128)(2,1)S(1)}, u32[]{:S(2)}, u32[]{:S(2)}) collective-permute-start(bf16[256,2048]{1,0:T(8,128)(2,1)S(1)} %constant_dynamic-update-slice_fusion.14.refs_2_), channel_id=1, source_target_pairs={{0,4},{1,5},{2,6},{3,7},{4,0},{5,1},{6,2},{7,3},{8,12},{9,13},{10,... | collective-permute-start | bytes 3145736 | tf_op jit(solution)/shard_map/ppermute | solution.py:799
  306.4 24.2 %collective-permute-start.47 = (bf16[2,256,1024]{2,1,0:T(8,128)(2,1)S(1)}, bf16[2,256,1024]{2,1,0:T(8,128)(2,1)S(1)}, u32[]{:S(2)}, u32[]{:S(2)}) collective-permute-start(bf16[2,256,1024]{2,1,0:T(8,128)(2,1)S(1)} %broadcast_select_fusion.2.refs_8_.refs_13_.refs_7_), channel_id=1, source_target_pairs={{0,16},{1,17},{2,18},{3,19},{4,20},{5,21},{6,22},{7,23},{8,24},{9,... | collective-permute-start | bytes 3145736 | tf_op jit(solution)/shard_map/ppermute | solution.py:799
  331.9 24.3 %collective-permute-start.50 = (bf16[2,256,1024]{2,1,0:T(8,128)(2,1)S(1)}, bf16[2,256,1024]{2,1,0:T(8,128)(2,1)S(1)}, u32[]{:S(2)}, u32[]{:S(2)}) collective-permute-start(bf16[2,256,1024]{2,1,0:T(8,128)(2,1)S(1)} %collective-permute-done.41.refs_6_.refs_11_.refs_5_), channel_id=1, source_target_pairs={{0,8},{1,9},{2,10},{3,11},{4,12},{5,13},{6,14},{7,15},{8,0},{9,1},... | collective-permute-start | bytes 3145736 | tf_op jit(solution)/shard_map/ppermute | solution.py:799
  332.8 24.0 %collective-permute-start.51 = (bf16[2,256,1024]{2,1,0:T(8,128)(2,1)S(1)}, bf16[2,256,1024]{2,1,0:T(8,128)(2,1)}, u32[]{:S(2)}, u32[]{:S(2)}) collective-permute-start(bf16[2,256,1024]{2,1,0:T(8,128)(2,1)S(1)} %collective-permute-done.43.refs_9_.refs_14_.refs_8_), channel_id=1, source_target_pairs={{0,16},{1,17},{2,18},{3,19},{4,20},{5,21},{6,22},{7,23},{8,24},{9,... | collective-permute-start | bytes 3145736 | tf_op jit(solution)/shard_map/ppermute | solution.py:799
  395.5 23.7 %collective-permute-start.56 = (bf16[256,2048]{1,0:T(8,128)(2,1)}, bf16[256,2048]{1,0:T(8,128)(2,1)}, u32[]{:S(2)}, u32[]{:S(2)}) collective-permute-start(bf16[256,2048]{1,0:T(8,128)(2,1)} %add_convert_fusion.3), channel_id=1, source_target_pairs={{0,1},{1,0},{2,3},{3,2},{4,5},{5,4},{6,7},{7,6},{8,9},{9,8},{10,11... | collective-permute-start | bytes 3145736 | tf_op jit(solution)/shard_map/ppermute | solution.py:799
  425.2 27.4 %collective-permute-start.57 = (bf16[256,2048]{1,0:T(8,128)(2,1)S(1)}, bf16[256,2048]{1,0:T(8,128)(2,1)S(1)}, u32[]{:S(2)}, u32[]{:S(2)}) collective-permute-start(bf16[256,2048]{1,0:T(8,128)(2,1)S(1)} %copy-done.128), channel_id=1, source_target_pairs={{0,4},{1,5},{2,6},{3,7},{4,0},{5,1},{6,2},{7,3},{8,12},{9,13},{10,... | collective-permute-start | bytes 3145736 | tf_op jit(solution)/shard_map/ppermute | solution.py:799
  425.3 27.3 %collective-permute-start.59 = (bf16[256,2048]{1,0:T(8,128)(2,1)}, bf16[256,2048]{1,0:T(8,128)(2,1)S(1)}, u32[]{:S(2)}, u32[]{:S(2)}) collective-permute-start(bf16[256,2048]{1,0:T(8,128)(2,1)} %rms_back.2.refs_0_.refs_4_.grad_in), channel_id=1, source_target_pairs={{0,4},{1,5},{2,6},{3,7},{4,0},{5,1},{6,2},{7,3},{8,12},{9,13},{10,... | collective-permute-start | bytes 3145736 | tf_op jit(solution)/shard_map/ppermute | solution.py:799
  425.7 28.3 %collective-permute-start.60 = (bf16[256,2048]{1,0:T(8,128)(2,1)}, bf16[256,2048]{1,0:T(8,128)(2,1)S(1)}, u32[]{:S(2)}, u32[]{:S(2)}) collective-permute-start(bf16[256,2048]{1,0:T(8,128)(2,1)} %rms_back.2.refs_0_.refs_4_.grad_in), channel_id=1, source_target_pairs={{0,1},{1,0},{2,3},{3,2},{4,5},{5,4},{6,7},{7,6},{8,9},{9,8},{10,11... | collective-permute-start | bytes 3145736 | tf_op jit(solution)/shard_map/ppermute | solution.py:799
  426.0 26.5 %collective-permute-start.61 = (bf16[304,512]{1,0:T(8,128)(2,1)S(1)}, bf16[304,512]{1,0:T(8,128)(2,1)S(1)}, u32[]{:S(2)}, u32[]{:S(2)}) collective-permute-start(bf16[304,512]{1,0:T(8,128)(2,1)S(1)} %maximum_maximum_fusion.1), channel_id=1, source_target_pairs={{2,4},{3,5},{4,2},{5,3},{10,12},{11,13},{12,10},{13,11},{18,20},{1... | collective-permute-start | bytes 933896 | tf_op jit(solution)/shard_map/ppermute | solution.py:799
  457.1 32.1 %collective-permute-start.63 = (bf16[256,2048]{1,0:T(8,128)(2,1)}, bf16[256,2048]{1,0:T(8,128)(2,1)}, u32[]{:S(2)}, u32[]{:S(2)}) collective-permute-start(bf16[256,2048]{1,0:T(8,128)(2,1)} %add_convert_fusion.2), channel_id=1, source_target_pairs={{0,1},{1,0},{2,3},{3,2},{4,5},{5,4},{6,7},{7,6},{8,9},{9,8},{10,11... | collective-permute-start | bytes 3145736 | tf_op jit(solution)/shard_map/ppermute | solution.py:799
  492.7 17.3 %collective-permute-start.64 = (bf16[128,2048]{1,0:T(8,128)(2,1)}, bf16[128,2048]{1,0:T(8,128)(2,1)}, u32[]{:S(2)}, u32[]{:S(2)}) collective-permute-start(bf16[128,2048]{1,0:T(8,128)(2,1)} %get-tuple-element.324), channel_id=1, source_target_pairs={{2,4},{3,5},{4,2},{5,3},{10,12},{11,13},{12,10},{13,11},{18,20},{1... | collective-permute-start | bytes 1572872 | tf_op jit(solution)/shard_map/ppermute | solution.py:799
  510.0 18.9 %collective-permute-start.67 = (bf16[256,2048]{1,0:T(8,128)(2,1)}, bf16[256,2048]{1,0:T(8,128)(2,1)S(1)}, u32[]{:S(2)}, u32[]{:S(2)}) collective-permute-start(bf16[256,2048]{1,0:T(8,128)(2,1)} %get-tuple-element.333), channel_id=1, source_target_pairs={{0,4},{1,5},{2,6},{3,7},{4,0},{5,1},{6,2},{7,3},{8,12},{9,13},{10,... | collective-permute-start | bytes 3145736 | tf_op jit(solution)/shard_map/ppermute | solution.py:799
  510.2 19.2 %collective-permute-start.66 = (bf16[128,2048]{1,0:T(8,128)(2,1)S(1)}, bf16[128,2048]{1,0:T(8,128)(2,1)S(1)}, u32[]{:S(2)}, u32[]{:S(2)}) collective-permute-start(bf16[128,2048]{1,0:T(8,128)(2,1)S(1)} %copy-done.110), channel_id=1, source_target_pairs={{2,4},{3,5},{4,2},{5,3},{10,12},{11,13},{12,10},{13,11},{18,20},{1... | collective-permute-start | bytes 1572872 | tf_op jit(solution)/shard_map/ppermute | solution.py:799
  530.1 21.1 %collective-permute-start.69 = (bf16[256,2048]{1,0:T(8,128)(2,1)S(1)}, bf16[256,2048]{1,0:T(8,128)(2,1)S(1)}, u32[]{:S(2)}, u32[]{:S(2)}) collective-permute-start(bf16[256,2048]{1,0:T(8,128)(2,1)S(1)} %copy-done.100), channel_id=1, source_target_pairs={{0,4},{1,5},{2,6},{3,7},{4,0},{5,1},{6,2},{7,3},{8,12},{9,13},{10,... | collective-permute-start | bytes 3145736 | tf_op jit(solution)/shard_map/ppermute | solution.py:799
  575.0 28.6 %collective-permute-start.78 = (bf16[256,2048]{1,0:T(8,128)(2,1)}, bf16[256,2048]{1,0:T(8,128)(2,1)}, u32[]{:S(2)}, u32[]{:S(2)}) collective-permute-start(bf16[256,2048]{1,0:T(8,128)(2,1)} %get-tuple-element.354), channel_id=1, source_target_pairs={{2,4},{3,5},{4,2},{5,3},{10,12},{11,13},{12,10},{13,11},{18,20},{1... | collective-permute-start | bytes 3145736 | tf_op jit(solution)/shard_map/ppermute | solution.py:799
  (164 other events, 3017.7 us)
Sparse Core Ops, SparseCore 0:
  496.3 29.0 all-gather.2

commit v3 on v2

--- a/solution.py
+++ b/solution.py
@@ -455,15 +455,22 @@
     subs = weights[0][0].shape[0]
     width = low_in.shape[1]
     pieces = [piece for weight in weights for piece in weight]
-    depth = sum(act.shape[1] for act in acts)
     count = len(blocks)
+    chosen = []
+    for at in blocks:
+        for act in acts:
+            if isinstance(act, tuple):
+                per = act[0].shape[0] // size
+                chosen.append((act[at // per], at % per))
+            else:
+                chosen.append((act, at))
+    depth = sum(act.shape[1] for act, _ in chosen) // count
     return pl.pallas_call(
         partial(unfold_kernel, (count, len(acts), len(weights))),
         grid=(subs,),
         in_specs=[smem(), full(low_in.shape)]
         + [pl.BlockSpec((low.shape[0], size), lambda s, at=at: (0, at)) for at in blocks]
-        + [pl.BlockSpec((size, act.shape[1]), lambda s, at=at: (at, 0))
-           for at in blocks for act in acts]
+        + [pl.BlockSpec((size, act.shape[1]), lambda s, at=at: (at, 0)) for act, at in chosen]
         + [pl.BlockSpec((1,) + w.shape[1:], lambda s: (s, 0, 0)) for w in pieces],
         out_specs=[full((size, width))] * count,
         out_shape=[far((size, width), BF)] * count,
@@ -472,11 +479,11 @@
             2 * count * size * depth * width, 2 * depth * width + 4 * count * size * depth
         ),
         name="unfold",
-    )(ids, low_in, *[low] * count, *in_hbm(*list(acts) * count, *pieces))
+    )(ids, low_in, *[low] * count, *in_hbm(*[act for act, _ in chosen], *pieces))
 
 
 def gate_back_kernel(parts, ids, low_back, low_in, gate, nrm, inverse, hold, low_gate, low_out,
-                     *refs):
+                     begin_in, begin_gate, *refs):
     act, pieces = refs[:parts], refs[parts:-6]
     dgate, dret, low, dlow, grad_in, grad_gate = refs[-6:]
 
@@ -497,40 +504,50 @@
     along = jnp.mean(grad * normed, axis=1, keepdims=True)
     dgate[...] = back_gate
     dret[...] = (inverse[0, :, :1] * (grad - mean - normed * along)).astype(BF)
-    grad_in[...] = dot(low[...], hold[...]).astype(BF)
-    grad_gate[...] = dot(low_gate[...], back_gate).astype(BF)
+    grad_in[...] = begin_in[...] + dot(low[...], hold[...])
+    grad_gate[...] = begin_gate[...] + dot(low_gate[...], back_gate)
     dlow[...] += dot_nt(low_out[...], back_gate)
 
 
-def gate_back(ids, act, low_back, low_in, gate, nrm, inverse, hold, low_gate, low_out, pieces):
-    rows, depth = row_count(act), act[0].shape[1]
+def gate_back(ids, act, low_back, low_in, gate, nrm, inverse, hold, low_gate, low_out, pieces,
+              half, begin_in, begin_gate):
+    if len(act) > 1:
+        act = act[len(act) // 2 * half:len(act) // 2 * (half + 1)]
+    rows, depth = gate.shape[0] // 2, act[0].shape[1]
     width = gate.shape[1]
     block = VALUE_DIM
     ranks = low_back.shape[0]
+    if len(act) == 1:
+        acts = [pl.BlockSpec((rows, depth), lambda n: (half, 0))]
+    else:
+        acts = whole(act)
     column = lambda height: pl.BlockSpec((height, block), lambda n: (0, n))
+    place = pl.BlockSpec((rows, block), lambda n: (half, n))
     return pl.pallas_call(
         partial(gate_back_kernel, len(act)),
         grid=(width // block,),
-        in_specs=[smem(), full(low_back.shape), column(ranks), column(rows),
-                  column(rows), pl.BlockSpec((1, rows, 128), lambda n: (n, 0, 0)), column(rows),
-                  pl.BlockSpec((ranks, rows), lambda n: (low_gate.shape[0] // ranks - 1, 0)),
-                  column(low_out.shape[0])]
-        + whole(act) + [pl.BlockSpec((w.shape[0], block, w.shape[2]), lambda n: (0, n, 0)) for w in pieces],
+        in_specs=[smem(), full(low_back.shape), column(ranks), place, place,
+                  pl.BlockSpec((1, rows, 128), lambda n: (n, half, 0)), place,
+                  pl.BlockSpec((ranks, rows), lambda n: (low_gate.shape[0] // ranks - 1, half)),
+                  column(low_out.shape[0]), column(ranks), column(ranks)]
+        + acts + [pl.BlockSpec((w.shape[0], block, w.shape[2]), lambda n: (0, n, 0))
+                  for w in pieces],
         out_specs=[column(rows), column(rows), full((ranks, rows)),
                    full((low_out.shape[0], rows)), column(ranks), column(ranks)],
         out_shape=[jax.ShapeDtypeStruct((rows, width), BF)] * 2
         + [jax.ShapeDtypeStruct((ranks, rows), BF),
            jax.ShapeDtypeStruct((low_out.shape[0], rows), F32),
-           jax.ShapeDtypeStruct((ranks, width), BF), jax.ShapeDtypeStruct((ranks, width), BF)],
+           jax.ShapeDtypeStruct((ranks, width), F32), jax.ShapeDtypeStruct((ranks, width), F32)],
         compiler_params=params(56),
         cost_estimate=estimate(2 * rows * depth * width, 2 * depth * width + 16 * rows * width),
         name="gate_back",
-    )(ids, low_back, low_in, *in_hbm(gate, nrm, inverse, hold), low_gate, low_out, *act, *pieces)
+    )(ids, low_back, low_in, *in_hbm(gate, nrm, inverse, hold), low_gate, low_out, begin_in,
+      begin_gate, *act, *pieces)
 
 
 def retention_back_kernel(spots, rates, seg_col, seg_row, cosine, sine_table, low, begin, q_out,
-                          k_out, v_out, q, k, v, dret, dq, dk, dv, dlow, grad_q, grad_k, grad_v,
-                          sums):
+                          k_out, v_out, q, k, v, dret0, dret1, dq, dk, dv, dlow, grad_q, grad_k,
+                          grad_v, sums):
     head = pl.program_id(0)
     rate = rates[head]
     count = spots.shape[0]
@@ -553,7 +570,9 @@
         value_sum = jnp.zeros((size, VALUE_DIM), F32)
         for i in range(j, count):
             here = aligned(spots[i] * size, size)
-            query, back = q[here, :], dret[here, :]
+            query = q[here, :]
+            within = aligned(spots[i] % (count // 2) * size, size)
+            back = jnp.where(spots[i] < count // 2, dret0[within, :], dret1[within, :])
             row_factor = jnp.exp(rate * ((i - j) * size - down))
             alive = seg_there == seg_row[:, i * size:(i + 1) * size]
             if i == j:
@@ -583,7 +602,7 @@
 
 
 def retention_back(spots, rates, seg_col, seg_row, cosine, sine_table, low, begin, qk_out, v_out,
-                   qk, v, dret):
+                   qk, v, dret0, dret1):
     rows = qk.shape[0]
     heads = v.shape[1] // VALUE_DIM
     ranks = low.shape[0]
@@ -597,7 +616,7 @@
         in_specs=[smem(), smem(), full(seg_col.shape), full(seg_row.shape), full(cosine.shape),
                   full(cosine.shape), full(low.shape), full(begin.shape), key(ranks),
                   later(ranks), value(ranks),
-                  key(rows), later(rows), value(rows), value(rows)],
+                  key(rows), later(rows), value(rows), value(rows // 2), value(rows // 2)],
         out_specs=[key(rows), key(rows), value(rows), full((ranks, rows)), key(RANK), key(RANK),
                    value(RANK)],
         out_shape=[jax.ShapeDtypeStruct((rows, keys), BF), jax.ShapeDtypeStruct((rows, keys), BF),
@@ -609,7 +628,7 @@
         cost_estimate=estimate(2 * rows * rows * 1792 * heads, 30 << 20),
         name="retention_back",
     )(spots, rates, seg_col, seg_row,
-      cosine, sine_table, low, begin, qk_out, qk_out, v_out, qk, qk, v, dret)
+      cosine, sine_table, low, begin, qk_out, qk_out, v_out, qk, qk, v, dret0, dret1)
 
 
 def share_kernel(heights, low, *refs):
@@ -734,7 +753,7 @@
         steps.ready(line, steps.tables(line, line)[0])
         a = self.gather(steps.norm(tokens))
         dy = self.gather(cotangent)
-        projected = steps.project(a, *blocks[:2])
+        projected = steps.project(a, blocks[1], blocks[0])
         mixed = steps.mix(a, *projected, blocks[2])
         *rows, low = steps.fold(mixed[0], blocks[3])
         middle, b = steps.join(tokens, self.scatter(rows))
@@ -750,9 +769,10 @@
         dz = self.gather(steps.dz(self.scatter(steps.unfold_mlp(256, (0, 1, 2, 3)))))
         output = steps.output(self.scatter(steps.fold_down(steps.hid)))
         early = lax.all_gather(steps.early(self.group_sum(steps.lows)), "dp")
-        early = steps.place_early(early)
-        steps.gate_back(dz)
-        steps.retention_back(steps.dret)
+        early = steps.place_early([early], jnp.arange(self.ndp, dtype=jnp.int32))
+        steps.gate_back(dz, 0)
+        steps.gate_back(dz, 1)
+        steps.retention_back(*steps.dret)
         late = lax.all_gather(steps.late(self.group_sum(steps.late_lows()), dz), "dp")
         late = steps.place_late([late], jnp.arange(self.ndp, dtype=jnp.int32))
         parts = self.scatter(steps.unfold_attn(256, (0, 1, 2, 3)))
@@ -900,7 +920,7 @@
         grad = self.mine(cotangent, grad)
         def attend(near, beyond, own, across, *weights):
             a = [own, near, across, beyond]
-            return a, steps.project(a, *weights)
+            return a, steps.project(a, *weights[::-1])
 
         moves = [(a, core), (across, core), hops["x"](3), hops["y"](3), over(4)]
         moved, _, (a, projected) = self.round(
@@ -949,6 +969,12 @@
         size = x.shape[1] // 2
         other = jnp.concatenate([other[:, size:], other[:, :size]], axis=1)
         return (x.astype(F32) + other.astype(F32)).astype(BF)
+
+    def both_halves(self, halves, one, two):
+        return jnp.concatenate(
+            [jnp.concatenate([halves[0], one]),
+             jnp.concatenate([halves[1][:1], two[:1], halves[1][1:], two[1:]])], axis=1
+        )
 
     def backward(self, steps):
         pair = lambda d, t: (d, t ^ 1)
@@ -977,61 +1003,73 @@
         own_out, near_out, far_out, beyond_out = folded
         dz = steps.dz((own, near, far))
 
-        (_, across, moved, dz_near, near_out), _, far_out = self.round(
-            [(beyond_out, core), (dz, pair), (early, swap), (dz, core), (near_out, core)],
-            self.add, (far_out,), feed=1
-        )
-        early = lax.all_gather(self.mine(early, moved), "dp")
+
+        def beside(beyond, dz_near, far, dz):
+            return self.add(far, beyond), steps.gate_back([dz, dz_near, dz, dz], 0)
+
+        (_, dz_near, across, moved, near_out), _, (far_out, dret0) = self.round(
+            [(beyond_out, core), (dz, core), (dz, pair), (early, swap), (near_out, core)],
+            beside, (far_out, dz), feed=2
+        )
+        early = self.mine(early, moved)
+        size = early.shape[0] // 2
+        early = [early[:size][None], early[size:][None]]
         (dz_beyond,), _, _ = self.round([(across, core)])
+        (one, two, far_out), _, dret1 = self.round(
+            [(early[0], by_one), (early[1], by_two)],
+            lambda across, beyond: steps.gate_back([across, across, across, beyond], 1),
+            (across, dz_beyond), slow=[(far_out, pair)]
+        )
+        early = [jnp.concatenate([early[0], one]), jnp.concatenate([early[1], two])]
+        (one, two), _, dpv = self.round(
+            [(early[0], by_two), (early[1], by_one)], steps.retention_back, (dret0, dret1)
+        )
         dz = [dz, dz_near, across, dz_beyond]
-        (far_out,), _, dret = self.round([], steps.gate_back, (dz,), slow=[(far_out, pair)])
-        _, _, dpv = self.round([], steps.retention_back, (dret,))
-        output = steps.output((own_out, near_out, far_out))
-
-        (dlow, out0), _, (far, beyond) = self.round(
-            [(steps.late_lows().astype(BF), core), (output[:half], swap)],
-            lambda dpv: steps.unfold_attn(256, (2, 3), dpv), (dpv,)
+        early = early, one, two
+
+        (dlow,), _, output = self.round(
+            [(steps.late_lows().astype(BF), core)], lambda *parts: steps.output(parts),
+            (own_out, near_out, far_out)
         )
         dlow = self.core_sum(steps.late_lows(), dlow)
-        def beside(other, dpv, dlow):
-            near, = steps.unfold_attn(256, (1,), dpv)
-            return near, steps.late(self.pair_sum(dlow, other), dz)
-
-        (_, beyond, out1), _, (near, late) = self.round(
-            [(dlow, pair), (beyond, core), (output[half:], swap)], beside, (dpv, dlow), feed=1
-        )
-        far = self.add(far, beyond)
-        (far0, near, moved), _, (own,) = self.round(
-            [(far[:half], pair), (near, core), (late, swap)],
-            lambda dpv: steps.unfold_attn(256, (0,), dpv), (dpv,)
+        (other, moved_out), _, ((near, far, beyond), early) = self.round(
+            [(dlow, pair), (output, swap)],
+            lambda dpv, early: (steps.unfold_attn(256, (1, 2, 3), dpv), self.both_halves(*early)),
+            (dpv, early)
+        )
+        (beyond, near), _, late = self.round(
+            [(beyond, core), (near, core)],
+            lambda dlow, other: steps.late(self.pair_sum(dlow, other), dz), (dlow, other)
+        )
+        (moved,), _, ((own,), far) = self.round(
+            [(late, swap)],
+            lambda dpv, far, beyond: (steps.unfold_attn(256, (0,), dpv), self.add(far, beyond)),
+            (dpv, far, beyond)
         )
         late = self.mine(late, moved)
         size = late.shape[0] // 2
         late = [late[:size][None], late[size:][None]]
-        three = half + half // 2
+        (one, two, far0), _, _ = self.round(
+            [(late[0], by_one), (late[1], by_two), (far[:half], pair)]
+        )
+        late = [jnp.concatenate([late[0], one]), jnp.concatenate([late[1], two])]
         (one, two, far1), _, _ = self.round(
-            [(late[0], by_one), (late[1], by_two), (far[half:three], pair)]
-        )
-        late = [jnp.concatenate([late[0], one]), jnp.concatenate([late[1], two])]
-        (one, two, far2), _, _ = self.round(
-            [(late[0], by_two), (late[1], by_one), (far[three:], pair)]
-        )
-        dx, low = steps.dx((own, near, jnp.concatenate([far0, far1, far2])))
-        late = jnp.concatenate(
-            [jnp.concatenate([late[0], one]),
-             jnp.concatenate([late[1][:1], two[:1], late[1][1:], two[1:]])], axis=1
-        )
+            [(late[0], by_two), (late[1], by_one), (far[half:], pair)]
+        )
+        dx, low = steps.dx((own, near, jnp.concatenate([far0, far1])))
+        late = self.both_halves(late, one, two)
         apart = jnp.arange(self.ndp, dtype=jnp.int32) ^ lax.axis_index("dp")
 
-        def put(other, late, early):
-            early = steps.place_early(early)
-            return early, steps.place_late([late, other], apart // 2 + 4 * (apart % 2))
-
-        (_, moved), _, (early, late) = self.round(
-            [(late, core), (low, swap)], put, (late, early), feed=1
+        def put(early_other, other, early, late):
+            at = apart // 2 + 4 * (apart % 2)
+            early = steps.place_early([early, early_other], at)
+            return early, steps.place_late([late, other], at)
+
+        (_, _, moved), _, (early, late) = self.round(
+            [(early, core), (late, core), (low, swap)], put, (early, late), feed=2
         )
         moved, early, late = lax.optimization_barrier((moved, early, late))
-        return (self.mine(output, jnp.concatenate([out0, out1])),
+        return (self.mine(output, moved_out),
                 self.mine(dx, moved.astype(F32)), early, late)
 
 
@@ -1144,9 +1182,9 @@
             return hidden_grad(ids, dy, self.down_back, self.down_in, w_d)
 
     steps = Steps()
-    ((w_qk, w_v, w_g, w_o, w_d, w_mg, w_mu), x, a, grad, dy, (qk, v, low_a),
+    ((w_v, w_qk, w_g, w_o, w_d, w_mg, w_mu), x, a, grad, dy, (qk, v, low_a),
      (o, nrm, inverse, gate), low_o, middle, b, (dhid, low_dy)) = links.forward(
-        [jnp.concatenate([weight_query, weight_key], axis=1), weight_value, weight_gate,
+        [weight_value, jnp.concatenate([weight_query, weight_key], axis=1), weight_gate,
          weight_out, weight_mlp_down, weight_mlp_gate, weight_mlp_up],
         tokens[0], cotangent[0], own_line, steps,
     )
@@ -1194,20 +1232,26 @@
                  halves(jnp.concatenate([self.grad_hidden, self.grad_down])), mark]
             )
 
-        def gate_back(self, dz):
-            (self.dpg, self.dret, _, self.dlow, self.grad_out_in, self.grad_gate) = gate_back(
-                ids, dz, out_back, out_in, gate, nrm, inverse, o, low_a, g_out, w_o
+        def gate_back(self, dz, half):
+            if half == 0:
+                self.grad_out_in = self.grad_gate = jnp.zeros((RANK, wide), F32)
+                self.dpg, self.dret, self.low_parts = (), (), ()
+            dpg, dret, _, dlow, self.grad_out_in, self.grad_gate = gate_back(
+                ids, dz, out_back, out_in, gate, nrm, inverse, o, low_a, g_out, w_o, half,
+                self.grad_out_in, self.grad_gate
             )
-            return self.dret
+            self.dpg, self.dret = self.dpg + (dpg,), self.dret + (dret,)
+            self.low_parts = self.low_parts + (dlow,)
+            return dret
 
         def late_lows(self):
             return jnp.concatenate([self.dlow, low_o])
 
-        def retention_back(self, dret):
+        def retention_back(self, *dret):
             (self.dpq, self.dpk, self.dpv, self.dlow, self.grad_q, self.grad_k,
              self.grad_v) = retention_back(
-                spots, rates, seg_col, seg_row, cosine, sine_table, low_a, self.dlow, qk_out,
-                v_out, qk, v, dret
+                spots, rates, seg_col, seg_row, cosine, sine_table, low_a,
+                jnp.concatenate(self.low_parts, axis=1), qk_out, v_out, qk, v, *dret
             )
             return self.dpv
 
@@ -1216,7 +1260,7 @@
                 [share(lows, span, ((4 * RANK, a), (RANK, dz))),
                  halves(jnp.concatenate(
                      [jnp.concatenate([self.grad_q, self.grad_k], axis=1), self.grad_v,
-                      self.grad_gate, self.grad_out_in]
+                      self.grad_gate.astype(BF), self.grad_out_in.astype(BF)]
                  ))]
             )
 
@@ -1228,32 +1272,33 @@
         def dx(self, parts):
             return rms_back(x, self.dmid, parts, gain_attn, (F32, BF))
 
-        def place_early(self, early):
-            sequences = early.shape[0]
+        def place_early(self, arrays, at):
+            sequences = sum(array.shape[0] for array in arrays)
             shares = nt * self.early_height
-            all_ids = early[:, shares + 6 * RANK, 0].astype(jnp.int32)
+            marks = [array[:, shares + 6 * RANK, 0] for array in arrays]
+            all_ids = jnp.concatenate(marks).astype(jnp.int32)[at]
             numbers = jnp.arange(adapters, dtype=jnp.int32)
             chosen = numbers[:, None] == all_ids[None, :]
             if sequences == adapters:
                 self.order = jnp.sum(jnp.where(chosen, numbers[None, :], 0), axis=1)
-                self.total = lambda y: y
+                self.total = None
             else:
                 self.order = numbers
                 self.total = lambda y: jnp.einsum(
                     "es,sij->eij", chosen.astype(BF), y, preferred_element_type=F32
                 )
+                arrays, at = [self.total(arrays[0])], numbers
             pitch = self.early_height
             return place(
-                self.order, [self.total(early)],
+                at[self.order], arrays,
                 ((0, RANK, "shares", pitch), (RANK, 2 * RANK, "shares", pitch),
                  (shares, 2 * RANK, "halves", 3 * RANK),
                  (shares + 2 * RANK, RANK, "halves", 3 * RANK)), nt
             )
 
         def place_late(self, arrays, at):
-            if arrays[0].shape[0] * len(arrays) != adapters:
-                arrays = [self.total(arrays[0])]
-                at = self.order
+            if self.total is not None:
+                arrays, at = [self.total(arrays[0])], self.order
             pitch = self.late_height
             shares = nt * pitch
             return place(

time: 623 us -> 600 us (0.963)
  between operations: 23.9 us -> 10.2 us
  waiting for transfers between devices: 243 us -> 235 us
    ppermute x72 -> x75, waiting for transfers between devices: 242 us -> 235 us  [send(): lax.ppermute(x, ('dp', 'tensor'), self.pairs(place))]
    pallas_call x5 -> x4, Pallas kernels: 49 us -> 44.9 us  [unfold(): pl.pallas_call(partial(unfold_kernel, (count, len(acts), len(weights))),...]
    pallas_call x1 -> x2, Pallas kernels: 15.3 us -> 17.8 us  [gate_back(): pl.pallas_call(partial(gate_back_kernel, len(act)), grid=(width // block,...]
    ppermute x72 -> x75, starting transfers between devices: 75.1 us -> 73 us  [send(): lax.ppermute(x, ('dp', 'tensor'), self.pairs(place))]
    unnamed x272 -> x244, local copies, waits for them, and re-layouts: 15.2 us -> 14.9 us
  transfers between devices with their start and end apart: 81 -> 83, of which waited for: 42 -> 40; matrix products, arithmetic and copies ran while one was open for 9% -> 10% of each run, Pallas kernels for 28% -> 28%
where the time goes in v3:
time: 600 us; the launch traced here: 591 us
  waiting for transfers between devices  235 us (39%)
  Pallas kernels  192 us (32%)
  starting transfers between devices  80.3 us (13%)
  other arithmetic  46.3 us (8%)
  local copies, waits for them, and re-layouts  27.5 us (5%)
  between operations  10.2 us (2%)
    ppermute x75, waiting for transfers between devices, send(): lax.ppermute(x, ('dp', 'tensor'), self.pairs(place))  235 us
    ppermute x75, starting transfers between devices, send(): lax.ppermute(x, ('dp', 'tensor'), self.pairs(place))  73 us
    pallas_call x4, Pallas kernels, unfold(): pl.pallas_call(partial(unfold_kernel, (count, len(acts), len(weights))),...  44.9 us
    pallas_call x2, Pallas kernels, project(): pl.pallas_call(partial(project_kernel, (len(act), len(weights[0]), length...  27.3 us
    pallas_call x2, Pallas kernels, fold(): pl.pallas_call(fold_kernel, grid=(subs,), in_specs=[smem(), full(act.shap...  21 us
    pallas_call x1, Pallas kernels, mlp(): pl.pallas_call(partial(mlp_kernel, len(act), len(gate_pieces)), grid=(wid...  18.4 us
    pallas_call x2, Pallas kernels, gate_back(): pl.pallas_call(partial(gate_back_kernel, len(act)), grid=(width // block,...  17.8 us
    pallas_call x2, Pallas kernels, place(): pl.pallas_call(partial(place_kernel, layout, len(arrays)), grid_spec=pltp...  15.3 us
  transfers between devices with their start and end apart: 83, of which 40 were waited for; matrix products, arithmetic and copies ran while one was open for 10% of the time, Pallas kernels for 28%

profile of v3, /device:TPU:1, one launch (start us, length us, event | category | flops | bytes accessed | tf_op | source)
XLA Modules:
  0.0 591.3 jit_solution(17708719400267085242)
XLA Ops:
  8.1 5.7 collective-permute-start.6
  26.1 9.1 %collective-permute-done.2 = bf16[2,256,1024]{2,1,0:T(8,128)(2,1)} collective-permute-done((bf16[2,256,1024]{2,1,0:T(8,128)(2,1)}, bf16[2,256,1024]{2,1,0:T(8,128)(2,1)}, u32[]{:S(2)}, u32[]{:S(2)}) %collective-permute-start.2) | collective-permute-done | bytes 1048608 | tf_op jit(solution)/shard_map/ppermute | solution.py:819
  51.8 8.4 %collective-permute-done.9 = bf16[2,256,1024]{2,1,0:T(8,128)(2,1)} collective-permute-done((bf16[2,256,1024]{2,1,0:T(8,128)(2,1)}, bf16[2,256,1024]{2,1,0:T(8,128)(2,1)}, u32[]{:S(2)}, u32[]{:S(2)}) %collective-permute-start.9) | collective-permute-done | bytes 1048608 | tf_op jit(solution)/shard_map/ppermute | solution.py:819
  68.8 16.2 %collective-permute-done.14.refs_7_.refs_16_.refs_6_ = bf16[2,256,1024]{2,1,0:T(8,128)(2,1)S(1)} collective-permute-done((bf16[2,256,1024]{2,1,0:T(8,128)(2,1)S(1)}, bf16[2,256,1024]{2,1,0:T(8,128)(2,1)S(1)}, u32[]{:S(2)}, u32[]{:S(2)}) %collective-permute-start.14) | collective-permute-done | bytes 1048608 | tf_op jit(solution)/shard_map/ppermute | solution.py:819
  88.7 28.6 %collective-permute-done.12 = bf16[256,2048]{1,0:T(8,128)(2,1)S(1)} collective-permute-done((bf16[256,2048]{1,0:T(8,128)(2,1)S(1)}, bf16[256,2048]{1,0:T(8,128)(2,1)S(1)}, u32[]{:S(2)}, u32[]{:S(2)}) %collective-permute-start.12) | collective-permute-done | bytes 1048608 | tf_op jit(solution)/shard_map/ppermute | solution.py:819
  123.9 2.8 fusion
  128.1 4.2 collective-permute-start.23
  132.3 3.9 collective-permute-done.20.refs_5_.refs_24_.refs_14_
  142.2 30.3 %collective-permute-done.19 = bf16[2,1024,256]{2,1,0:T(8,128)(2,1)} collective-permute-done((bf16[2,1024,256]{2,1,0:T(8,128)(2,1)}, bf16[2,1024,256]{2,1,0:T(8,128)(2,1)}, u32[]{:S(2)}, u32[]{:S(2)}) %collective-permute-start.19) | collective-permute-done | bytes 1048608 | tf_op jit(solution)/shard_map/ppermute | solution.py:819
  183.4 17.8 %project.2 = (bf16[1024,1024]{1,0:T(8,128)(2,1)}, bf16[1024,1024]{1,0:T(8,128)(2,1)}, bf16[64,1024]{1,0:T(8,128)(2,1)S(1)}) custom-call(s32[8]{0:T(128)S(1)} %xor.51.ids, s32[4]{0:T(128)S(1)} %broadcast_xor_fusion.chunks, bf16[64,2048]{1,0:T(8,128)(2,1)S(1)} %dynamic-slice_bitcast_fusion.low_in, bf16[64,2048]{1,0:T(8,128)(2,1)S(1)} %maximum_maximum_fusion.3.low_out, ...), custom_call_target="tpu_custom_call" | custom-call | flops 1 | bytes 1 | tf_op jit(solution)/shard_map/project/pallas_call | solution.py:190
  201.2 3.1 collective-permute-done.25
  212.7 9.5 %project.3.gate = bf16[1024,1024]{1,0:T(8,128)(2,1)} custom-call(s32[8]{0:T(128)S(1)} %xor.51.ids, s32[4]{0:T(128)S(1)} %broadcast_xor_fusion.chunks, bf16[64,1024]{1,0:T(8,128)(2,1)S(1)} %get-tuple-element.252.low_in.low_gate.low, bf16[64,1024]{1,0:T(8,128)(2,1)S(1)} %concatenate.124.low_out, bf16[256,2048]{1,0:T(8,128)(2,1)} %norm_rows.1.refs_2_.refs_0_, ...), custom_call_target="tpu_custom_call" | custom-call | flops 1 | bytes 1 | tf_op jit(solution)/shard_map/project/pallas_call | solution.py:190
  222.3 8.8 %retention.1 = (bf16[1024,1024]{1,0:T(8,128)(2,1)}, bf16[1024,1024]{1,0:T(8,128)(2,1)}, f32[2,1024,128]{2,1,0:T(8,128)}) custom-call(s32[4]{0:T(128)S(1)} %fusion.5.spots, f32[2]{0:T(128)S(1)} %copy-done.59, s32[1024,1]{1,0:T(8,128)S(1)} %copy-done.20, s32[1,1024]{1,0:T(1,128)S(1)} %get-tuple-element.469.seg_row, bf16[1024,1024]{1,0:T(8,128)(2,1)S(1)} %copy-done.2, ...), custom_call_target="tpu_custom_call" | custom-call | flops 1 | bytes 1 | tf_op jit(solution)/shard_map/retention/pallas_call | solution.py:242
  239.3 10.4 %fold.2 = (bf16[256,2048]{1,0:T(8,128)(2,1)}, bf16[256,2048]{1,0:T(8,128)(2,1)}, bf16[256,2048]{1,0:T(8,128)(2,1)}, bf16[256,2048]{1,0:T(8,128)(2,1)}, f32[16,1024]{1,0:T(8,128)S(1)}) custom-call(s32[8]{0:T(128)S(1)} %xor.51.ids, bf16[1024,1024]{1,0:T(8,128)(2,1)} %get-tuple-element.267.act.hold, bf16[16,1024]{1,0:T(8,128)(2,1)S(1)} %copy-done.47, ...), custom_call_target="tpu_custom_call" | custom-call | flops 1 | bytes 1 | tf_op jit(solution)/shard_map/fold/pallas_call | solution.py:285
  249.7 5.1 collective-permute-done.37
  254.8 4.9 collective-permute-done.34.refs_6_.refs_2_
  259.7 5.1 collective-permute-done.36
  274.7 20.4 %collective-permute-done.40.part2 = bf16[256,2048]{1,0:T(8,128)(2,1)S(1)} collective-permute-done((bf16[256,2048]{1,0:T(8,128)(2,1)S(1)}, bf16[256,2048]{1,0:T(8,128)(2,1)S(1)}, u32[]{:S(2)}, u32[]{:S(2)}) %collective-permute-start.40) | collective-permute-done | bytes 1048608 | tf_op jit(solution)/shard_map/ppermute | solution.py:819
  301.7 19.1 %collective-permute-done.43.refs_9_.refs_14_.refs_8_ = bf16[2,256,1024]{2,1,0:T(8,128)(2,1)S(1)} collective-permute-done((bf16[2,256,1024]{2,1,0:T(8,128)(2,1)S(1)}, bf16[2,256,1024]{2,1,0:T(8,128)(2,1)S(1)}, u32[]{:S(2)}, u32[]{:S(2)}) %collective-permute-start.43) | collective-permute-done | bytes 1048608 | tf_op jit(solution)/shard_map/ppermute | solution.py:819
  321.4 3.7 collective-permute-done.47.refs_10_.refs_15_.refs_9_
  330.1 8.4 %hidden_grad.1 = (f32[1024,1024]{1,0:T(8,128)S(1)}, bf16[16,1024]{1,0:T(8,128)(2,1)S(1)}) custom-call(s32[8]{0:T(128)S(1)} %xor.51.ids, bf16[16,2048]{1,0:T(8,128)(2,1)S(1)} %dynamic-slice_bitcast_fusion.2.low_back.low_out, bf16[16,1024]{1,0:T(8,128)(2,1)S(1)} %copy-done.48, bf16[256,2048]{1,0:T(8,128)(2,1)S(1)} %broadcast_select_fusion.7.refs_0_.grad_in, ...), custom_call_target="tpu_custom_call" | custom-call | flops 1 | bytes 1 | tf_op jit(solution)/shard_map/hidden_grad/pallas_call | solution.py:360
  340.7 10.1 %collective-permute-done.50.refs_7_.refs_12_.refs_6_ = bf16[2,256,1024]{2,1,0:T(8,128)(2,1)S(1)} collective-permute-done((bf16[2,256,1024]{2,1,0:T(8,128)(2,1)S(1)}, bf16[2,256,1024]{2,1,0:T(8,128)(2,1)S(1)}, u32[]{:S(2)}, u32[]{:S(2)}) %collective-permute-start.50) | collective-permute-done | bytes 1048608 | tf_op jit(solution)/shard_map/ppermute | solution.py:819
  351.7 18.4 %mlp.1 = (bf16[1024,1024]{1,0:T(8,128)(2,1)}, bf16[1024,1024]{1,0:T(8,128)(2,1)}, bf16[1024,1024]{1,0:T(8,128)(2,1)}, bf16[32,1024]{1,0:T(8,128)(2,1)}, f32[48,1...) custom-call(s32[8]{0:T(128)S(1)} %xor.51.ids, ...), custom_call_target="tpu_custom_call" | custom-call | flops 1 | bytes 1 | tf_op jit(solution)/shard_map/mlp/pallas_call | solution.py:413
  371.5 12.8 %unfold.4 = (bf16[256,2048]{1,0:T(8,128)(2,1)}, bf16[256,2048]{1,0:T(8,128)(2,1)}, bf16[256,2048]{1,0:T(8,128)(2,1)}) custom-call(s32[8]{0:T(128)S(1)} %xor.51.ids, bf16[32,2048]{1,0:T(8,128)(2,1)S(1)} %dynamic-slice_bitcast_fusion.1.low_in, f32[32,1024]{1,0:T(8,128)S(1)} %slice.187.refs_0_.refs_1_.refs_2_, f32[32,1024]{1,0:T(8,128)S(1)} %slice.187.refs_0_.refs_1_.refs_2_, ...), custom_call_target="tpu_custom_call" | custom-call | flops 1 | bytes 1 | tf_op jit(solution)/shard_map/unfold/pallas_call | solution.py:468
  385.5 3.0 collective-permute-done.54
  390.9 4.7 share.2
  395.6 6.6 %unfold.5.part0 = bf16[256,2048]{1,0:T(8,128)(2,1)} custom-call(s32[8]{0:T(128)S(1)} %xor.51.ids, bf16[32,2048]{1,0:T(8,128)(2,1)S(1)} %dynamic-slice_bitcast_fusion.1.low_in, f32[32,1024]{1,0:T(8,128)S(1)} %slice.187.refs_0_.refs_1_.refs_2_, bf16[1024,1024]{1,0:T(8,128)(2,1)} %get-tuple-element.308.refs_3_.refs_5_.refs_7_.refs_1_, ...), custom_call_target="tpu_custom_call" | custom-call | flops 1 | bytes 1 | tf_op jit(solution)/shard_map/unfold/pallas_call | solution.py:468
  402.3 10.6 %fold.3 = (bf16[256,2048]{1,0:T(8,128)(2,1)}, bf16[256,2048]{1,0:T(8,128)(2,1)}, bf16[256,2048]{1,0:T(8,128)(2,1)}, bf16[256,2048]{1,0:T(8,128)(2,1)}, f32[16,1024]{1,0:T(8,128)}) custom-call(s32[8]{0:T(128)S(1)} %xor.51.ids, bf16[1024,1024]{1,0:T(8,128)(2,1)} %get-tuple-element.317.act, bf16[16,1024]{1,0:T(8,128)(2,1)S(1)} %copy-done.49, ...), custom_call_target="tpu_custom_call" | custom-call | flops 1 | bytes 1 | tf_op jit(solution)/shard_map/fold/pallas_call | solution.py:285
  413.6 3.5 rms_back.2.refs_0_.refs_4_.grad_in
  420.3 4.9 collective-permute-start.58
  426.3 9.0 %gate_back.2 = (bf16[512,1024]{1,0:T(8,128)(2,1)}, bf16[512,1024]{1,0:T(8,128)(2,1)}, bf16[16,512]{1,0:T(8,128)(2,1)}, f32[64,512]{1,0:T(8,128)}, f32[16,1024]{1,0:T(8,128)}, /*index=5*/f32[16,1024]{1,0:T(8,128)}) custom-call(s32[8]{0:T(128)} %copy-done.50, bf16[16,2048]{1,0:T(8,128)(2,1)} %copy-done.40, bf16[16,1024]{1,0:T(8,128)(2,1)} %get-tuple-element.446.low_in, ...), custom_call_target="tpu_custom_call" | custom-call | flops 1 | bytes 1 | tf_op jit(solution)/shard_map/gate_back/pallas_call | solution.py:526
  437.9 8.1 %collective-permute-done.58 = bf16[304,512]{1,0:T(8,128)(2,1)S(1)} collective-permute-done((bf16[304,512]{1,0:T(8,128)(2,1)S(1)}, bf16[304,512]{1,0:T(8,128)(2,1)S(1)}, u32[]{:S(2)}, u32[]{:S(2)}) %collective-permute-start.58) | collective-permute-done | bytes 311328 | tf_op jit(solution)/shard_map/ppermute | solution.py:819
  455.5 8.8 %gate_back.3 = (bf16[512,1024]{1,0:T(8,128)(2,1)}, bf16[512,1024]{1,0:T(8,128)(2,1)}, bf16[16,512]{1,0:T(8,128)(2,1)}, f32[64,512]{1,0:T(8,128)}, f32[16,1024]{1,0:T(8,128)}, /*index=5*/f32[16,1024]{1,0:T(8,128)}) custom-call(s32[8]{0:T(128)} %copy-done.50, bf16[16,2048]{1,0:T(8,128)(2,1)} %copy-done.40, bf16[16,1024]{1,0:T(8,128)(2,1)} %get-tuple-element.446.low_in, ...), custom_call_target="tpu_custom_call" | custom-call | flops 1 | bytes 1 | tf_op jit(solution)/shard_map/gate_back/pallas_call | solution.py:526
  467.6 12.0 %retention_back.1 = (bf16[1024,512]{1,0:T(8,128)(2,1)S(1)}, bf16[1024,512]{1,0:T(8,128)(2,1)S(1)}, bf16[1024,1024]{1,0:T(8,128)(2,1)}, f32[64,1024]{1,0:T(8,128)...) custom-call(s32[4]{0:T(128)S(1)} %copy-done.58, f32[2]{0:T(128)S(1)} %copy-done.60, ...), custom_call_target="tpu_custom_call" | custom-call | flops 1 | bytes 1 | tf_op jit(solution)/shard_map/retention_back/pallas_call | solution.py:613
  483.4 3.1 collective-permute-start.69
  486.6 17.2 %unfold.6 = (bf16[256,2048]{1,0:T(8,128)(2,1)}, bf16[256,2048]{1,0:T(8,128)(2,1)}, bf16[256,2048]{1,0:T(8,128)(2,1)}) custom-call(s32[8]{0:T(128)S(1)} %copy-done.51, bf16[64,2048]{1,0:T(8,128)(2,1)S(1)} %dynamic-slice_bitcast_fusion.low_in, f32[64,1024]{1,0:T(8,128)S(1)} %get-tuple-element.347.refs_0_.refs_1_.refs_2_, ...), custom_call_target="tpu_custom_call" | custom-call | flops 1 | bytes 1 | tf_op jit(solution)/shard_map/unfold/pallas_call | solution.py:468
  504.1 7.2 %collective-permute-done.69 = bf16[256,2048]{1,0:T(8,128)(2,1)S(1)} collective-permute-done((bf16[256,2048]{1,0:T(8,128)(2,1)S(1)}, bf16[256,2048]{1,0:T(8,128)(2,1)S(1)}, u32[]{:S(2)}, u32[]{:S(2)}) %collective-permute-start.69) | collective-permute-done | bytes 1048608 | tf_op jit(solution)/shard_map/ppermute | solution.py:819
  512.0 4.8 share.3
  519.2 8.3 %unfold.7.part0 = bf16[256,2048]{1,0:T(8,128)(2,1)} custom-call(s32[8]{0:T(128)S(1)} %copy-done.51, bf16[64,2048]{1,0:T(8,128)(2,1)S(1)} %dynamic-slice_bitcast_fusion.low_in, f32[64,1024]{1,0:T(8,128)S(1)} %get-tuple-element.347.refs_0_.refs_1_.refs_2_, bf16[1024,512]{1,0:T(8,128)(2,1)} %copy-done.5, bf16[1024,512]{1,0:T(8,128)(2,1)} %copy-done.6, ...), custom_call_target="tpu_custom_call" | custom-call | flops 1 | bytes 1 | tf_op jit(solution)/shard_map/unfold/pallas_call | solution.py:468
  527.6 3.3 collective-permute-done.73
  532.8 3.6 collective-permute-done.76
  537.2 4.9 collective-permute-done.74
  543.6 9.3 %collective-permute-done.79 = bf16[2,224,512]{2,1,0:T(8,128)(2,1)S(1)} collective-permute-done((bf16[2,224,512]{2,1,0:T(8,128)(2,1)S(1)}, bf16[2,224,512]{2,1,0:T(8,128)(2,1)S(1)}, u32[]{:S(2)}, u32[]{:S(2)}) %collective-permute-start.79) | collective-permute-done | bytes 458784 | tf_op jit(solution)/shard_map/ppermute | solution.py:819
  556.3 2.9 rms_back.3
  567.7 7.0 %place.2 = (f32[8,16,2048]{2,1,0:T(8,128)}, f32[8,32,2048]{2,1,0:T(8,128)}, f32[8,32,1024]{2,1,0:T(8,128)}, f32[8,16,1024]{2,1,0:T(8,128)}) custom-call(s32[9]{0:T(128)S(1)} %pad_add_fusion.order, bf16[4,304,512]{2,1,0:T(8,128)(2,1)} %copy-done.75, bf16[4,304,512]{2,1,0:T(8,128)(2,1)} %copy-done.95), custom_call_target="tpu_custom_call" | custom-call | flops 1 | bytes 1 | tf_op jit(solution)/shard_map/place/pallas_call | solution.py:701
  574.8 8.3 %place.3 = (f32[8,64,2048]{2,1,0:T(8,128)}, f32[8,16,2048]{2,1,0:T(8,128)}, f32[8,2,16,512]{3,2,1,0:T(8,128)}, f32[8,32,1024]{2,1,0:T(8,128)}, f32[8,16,1024]{2,1,0:T(8,128)}) custom-call(s32[9]{0:T(128)S(1)} %pad_add_fusion.order, bf16[4,448,512]{2,1,0:T(8,128)(2,1)} %maximum_maximum_fusion.refs_0_, bf16[4,448,512]{2,1,0:T(8,128)(2,1)} %collective-permute-done.82.refs_1_), custom_call_target="tpu_custom_call" | custom-call | flops 1 | bytes 1 | tf_op jit(solution)/shard_map/place/pallas_call | solution.py:701
  583.0 4.7 collective-permute-done.80
  587.7 3.1 select_bitcast_fusion
  (494 shorter events, 155.5 us)
Async XLA Ops:
  3.5 15.9 %collective-permute-start.5 = (bf16[1024,256]{1,0:T(8,128)(2,1)}, bf16[1024,256]{1,0:T(8,128)(2,1)}, u32[]{:S(2)}, u32[]{:S(2)}) collective-permute-start(bf16[1024,256]{1,0:T(8,128)(2,1)} %param.34), channel_id=1, source_target_pairs={{0,4},{1,5},{2,6},{3,7},{4,0},{5,1},{6,2},{7,3},{8,12},{9,13},{10,... | collective-permute-start | bytes 1572872 | tf_op jit(solution)/shard_map/ppermute | solution.py:813
  6.8 28.4 %collective-permute-start.2 = (bf16[2,256,1024]{2,1,0:T(8,128)(2,1)}, bf16[2,256,1024]{2,1,0:T(8,128)(2,1)}, u32[]{:S(2)}, u32[]{:S(2)}) collective-permute-start(bf16[2,256,1024]{2,1,0:T(8,128)(2,1)} %pad_maximum_fusion.1), channel_id=1, source_target_pairs={{0,2},{1,3},{6,4},{7,5},{8,10},{9,11},{14,12},{15,13},{16,18},{17,... | collective-permute-start | bytes 3145736 | tf_op jit(solution)/shard_map/ppermute | solution.py:819
  19.4 17.2 %collective-permute-start.3 = (s32[1,1152]{1,0:T(1,128)S(1)}, s32[1,1152]{1,0:T(1,128)S(1)}, u32[]{:S(2)}, u32[]{:S(2)}) collective-permute-start(s32[1,1152]{1,0:T(1,128)S(1)} %concatenate.116), channel_id=1, source_target_pairs={{0,4},{1,5},{2,6},{3,7},{4,0},{5,1},{6,2},{7,3},{8,12},{9,13},{10,... | collective-permute-start | bytes 13832 | tf_op jit(solution)/shard_map/ppermute | solution.py:813
  40.3 19.9 %collective-permute-start.9 = (bf16[2,256,1024]{2,1,0:T(8,128)(2,1)}, bf16[2,256,1024]{2,1,0:T(8,128)(2,1)}, u32[]{:S(2)}, u32[]{:S(2)}) collective-permute-start(bf16[2,256,1024]{2,1,0:T(8,128)(2,1)} %pad_maximum_fusion), channel_id=1, source_target_pairs={{0,2},{1,3},{6,4},{7,5},{8,10},{9,11},{14,12},{15,13},{16,18},{17,... | collective-permute-start | bytes 3145736 | tf_op jit(solution)/shard_map/ppermute | solution.py:819
  41.6 20.7 %collective-permute-start.10 = (bf16[2,256,1024]{2,1,0:T(8,128)(2,1)S(1)}, bf16[2,256,1024]{2,1,0:T(8,128)(2,1)}, u32[]{:S(2)}, u32[]{:S(2)}) collective-permute-start(bf16[2,256,1024]{2,1,0:T(8,128)(2,1)S(1)} %broadcast_select_fusion.6.refs_10_.refs_19_.refs_9_), channel_id=1, source_target_pairs={{0,8},{1,9},{2,10},{3,11},{4,12},{5,13},{6,14},{7,15},{8,0},{9,1},... | collective-permute-start | bytes 3145736 | tf_op jit(solution)/shard_map/ppermute | solution.py:819
  43.5 20.6 %collective-permute-start.11 = (bf16[2,256,1024]{2,1,0:T(8,128)(2,1)S(1)}, bf16[2,256,1024]{2,1,0:T(8,128)(2,1)}, u32[]{:S(2)}, u32[]{:S(2)}) collective-permute-start(bf16[2,256,1024]{2,1,0:T(8,128)(2,1)S(1)} %broadcast_select_fusion.6.refs_10_.refs_19_.refs_9_), channel_id=1, source_target_pairs={{0,16},{1,17},{2,18},{3,19},{4,20},{5,21},{6,22},{7,23},{8,24},{9,... | collective-permute-start | bytes 3145736 | tf_op jit(solution)/shard_map/ppermute | solution.py:819
  64.1 20.8 %collective-permute-start.14 = (bf16[2,256,1024]{2,1,0:T(8,128)(2,1)S(1)}, bf16[2,256,1024]{2,1,0:T(8,128)(2,1)S(1)}, u32[]{:S(2)}, u32[]{:S(2)}) collective-permute-start(bf16[2,256,1024]{2,1,0:T(8,128)(2,1)S(1)} %broadcast_select_fusion.5.refs_6_.refs_15_.refs_5_), channel_id=1, source_target_pairs={{0,8},{1,9},{2,10},{3,11},{4,12},{5,13},{6,14},{7,15},{8,0},{9,1},... | collective-permute-start | bytes 3145736 | tf_op jit(solution)/shard_map/ppermute | solution.py:819
  64.2 21.9 %collective-permute-start.15 = (bf16[2,256,1024]{2,1,0:T(8,128)(2,1)}, bf16[2,256,1024]{2,1,0:T(8,128)(2,1)S(1)}, u32[]{:S(2)}, u32[]{:S(2)}) collective-permute-start(bf16[2,256,1024]{2,1,0:T(8,128)(2,1)} %collective-permute-done.10.refs_11_.refs_20_.refs_10_), channel_id=1, source_target_pairs={{0,16},{1,17},{2,18},{3,19},{4,20},{5,21},{6,22},{7,23},{8,24},{9,... | collective-permute-start | bytes 3145736 | tf_op jit(solution)/shard_map/ppermute | solution.py:819
  65.5 51.8 %collective-permute-start.12 = (bf16[256,2048]{1,0:T(8,128)(2,1)S(1)}, bf16[256,2048]{1,0:T(8,128)(2,1)S(1)}, u32[]{:S(2)}, u32[]{:S(2)}) collective-permute-start(bf16[256,2048]{1,0:T(8,128)(2,1)S(1)} %bitcast.134), channel_id=1, source_target_pairs={{2,4},{3,5},{4,2},{5,3},{10,12},{11,13},{12,10},{13,11},{18,20},{1... | collective-permute-start | bytes 3145736 | tf_op jit(solution)/shard_map/ppermute | solution.py:819
  67.5 51.3 %collective-permute-start.13 = (bf16[2,256,1024]{2,1,0:T(8,128)(2,1)S(1)}, bf16[2,256,1024]{2,1,0:T(8,128)(2,1)S(1)}, u32[]{:S(2)}, u32[]{:S(2)}) collective-permute-start(bf16[2,256,1024]{2,1,0:T(8,128)(2,1)S(1)} %copy-done.104), channel_id=1, source_target_pairs={{0,2},{1,3},{6,4},{7,5},{8,10},{9,11},{14,12},{15,13},{16,18},{17,... | collective-permute-start | bytes 3145736 | tf_op jit(solution)/shard_map/ppermute | solution.py:819
  86.1 35.1 %collective-permute-start.17 = (bf16[2,256,1024]{2,1,0:T(8,128)(2,1)S(1)}, bf16[2,256,1024]{2,1,0:T(8,128)(2,1)S(1)}, u32[]{:S(2)}, u32[]{:S(2)}) collective-permute-start(bf16[2,256,1024]{2,1,0:T(8,128)(2,1)S(1)} %broadcast_select_fusion.5.refs_6_.refs_15_.refs_5_), channel_id=1, source_target_pairs={{0,16},{1,17},{2,18},{3,19},{4,20},{5,21},{6,22},{7,23},{8,24},{9,... | collective-permute-start | bytes 3145736 | tf_op jit(solution)/shard_map/ppermute | solution.py:819
  87.4 33.8 %collective-permute-start.16 = (bf16[112,1024]{1,0:T(8,128)(2,1)S(1)}, bf16[112,1024]{1,0:T(8,128)(2,1)S(1)}, u32[]{:S(2)}, u32[]{:S(2)}) collective-permute-start(bf16[112,1024]{1,0:T(8,128)(2,1)S(1)} %get-tuple-element.222), channel_id=1, source_target_pairs={{0,2},{1,3},{6,4},{7,5},{8,10},{9,11},{14,12},{15,13},{16,18},{17,... | collective-permute-start | bytes 688136 | tf_op jit(solution)/shard_map/ppermute | solution.py:819
  126.8 45.7 %collective-permute-start.19 = (bf16[2,1024,256]{2,1,0:T(8,128)(2,1)}, bf16[2,1024,256]{2,1,0:T(8,128)(2,1)}, u32[]{:S(2)}, u32[]{:S(2)}) collective-permute-start(bf16[2,1024,256]{2,1,0:T(8,128)(2,1)} %pad_maximum_fusion.3), channel_id=1, source_target_pairs={{0,2},{1,3},{6,4},{7,5},{8,10},{9,11},{14,12},{15,13},{16,18},{17,... | collective-permute-start | bytes 3145736 | tf_op jit(solution)/shard_map/ppermute | solution.py:819
  128.1 46.0 %collective-permute-start.18 = (bf16[256,2048]{1,0:T(8,128)(2,1)}, bf16[256,2048]{1,0:T(8,128)(2,1)}, u32[]{:S(2)}, u32[]{:S(2)}) collective-permute-start(bf16[256,2048]{1,0:T(8,128)(2,1)} %norm_rows.1.refs_2_.refs_0_), channel_id=1, source_target_pairs={{0,1},{1,0},{2,3},{3,2},{4,5},{5,4},{6,7},{7,6},{8,9},{9,8},{10,11... | collective-permute-start | bytes 3145736 | tf_op jit(solution)/shard_map/ppermute | solution.py:819
  128.1 47.4 %collective-permute-start.23 = (bf16[256,2048]{1,0:T(8,128)(2,1)}, bf16[256,2048]{1,0:T(8,128)(2,1)}, u32[]{:S(2)}, u32[]{:S(2)}) collective-permute-start(bf16[256,2048]{1,0:T(8,128)(2,1)} %bitcast.135), channel_id=1, source_target_pairs={{2,4},{3,5},{4,2},{5,3},{10,12},{11,13},{12,10},{13,11},{18,20},{1... | collective-permute-start | bytes 3145736 | tf_op jit(solution)/shard_map/ppermute | solution.py:819
  137.7 37.9 %collective-permute-start.22 = (bf16[2,256,1024]{2,1,0:T(8,128)(2,1)}, bf16[2,256,1024]{2,1,0:T(8,128)(2,1)}, u32[]{:S(2)}, u32[]{:S(2)}) collective-permute-start(bf16[2,256,1024]{2,1,0:T(8,128)(2,1)} %copy-done.67), channel_id=1, source_target_pairs={{0,8},{1,9},{2,10},{3,11},{4,12},{5,13},{6,14},{7,15},{8,0},{9,1},... | collective-permute-start | bytes 3145736 | tf_op jit(solution)/shard_map/ppermute | solution.py:819
  137.7 37.9 %collective-permute-start.24 = (bf16[2,256,1024]{2,1,0:T(8,128)(2,1)}, bf16[2,256,1024]{2,1,0:T(8,128)(2,1)}, u32[]{:S(2)}, u32[]{:S(2)}) collective-permute-start(bf16[2,256,1024]{2,1,0:T(8,128)(2,1)} %collective-permute-done.20.refs_5_.refs_24_.refs_14_), channel_id=1, source_target_pairs={{0,16},{1,17},{2,18},{3,19},{4,20},{5,21},{6,22},{7,23},{8,24},{9,... | collective-permute-start | bytes 3145736 | tf_op jit(solution)/shard_map/ppermute | solution.py:819
  176.6 27.7 %collective-permute-start.25 = (bf16[2,1024,256]{2,1,0:T(8,128)(2,1)S(1)}, bf16[2,1024,256]{2,1,0:T(8,128)(2,1)S(1)}, u32[]{:S(2)}, u32[]{:S(2)}) collective-permute-start(bf16[2,1024,256]{2,1,0:T(8,128)(2,1)S(1)} %copy-done.103), channel_id=1, source_target_pairs={{0,2},{1,3},{6,4},{7,5},{8,10},{9,11},{14,12},{15,13},{16,18},{17,... | collective-permute-start | bytes 3145736 | tf_op jit(solution)/shard_map/ppermute | solution.py:819
  178.0 28.7 %collective-permute-start.26 = (bf16[2,1024,256]{2,1,0:T(8,128)(2,1)S(1)}, bf16[2,1024,256]{2,1,0:T(8,128)(2,1)}, u32[]{:S(2)}, u32[]{:S(2)}) collective-permute-start(bf16[2,1024,256]{2,1,0:T(8,128)(2,1)S(1)} %broadcast_select_fusion.1.refs_0_.refs_2_), channel_id=1, source_target_pairs={{0,8},{1,9},{2,10},{3,11},{4,12},{5,13},{6,14},{7,15},{8,0},{9,1},... | collective-permute-start | bytes 3145736 | tf_op jit(solution)/shard_map/ppermute | solution.py:819
  178.3 28.4 %collective-permute-start.29 = (bf16[2,1024,256]{2,1,0:T(8,128)(2,1)S(1)}, bf16[2,1024,256]{2,1,0:T(8,128)(2,1)S(1)}, u32[]{:S(2)}, u32[]{:S(2)}) collective-permute-start(bf16[2,1024,256]{2,1,0:T(8,128)(2,1)S(1)} %broadcast_select_fusion.1.refs_0_.refs_2_), channel_id=1, source_target_pairs={{0,16},{1,17},{2,18},{3,19},{4,20},{5,21},{6,22},{7,23},{8,24},{9,... | collective-permute-start | bytes 3145736 | tf_op jit(solution)/shard_map/ppermute | solution.py:819
  207.7 25.9 %collective-permute-start.30 = (bf16[2,256,1024]{2,1,0:T(8,128)(2,1)}, bf16[2,256,1024]{2,1,0:T(8,128)(2,1)}, u32[]{:S(2)}, u32[]{:S(2)}) collective-permute-start(bf16[2,256,1024]{2,1,0:T(8,128)(2,1)} %pad_maximum_fusion.5), channel_id=1, source_target_pairs={{0,2},{1,3},{6,4},{7,5},{8,10},{9,11},{14,12},{15,13},{16,18},{17,... | collective-permute-start | bytes 3145736 | tf_op jit(solution)/shard_map/ppermute | solution.py:819
  209.4 25.6 %collective-permute-start.31 = (bf16[2,1024,256]{2,1,0:T(8,128)(2,1)}, bf16[2,1024,256]{2,1,0:T(8,128)(2,1)}, u32[]{:S(2)}, u32[]{:S(2)}) collective-permute-start(bf16[2,1024,256]{2,1,0:T(8,128)(2,1)} %collective-permute-done.26.refs_1_.refs_3_), channel_id=1, source_target_pairs={{0,16},{1,17},{2,18},{3,19},{4,20},{5,21},{6,22},{7,23},{8,24},{9,... | collective-permute-start | bytes 3145736 | tf_op jit(solution)/shard_map/ppermute | solution.py:819
  210.9 25.2 %collective-permute-start.32 = (bf16[2,1024,256]{2,1,0:T(8,128)(2,1)}, bf16[2,1024,256]{2,1,0:T(8,128)(2,1)}, u32[]{:S(2)}, u32[]{:S(2)}) collective-permute-start(bf16[2,1024,256]{2,1,0:T(8,128)(2,1)} %broadcast_select_fusion.refs_4_.refs_0_), channel_id=1, source_target_pairs={{0,8},{1,9},{2,10},{3,11},{4,12},{5,13},{6,14},{7,15},{8,0},{9,1},... | collective-permute-start | bytes 3145736 | tf_op jit(solution)/shard_map/ppermute | solution.py:819
  210.9 24.1 %collective-permute-start.33 = (bf16[128,2048]{1,0:T(8,128)(2,1)}, bf16[128,2048]{1,0:T(8,128)(2,1)}, u32[]{:S(2)}, u32[]{:S(2)}) collective-permute-start(bf16[128,2048]{1,0:T(8,128)(2,1)} %get-tuple-element.264), channel_id=1, source_target_pairs={{0,1},{1,0},{2,3},{3,2},{4,5},{5,4},{6,7},{7,6},{8,9},{9,8},{10,11... | collective-permute-start | bytes 1572872 | tf_op jit(solution)/shard_map/ppermute | solution.py:819
  236.1 23.6 %collective-permute-start.34 = (bf16[2,1024,256]{2,1,0:T(8,128)(2,1)}, bf16[2,1024,256]{2,1,0:T(8,128)(2,1)S(1)}, u32[]{:S(2)}, u32[]{:S(2)}) collective-permute-start(bf16[2,1024,256]{2,1,0:T(8,128)(2,1)} %broadcast_select_fusion.refs_4_.refs_0_), channel_id=1, source_target_pairs={{0,16},{1,17},{2,18},{3,19},{4,20},{5,21},{6,22},{7,23},{8,24},{9,... | collective-permute-start | bytes 3145736 | tf_op jit(solution)/shard_map/ppermute | solution.py:819
  236.1 23.6 %collective-permute-start.35 = (bf16[2,256,1024]{2,1,0:T(8,128)(2,1)S(1)}, bf16[2,256,1024]{2,1,0:T(8,128)(2,1)S(1)}, u32[]{:S(2)}, u32[]{:S(2)}) collective-permute-start(bf16[2,256,1024]{2,1,0:T(8,128)(2,1)S(1)} %broadcast_select_fusion.3.refs_4_.refs_9_.refs_3_), channel_id=1, source_target_pairs={{0,8},{1,9},{2,10},{3,11},{4,12},{5,13},{6,14},{7,15},{8,0},{9,1},... | collective-permute-start | bytes 3145736 | tf_op jit(solution)/shard_map/ppermute | solution.py:819
  237.0 27.7 %collective-permute-start.36 = (bf16[2,256,1024]{2,1,0:T(8,128)(2,1)S(1)}, bf16[2,256,1024]{2,1,0:T(8,128)(2,1)S(1)}, u32[]{:S(2)}, u32[]{:S(2)}) collective-permute-start(bf16[2,256,1024]{2,1,0:T(8,128)(2,1)S(1)} %copy-done.102), channel_id=1, source_target_pairs={{0,2},{1,3},{6,4},{7,5},{8,10},{9,11},{14,12},{15,13},{16,18},{17,... | collective-permute-start | bytes 3145736 | tf_op jit(solution)/shard_map/ppermute | solution.py:819
  238.3 16.5 %collective-permute-start.37 = (bf16[128,2048]{1,0:T(8,128)(2,1)S(1)}, bf16[128,2048]{1,0:T(8,128)(2,1)S(1)}, u32[]{:S(2)}, u32[]{:S(2)}) collective-permute-start(bf16[128,2048]{1,0:T(8,128)(2,1)S(1)} %copy-done.105), channel_id=1, source_target_pairs={{0,1},{1,0},{2,3},{3,2},{4,5},{5,4},{6,7},{7,6},{8,9},{9,8},{10,11... | collective-permute-start | bytes 1572872 | tf_op jit(solution)/shard_map/ppermute | solution.py:819
  269.2 25.9 %collective-permute-start.40 = (bf16[256,2048]{1,0:T(8,128)(2,1)S(1)}, bf16[256,2048]{1,0:T(8,128)(2,1)S(1)}, u32[]{:S(2)}, u32[]{:S(2)}) collective-permute-start(bf16[256,2048]{1,0:T(8,128)(2,1)S(1)} %add_convert_fusion.4), channel_id=1, source_target_pairs={{0,1},{1,0},{2,3},{3,2},{4,5},{5,4},{6,7},{7,6},{8,9},{9,8},{10,11... | collective-permute-start | bytes 3145736 | tf_op jit(solution)/shard_map/ppermute | solution.py:819
  271.9 25.3 %collective-permute-start.41 = (bf16[2,256,1024]{2,1,0:T(8,128)(2,1)S(1)}, bf16[2,256,1024]{2,1,0:T(8,128)(2,1)S(1)}, u32[]{:S(2)}, u32[]{:S(2)}) collective-permute-start(bf16[2,256,1024]{2,1,0:T(8,128)(2,1)S(1)} %broadcast_select_fusion.3.refs_4_.refs_9_.refs_3_), channel_id=1, source_target_pairs={{0,16},{1,17},{2,18},{3,19},{4,20},{5,21},{6,22},{7,23},{8,24},{9,... | collective-permute-start | bytes 3145736 | tf_op jit(solution)/shard_map/ppermute | solution.py:819
  272.9 24.3 %collective-permute-start.42 = (bf16[2,1024,256]{2,1,0:T(8,128)(2,1)S(1)}, bf16[2,1024,256]{2,1,0:T(8,128)(2,1)S(1)}, u32[]{:S(2)}, u32[]{:S(2)}) collective-permute-start(bf16[2,1024,256]{2,1,0:T(8,128)(2,1)S(1)} %collective-permute-done.34.refs_6_.refs_2_), channel_id=1, source_target_pairs={{0,8},{1,9},{2,10},{3,11},{4,12},{5,13},{6,14},{7,15},{8,0},{9,1},... | collective-permute-start | bytes 3145736 | tf_op jit(solution)/shard_map/ppermute | solution.py:819
  297.2 23.6 %collective-permute-start.43 = (bf16[2,256,1024]{2,1,0:T(8,128)(2,1)S(1)}, bf16[2,256,1024]{2,1,0:T(8,128)(2,1)S(1)}, u32[]{:S(2)}, u32[]{:S(2)}) collective-permute-start(bf16[2,256,1024]{2,1,0:T(8,128)(2,1)S(1)} %broadcast_select_fusion.2.refs_8_.refs_13_.refs_7_), channel_id=1, source_target_pairs={{0,8},{1,9},{2,10},{3,11},{4,12},{5,13},{6,14},{7,15},{8,0},{9,1},... | collective-permute-start | bytes 3145736 | tf_op jit(solution)/shard_map/ppermute | solution.py:819
  297.9 23.4 %collective-permute-start.44 = (bf16[256,2048]{1,0:T(8,128)(2,1)S(1)}, bf16[256,2048]{1,0:T(8,128)(2,1)S(1)}, u32[]{:S(2)}, u32[]{:S(2)}) collective-permute-start(bf16[256,2048]{1,0:T(8,128)(2,1)S(1)} %get-tuple-element.303.refs_0_.refs_4_), channel_id=1, source_target_pairs={{0,1},{1,0},{2,3},{3,2},{4,5},{5,4},{6,7},{7,6},{8,9},{9,8},{10,11... | collective-permute-start | bytes 3145736 | tf_op jit(solution)/shard_map/ppermute | solution.py:819
  299.1 22.3 %collective-permute-start.45 = (bf16[256,2048]{1,0:T(8,128)(2,1)S(1)}, bf16[256,2048]{1,0:T(8,128)(2,1)S(1)}, u32[]{:S(2)}, u32[]{:S(2)}) collective-permute-start(bf16[256,2048]{1,0:T(8,128)(2,1)S(1)} %broadcast_select_fusion.7.refs_0_.grad_in), channel_id=1, source_target_pairs={{0,4},{1,5},{2,6},{3,7},{4,0},{5,1},{6,2},{7,3},{8,12},{9,13},{10,... | collective-permute-start | bytes 3145736 | tf_op jit(solution)/shard_map/ppermute | solution.py:819
  300.8 20.5 %collective-permute-start.46 = (bf16[256,2048]{1,0:T(8,128)(2,1)S(1)}, bf16[256,2048]{1,0:T(8,128)(2,1)S(1)}, u32[]{:S(2)}, u32[]{:S(2)}) collective-permute-start(bf16[256,2048]{1,0:T(8,128)(2,1)S(1)} %constant_dynamic-update-slice_fusion.14.refs_2_), channel_id=1, source_target_pairs={{0,4},{1,5},{2,6},{3,7},{4,0},{5,1},{6,2},{7,3},{8,12},{9,13},{10,... | collective-permute-start | bytes 3145736 | tf_op jit(solution)/shard_map/ppermute | solution.py:819
  300.8 24.2 %collective-permute-start.47 = (bf16[2,256,1024]{2,1,0:T(8,128)(2,1)S(1)}, bf16[2,256,1024]{2,1,0:T(8,128)(2,1)S(1)}, u32[]{:S(2)}, u32[]{:S(2)}) collective-permute-start(bf16[2,256,1024]{2,1,0:T(8,128)(2,1)S(1)} %broadcast_select_fusion.2.refs_8_.refs_13_.refs_7_), channel_id=1, source_target_pairs={{0,16},{1,17},{2,18},{3,19},{4,20},{5,21},{6,22},{7,23},{8,24},{9,... | collective-permute-start | bytes 3145736 | tf_op jit(solution)/shard_map/ppermute | solution.py:819
  326.4 24.3 %collective-permute-start.50 = (bf16[2,256,1024]{2,1,0:T(8,128)(2,1)S(1)}, bf16[2,256,1024]{2,1,0:T(8,128)(2,1)S(1)}, u32[]{:S(2)}, u32[]{:S(2)}) collective-permute-start(bf16[2,256,1024]{2,1,0:T(8,128)(2,1)S(1)} %collective-permute-done.41.refs_6_.refs_11_.refs_5_), channel_id=1, source_target_pairs={{0,8},{1,9},{2,10},{3,11},{4,12},{5,13},{6,14},{7,15},{8,0},{9,1},... | collective-permute-start | bytes 3145736 | tf_op jit(solution)/shard_map/ppermute | solution.py:819
  327.3 24.0 %collective-permute-start.51 = (bf16[2,256,1024]{2,1,0:T(8,128)(2,1)S(1)}, bf16[2,256,1024]{2,1,0:T(8,128)(2,1)}, u32[]{:S(2)}, u32[]{:S(2)}) collective-permute-start(bf16[2,256,1024]{2,1,0:T(8,128)(2,1)S(1)} %collective-permute-done.43.refs_9_.refs_14_.refs_8_), channel_id=1, source_target_pairs={{0,16},{1,17},{2,18},{3,19},{4,20},{5,21},{6,22},{7,23},{8,24},{9,... | collective-permute-start | bytes 3145736 | tf_op jit(solution)/shard_map/ppermute | solution.py:819
  389.8 23.7 %collective-permute-start.56 = (bf16[256,2048]{1,0:T(8,128)(2,1)}, bf16[256,2048]{1,0:T(8,128)(2,1)}, u32[]{:S(2)}, u32[]{:S(2)}) collective-permute-start(bf16[256,2048]{1,0:T(8,128)(2,1)} %add_convert_fusion.3), channel_id=1, source_target_pairs={{0,1},{1,0},{2,3},{3,2},{4,5},{5,4},{6,7},{7,6},{8,9},{9,8},{10,11... | collective-permute-start | bytes 3145736 | tf_op jit(solution)/shard_map/ppermute | solution.py:819
  419.3 16.0 %collective-permute-start.59 = (bf16[256,2048]{1,0:T(8,128)(2,1)}, bf16[256,2048]{1,0:T(8,128)(2,1)}, u32[]{:S(2)}, u32[]{:S(2)}) collective-permute-start(bf16[256,2048]{1,0:T(8,128)(2,1)} %get-tuple-element.334), channel_id=1, source_target_pairs={{0,4},{1,5},{2,6},{3,7},{4,0},{5,1},{6,2},{7,3},{8,12},{9,13},{10,... | collective-permute-start | bytes 3145736 | tf_op jit(solution)/shard_map/ppermute | solution.py:819
  419.3 27.8 %collective-permute-start.60 = (bf16[256,2048]{1,0:T(8,128)(2,1)}, bf16[256,2048]{1,0:T(8,128)(2,1)S(1)}, u32[]{:S(2)}, u32[]{:S(2)}) collective-permute-start(bf16[256,2048]{1,0:T(8,128)(2,1)} %rms_back.2.refs_0_.refs_4_.grad_in), channel_id=1, source_target_pairs={{0,1},{1,0},{2,3},{3,2},{4,5},{5,4},{6,7},{7,6},{8,9},{9,8},{10,11... | collective-permute-start | bytes 3145736 | tf_op jit(solution)/shard_map/ppermute | solution.py:819
  419.5 27.5 %collective-permute-start.61 = (bf16[256,2048]{1,0:T(8,128)(2,1)}, bf16[256,2048]{1,0:T(8,128)(2,1)S(1)}, u32[]{:S(2)}, u32[]{:S(2)}) collective-permute-start(bf16[256,2048]{1,0:T(8,128)(2,1)} %get-tuple-element.336), channel_id=1, source_target_pairs={{0,4},{1,5},{2,6},{3,7},{4,0},{5,1},{6,2},{7,3},{8,12},{9,13},{10,... | collective-permute-start | bytes 3145736 | tf_op jit(solution)/shard_map/ppermute | solution.py:819
  420.3 25.7 %collective-permute-start.58 = (bf16[304,512]{1,0:T(8,128)(2,1)S(1)}, bf16[304,512]{1,0:T(8,128)(2,1)S(1)}, u32[]{:S(2)}, u32[]{:S(2)}) collective-permute-start(bf16[304,512]{1,0:T(8,128)(2,1)S(1)} %maximum_maximum_fusion.2), channel_id=1, source_target_pairs={{2,4},{3,5},{4,2},{5,3},{10,12},{11,13},{12,10},{13,11},{18,20},{1... | collective-permute-start | bytes 933896 | tf_op jit(solution)/shard_map/ppermute | solution.py:819
  450.7 29.0 %collective-permute-start.65 = (bf16[256,2048]{1,0:T(8,128)(2,1)}, bf16[256,2048]{1,0:T(8,128)(2,1)}, u32[]{:S(2)}, u32[]{:S(2)}) collective-permute-start(bf16[256,2048]{1,0:T(8,128)(2,1)} %add_convert_fusion.2), channel_id=1, source_target_pairs={{0,1},{1,0},{2,3},{3,2},{4,5},{5,4},{6,7},{7,6},{8,9},{9,8},{10,11... | collective-permute-start | bytes 3145736 | tf_op jit(solution)/shard_map/ppermute | solution.py:819
  483.4 27.9 %collective-permute-start.69 = (bf16[256,2048]{1,0:T(8,128)(2,1)S(1)}, bf16[256,2048]{1,0:T(8,128)(2,1)S(1)}, u32[]{:S(2)}, u32[]{:S(2)}) collective-permute-start(bf16[256,2048]{1,0:T(8,128)(2,1)S(1)} %add_convert_fusion.1), channel_id=1, source_target_pairs={{2,4},{3,5},{4,2},{5,3},{10,12},{11,13},{12,10},{13,11},{18,20},{1... | collective-permute-start | bytes 3145736 | tf_op jit(solution)/shard_map/ppermute | solution.py:819
  486.5 17.6 %collective-permute-start.70 = (bf16[80,1024]{1,0:T(8,128)(2,1)S(1)}, bf16[80,1024]{1,0:T(8,128)(2,1)S(1)}, u32[]{:S(2)}, u32[]{:S(2)}) collective-permute-start(bf16[80,1024]{1,0:T(8,128)(2,1)S(1)} %fusion.2), channel_id=1, source_target_pairs={{0,1},{1,0},{2,3},{3,2},{4,5},{5,4},{6,7},{7,6},{8,9},{9,8},{10,11... | collective-permute-start | bytes 491528 | tf_op jit(solution)/shard_map/ppermute | solution.py:819
  559.2 15.6 %collective-permute-start.82 = (bf16[4,448,512]{2,1,0:T(8,128)(2,1)}, bf16[4,448,512]{2,1,0:T(8,128)(2,1)}, u32[]{:S(2)}, u32[]{:S(2)}) collective-permute-start(bf16[4,448,512]{2,1,0:T(8,128)(2,1)} %maximum_maximum_fusion.refs_0_), channel_id=1, source_target_pairs={{0,4},{1,5},{2,6},{3,7},{4,0},{5,1},{6,2},{7,3},{8,12},{9,13},{10,... | collective-permute-start | bytes 5505032 | tf_op jit(solution)/shard_map/ppermute | solution.py:819
  559.7 28.0 %collective-permute-start.80 = (bf16[256,2048]{1,0:T(8,128)(2,1)}, bf16[256,2048]{1,0:T(8,128)(2,1)}, u32[]{:S(2)}, u32[]{:S(2)}) collective-permute-start(bf16[256,2048]{1,0:T(8,128)(2,1)} %get-tuple-element.391), channel_id=1, source_target_pairs={{2,4},{3,5},{4,2},{5,3},{10,12},{11,13},{12,10},{13,11},{18,20},{1... | collective-permute-start | bytes 3145736 | tf_op jit(solution)/shard_map/ppermute | solution.py:819
  (152 other events, 2643.6 us)

commit v4 on v3

--- a/solution.py
+++ b/solution.py
@@ -60,14 +60,15 @@
     return pl.BlockSpec(memory_space=pltpu.SMEM)
 
 
-def columns(refs, ids):
+def columns(refs, ids, begin=0, end=None):
     count = ids.shape[0]
     width = refs[0].shape[1] // count
     if count == 1:
         return all_rows(refs)
+    chosen = range(begin, count if end is None else end)
     return jnp.concatenate(
         [
-            jnp.concatenate([ref[:, aligned(ids[i] * width, width)] for i in range(count)], axis=1)
+            jnp.concatenate([ref[:, aligned(ids[i] * width, width)] for i in chosen], axis=1)
             for ref in refs
         ],
         axis=0,
@@ -350,7 +351,7 @@
         low[...] = low_rows(low_back[...], act).astype(BF)
 
     weights = jnp.concatenate([w[s] for w in pieces for s in range(w.shape[0])], axis=1)
-    out[...] = dot_nt(columns(act, ids), weights) + dot_tn(low[...], low_in[...])
+    out[...] = (dot_nt(columns(act, ids), weights) + dot_tn(low[...], low_in[...])).astype(BF)
 
 
 def hidden_grad(ids, act, low_back, low_in, pieces):
@@ -365,7 +366,7 @@
         + whole(act) + [pl.BlockSpec((w.shape[0], block, w.shape[2]), lambda n: (0, n, 0)) for w in pieces],
         out_specs=[pl.BlockSpec((rows, block), lambda n: (0, n)),
                    full((low_back.shape[0], rows))],
-        out_shape=[jax.ShapeDtypeStruct((rows, width), F32),
+        out_shape=[far((rows, width), BF),
                    jax.ShapeDtypeStruct((low_back.shape[0], rows), BF)],
         compiler_params=params(40),
         cost_estimate=estimate(2 * rows * depth * width, 2 * depth * width + 8 * rows * depth),
@@ -373,25 +374,62 @@
     )(ids, low_back, low_in, *act, *pieces)
 
 
-def mlp_kernel(parts, count, ids, low_in, gate_out, up_out, down_in, grad, grad_low, *refs):
+def mlp_begin_kernel(parts, count, ids, low_in, *refs):
     act, refs = refs[:parts], refs[parts:]
     gate_pieces, up_pieces = refs[:count], refs[count:2 * count]
-    hid, dgate, dup, low, lows, grad_hidden, grad_down = refs[2 * count:]
+    gate, up, low = refs[2 * count:]
 
     @pl.when(pl.program_id(0) == 0)
     def _():
         low[...] = low_rows(low_in[...], act).astype(BF)
+
+    rows = columns(act, ids, 0, sum(w.shape[0] for w in gate_pieces))
+    gate[...] = dot(rows, stacked(gate_pieces))
+    up[...] = dot(rows, stacked(up_pieces))
+
+
+def mlp_begin(ids, act, low_in, gate_pieces, up_pieces):
+    rows, depth = row_count(act), act[0].shape[1]
+    width = gate_pieces[0].shape[2]
+    block = 256
+    ranks = low_in.shape[0]
+    column = pl.BlockSpec((rows, block), lambda n: (0, n))
+    return pl.pallas_call(
+        partial(mlp_begin_kernel, len(act), len(gate_pieces)),
+        grid=(width // block,),
+        in_specs=[smem(), full(low_in.shape)] + whole(act) + piece_specs(gate_pieces, block)
+        + piece_specs(up_pieces, block),
+        out_specs=[column, column, full((ranks, rows))],
+        out_shape=[far((rows, width), F32)] * 2 + [jax.ShapeDtypeStruct((ranks, rows), BF)],
+        compiler_params=params(48),
+        cost_estimate=estimate(0, 0),
+        name="mlp_begin",
+    )(ids, low_in, *act, *gate_pieces, *up_pieces)
+
+
+def mlp_kernel(parts, count, ids, gate_in, up_in, low, gate_out, up_out, down_in, grad, grad_low,
+               *refs):
+    act, refs = refs[:parts], refs[parts:]
+    gate_pieces, up_pieces = refs[:count], refs[count:2 * count]
+    hid, dgate, dup, lows, grad_hidden, grad_down = refs[2 * count:]
+
+    @pl.when(pl.program_id(0) == 0)
+    def _():
         lows[...] = jnp.zeros(lows.shape, F32)
 
-    rows = columns(act, ids)
     extra = low[...]
-    gate = dot(rows, stacked(gate_pieces)) + dot_tn(extra, gate_out[...])
-    up = dot(rows, stacked(up_pieces)) + dot_tn(extra, up_out[...])
+    gate = gate_in[...] + dot_tn(extra, gate_out[...])
+    up = up_in[...] + dot_tn(extra, up_out[...])
+    if count:
+        last = sum(w.shape[0] for w in gate_pieces)
+        rows = columns(act, ids, ids.shape[0] - last)
+        gate = gate + dot(rows, stacked(gate_pieces))
+        up = up + dot(rows, stacked(up_pieces))
     chance = 0.5 * (1.0 + lax.erf(gate * (0.5**0.5)))
     active = gate * chance
     slope = chance + gate * (jnp.exp(-0.5 * gate * gate) * 0.3989422804014327)
     hidden = (active * up).astype(BF)
-    back = grad[...]
+    back = grad[...].astype(F32)
     back_gate = (back * up * slope).astype(BF)
     back_up = (back * active).astype(BF)
     hid[...] = hidden
@@ -404,29 +442,29 @@
     grad_down[...] = dot(grad_low[...], hidden).astype(BF)
 
 
-def mlp(ids, act, low_in, gate_out, up_out, down_in, grad, grad_low, gate_pieces, up_pieces):
-    rows, depth = row_count(act), act[0].shape[1]
-    width = gate_pieces[0].shape[2]
+def mlp(ids, begun, act, gate_out, up_out, down_in, grad, grad_low, gate_pieces, up_pieces):
+    gate_in, up_in, low = begun
+    rows, width = gate_in.shape
     block = 256
-    ranks = low_in.shape[0]
+    ranks = low.shape[0]
     column = lambda height: pl.BlockSpec((height, block), lambda n: (0, n))
     return pl.pallas_call(
         partial(mlp_kernel, len(act), len(gate_pieces)),
         grid=(width // block,),
-        in_specs=[smem(), full(low_in.shape), column(ranks), column(ranks),
-                  column(down_in.shape[0]), column(rows), full(grad_low.shape)]
+        in_specs=[smem(), column(rows), column(rows), full(low.shape), column(ranks),
+                  column(ranks), column(down_in.shape[0]), column(rows), full(grad_low.shape)]
         + whole(act) + piece_specs(gate_pieces, block) + piece_specs(up_pieces, block),
-        out_specs=[column(rows), column(rows), column(rows), full((ranks, rows)),
-                   full((ranks + RANK, rows)), column(ranks), column(grad_low.shape[0])],
+        out_specs=[column(rows), column(rows), column(rows), full((ranks + RANK, rows)),
+                   column(ranks), column(grad_low.shape[0])],
         out_shape=[jax.ShapeDtypeStruct((rows, width), BF)] * 3
-        + [jax.ShapeDtypeStruct((ranks, rows), BF),
-           jax.ShapeDtypeStruct((ranks + RANK, rows), F32),
+        + [jax.ShapeDtypeStruct((ranks + RANK, rows), F32),
            jax.ShapeDtypeStruct((ranks, width), BF),
            jax.ShapeDtypeStruct((grad_low.shape[0], width), BF)],
         compiler_params=params(48),
-        cost_estimate=estimate(4 * rows * depth * width, 4 * depth * width + 8 * rows * depth),
+        cost_estimate=estimate(0, 0),
         name="mlp",
-    )(ids, low_in, gate_out, up_out, down_in, grad, grad_low, *act, *gate_pieces, *up_pieces)
+    )(ids, gate_in, up_in, low, gate_out, up_out, down_in, grad, grad_low, *act, *gate_pieces,
+      *up_pieces)
 
 
 def unfold_kernel(layout, ids, low_in, *refs):
@@ -745,6 +783,7 @@
         return (total, zero, zero)
 
     def forward(self, shards, tokens, cotangent, line, steps):
+        steps.rotation()
         blocks = [
             [lax.all_gather(shard, "dp", axis=int(shard.shape[1] * self.ndp == tokens.shape[1]),
                             tiled=True)[None]]
@@ -757,9 +796,10 @@
         mixed = steps.mix(a, *projected, blocks[2])
         *rows, low = steps.fold(mixed[0], blocks[3])
         middle, b = steps.join(tokens, self.scatter(rows))
-        dhid = steps.hidden_grad(dy, blocks[4])
-        return (blocks, tokens, a, cotangent, dy, projected, mixed, low, middle,
-                self.gather(b), dhid)
+        b = self.gather(b)
+        begun = steps.mlp_begin(b, blocks[5], blocks[6])
+        dhid = (*steps.hidden_grad(dy, blocks[4]), begun, ([], []))
+        return blocks, tokens, a, cotangent, dy, projected, mixed, low, middle, b, dhid
 
     def group_sum(self, x):
         return lax.psum(x.astype(BF), "tensor")
@@ -768,12 +808,16 @@
         steps.mlp()
         dz = self.gather(steps.dz(self.scatter(steps.unfold_mlp(256, (0, 1, 2, 3)))))
         output = steps.output(self.scatter(steps.fold_down(steps.hid)))
-        early = lax.all_gather(steps.early(self.group_sum(steps.lows)), "dp")
+        lows = self.group_sum(steps.early_lows())
+        early = lax.all_gather(steps.early(lows), "dp")
         early = steps.place_early([early], jnp.arange(self.ndp, dtype=jnp.int32))
         steps.gate_back(dz, 0)
         steps.gate_back(dz, 1)
         steps.retention_back(*steps.dret)
-        late = lax.all_gather(steps.late(self.group_sum(steps.late_lows()), dz), "dp")
+        late = jnp.concatenate(
+            [steps.late_shares(self.group_sum(steps.dlow)), steps.late_rest(lows, dz)]
+        )
+        late = lax.all_gather(late, "dp")
         late = steps.place_late([late], jnp.arange(self.ndp, dtype=jnp.int32))
         parts = self.scatter(steps.unfold_attn(256, (0, 1, 2, 3)))
         dx, _ = steps.dx(parts)
@@ -901,7 +945,11 @@
             return [jnp.stack([shard, self.core(shard)]) for shard in rest]
 
         other = self.core(line)
-        (moved,), made = go([], [], [over(0)], double, (shards[1:],))
+        def begin(rest):
+            return double(rest), steps.rotation()
+
+        (moved,), (made, turn) = go([], [], [over(0)], begin, (shards[1:],))
+        steps.turn = turn
         doubled += made
         arrived(0, moved)
         (moved,), (home_table, sent_table) = go(
@@ -950,9 +998,17 @@
         (far, near_grad, beyond_grad), _ = go([(6, "x"), (6, "y")], [],
                                               [(b, pair), (grad, core), (across, core)])
         dy = [grad, near_grad, across, beyond_grad]
-        (near, beyond), dhid = go([(5, "yx"), (6, "xy")], [], [(b, core), (far, core)],
-                                  steps.hidden_grad, (dy, blocks[4]))
-        b = [b, near, far, beyond]
+
+        def beside(near, beyond, own, across, dy, w_d, *weights):
+            rows = [own, near, across, beyond]
+            return steps.hidden_grad(dy, w_d), rows, steps.mlp_begin(rows, *weights)
+
+        moves = [(b, core), (far, core), hops["yx"](5), hops["xy"](6)]
+        moved, _, (dhid, b, begun) = self.round(
+            moves, beside, (b, far, dy, blocks[4], blocks[5][:3], blocks[6][:3]), feed=2
+        )
+        blocks[5][3], blocks[6][3] = moved[2:]
+        dhid = (*dhid, begun, (blocks[5][3:], blocks[6][3:]))
         return blocks, x, a, grad, dy, projected, mixed, low, middle, b, dhid
 
     def add(self, one, two):
@@ -986,10 +1042,10 @@
         self.last_round = ()
         steps.mlp()
         (lows,), _, (near, far, beyond) = self.round(
-            [(steps.lows.astype(BF), core)],
+            [(steps.early_lows().astype(BF), core)],
             lambda dup: steps.unfold_mlp(256, (1, 2, 3), dup), (steps.dup,)
         )
-        lows = self.core_sum(steps.lows, lows)
+        lows = self.core_sum(steps.early_lows(), lows)
         (beyond, near, other), _, _ = self.round([(beyond, core), (near, core), (lows, pair)])
         far = self.add(far, beyond)
         half = far.shape[0] // 2
@@ -1007,48 +1063,47 @@
         def beside(beyond, dz_near, far, dz):
             return self.add(far, beyond), steps.gate_back([dz, dz_near, dz, dz], 0)
 
-        (_, dz_near, across, moved, near_out), _, (far_out, dret0) = self.round(
-            [(beyond_out, core), (dz, core), (dz, pair), (early, swap), (near_out, core)],
+        (_, dz_near, across, near_out), _, (far_out, dret0) = self.round(
+            [(beyond_out, core), (dz, core), (dz, pair), (near_out, core)],
             beside, (far_out, dz), feed=2
+        )
+        (dz_beyond,), _, _ = self.round([(across, core)])
+        (moved, far_out), _, dret1 = self.round(
+            [(early, swap)],
+            lambda across, beyond: steps.gate_back([across, across, across, beyond], 1),
+            (across, dz_beyond), slow=[(far_out, pair)]
         )
         early = self.mine(early, moved)
         size = early.shape[0] // 2
         early = [early[:size][None], early[size:][None]]
-        (dz_beyond,), _, _ = self.round([(across, core)])
-        (one, two, far_out), _, dret1 = self.round(
-            [(early[0], by_one), (early[1], by_two)],
-            lambda across, beyond: steps.gate_back([across, across, across, beyond], 1),
-            (across, dz_beyond), slow=[(far_out, pair)]
+        (one, two), _, dpv = self.round(
+            [(early[0], by_one), (early[1], by_two)], steps.retention_back, (dret0, dret1)
         )
         early = [jnp.concatenate([early[0], one]), jnp.concatenate([early[1], two])]
-        (one, two), _, dpv = self.round(
-            [(early[0], by_two), (early[1], by_one)], steps.retention_back, (dret0, dret1)
-        )
         dz = [dz, dz_near, across, dz_beyond]
-        early = early, one, two
 
         (dlow,), _, output = self.round(
-            [(steps.late_lows().astype(BF), core)], lambda *parts: steps.output(parts),
+            [(steps.dlow.astype(BF), core)], lambda *parts: steps.output(parts),
             (own_out, near_out, far_out)
         )
-        dlow = self.core_sum(steps.late_lows(), dlow)
-        (other, moved_out), _, ((near, far, beyond), early) = self.round(
-            [(dlow, pair), (output, swap)],
-            lambda dpv, early: (steps.unfold_attn(256, (1, 2, 3), dpv), self.both_halves(*early)),
-            (dpv, early)
-        )
-        (beyond, near), _, late = self.round(
-            [(beyond, core), (near, core)],
-            lambda dlow, other: steps.late(self.pair_sum(dlow, other), dz), (dlow, other)
-        )
-        (moved,), _, ((own,), far) = self.round(
-            [(late, swap)],
-            lambda dpv, far, beyond: (steps.unfold_attn(256, (0,), dpv), self.add(far, beyond)),
-            (dpv, far, beyond)
-        )
-        late = self.mine(late, moved)
-        size = late.shape[0] // 2
-        late = [late[:size][None], late[size:][None]]
+        dlow = self.core_sum(steps.dlow, dlow)
+        (other, moved_out, one, two), _, ((own, near, far, beyond), rest) = self.round(
+            [(dlow, pair), (output, swap), (early[0], by_two), (early[1], by_one)],
+            lambda dpv, lows: (steps.unfold_attn(256, (0, 1, 2, 3), dpv),
+                               steps.late_rest(lows, dz)),
+            (dpv, lows)
+        )
+        (beyond, near, moved), _, shares = self.round(
+            [(beyond, core), (near, core), (rest, swap)],
+            lambda dlow, other: steps.late_shares(self.pair_sum(dlow, other)), (dlow, other)
+        )
+        rest = self.mine(rest, moved)
+        (moved,), _, (far, early) = self.round(
+            [(shares, swap)],
+            lambda far, beyond, *early: (self.add(far, beyond), self.both_halves(*early)),
+            (far, beyond, early, one, two)
+        )
+        late = [self.mine(shares, moved)[None], rest[None]]
         (one, two, far0), _, _ = self.round(
             [(late[0], by_one), (late[1], by_two), (far[:half], pair)]
         )
@@ -1132,8 +1187,6 @@
     heads_local = wide // VALUE_DIM
     head_ids = (rank * heads_local + jnp.arange(heads_local, dtype=jnp.int32)).astype(F32)
     rates = jnp.log(1.0 - jnp.exp2(-5.0 - head_ids))
-    cosine, sine_table = rotation_tables(seq_length, HALF)
-
     class Steps:
         def tables(self, line, other):
             return packed(line[0, seq_length]), packed(other[0, seq_length])
@@ -1159,13 +1212,17 @@
             self.mlp_in = pick(adapt_mlp_in, work_id).T
             self.down_back = pick(adapt_down_back, work_id)
 
+        def rotation(self):
+            self.turn = rotation_tables(seq_length, HALF)
+            return self.turn
+
         def norm(self, x):
             return norm_rows(x, gain_attn)
 
         def project(self, a, w_qk, w_v):
             return project(
                 ids, chunks, a, self.attn_in, jnp.concatenate([self.qk_out, self.v_out], axis=1),
-                (w_qk, w_v), (cosine, sine_table)
+                (w_qk, w_v), self.turn
             )
 
         def mix(self, a, qk, v, low, w_g):
@@ -1178,12 +1235,15 @@
         def join(self, x, parts):
             return join_rows(x, parts, gain_mlp)
 
+        def mlp_begin(self, b, w_mg, w_mu):
+            return mlp_begin(ids, b, self.mlp_in, w_mg, w_mu)
+
         def hidden_grad(self, dy, w_d):
             return hidden_grad(ids, dy, self.down_back, self.down_in, w_d)
 
     steps = Steps()
     ((w_v, w_qk, w_g, w_o, w_d, w_mg, w_mu), x, a, grad, dy, (qk, v, low_a),
-     (o, nrm, inverse, gate), low_o, middle, b, (dhid, low_dy)) = links.forward(
+     (o, nrm, inverse, gate), low_o, middle, b, (dhid, low_dy, begun, late_weights)) = links.forward(
         [weight_value, jnp.concatenate([weight_query, weight_key], axis=1), weight_gate,
          weight_out, weight_mlp_down, weight_mlp_gate, weight_mlp_up],
         tokens[0], cotangent[0], own_line, steps,
@@ -1200,12 +1260,11 @@
 
     class Back:
         early_height = 3 * RANK
-        late_height = 5 * RANK
 
         def mlp(self):
-            (self.hid, self.dgate, self.dup, _, self.lows, self.grad_hidden,
+            (self.hid, self.dgate, self.dup, self.lows, self.grad_hidden,
              self.grad_down) = mlp(
-                ids, b, mlp_in, mg_out, mu_out, down_in, dhid, low_dy, w_mg, w_mu
+                ids, begun, b, mg_out, mu_out, down_in, dhid, low_dy, *late_weights
             )
 
         def unfold_mlp(self, size, blocks, dup=None):
@@ -1225,10 +1284,13 @@
                 parts[0].astype(F32) + parts[1].astype(F32) + parts[2].astype(F32)
             )).astype(BF)
 
+        def early_lows(self):
+            return jnp.concatenate([self.lows, low_o])
+
         def early(self, lows):
             mark = jnp.full((RANK, span), work_id, F32).astype(BF)
             return jnp.concatenate(
-                [share(lows, span, ((RANK, dy), (2 * RANK, b))),
+                [share(lows[:3 * RANK], span, ((RANK, dy), (2 * RANK, b))),
                  halves(jnp.concatenate([self.grad_hidden, self.grad_down])), mark]
             )
 
@@ -1244,20 +1306,20 @@
             self.low_parts = self.low_parts + (dlow,)
             return dret
 
-        def late_lows(self):
-            return jnp.concatenate([self.dlow, low_o])
-
         def retention_back(self, *dret):
             (self.dpq, self.dpk, self.dpv, self.dlow, self.grad_q, self.grad_k,
              self.grad_v) = retention_back(
-                spots, rates, seg_col, seg_row, cosine, sine_table, low_a,
+                spots, rates, seg_col, seg_row, *steps.turn, low_a,
                 jnp.concatenate(self.low_parts, axis=1), qk_out, v_out, qk, v, *dret
             )
             return self.dpv
 
-        def late(self, lows, dz):
+        def late_shares(self, lows):
+            return share(lows, span, ((4 * RANK, a),))
+
+        def late_rest(self, lows, dz):
             return jnp.concatenate(
-                [share(lows, span, ((4 * RANK, a), (RANK, dz))),
+                [share(lows[3 * RANK:], span, ((RANK, dz),)),
                  halves(jnp.concatenate(
                      [jnp.concatenate([self.grad_q, self.grad_k], axis=1), self.grad_v,
                       self.grad_gate.astype(BF), self.grad_out_in.astype(BF)]
@@ -1299,13 +1361,13 @@
         def place_late(self, arrays, at):
             if self.total is not None:
                 arrays, at = [self.total(arrays[0])], self.order
-            pitch = self.late_height
-            shares = nt * pitch
+            pitch = 4 * RANK
+            first, rest = nt * pitch, nt * (pitch + RANK)
             return place(
                 at[self.order], arrays,
-                ((0, 4 * RANK, "shares", pitch), (4 * RANK, RANK, "shares", pitch),
-                 (shares, RANK, "two", 4 * RANK), (shares + RANK, 2 * RANK, "halves", 4 * RANK),
-                 (shares + 3 * RANK, RANK, "halves", 4 * RANK)), nt
+                ((0, pitch, "shares", pitch), (first, RANK, "shares", RANK),
+                 (rest, RANK, "two", 4 * RANK), (rest + RANK, 2 * RANK, "halves", 4 * RANK),
+                 (rest + 3 * RANK, RANK, "halves", 4 * RANK)), nt
             )
 
     output, input_grad, early, late = links.backward(Back())

time: 600 us -> 593 us (0.988)
  waiting for transfers between devices: 235 us -> 219 us
  starting transfers between devices: 80.3 us -> 86.4 us
    ppermute x75 -> x76, waiting for transfers between devices: 235 us -> 219 us  [send(): lax.ppermute(x, ('dp', 'tensor'), self.pairs(place))]
    pallas_call x0 -> x1, Pallas kernels: none -> 12.3 us  [mlp_begin(): pl.pallas_call(partial(mlp_begin_kernel, len(act), len(gate_pieces)), gri...]
    pallas_call x1, Pallas kernels: 18.4 us -> 11.3 us  [mlp(): pl.pallas_call(partial(mlp_kernel, len(act), len(gate_pieces)), grid=(wid...]
    ppermute x75 -> x76, starting transfers between devices: 73 us -> 78.9 us  [send(): lax.ppermute(x, ('dp', 'tensor'), self.pairs(place))]
    pallas_call x4 -> x3, Pallas kernels: 44.9 us -> 41 us  [unfold(): pl.pallas_call(partial(unfold_kernel, (count, len(acts), len(weights))),...]
    unnamed x244 -> x248, local copies, waits for them, and re-layouts: 14.9 us -> 16.4 us
    select_n x13 -> x12, other arithmetic: 12.6 us -> 12.2 us  [mine(): return jnp.where(self.home, own, other)]
  transfers between devices with their start and end apart: 83 -> 84, of which waited for: 40 -> 33; matrix products, arithmetic and copies ran while one was open for 10% -> 10% of each run, Pallas kernels for 28% -> 31%
where the time goes in v4:
time: 593 us; the launch traced here: 583 us
  waiting for transfers between devices  219 us (37%)
  Pallas kernels  195 us (33%)
  starting transfers between devices  86.4 us (15%)
  other arithmetic  43.3 us (7%)
  local copies, waits for them, and re-layouts  29.7 us (5%)
  between operations  9.88 us (2%)
    ppermute x76, waiting for transfers between devices, send(): lax.ppermute(x, ('dp', 'tensor'), self.pairs(place))  219 us
    ppermute x76, starting transfers between devices, send(): lax.ppermute(x, ('dp', 'tensor'), self.pairs(place))  78.9 us
    pallas_call x3, Pallas kernels, unfold(): pl.pallas_call(partial(unfold_kernel, (count, len(acts), len(weights))),...  41 us
    pallas_call x2, Pallas kernels, project(): pl.pallas_call(partial(project_kernel, (len(act), len(weights[0]), length...  27.2 us
    pallas_call x2, Pallas kernels, fold(): pl.pallas_call(fold_kernel, grid=(subs,), in_specs=[smem(), full(act.shap...  21.1 us
    pallas_call x2, Pallas kernels, gate_back(): pl.pallas_call(partial(gate_back_kernel, len(act)), grid=(width // block,...  17.9 us
    unnamed x248, local copies, waits for them, and re-layouts  16.4 us
    pallas_call x2, Pallas kernels, place(): pl.pallas_call(partial(place_kernel, layout, len(arrays)), grid_spec=pltp...  14.5 us
  transfers between devices with their start and end apart: 84, of which 33 were waited for; matrix products, arithmetic and copies ran while one was open for 10% of the time, Pallas kernels for 31%

profile of v4, /device:TPU:1, one launch (start us, length us, event | category | flops | bytes accessed | tf_op | source)
XLA Modules:
  0.0 583.2 jit_solution(1381458777643950709)
XLA Ops:
  11.8 5.7 collective-permute-start.7
  29.0 6.7 %collective-permute-done.2 = bf16[2,256,1024]{2,1,0:T(8,128)(2,1)} collective-permute-done((bf16[2,256,1024]{2,1,0:T(8,128)(2,1)}, bf16[2,256,1024]{2,1,0:T(8,128)(2,1)}, u32[]{:S(2)}, u32[]{:S(2)}) %collective-permute-start.2) | collective-permute-done | bytes 1048608 | tf_op jit(solution)/shard_map/ppermute | solution.py:863
  53.0 10.2 %collective-permute-done.9 = bf16[2,256,1024]{2,1,0:T(8,128)(2,1)} collective-permute-done((bf16[2,256,1024]{2,1,0:T(8,128)(2,1)}, bf16[2,256,1024]{2,1,0:T(8,128)(2,1)}, u32[]{:S(2)}, u32[]{:S(2)}) %collective-permute-start.9) | collective-permute-done | bytes 1048608 | tf_op jit(solution)/shard_map/ppermute | solution.py:863
  70.6 15.2 %collective-permute-done.14.refs_7_.refs_21_ = bf16[2,256,1024]{2,1,0:T(8,128)(2,1)S(1)} collective-permute-done((bf16[2,256,1024]{2,1,0:T(8,128)(2,1)S(1)}, bf16[2,256,1024]{2,1,0:T(8,128)(2,1)S(1)}, u32[]{:S(2)}, u32[]{:S(2)}) %collective-permute-start.14) | collective-permute-done | bytes 1048608 | tf_op jit(solution)/shard_map/ppermute | solution.py:863
  90.5 28.6 %collective-permute-done.12 = bf16[256,2048]{1,0:T(8,128)(2,1)S(1)} collective-permute-done((bf16[256,2048]{1,0:T(8,128)(2,1)S(1)}, bf16[256,2048]{1,0:T(8,128)(2,1)S(1)}, u32[]{:S(2)}, u32[]{:S(2)}) %collective-permute-start.12) | collective-permute-done | bytes 1048608 | tf_op jit(solution)/shard_map/ppermute | solution.py:863
  126.4 4.2 collective-permute-start.23
  130.6 9.7 %collective-permute-done.20.refs_5_.refs_29_ = bf16[2,256,1024]{2,1,0:T(8,128)(2,1)} collective-permute-done((bf16[2,256,1024]{2,1,0:T(8,128)(2,1)S(1)}, bf16[2,256,1024]{2,1,0:T(8,128)(2,1)}, u32[]{:S(2)}, u32[]{:S(2)}) %collective-permute-start.20) | collective-permute-done | bytes 1048608 | tf_op jit(solution)/shard_map/ppermute | solution.py:863
  145.5 25.2 %collective-permute-done.19 = bf16[2,1024,256]{2,1,0:T(8,128)(2,1)} collective-permute-done((bf16[2,1024,256]{2,1,0:T(8,128)(2,1)}, bf16[2,1024,256]{2,1,0:T(8,128)(2,1)}, u32[]{:S(2)}, u32[]{:S(2)}) %collective-permute-start.19) | collective-permute-done | bytes 1048608 | tf_op jit(solution)/shard_map/ppermute | solution.py:863
  183.0 17.7 %project.2 = (bf16[1024,1024]{1,0:T(8,128)(2,1)}, bf16[1024,1024]{1,0:T(8,128)(2,1)}, bf16[64,1024]{1,0:T(8,128)(2,1)S(1)}) custom-call(s32[8]{0:T(128)S(1)} %xor.51.ids, s32[4]{0:T(128)S(1)} %broadcast_xor_fusion.chunks, bf16[64,2048]{1,0:T(8,128)(2,1)S(1)} %dynamic-slice_bitcast_fusion.low_in, bf16[64,2048]{1,0:T(8,128)(2,1)S(1)} %maximum_maximum_fusion.3.low_out, ...), custom_call_target="tpu_custom_call" | custom-call | flops 1 | bytes 1 | tf_op jit(solution)/shard_map/project/pallas_call | solution.py:191
  211.3 9.5 %project.3.gate = bf16[1024,1024]{1,0:T(8,128)(2,1)} custom-call(s32[8]{0:T(128)S(1)} %xor.51.ids, s32[4]{0:T(128)S(1)} %broadcast_xor_fusion.chunks, bf16[64,1024]{1,0:T(8,128)(2,1)S(1)} %get-tuple-element.265.low_in.low_gate.low, bf16[64,1024]{1,0:T(8,128)(2,1)S(1)} %concatenate.124.low_out, bf16[256,2048]{1,0:T(8,128)(2,1)} %norm_rows.1.refs_2_.refs_0_, ...), custom_call_target="tpu_custom_call" | custom-call | flops 1 | bytes 1 | tf_op jit(solution)/shard_map/project/pallas_call | solution.py:191
  220.9 8.7 %retention.1 = (bf16[1024,1024]{1,0:T(8,128)(2,1)}, bf16[1024,1024]{1,0:T(8,128)(2,1)}, f32[2,1024,128]{2,1,0:T(8,128)}) custom-call(s32[4]{0:T(128)S(1)} %fusion.5.spots, f32[2]{0:T(128)S(1)} %copy-done.55, s32[1024,1]{1,0:T(8,128)S(1)} %copy-done.25, s32[1,1024]{1,0:T(1,128)S(1)} %get-tuple-element.493.seg_row, bf16[1024,1024]{1,0:T(8,128)(2,1)S(1)} %copy-done.2, ...), custom_call_target="tpu_custom_call" | custom-call | flops 1 | bytes 1 | tf_op jit(solution)/shard_map/retention/pallas_call | solution.py:243
  229.6 3.3 collective-permute-done.30
  237.4 10.5 %fold.2 = (bf16[256,2048]{1,0:T(8,128)(2,1)}, bf16[256,2048]{1,0:T(8,128)(2,1)}, bf16[256,2048]{1,0:T(8,128)(2,1)}, bf16[256,2048]{1,0:T(8,128)(2,1)}, f32[16,1024]{1,0:T(8,128)S(1)}) custom-call(s32[8]{0:T(128)S(1)} %xor.51.ids, bf16[1024,1024]{1,0:T(8,128)(2,1)} %get-tuple-element.280.act.hold, bf16[16,1024]{1,0:T(8,128)(2,1)S(1)} %copy-done.45, ...), custom_call_target="tpu_custom_call" | custom-call | flops 1 | bytes 1 | tf_op jit(solution)/shard_map/fold/pallas_call | solution.py:286
  247.9 3.4 collective-permute-done.37
  251.3 6.4 %collective-permute-done.34.refs_6_.refs_2_ = bf16[2,1024,256]{2,1,0:T(8,128)(2,1)S(1)} collective-permute-done((bf16[2,1024,256]{2,1,0:T(8,128)(2,1)}, bf16[2,1024,256]{2,1,0:T(8,128)(2,1)S(1)}, u32[]{:S(2)}, u32[]{:S(2)}) %collective-permute-start.34) | collective-permute-done | bytes 1048608 | tf_op jit(solution)/shard_map/ppermute | solution.py:863
  257.7 5.2 collective-permute-done.36
  273.6 19.9 %collective-permute-done.40.part2 = bf16[256,2048]{1,0:T(8,128)(2,1)S(1)} collective-permute-done((bf16[256,2048]{1,0:T(8,128)(2,1)S(1)}, bf16[256,2048]{1,0:T(8,128)(2,1)S(1)}, u32[]{:S(2)}, u32[]{:S(2)}) %collective-permute-start.40) | collective-permute-done | bytes 1048608 | tf_op jit(solution)/shard_map/ppermute | solution.py:863
  300.5 19.0 %collective-permute-done.43.refs_2_.refs_6_ = bf16[256,2048]{1,0:T(8,128)(2,1)S(1)} collective-permute-done((bf16[256,2048]{1,0:T(8,128)(2,1)S(1)}, bf16[256,2048]{1,0:T(8,128)(2,1)S(1)}, u32[]{:S(2)}, u32[]{:S(2)}) %collective-permute-start.43) | collective-permute-done | bytes 1048608 | tf_op jit(solution)/shard_map/ppermute | solution.py:863
  320.0 3.5 collective-permute-done.47.refs_9_.refs_15_
  328.2 9.0 %hidden_grad.1 = (bf16[1024,1024]{1,0:T(8,128)(2,1)}, bf16[16,1024]{1,0:T(8,128)(2,1)S(1)}) custom-call(s32[8]{0:T(128)S(1)} %xor.51.ids, bf16[16,2048]{1,0:T(8,128)(2,1)S(1)} %dynamic-slice_bitcast_fusion.2.low_back.low_out, bf16[16,1024]{1,0:T(8,128)(2,1)S(1)} %copy-done.46, bf16[256,2048]{1,0:T(8,128)(2,1)S(1)} %broadcast_select_fusion.7.refs_0_.grad_in, ...), custom_call_target="tpu_custom_call" | custom-call | flops 1 | bytes 1 | tf_op jit(solution)/shard_map/hidden_grad/pallas_call | solution.py:361
  337.3 12.3 %mlp_begin.1 = (f32[1024,1024]{1,0:T(8,128)}, f32[1024,1024]{1,0:T(8,128)}, bf16[32,1024]{1,0:T(8,128)(2,1)S(1)}) custom-call(s32[8]{0:T(128)S(1)} %xor.51.ids, bf16[32,2048]{1,0:T(8,128)(2,1)S(1)} %dynamic-slice_bitcast_fusion.1.low_in, bf16[256,2048]{1,0:T(8,128)(2,1)S(1)} %get-tuple-element.307.refs_0_.refs_4_, ...), custom_call_target="tpu_custom_call" | custom-call | flops 1 | bytes 1 | tf_op jit(solution)/shard_map/mlp_begin/pallas_call | solution.py:397
  350.7 11.3 %mlp.1 = (bf16[1024,1024]{1,0:T(8,128)(2,1)}, bf16[1024,1024]{1,0:T(8,128)(2,1)}, bf16[1024,1024]{1,0:T(8,128)(2,1)}, f32[48,1024]{1,0:T(8,128)S(1)}, bf16[32,10...) custom-call(s32[8]{0:T(128)S(1)} %xor.51.ids, f32[1024,1024]{1,0:T(8,128)} %get-tuple-element.316.gate_in, ...), custom_call_target="tpu_custom_call" | custom-call | flops 1 | bytes 1 | tf_op jit(solution)/shard_map/mlp/pallas_call | solution.py:451
  363.7 13.1 %unfold.3 = (bf16[256,2048]{1,0:T(8,128)(2,1)}, bf16[256,2048]{1,0:T(8,128)(2,1)}, bf16[256,2048]{1,0:T(8,128)(2,1)}) custom-call(s32[8]{0:T(128)S(1)} %xor.51.ids, bf16[32,2048]{1,0:T(8,128)(2,1)S(1)} %dynamic-slice_bitcast_fusion.1.low_in, f32[32,1024]{1,0:T(8,128)S(1)} %slice.187.refs_0_.refs_1_.refs_2_, f32[32,1024]{1,0:T(8,128)S(1)} %slice.187.refs_0_.refs_1_.refs_2_, ...), custom_call_target="tpu_custom_call" | custom-call | flops 1 | bytes 1 | tf_op jit(solution)/shard_map/unfold/pallas_call | solution.py:506
  377.8 3.9 collective-permute-done.54
  383.9 4.7 share.3
  388.7 6.6 %unfold.4.part0 = bf16[256,2048]{1,0:T(8,128)(2,1)} custom-call(s32[8]{0:T(128)S(1)} %xor.51.ids, bf16[32,2048]{1,0:T(8,128)(2,1)S(1)} %dynamic-slice_bitcast_fusion.1.low_in, f32[32,1024]{1,0:T(8,128)S(1)} %slice.187.refs_0_.refs_1_.refs_2_, bf16[1024,1024]{1,0:T(8,128)(2,1)} %get-tuple-element.332.refs_3_.refs_5_.refs_7_.refs_1_, ...), custom_call_target="tpu_custom_call" | custom-call | flops 1 | bytes 1 | tf_op jit(solution)/shard_map/unfold/pallas_call | solution.py:506
  395.3 10.6 %fold.3 = (bf16[256,2048]{1,0:T(8,128)(2,1)}, bf16[256,2048]{1,0:T(8,128)(2,1)}, bf16[256,2048]{1,0:T(8,128)(2,1)}, bf16[256,2048]{1,0:T(8,128)(2,1)}, f32[16,1024]{1,0:T(8,128)}) custom-call(s32[8]{0:T(128)S(1)} %xor.51.ids, bf16[1024,1024]{1,0:T(8,128)(2,1)} %get-tuple-element.341.act, bf16[16,1024]{1,0:T(8,128)(2,1)S(1)} %copy-done.47, ...), custom_call_target="tpu_custom_call" | custom-call | flops 1 | bytes 1 | tf_op jit(solution)/shard_map/fold/pallas_call | solution.py:286
  406.8 3.5 rms_back.2.refs_0_.grad_in
  413.4 3.1 collective-permute-done.57.refs_1_
  417.5 8.8 %gate_back.2 = (bf16[512,1024]{1,0:T(8,128)(2,1)}, bf16[512,1024]{1,0:T(8,128)(2,1)}, bf16[16,512]{1,0:T(8,128)(2,1)}, f32[64,512]{1,0:T(8,128)}, f32[16,1024]{1,0:T(8,128)}, /*index=5*/f32[16,1024]{1,0:T(8,128)}) custom-call(s32[8]{0:T(128)} %copy-done.48, bf16[16,2048]{1,0:T(8,128)(2,1)} %copy-done.39, bf16[16,1024]{1,0:T(8,128)(2,1)} %get-tuple-element.470.low_in, ...), custom_call_target="tpu_custom_call" | custom-call | flops 1 | bytes 1 | tf_op jit(solution)/shard_map/gate_back/pallas_call | solution.py:564
  428.3 8.6 %collective-permute-done.59.refs_0_.refs_2_ = bf16[256,2048]{1,0:T(8,128)(2,1)S(1)} collective-permute-done((bf16[256,2048]{1,0:T(8,128)(2,1)}, bf16[256,2048]{1,0:T(8,128)(2,1)S(1)}, u32[]{:S(2)}, u32[]{:S(2)}) %collective-permute-start.59) | collective-permute-done | bytes 1048608 | tf_op jit(solution)/shard_map/ppermute | solution.py:863
  441.6 5.2 collective-permute-start.62
  447.0 9.0 %gate_back.3 = (bf16[512,1024]{1,0:T(8,128)(2,1)}, bf16[512,1024]{1,0:T(8,128)(2,1)}, bf16[16,512]{1,0:T(8,128)(2,1)}, f32[64,512]{1,0:T(8,128)}, f32[16,1024]{1,0:T(8,128)}, /*index=5*/f32[16,1024]{1,0:T(8,128)}) custom-call(s32[8]{0:T(128)} %copy-done.48, bf16[16,2048]{1,0:T(8,128)(2,1)} %copy-done.39, bf16[16,1024]{1,0:T(8,128)(2,1)} %get-tuple-element.470.low_in, ...), custom_call_target="tpu_custom_call" | custom-call | flops 1 | bytes 1 | tf_op jit(solution)/shard_map/gate_back/pallas_call | solution.py:564
  458.5 11.7 %retention_back.1 = (bf16[1024,512]{1,0:T(8,128)(2,1)S(1)}, bf16[1024,512]{1,0:T(8,128)(2,1)S(1)}, bf16[1024,1024]{1,0:T(8,128)(2,1)}, f32[64,1024]{1,0:T(8,128)...) custom-call(s32[4]{0:T(128)S(1)} %copy-done.54, f32[2]{0:T(128)S(1)} %copy-done.56, ...), custom_call_target="tpu_custom_call" | custom-call | flops 1 | bytes 1 | tf_op jit(solution)/shard_map/retention_back/pallas_call | solution.py:651
  474.2 4.2 collective-permute-start.67
  481.1 3.3 share.4
  484.4 21.3 %unfold.5 = (bf16[256,2048]{1,0:T(8,128)(2,1)}, bf16[256,2048]{1,0:T(8,128)(2,1)}, bf16[256,2048]{1,0:T(8,128)(2,1)}, bf16[256,2048]{1,0:T(8,128)(2,1)}) custom-call(s32[8]{0:T(128)S(1)} %copy-done.49, bf16[64,2048]{1,0:T(8,128)(2,1)S(1)} %dynamic-slice_bitcast_fusion.low_in, f32[64,1024]{1,0:T(8,128)S(1)} %get-tuple-element.369.refs_0_.refs_1_.refs_2_.refs_3_, ...), custom_call_target="tpu_custom_call" | custom-call | flops 1 | bytes 1 | tf_op jit(solution)/shard_map/unfold/pallas_call | solution.py:506
  506.4 3.7 collective-permute-start.73
  510.2 3.7 share.5
  519.1 8.8 %collective-permute-done.74 = bf16[256,512]{1,0:T(8,128)(2,1)S(1)} collective-permute-done((bf16[256,512]{1,0:T(8,128)(2,1)S(1)}, bf16[256,512]{1,0:T(8,128)(2,1)S(1)}, u32[]{:S(2)}, u32[]{:S(2)}) %collective-permute-start.74) | collective-permute-done | bytes 262176 | tf_op jit(solution)/shard_map/ppermute | solution.py:863
  529.6 5.6 collective-permute-done.77
  535.3 3.8 collective-permute-done.75
  540.5 5.2 collective-permute-done.80
  551.3 3.9 collective-permute-start.81
  560.5 6.8 %place.2 = (f32[8,16,2048]{2,1,0:T(8,128)}, f32[8,32,2048]{2,1,0:T(8,128)}, f32[8,32,1024]{2,1,0:T(8,128)}, f32[8,16,1024]{2,1,0:T(8,128)}) custom-call(s32[9]{0:T(128)S(1)} %pad_add_fusion.order, bf16[4,304,512]{2,1,0:T(8,128)(2,1)} %copy-done.69, bf16[4,304,512]{2,1,0:T(8,128)(2,1)} %copy-done.94), custom_call_target="tpu_custom_call" | custom-call | flops 1 | bytes 1 | tf_op jit(solution)/shard_map/place/pallas_call | solution.py:739
  567.3 7.7 %place.3 = (f32[8,64,2048]{2,1,0:T(8,128)}, f32[8,16,2048]{2,1,0:T(8,128)}, f32[8,2,16,512]{3,2,1,0:T(8,128)}, f32[8,32,1024]{2,1,0:T(8,128)}, f32[8,16,1024]{2,1,0:T(8,128)}) custom-call(s32[9]{0:T(128)S(1)} %pad_add_fusion.order, bf16[4,448,512]{2,1,0:T(8,128)(2,1)} %copy-done.68, bf16[4,448,512]{2,1,0:T(8,128)(2,1)} %collective-permute-done.83.refs_1_), custom_call_target="tpu_custom_call" | custom-call | flops 1 | bytes 1 | tf_op jit(solution)/shard_map/place/pallas_call | solution.py:739
  575.0 4.9 collective-permute-done.81
  579.9 3.1 select_bitcast_fusion
  (503 shorter events, 153.5 us)
Async XLA Ops:
  3.3 16.4 %collective-permute-start.4 = (bf16[256,1024]{1,0:T(8,128)(2,1)}, bf16[256,1024]{1,0:T(8,128)(2,1)}, u32[]{:S(2)}, u32[]{:S(2)}) collective-permute-start(bf16[256,1024]{1,0:T(8,128)(2,1)} %param.33), channel_id=1, source_target_pairs={{0,4},{1,5},{2,6},{3,7},{4,0},{5,1},{6,2},{7,3},{8,12},{9,13},{10,... | collective-permute-start | bytes 1572872 | tf_op jit(solution)/shard_map/ppermute | solution.py:857
  3.5 18.5 %collective-permute-start.5 = (bf16[1024,256]{1,0:T(8,128)(2,1)}, bf16[1024,256]{1,0:T(8,128)(2,1)}, u32[]{:S(2)}, u32[]{:S(2)}) collective-permute-start(bf16[1024,256]{1,0:T(8,128)(2,1)} %param.34), channel_id=1, source_target_pairs={{0,4},{1,5},{2,6},{3,7},{4,0},{5,1},{6,2},{7,3},{8,12},{9,13},{10,... | collective-permute-start | bytes 1572872 | tf_op jit(solution)/shard_map/ppermute | solution.py:857
  3.8 20.8 %collective-permute-start.6 = (bf16[1024,256]{1,0:T(8,128)(2,1)}, bf16[1024,256]{1,0:T(8,128)(2,1)}, u32[]{:S(2)}, u32[]{:S(2)}) collective-permute-start(bf16[1024,256]{1,0:T(8,128)(2,1)} %param.37), channel_id=1, source_target_pairs={{0,4},{1,5},{2,6},{3,7},{4,0},{5,1},{6,2},{7,3},{8,12},{9,13},{10,... | collective-permute-start | bytes 1572872 | tf_op jit(solution)/shard_map/ppermute | solution.py:857
  6.9 28.8 %collective-permute-start.2 = (bf16[2,256,1024]{2,1,0:T(8,128)(2,1)}, bf16[2,256,1024]{2,1,0:T(8,128)(2,1)}, u32[]{:S(2)}, u32[]{:S(2)}) collective-permute-start(bf16[2,256,1024]{2,1,0:T(8,128)(2,1)} %pad_maximum_fusion.1), channel_id=1, source_target_pairs={{0,2},{1,3},{6,4},{7,5},{8,10},{9,11},{14,12},{15,13},{16,18},{17,... | collective-permute-start | bytes 3145736 | tf_op jit(solution)/shard_map/ppermute | solution.py:863
  40.7 22.4 %collective-permute-start.9 = (bf16[2,256,1024]{2,1,0:T(8,128)(2,1)}, bf16[2,256,1024]{2,1,0:T(8,128)(2,1)}, u32[]{:S(2)}, u32[]{:S(2)}) collective-permute-start(bf16[2,256,1024]{2,1,0:T(8,128)(2,1)} %pad_maximum_fusion), channel_id=1, source_target_pairs={{0,2},{1,3},{6,4},{7,5},{8,10},{9,11},{14,12},{15,13},{16,18},{17,... | collective-permute-start | bytes 3145736 | tf_op jit(solution)/shard_map/ppermute | solution.py:863
  42.0 22.8 %collective-permute-start.10 = (bf16[2,256,1024]{2,1,0:T(8,128)(2,1)S(1)}, bf16[2,256,1024]{2,1,0:T(8,128)(2,1)}, u32[]{:S(2)}, u32[]{:S(2)}) collective-permute-start(bf16[2,256,1024]{2,1,0:T(8,128)(2,1)S(1)} %broadcast_select_fusion.6.refs_10_.refs_24_), channel_id=1, source_target_pairs={{0,8},{1,9},{2,10},{3,11},{4,12},{5,13},{6,14},{7,15},{8,0},{9,1},... | collective-permute-start | bytes 3145736 | tf_op jit(solution)/shard_map/ppermute | solution.py:863
  44.0 21.3 %collective-permute-start.11 = (bf16[2,256,1024]{2,1,0:T(8,128)(2,1)S(1)}, bf16[2,256,1024]{2,1,0:T(8,128)(2,1)}, u32[]{:S(2)}, u32[]{:S(2)}) collective-permute-start(bf16[2,256,1024]{2,1,0:T(8,128)(2,1)S(1)} %broadcast_select_fusion.6.refs_10_.refs_24_), channel_id=1, source_target_pairs={{0,16},{1,17},{2,18},{3,19},{4,20},{5,21},{6,22},{7,23},{8,24},{9,... | collective-permute-start | bytes 3145736 | tf_op jit(solution)/shard_map/ppermute | solution.py:863
  65.3 20.5 %collective-permute-start.14 = (bf16[2,256,1024]{2,1,0:T(8,128)(2,1)S(1)}, bf16[2,256,1024]{2,1,0:T(8,128)(2,1)S(1)}, u32[]{:S(2)}, u32[]{:S(2)}) collective-permute-start(bf16[2,256,1024]{2,1,0:T(8,128)(2,1)S(1)} %broadcast_select_fusion.5.refs_6_.refs_20_), channel_id=1, source_target_pairs={{0,8},{1,9},{2,10},{3,11},{4,12},{5,13},{6,14},{7,15},{8,0},{9,1},... | collective-permute-start | bytes 3145736 | tf_op jit(solution)/shard_map/ppermute | solution.py:863
  66.1 21.8 %collective-permute-start.15 = (bf16[2,256,1024]{2,1,0:T(8,128)(2,1)}, bf16[2,256,1024]{2,1,0:T(8,128)(2,1)S(1)}, u32[]{:S(2)}, u32[]{:S(2)}) collective-permute-start(bf16[2,256,1024]{2,1,0:T(8,128)(2,1)} %collective-permute-done.10.refs_11_.refs_25_), channel_id=1, source_target_pairs={{0,16},{1,17},{2,18},{3,19},{4,20},{5,21},{6,22},{7,23},{8,24},{9,... | collective-permute-start | bytes 3145736 | tf_op jit(solution)/shard_map/ppermute | solution.py:863
  67.4 51.8 %collective-permute-start.12 = (bf16[256,2048]{1,0:T(8,128)(2,1)S(1)}, bf16[256,2048]{1,0:T(8,128)(2,1)S(1)}, u32[]{:S(2)}, u32[]{:S(2)}) collective-permute-start(bf16[256,2048]{1,0:T(8,128)(2,1)S(1)} %bitcast.139), channel_id=1, source_target_pairs={{2,4},{3,5},{4,2},{5,3},{10,12},{11,13},{12,10},{13,11},{18,20},{1... | collective-permute-start | bytes 3145736 | tf_op jit(solution)/shard_map/ppermute | solution.py:863
  69.3 51.3 %collective-permute-start.13 = (bf16[2,256,1024]{2,1,0:T(8,128)(2,1)S(1)}, bf16[2,256,1024]{2,1,0:T(8,128)(2,1)S(1)}, u32[]{:S(2)}, u32[]{:S(2)}) collective-permute-start(bf16[2,256,1024]{2,1,0:T(8,128)(2,1)S(1)} %copy-done.105), channel_id=1, source_target_pairs={{0,2},{1,3},{6,4},{7,5},{8,10},{9,11},{14,12},{15,13},{16,18},{17,... | collective-permute-start | bytes 3145736 | tf_op jit(solution)/shard_map/ppermute | solution.py:863
  87.9 35.0 %collective-permute-start.17 = (bf16[2,256,1024]{2,1,0:T(8,128)(2,1)S(1)}, bf16[2,256,1024]{2,1,0:T(8,128)(2,1)S(1)}, u32[]{:S(2)}, u32[]{:S(2)}) collective-permute-start(bf16[2,256,1024]{2,1,0:T(8,128)(2,1)S(1)} %broadcast_select_fusion.5.refs_6_.refs_20_), channel_id=1, source_target_pairs={{0,16},{1,17},{2,18},{3,19},{4,20},{5,21},{6,22},{7,23},{8,24},{9,... | collective-permute-start | bytes 3145736 | tf_op jit(solution)/shard_map/ppermute | solution.py:863
  89.2 33.8 %collective-permute-start.16 = (bf16[112,1024]{1,0:T(8,128)(2,1)S(1)}, bf16[112,1024]{1,0:T(8,128)(2,1)S(1)}, u32[]{:S(2)}, u32[]{:S(2)}) collective-permute-start(bf16[112,1024]{1,0:T(8,128)(2,1)S(1)} %get-tuple-element.235), channel_id=1, source_target_pairs={{0,2},{1,3},{6,4},{7,5},{8,10},{9,11},{14,12},{15,13},{16,18},{17,... | collective-permute-start | bytes 688136 | tf_op jit(solution)/shard_map/ppermute | solution.py:863
  125.1 45.7 %collective-permute-start.19 = (bf16[2,1024,256]{2,1,0:T(8,128)(2,1)}, bf16[2,1024,256]{2,1,0:T(8,128)(2,1)}, u32[]{:S(2)}, u32[]{:S(2)}) collective-permute-start(bf16[2,1024,256]{2,1,0:T(8,128)(2,1)} %pad_maximum_fusion.3), channel_id=1, source_target_pairs={{0,2},{1,3},{6,4},{7,5},{8,10},{9,11},{14,12},{15,13},{16,18},{17,... | collective-permute-start | bytes 3145736 | tf_op jit(solution)/shard_map/ppermute | solution.py:863
  126.4 46.1 %collective-permute-start.18 = (bf16[256,2048]{1,0:T(8,128)(2,1)}, bf16[256,2048]{1,0:T(8,128)(2,1)}, u32[]{:S(2)}, u32[]{:S(2)}) collective-permute-start(bf16[256,2048]{1,0:T(8,128)(2,1)} %norm_rows.1.refs_2_.refs_0_), channel_id=1, source_target_pairs={{0,1},{1,0},{2,3},{3,2},{4,5},{5,4},{6,7},{7,6},{8,9},{9,8},{10,11... | collective-permute-start | bytes 3145736 | tf_op jit(solution)/shard_map/ppermute | solution.py:863
  126.4 47.4 %collective-permute-start.23 = (bf16[256,2048]{1,0:T(8,128)(2,1)}, bf16[256,2048]{1,0:T(8,128)(2,1)}, u32[]{:S(2)}, u32[]{:S(2)}) collective-permute-start(bf16[256,2048]{1,0:T(8,128)(2,1)} %bitcast.140), channel_id=1, source_target_pairs={{2,4},{3,5},{4,2},{5,3},{10,12},{11,13},{12,10},{13,11},{18,20},{1... | collective-permute-start | bytes 3145736 | tf_op jit(solution)/shard_map/ppermute | solution.py:863
  140.3 33.6 %collective-permute-start.22 = (bf16[2,256,1024]{2,1,0:T(8,128)(2,1)}, bf16[2,256,1024]{2,1,0:T(8,128)(2,1)}, u32[]{:S(2)}, u32[]{:S(2)}) collective-permute-start(bf16[2,256,1024]{2,1,0:T(8,128)(2,1)} %copy-done.72), channel_id=1, source_target_pairs={{0,8},{1,9},{2,10},{3,11},{4,12},{5,13},{6,14},{7,15},{8,0},{9,1},... | collective-permute-start | bytes 3145736 | tf_op jit(solution)/shard_map/ppermute | solution.py:863
  141.5 32.4 %collective-permute-start.24 = (bf16[2,256,1024]{2,1,0:T(8,128)(2,1)}, bf16[2,256,1024]{2,1,0:T(8,128)(2,1)}, u32[]{:S(2)}, u32[]{:S(2)}) collective-permute-start(bf16[2,256,1024]{2,1,0:T(8,128)(2,1)} %collective-permute-done.20.refs_5_.refs_29_), channel_id=1, source_target_pairs={{0,16},{1,17},{2,18},{3,19},{4,20},{5,21},{6,22},{7,23},{8,24},{9,... | collective-permute-start | bytes 3145736 | tf_op jit(solution)/shard_map/ppermute | solution.py:863
  175.0 27.7 %collective-permute-start.25 = (bf16[2,1024,256]{2,1,0:T(8,128)(2,1)S(1)}, bf16[2,1024,256]{2,1,0:T(8,128)(2,1)S(1)}, u32[]{:S(2)}, u32[]{:S(2)}) collective-permute-start(bf16[2,1024,256]{2,1,0:T(8,128)(2,1)S(1)} %copy-done.103), channel_id=1, source_target_pairs={{0,2},{1,3},{6,4},{7,5},{8,10},{9,11},{14,12},{15,13},{16,18},{17,... | collective-permute-start | bytes 3145736 | tf_op jit(solution)/shard_map/ppermute | solution.py:863
  176.3 28.5 %collective-permute-start.26 = (bf16[2,1024,256]{2,1,0:T(8,128)(2,1)S(1)}, bf16[2,1024,256]{2,1,0:T(8,128)(2,1)}, u32[]{:S(2)}, u32[]{:S(2)}) collective-permute-start(bf16[2,1024,256]{2,1,0:T(8,128)(2,1)S(1)} %broadcast_select_fusion.1.refs_0_.refs_2_), channel_id=1, source_target_pairs={{0,8},{1,9},{2,10},{3,11},{4,12},{5,13},{6,14},{7,15},{8,0},{9,1},... | collective-permute-start | bytes 3145736 | tf_op jit(solution)/shard_map/ppermute | solution.py:863
  177.3 27.6 %collective-permute-start.29 = (bf16[2,1024,256]{2,1,0:T(8,128)(2,1)S(1)}, bf16[2,1024,256]{2,1,0:T(8,128)(2,1)S(1)}, u32[]{:S(2)}, u32[]{:S(2)}) collective-permute-start(bf16[2,1024,256]{2,1,0:T(8,128)(2,1)S(1)} %broadcast_select_fusion.1.refs_0_.refs_2_), channel_id=1, source_target_pairs={{0,16},{1,17},{2,18},{3,19},{4,20},{5,21},{6,22},{7,23},{8,24},{9,... | collective-permute-start | bytes 3145736 | tf_op jit(solution)/shard_map/ppermute | solution.py:863
  205.8 27.0 %collective-permute-start.30 = (bf16[2,256,1024]{2,1,0:T(8,128)(2,1)}, bf16[2,256,1024]{2,1,0:T(8,128)(2,1)}, u32[]{:S(2)}, u32[]{:S(2)}) collective-permute-start(bf16[2,256,1024]{2,1,0:T(8,128)(2,1)} %pad_maximum_fusion.5), channel_id=1, source_target_pairs={{0,2},{1,3},{6,4},{7,5},{8,10},{9,11},{14,12},{15,13},{16,18},{17,... | collective-permute-start | bytes 3145736 | tf_op jit(solution)/shard_map/ppermute | solution.py:863
  207.3 27.0 %collective-permute-start.31 = (bf16[2,1024,256]{2,1,0:T(8,128)(2,1)}, bf16[2,1024,256]{2,1,0:T(8,128)(2,1)}, u32[]{:S(2)}, u32[]{:S(2)}) collective-permute-start(bf16[2,1024,256]{2,1,0:T(8,128)(2,1)} %collective-permute-done.26.refs_1_.refs_3_), channel_id=1, source_target_pairs={{0,16},{1,17},{2,18},{3,19},{4,20},{5,21},{6,22},{7,23},{8,24},{9,... | collective-permute-start | bytes 3145736 | tf_op jit(solution)/shard_map/ppermute | solution.py:863
  208.3 26.0 %collective-permute-start.32 = (bf16[2,1024,256]{2,1,0:T(8,128)(2,1)}, bf16[2,1024,256]{2,1,0:T(8,128)(2,1)}, u32[]{:S(2)}, u32[]{:S(2)}) collective-permute-start(bf16[2,1024,256]{2,1,0:T(8,128)(2,1)} %broadcast_select_fusion.refs_4_.refs_0_), channel_id=1, source_target_pairs={{0,8},{1,9},{2,10},{3,11},{4,12},{5,13},{6,14},{7,15},{8,0},{9,1},... | collective-permute-start | bytes 3145736 | tf_op jit(solution)/shard_map/ppermute | solution.py:863
  209.5 24.8 %collective-permute-start.33 = (bf16[128,2048]{1,0:T(8,128)(2,1)}, bf16[128,2048]{1,0:T(8,128)(2,1)}, u32[]{:S(2)}, u32[]{:S(2)}) collective-permute-start(bf16[128,2048]{1,0:T(8,128)(2,1)} %get-tuple-element.277), channel_id=1, source_target_pairs={{0,1},{1,0},{2,3},{3,2},{4,5},{5,4},{6,7},{7,6},{8,9},{9,8},{10,11... | collective-permute-start | bytes 1572872 | tf_op jit(solution)/shard_map/ppermute | solution.py:863
  234.3 23.4 %collective-permute-start.34 = (bf16[2,1024,256]{2,1,0:T(8,128)(2,1)}, bf16[2,1024,256]{2,1,0:T(8,128)(2,1)S(1)}, u32[]{:S(2)}, u32[]{:S(2)}) collective-permute-start(bf16[2,1024,256]{2,1,0:T(8,128)(2,1)} %broadcast_select_fusion.refs_4_.refs_0_), channel_id=1, source_target_pairs={{0,16},{1,17},{2,18},{3,19},{4,20},{5,21},{6,22},{7,23},{8,24},{9,... | collective-permute-start | bytes 3145736 | tf_op jit(solution)/shard_map/ppermute | solution.py:863
  234.6 23.1 %collective-permute-start.35 = (bf16[2,256,1024]{2,1,0:T(8,128)(2,1)S(1)}, bf16[2,256,1024]{2,1,0:T(8,128)(2,1)S(1)}, u32[]{:S(2)}, u32[]{:S(2)}) collective-permute-start(bf16[2,256,1024]{2,1,0:T(8,128)(2,1)S(1)} %broadcast_select_fusion.3.refs_4_.refs_9_.refs_3_), channel_id=1, source_target_pairs={{0,8},{1,9},{2,10},{3,11},{4,12},{5,13},{6,14},{7,15},{8,0},{9,1},... | collective-permute-start | bytes 3145736 | tf_op jit(solution)/shard_map/ppermute | solution.py:863
  235.2 27.7 %collective-permute-start.36 = (bf16[2,256,1024]{2,1,0:T(8,128)(2,1)S(1)}, bf16[2,256,1024]{2,1,0:T(8,128)(2,1)S(1)}, u32[]{:S(2)}, u32[]{:S(2)}) collective-permute-start(bf16[2,256,1024]{2,1,0:T(8,128)(2,1)S(1)} %copy-done.102), channel_id=1, source_target_pairs={{0,2},{1,3},{6,4},{7,5},{8,10},{9,11},{14,12},{15,13},{16,18},{17,... | collective-permute-start | bytes 3145736 | tf_op jit(solution)/shard_map/ppermute | solution.py:863
  267.4 26.1 %collective-permute-start.40 = (bf16[256,2048]{1,0:T(8,128)(2,1)S(1)}, bf16[256,2048]{1,0:T(8,128)(2,1)S(1)}, u32[]{:S(2)}, u32[]{:S(2)}) collective-permute-start(bf16[256,2048]{1,0:T(8,128)(2,1)S(1)} %add_convert_fusion.4), channel_id=1, source_target_pairs={{0,1},{1,0},{2,3},{3,2},{4,5},{5,4},{6,7},{7,6},{8,9},{9,8},{10,11... | collective-permute-start | bytes 3145736 | tf_op jit(solution)/shard_map/ppermute | solution.py:863
  270.3 25.3 %collective-permute-start.41 = (bf16[2,1024,256]{2,1,0:T(8,128)(2,1)S(1)}, bf16[2,1024,256]{2,1,0:T(8,128)(2,1)S(1)}, u32[]{:S(2)}, u32[]{:S(2)}) collective-permute-start(bf16[2,1024,256]{2,1,0:T(8,128)(2,1)S(1)} %collective-permute-done.34.refs_6_.refs_2_), channel_id=1, source_target_pairs={{0,8},{1,9},{2,10},{3,11},{4,12},{5,13},{6,14},{7,15},{8,0},{9,1},... | collective-permute-start | bytes 3145736 | tf_op jit(solution)/shard_map/ppermute | solution.py:863
  271.0 24.7 %collective-permute-start.42 = (bf16[2,256,1024]{2,1,0:T(8,128)(2,1)S(1)}, bf16[2,256,1024]{2,1,0:T(8,128)(2,1)S(1)}, u32[]{:S(2)}, u32[]{:S(2)}) collective-permute-start(bf16[2,256,1024]{2,1,0:T(8,128)(2,1)S(1)} %broadcast_select_fusion.3.refs_4_.refs_9_.refs_3_), channel_id=1, source_target_pairs={{0,16},{1,17},{2,18},{3,19},{4,20},{5,21},{6,22},{7,23},{8,24},{9,... | collective-permute-start | bytes 3145736 | tf_op jit(solution)/shard_map/ppermute | solution.py:863
  295.6 23.9 %collective-permute-start.43 = (bf16[256,2048]{1,0:T(8,128)(2,1)S(1)}, bf16[256,2048]{1,0:T(8,128)(2,1)S(1)}, u32[]{:S(2)}, u32[]{:S(2)}) collective-permute-start(bf16[256,2048]{1,0:T(8,128)(2,1)S(1)} %get-tuple-element.307.refs_0_.refs_4_), channel_id=1, source_target_pairs={{0,1},{1,0},{2,3},{3,2},{4,5},{5,4},{6,7},{7,6},{8,9},{9,8},{10,11... | collective-permute-start | bytes 3145736 | tf_op jit(solution)/shard_map/ppermute | solution.py:863
  296.8 23.2 %collective-permute-start.44 = (bf16[2,256,1024]{2,1,0:T(8,128)(2,1)S(1)}, bf16[2,256,1024]{2,1,0:T(8,128)(2,1)S(1)}, u32[]{:S(2)}, u32[]{:S(2)}) collective-permute-start(bf16[2,256,1024]{2,1,0:T(8,128)(2,1)S(1)} %broadcast_select_fusion.2.refs_7_.refs_13_), channel_id=1, source_target_pairs={{0,8},{1,9},{2,10},{3,11},{4,12},{5,13},{6,14},{7,15},{8,0},{9,1},... | collective-permute-start | bytes 3145736 | tf_op jit(solution)/shard_map/ppermute | solution.py:863
  297.5 22.5 %collective-permute-start.45 = (bf16[256,2048]{1,0:T(8,128)(2,1)S(1)}, bf16[256,2048]{1,0:T(8,128)(2,1)S(1)}, u32[]{:S(2)}, u32[]{:S(2)}) collective-permute-start(bf16[256,2048]{1,0:T(8,128)(2,1)S(1)} %broadcast_select_fusion.7.refs_0_.grad_in), channel_id=1, source_target_pairs={{0,4},{1,5},{2,6},{3,7},{4,0},{5,1},{6,2},{7,3},{8,12},{9,13},{10,... | collective-permute-start | bytes 3145736 | tf_op jit(solution)/shard_map/ppermute | solution.py:863
  299.3 20.7 %collective-permute-start.46 = (bf16[256,2048]{1,0:T(8,128)(2,1)S(1)}, bf16[256,2048]{1,0:T(8,128)(2,1)S(1)}, u32[]{:S(2)}, u32[]{:S(2)}) collective-permute-start(bf16[256,2048]{1,0:T(8,128)(2,1)S(1)} %constant_dynamic-update-slice_fusion.14.refs_2_), channel_id=1, source_target_pairs={{0,4},{1,5},{2,6},{3,7},{4,0},{5,1},{6,2},{7,3},{8,12},{9,13},{10,... | collective-permute-start | bytes 3145736 | tf_op jit(solution)/shard_map/ppermute | solution.py:863
  299.3 24.2 %collective-permute-start.47 = (bf16[2,256,1024]{2,1,0:T(8,128)(2,1)S(1)}, bf16[2,256,1024]{2,1,0:T(8,128)(2,1)S(1)}, u32[]{:S(2)}, u32[]{:S(2)}) collective-permute-start(bf16[2,256,1024]{2,1,0:T(8,128)(2,1)S(1)} %broadcast_select_fusion.2.refs_7_.refs_13_), channel_id=1, source_target_pairs={{0,16},{1,17},{2,18},{3,19},{4,20},{5,21},{6,22},{7,23},{8,24},{9,... | collective-permute-start | bytes 3145736 | tf_op jit(solution)/shard_map/ppermute | solution.py:863
  324.9 24.8 %collective-permute-start.50 = (bf16[2,256,1024]{2,1,0:T(8,128)(2,1)S(1)}, bf16[2,256,1024]{2,1,0:T(8,128)(2,1)S(1)}, u32[]{:S(2)}, u32[]{:S(2)}) collective-permute-start(bf16[2,256,1024]{2,1,0:T(8,128)(2,1)S(1)} %collective-permute-done.42.refs_6_.refs_11_.refs_5_), channel_id=1, source_target_pairs={{0,8},{1,9},{2,10},{3,11},{4,12},{5,13},{6,14},{7,15},{8,0},{9,1},... | collective-permute-start | bytes 3145736 | tf_op jit(solution)/shard_map/ppermute | solution.py:863
  325.6 24.0 %collective-permute-start.51 = (bf16[2,256,1024]{2,1,0:T(8,128)(2,1)S(1)}, bf16[2,256,1024]{2,1,0:T(8,128)(2,1)S(1)}, u32[]{:S(2)}, u32[]{:S(2)}) collective-permute-start(bf16[2,256,1024]{2,1,0:T(8,128)(2,1)S(1)} %collective-permute-done.44.refs_8_.refs_14_), channel_id=1, source_target_pairs={{0,16},{1,17},{2,18},{3,19},{4,20},{5,21},{6,22},{7,23},{8,24},{9,... | collective-permute-start | bytes 3145736 | tf_op jit(solution)/shard_map/ppermute | solution.py:863
  383.1 23.7 %collective-permute-start.56 = (bf16[256,2048]{1,0:T(8,128)(2,1)}, bf16[256,2048]{1,0:T(8,128)(2,1)}, u32[]{:S(2)}, u32[]{:S(2)}) collective-permute-start(bf16[256,2048]{1,0:T(8,128)(2,1)} %add_convert_fusion.3), channel_id=1, source_target_pairs={{0,1},{1,0},{2,3},{3,2},{4,5},{5,4},{6,7},{7,6},{8,9},{9,8},{10,11... | collective-permute-start | bytes 3145736 | tf_op jit(solution)/shard_map/ppermute | solution.py:863
  412.5 24.4 %collective-permute-start.59 = (bf16[256,2048]{1,0:T(8,128)(2,1)}, bf16[256,2048]{1,0:T(8,128)(2,1)S(1)}, u32[]{:S(2)}, u32[]{:S(2)}) collective-permute-start(bf16[256,2048]{1,0:T(8,128)(2,1)} %rms_back.2.refs_0_.grad_in), channel_id=1, source_target_pairs={{0,1},{1,0},{2,3},{3,2},{4,5},{5,4},{6,7},{7,6},{8,9},{9,8},{10,11... | collective-permute-start | bytes 3145736 | tf_op jit(solution)/shard_map/ppermute | solution.py:863
  412.6 24.4 %collective-permute-start.60 = (bf16[256,2048]{1,0:T(8,128)(2,1)}, bf16[256,2048]{1,0:T(8,128)(2,1)S(1)}, u32[]{:S(2)}, u32[]{:S(2)}) collective-permute-start(bf16[256,2048]{1,0:T(8,128)(2,1)} %get-tuple-element.359), channel_id=1, source_target_pairs={{0,4},{1,5},{2,6},{3,7},{4,0},{5,1},{6,2},{7,3},{8,12},{9,13},{10,... | collective-permute-start | bytes 3145736 | tf_op jit(solution)/shard_map/ppermute | solution.py:863
  446.9 24.6 %collective-permute-start.63 = (bf16[256,2048]{1,0:T(8,128)(2,1)S(1)}, bf16[256,2048]{1,0:T(8,128)(2,1)}, u32[]{:S(2)}, u32[]{:S(2)}) collective-permute-start(bf16[256,2048]{1,0:T(8,128)(2,1)S(1)} %add_convert_fusion.2), channel_id=1, source_target_pairs={{0,1},{1,0},{2,3},{3,2},{4,5},{5,4},{6,7},{7,6},{8,9},{9,8},{10,11... | collective-permute-start | bytes 3145736 | tf_op jit(solution)/shard_map/ppermute | solution.py:863
  474.2 31.6 %collective-permute-start.67 = (bf16[256,2048]{1,0:T(8,128)(2,1)S(1)}, bf16[256,2048]{1,0:T(8,128)(2,1)S(1)}, u32[]{:S(2)}, u32[]{:S(2)}) collective-permute-start(bf16[256,2048]{1,0:T(8,128)(2,1)S(1)} %add_convert_fusion.1), channel_id=1, source_target_pairs={{2,4},{3,5},{4,2},{5,3},{10,12},{11,13},{12,10},{13,11},{18,20},{1... | collective-permute-start | bytes 3145736 | tf_op jit(solution)/shard_map/ppermute | solution.py:863
  479.2 26.6 %collective-permute-start.69 = (bf16[2,152,512]{2,1,0:T(8,128)(2,1)S(1)}, bf16[2,152,512]{2,1,0:T(8,128)(2,1)S(1)}, u32[]{:S(2)}, u32[]{:S(2)}) collective-permute-start(bf16[2,152,512]{2,1,0:T(8,128)(2,1)S(1)} %pad_maximum_fusion.10), channel_id=1, source_target_pairs={{0,16},{1,17},{2,18},{3,19},{4,20},{5,21},{6,22},{7,23},{8,24},{9,... | collective-permute-start | bytes 933896 | tf_op jit(solution)/shard_map/ppermute | solution.py:863
  480.0 25.8 %collective-permute-start.70 = (bf16[2,152,512]{2,1,0:T(8,128)(2,1)S(1)}, bf16[2,152,512]{2,1,0:T(8,128)(2,1)S(1)}, u32[]{:S(2)}, u32[]{:S(2)}) collective-permute-start(bf16[2,152,512]{2,1,0:T(8,128)(2,1)S(1)} %pad_maximum_fusion.11), channel_id=1, source_target_pairs={{0,8},{1,9},{2,10},{3,11},{4,12},{5,13},{6,14},{7,15},{8,0},{9,1},... | collective-permute-start | bytes 933896 | tf_op jit(solution)/shard_map/ppermute | solution.py:863
  481.1 24.7 %collective-permute-start.68 = (bf16[64,1024]{1,0:T(8,128)(2,1)S(1)}, bf16[64,1024]{1,0:T(8,128)(2,1)S(1)}, u32[]{:S(2)}, u32[]{:S(2)}) collective-permute-start(bf16[64,1024]{1,0:T(8,128)(2,1)S(1)} %fusion.3), channel_id=1, source_target_pairs={{0,1},{1,0},{2,3},{3,2},{4,5},{5,4},{6,7},{7,6},{8,9},{9,8},{10,11... | collective-permute-start | bytes 393224 | tf_op jit(solution)/shard_map/ppermute | solution.py:863
  550.8 16.6 %collective-permute-start.83 = (bf16[4,448,512]{2,1,0:T(8,128)(2,1)S(1)}, bf16[4,448,512]{2,1,0:T(8,128)(2,1)}, u32[]{:S(2)}, u32[]{:S(2)}) collective-permute-start(bf16[4,448,512]{2,1,0:T(8,128)(2,1)S(1)} %maximum_maximum_fusion.refs_0_), channel_id=1, source_target_pairs={{0,4},{1,5},{2,6},{3,7},{4,0},{5,1},{6,2},{7,3},{8,12},{9,13},{10,... | collective-permute-start | bytes 5505032 | tf_op jit(solution)/shard_map/ppermute | solution.py:863
  551.3 28.6 %collective-permute-start.81 = (bf16[256,2048]{1,0:T(8,128)(2,1)}, bf16[256,2048]{1,0:T(8,128)(2,1)}, u32[]{:S(2)}, u32[]{:S(2)}) collective-permute-start(bf16[256,2048]{1,0:T(8,128)(2,1)} %get-tuple-element.417), channel_id=1, source_target_pairs={{2,4},{3,5},{4,2},{5,3},{10,12},{11,13},{12,10},{13,11},{18,20},{1... | collective-permute-start | bytes 3145736 | tf_op jit(solution)/shard_map/ppermute | solution.py:863
  (155 other events, 2546.6 us)

commit v5 on v4

--- a/solution.py
+++ b/solution.py
@@ -511,7 +511,7 @@
         + [pl.BlockSpec((size, act.shape[1]), lambda s, at=at: (at, 0)) for act, at in chosen]
         + [pl.BlockSpec((1,) + w.shape[1:], lambda s: (s, 0, 0)) for w in pieces],
         out_specs=[full((size, width))] * count,
-        out_shape=[far((size, width), BF)] * count,
+        out_shape=[jax.ShapeDtypeStruct((size, width), BF)] * count,
         compiler_params=params(48),
         cost_estimate=estimate(
             2 * count * size * depth * width, 2 * depth * width + 4 * count * size * depth

time: 593 us -> 589 us (level)
    unnamed x248 -> x242, local copies, waits for them, and re-layouts: 16.4 us -> 16.3 us
  transfers between devices with their start and end apart: 84 -> 84, of which waited for: 33 -> 33; matrix products, arithmetic and copies ran while one was open for 10% -> 10% of each run, Pallas kernels for 31% -> 30%
where the time goes in v5:
time: 589 us; the launch traced here: 580 us
  waiting for transfers between devices  219 us (37%)
  Pallas kernels  191 us (32%)
  starting transfers between devices  86.4 us (15%)
  other arithmetic  43.3 us (7%)
  local copies, waits for them, and re-layouts  29.7 us (5%)
  between operations  10.3 us (2%)
    ppermute x76, waiting for transfers between devices, send(): lax.ppermute(x, ('dp', 'tensor'), self.pairs(place))  219 us
    ppermute x76, starting transfers between devices, send(): lax.ppermute(x, ('dp', 'tensor'), self.pairs(place))  78.9 us
    pallas_call x3, Pallas kernels, unfold(): pl.pallas_call(partial(unfold_kernel, (count, len(acts), len(weights))),...  36.7 us
    pallas_call x2, Pallas kernels, project(): pl.pallas_call(partial(project_kernel, (len(act), len(weights[0]), length...  27.2 us
    pallas_call x2, Pallas kernels, fold(): pl.pallas_call(fold_kernel, grid=(subs,), in_specs=[smem(), full(act.shap...  21 us
    pallas_call x2, Pallas kernels, gate_back(): pl.pallas_call(partial(gate_back_kernel, len(act)), grid=(width // block,...  17.8 us
    unnamed x242, local copies, waits for them, and re-layouts  16.3 us
    pallas_call x2, Pallas kernels, place(): pl.pallas_call(partial(place_kernel, layout, len(arrays)), grid_spec=pltp...  15 us
  transfers between devices with their start and end apart: 84, of which 33 were waited for; matrix products, arithmetic and copies ran while one was open for 10% of the time, Pallas kernels for 30%

profile of v5, /device:TPU:1, one launch (start us, length us, event | category | flops | bytes accessed | tf_op | source)
XLA Modules:
  0.0 579.8 jit_solution(17403294185834932070)
XLA Ops:
  11.8 5.7 collective-permute-start.7
  29.0 6.7 %collective-permute-done.2 = bf16[2,256,1024]{2,1,0:T(8,128)(2,1)} collective-permute-done((bf16[2,256,1024]{2,1,0:T(8,128)(2,1)}, bf16[2,256,1024]{2,1,0:T(8,128)(2,1)}, u32[]{:S(2)}, u32[]{:S(2)}) %collective-permute-start.2) | collective-permute-done | bytes 1048608 | tf_op jit(solution)/shard_map/ppermute | solution.py:863
  53.0 10.1 %collective-permute-done.9 = bf16[2,256,1024]{2,1,0:T(8,128)(2,1)} collective-permute-done((bf16[2,256,1024]{2,1,0:T(8,128)(2,1)}, bf16[2,256,1024]{2,1,0:T(8,128)(2,1)}, u32[]{:S(2)}, u32[]{:S(2)}) %collective-permute-start.9) | collective-permute-done | bytes 1048608 | tf_op jit(solution)/shard_map/ppermute | solution.py:863
  70.6 15.2 %collective-permute-done.14.refs_7_.refs_21_ = bf16[2,256,1024]{2,1,0:T(8,128)(2,1)S(1)} collective-permute-done((bf16[2,256,1024]{2,1,0:T(8,128)(2,1)S(1)}, bf16[2,256,1024]{2,1,0:T(8,128)(2,1)S(1)}, u32[]{:S(2)}, u32[]{:S(2)}) %collective-permute-start.14) | collective-permute-done | bytes 1048608 | tf_op jit(solution)/shard_map/ppermute | solution.py:863
  90.5 28.6 %collective-permute-done.12 = bf16[256,2048]{1,0:T(8,128)(2,1)S(1)} collective-permute-done((bf16[256,2048]{1,0:T(8,128)(2,1)S(1)}, bf16[256,2048]{1,0:T(8,128)(2,1)S(1)}, u32[]{:S(2)}, u32[]{:S(2)}) %collective-permute-start.12) | collective-permute-done | bytes 1048608 | tf_op jit(solution)/shard_map/ppermute | solution.py:863
  126.4 4.2 collective-permute-start.23
  130.6 9.7 %collective-permute-done.20.refs_5_.refs_29_ = bf16[2,256,1024]{2,1,0:T(8,128)(2,1)} collective-permute-done((bf16[2,256,1024]{2,1,0:T(8,128)(2,1)S(1)}, bf16[2,256,1024]{2,1,0:T(8,128)(2,1)}, u32[]{:S(2)}, u32[]{:S(2)}) %collective-permute-start.20) | collective-permute-done | bytes 1048608 | tf_op jit(solution)/shard_map/ppermute | solution.py:863
  145.9 24.8 %collective-permute-done.19 = bf16[2,1024,256]{2,1,0:T(8,128)(2,1)} collective-permute-done((bf16[2,1024,256]{2,1,0:T(8,128)(2,1)}, bf16[2,1024,256]{2,1,0:T(8,128)(2,1)}, u32[]{:S(2)}, u32[]{:S(2)}) %collective-permute-start.19) | collective-permute-done | bytes 1048608 | tf_op jit(solution)/shard_map/ppermute | solution.py:863
  182.9 17.7 %project.2 = (bf16[1024,1024]{1,0:T(8,128)(2,1)}, bf16[1024,1024]{1,0:T(8,128)(2,1)}, bf16[64,1024]{1,0:T(8,128)(2,1)S(1)}) custom-call(s32[8]{0:T(128)S(1)} %xor.51.ids, s32[4]{0:T(128)S(1)} %broadcast_xor_fusion.chunks, bf16[64,2048]{1,0:T(8,128)(2,1)S(1)} %dynamic-slice_bitcast_fusion.low_in, bf16[64,2048]{1,0:T(8,128)(2,1)S(1)} %maximum_maximum_fusion.3.low_out, ...), custom_call_target="tpu_custom_call" | custom-call | flops 1 | bytes 1 | tf_op jit(solution)/shard_map/project/pallas_call | solution.py:191
  211.2 9.5 %project.3.gate = bf16[1024,1024]{1,0:T(8,128)(2,1)} custom-call(s32[8]{0:T(128)S(1)} %xor.51.ids, s32[4]{0:T(128)S(1)} %broadcast_xor_fusion.chunks, bf16[64,1024]{1,0:T(8,128)(2,1)S(1)} %get-tuple-element.265.low_in.low_gate.low, bf16[64,1024]{1,0:T(8,128)(2,1)S(1)} %concatenate.124.low_out, bf16[256,2048]{1,0:T(8,128)(2,1)} %norm_rows.1.refs_2_.refs_0_, ...), custom_call_target="tpu_custom_call" | custom-call | flops 1 | bytes 1 | tf_op jit(solution)/shard_map/project/pallas_call | solution.py:191
  220.7 8.7 %retention.1 = (bf16[1024,1024]{1,0:T(8,128)(2,1)}, bf16[1024,1024]{1,0:T(8,128)(2,1)}, f32[2,1024,128]{2,1,0:T(8,128)}) custom-call(s32[4]{0:T(128)S(1)} %fusion.5.spots, f32[2]{0:T(128)S(1)} %copy-done.53, s32[1024,1]{1,0:T(8,128)S(1)} %copy-done.25, s32[1,1024]{1,0:T(1,128)S(1)} %get-tuple-element.493.seg_row, bf16[1024,1024]{1,0:T(8,128)(2,1)S(1)} %copy-done.2, ...), custom_call_target="tpu_custom_call" | custom-call | flops 1 | bytes 1 | tf_op jit(solution)/shard_map/retention/pallas_call | solution.py:243
  229.5 3.4 collective-permute-done.30
  237.4 10.5 %fold.2 = (bf16[256,2048]{1,0:T(8,128)(2,1)}, bf16[256,2048]{1,0:T(8,128)(2,1)}, bf16[256,2048]{1,0:T(8,128)(2,1)}, bf16[256,2048]{1,0:T(8,128)(2,1)}, f32[16,1024]{1,0:T(8,128)S(1)}) custom-call(s32[8]{0:T(128)S(1)} %xor.51.ids, bf16[1024,1024]{1,0:T(8,128)(2,1)} %get-tuple-element.280.act.hold, bf16[16,1024]{1,0:T(8,128)(2,1)S(1)} %copy-done.43, ...), custom_call_target="tpu_custom_call" | custom-call | flops 1 | bytes 1 | tf_op jit(solution)/shard_map/fold/pallas_call | solution.py:286
  247.9 3.5 collective-permute-done.37
  251.4 6.3 %collective-permute-done.34.refs_6_.refs_2_ = bf16[2,1024,256]{2,1,0:T(8,128)(2,1)S(1)} collective-permute-done((bf16[2,1024,256]{2,1,0:T(8,128)(2,1)}, bf16[2,1024,256]{2,1,0:T(8,128)(2,1)S(1)}, u32[]{:S(2)}, u32[]{:S(2)}) %collective-permute-start.34) | collective-permute-done | bytes 1048608 | tf_op jit(solution)/shard_map/ppermute | solution.py:863
  257.7 5.1 collective-permute-done.36
  273.5 20.0 %collective-permute-done.40.part2 = bf16[256,2048]{1,0:T(8,128)(2,1)S(1)} collective-permute-done((bf16[256,2048]{1,0:T(8,128)(2,1)S(1)}, bf16[256,2048]{1,0:T(8,128)(2,1)S(1)}, u32[]{:S(2)}, u32[]{:S(2)}) %collective-permute-start.40) | collective-permute-done | bytes 1048608 | tf_op jit(solution)/shard_map/ppermute | solution.py:863
  300.5 19.0 %collective-permute-done.43.refs_2_.refs_6_ = bf16[256,2048]{1,0:T(8,128)(2,1)S(1)} collective-permute-done((bf16[256,2048]{1,0:T(8,128)(2,1)S(1)}, bf16[256,2048]{1,0:T(8,128)(2,1)S(1)}, u32[]{:S(2)}, u32[]{:S(2)}) %collective-permute-start.43) | collective-permute-done | bytes 1048608 | tf_op jit(solution)/shard_map/ppermute | solution.py:863
  320.0 3.4 collective-permute-done.47.refs_9_.refs_15_
  328.2 9.0 %hidden_grad.1 = (bf16[1024,1024]{1,0:T(8,128)(2,1)}, bf16[16,1024]{1,0:T(8,128)(2,1)S(1)}) custom-call(s32[8]{0:T(128)S(1)} %xor.51.ids, bf16[16,2048]{1,0:T(8,128)(2,1)S(1)} %dynamic-slice_bitcast_fusion.2.low_back.low_out, bf16[16,1024]{1,0:T(8,128)(2,1)S(1)} %copy-done.44, bf16[256,2048]{1,0:T(8,128)(2,1)S(1)} %broadcast_select_fusion.7.refs_0_.grad_in, ...), custom_call_target="tpu_custom_call" | custom-call | flops 1 | bytes 1 | tf_op jit(solution)/shard_map/hidden_grad/pallas_call | solution.py:361
  337.3 12.3 %mlp_begin.1 = (f32[1024,1024]{1,0:T(8,128)}, f32[1024,1024]{1,0:T(8,128)}, bf16[32,1024]{1,0:T(8,128)(2,1)S(1)}) custom-call(s32[8]{0:T(128)S(1)} %xor.51.ids, bf16[32,2048]{1,0:T(8,128)(2,1)S(1)} %dynamic-slice_bitcast_fusion.1.low_in, bf16[256,2048]{1,0:T(8,128)(2,1)S(1)} %get-tuple-element.307.refs_0_.refs_4_, ...), custom_call_target="tpu_custom_call" | custom-call | flops 1 | bytes 1 | tf_op jit(solution)/shard_map/mlp_begin/pallas_call | solution.py:397
  350.6 11.3 %mlp.1 = (bf16[1024,1024]{1,0:T(8,128)(2,1)}, bf16[1024,1024]{1,0:T(8,128)(2,1)}, bf16[1024,1024]{1,0:T(8,128)(2,1)}, f32[48,1024]{1,0:T(8,128)S(1)}, bf16[32,10...) custom-call(s32[8]{0:T(128)S(1)} %xor.51.ids, f32[1024,1024]{1,0:T(8,128)} %get-tuple-element.316.gate_in, ...), custom_call_target="tpu_custom_call" | custom-call | flops 1 | bytes 1 | tf_op jit(solution)/shard_map/mlp/pallas_call | solution.py:451
  363.7 11.5 %unfold.3 = (bf16[256,2048]{1,0:T(8,128)(2,1)S(1)}, bf16[256,2048]{1,0:T(8,128)(2,1)S(1)}, bf16[256,2048]{1,0:T(8,128)(2,1)S(1)}) custom-call(s32[8]{0:T(128)S(1)} %xor.51.ids, bf16[32,2048]{1,0:T(8,128)(2,1)S(1)} %dynamic-slice_bitcast_fusion.1.low_in, f32[32,1024]{1,0:T(8,128)S(1)} %slice.187.refs_0_.refs_1_.refs_2_, ...), custom_call_target="tpu_custom_call" | custom-call | flops 1 | bytes 1 | tf_op jit(solution)/shard_map/unfold/pallas_call | solution.py:506
  376.2 3.9 collective-permute-done.54
  382.5 4.7 share.3
  387.2 5.6 unfold.4.part0
  392.9 10.6 %fold.3 = (bf16[256,2048]{1,0:T(8,128)(2,1)}, bf16[256,2048]{1,0:T(8,128)(2,1)}, bf16[256,2048]{1,0:T(8,128)(2,1)}, bf16[256,2048]{1,0:T(8,128)(2,1)}, f32[16,1024]{1,0:T(8,128)}) custom-call(s32[8]{0:T(128)S(1)} %xor.51.ids, bf16[1024,1024]{1,0:T(8,128)(2,1)} %get-tuple-element.341.act, bf16[16,1024]{1,0:T(8,128)(2,1)S(1)} %copy-done.45, ...), custom_call_target="tpu_custom_call" | custom-call | flops 1 | bytes 1 | tf_op jit(solution)/shard_map/fold/pallas_call | solution.py:286
  405.3 3.5 rms_back.2.refs_0_.grad_in
  411.8 3.1 collective-permute-done.57.refs_1_
  416.0 8.8 %gate_back.2 = (bf16[512,1024]{1,0:T(8,128)(2,1)}, bf16[512,1024]{1,0:T(8,128)(2,1)}, bf16[16,512]{1,0:T(8,128)(2,1)}, f32[64,512]{1,0:T(8,128)}, f32[16,1024]{1,0:T(8,128)}, /*index=5*/f32[16,1024]{1,0:T(8,128)}) custom-call(s32[8]{0:T(128)} %copy-done.46, bf16[16,2048]{1,0:T(8,128)(2,1)} %copy-done.38, bf16[16,1024]{1,0:T(8,128)(2,1)} %get-tuple-element.470.low_in, ...), custom_call_target="tpu_custom_call" | custom-call | flops 1 | bytes 1 | tf_op jit(solution)/shard_map/gate_back/pallas_call | solution.py:564
  426.7 8.7 %collective-permute-done.59.refs_0_.refs_2_ = bf16[256,2048]{1,0:T(8,128)(2,1)S(1)} collective-permute-done((bf16[256,2048]{1,0:T(8,128)(2,1)}, bf16[256,2048]{1,0:T(8,128)(2,1)S(1)}, u32[]{:S(2)}, u32[]{:S(2)}) %collective-permute-start.59) | collective-permute-done | bytes 1048608 | tf_op jit(solution)/shard_map/ppermute | solution.py:863
  440.1 5.3 collective-permute-start.62
  445.5 9.0 %gate_back.3 = (bf16[512,1024]{1,0:T(8,128)(2,1)}, bf16[512,1024]{1,0:T(8,128)(2,1)}, bf16[16,512]{1,0:T(8,128)(2,1)}, f32[64,512]{1,0:T(8,128)}, f32[16,1024]{1,0:T(8,128)}, /*index=5*/f32[16,1024]{1,0:T(8,128)}) custom-call(s32[8]{0:T(128)} %copy-done.46, bf16[16,2048]{1,0:T(8,128)(2,1)} %copy-done.38, bf16[16,1024]{1,0:T(8,128)(2,1)} %get-tuple-element.470.low_in, ...), custom_call_target="tpu_custom_call" | custom-call | flops 1 | bytes 1 | tf_op jit(solution)/shard_map/gate_back/pallas_call | solution.py:564
  456.9 11.7 %retention_back.1 = (bf16[1024,512]{1,0:T(8,128)(2,1)S(1)}, bf16[1024,512]{1,0:T(8,128)(2,1)S(1)}, bf16[1024,1024]{1,0:T(8,128)(2,1)}, f32[64,1024]{1,0:T(8,128)...) custom-call(s32[4]{0:T(128)S(1)} %copy-done.52, f32[2]{0:T(128)S(1)} %copy-done.54, ...), custom_call_target="tpu_custom_call" | custom-call | flops 1 | bytes 1 | tf_op jit(solution)/shard_map/retention_back/pallas_call | solution.py:651
  472.6 4.2 collective-permute-start.67
  479.6 3.3 share.4
  482.8 19.5 %unfold.5 = (bf16[256,2048]{1,0:T(8,128)(2,1)S(1)}, bf16[256,2048]{1,0:T(8,128)(2,1)S(1)}, bf16[256,2048]{1,0:T(8,128)(2,1)S(1)}, bf16[256,2048]{1,0:T(8,128)(2,1)S(1)}) custom-call(s32[8]{0:T(128)S(1)} %copy-done.47, bf16[64,2048]{1,0:T(8,128)(2,1)S(1)} %dynamic-slice_bitcast_fusion.low_in, ...), custom_call_target="tpu_custom_call" | custom-call | flops 1 | bytes 1 | tf_op jit(solution)/shard_map/unfold/pallas_call | solution.py:506
  503.0 3.7 collective-permute-start.73
  506.8 3.6 share.5
  515.8 8.8 %collective-permute-done.74 = bf16[256,512]{1,0:T(8,128)(2,1)S(1)} collective-permute-done((bf16[256,512]{1,0:T(8,128)(2,1)S(1)}, bf16[256,512]{1,0:T(8,128)(2,1)S(1)}, u32[]{:S(2)}, u32[]{:S(2)}) %collective-permute-start.74) | collective-permute-done | bytes 262176 | tf_op jit(solution)/shard_map/ppermute | solution.py:863
  526.2 5.6 collective-permute-done.77
  531.9 3.8 collective-permute-done.75
  537.1 5.2 collective-permute-done.80
  547.9 4.1 collective-permute-start.81
  557.2 7.0 %place.2 = (f32[8,16,2048]{2,1,0:T(8,128)}, f32[8,32,2048]{2,1,0:T(8,128)}, f32[8,32,1024]{2,1,0:T(8,128)}, f32[8,16,1024]{2,1,0:T(8,128)}) custom-call(s32[9]{0:T(128)S(1)} %pad_add_fusion.order, bf16[4,304,512]{2,1,0:T(8,128)(2,1)} %copy-done.67, bf16[4,304,512]{2,1,0:T(8,128)(2,1)} %copy-done.92), custom_call_target="tpu_custom_call" | custom-call | flops 1 | bytes 1 | tf_op jit(solution)/shard_map/place/pallas_call | solution.py:739
  564.2 8.0 %place.3 = (f32[8,64,2048]{2,1,0:T(8,128)}, f32[8,16,2048]{2,1,0:T(8,128)}, f32[8,2,16,512]{3,2,1,0:T(8,128)}, f32[8,32,1024]{2,1,0:T(8,128)}, f32[8,16,1024]{2,1,0:T(8,128)}) custom-call(s32[9]{0:T(128)S(1)} %pad_add_fusion.order, bf16[4,448,512]{2,1,0:T(8,128)(2,1)} %copy-done.66, bf16[4,448,512]{2,1,0:T(8,128)(2,1)} %collective-permute-done.83.refs_1_), custom_call_target="tpu_custom_call" | custom-call | flops 1 | bytes 1 | tf_op jit(solution)/shard_map/place/pallas_call | solution.py:739
  572.2 4.2 collective-permute-done.81
  576.5 3.1 select_bitcast_fusion
  (497 shorter events, 154.1 us)
Async XLA Ops:
  3.3 16.4 %collective-permute-start.4 = (bf16[256,1024]{1,0:T(8,128)(2,1)}, bf16[256,1024]{1,0:T(8,128)(2,1)}, u32[]{:S(2)}, u32[]{:S(2)}) collective-permute-start(bf16[256,1024]{1,0:T(8,128)(2,1)} %param.33), channel_id=1, source_target_pairs={{0,4},{1,5},{2,6},{3,7},{4,0},{5,1},{6,2},{7,3},{8,12},{9,13},{10,... | collective-permute-start | bytes 1572872 | tf_op jit(solution)/shard_map/ppermute | solution.py:857
  3.5 18.5 %collective-permute-start.5 = (bf16[1024,256]{1,0:T(8,128)(2,1)}, bf16[1024,256]{1,0:T(8,128)(2,1)}, u32[]{:S(2)}, u32[]{:S(2)}) collective-permute-start(bf16[1024,256]{1,0:T(8,128)(2,1)} %param.34), channel_id=1, source_target_pairs={{0,4},{1,5},{2,6},{3,7},{4,0},{5,1},{6,2},{7,3},{8,12},{9,13},{10,... | collective-permute-start | bytes 1572872 | tf_op jit(solution)/shard_map/ppermute | solution.py:857
  3.8 20.8 %collective-permute-start.6 = (bf16[1024,256]{1,0:T(8,128)(2,1)}, bf16[1024,256]{1,0:T(8,128)(2,1)}, u32[]{:S(2)}, u32[]{:S(2)}) collective-permute-start(bf16[1024,256]{1,0:T(8,128)(2,1)} %param.37), channel_id=1, source_target_pairs={{0,4},{1,5},{2,6},{3,7},{4,0},{5,1},{6,2},{7,3},{8,12},{9,13},{10,... | collective-permute-start | bytes 1572872 | tf_op jit(solution)/shard_map/ppermute | solution.py:857
  6.9 28.8 %collective-permute-start.2 = (bf16[2,256,1024]{2,1,0:T(8,128)(2,1)}, bf16[2,256,1024]{2,1,0:T(8,128)(2,1)}, u32[]{:S(2)}, u32[]{:S(2)}) collective-permute-start(bf16[2,256,1024]{2,1,0:T(8,128)(2,1)} %pad_maximum_fusion.1), channel_id=1, source_target_pairs={{0,2},{1,3},{6,4},{7,5},{8,10},{9,11},{14,12},{15,13},{16,18},{17,... | collective-permute-start | bytes 3145736 | tf_op jit(solution)/shard_map/ppermute | solution.py:863
  40.7 22.4 %collective-permute-start.9 = (bf16[2,256,1024]{2,1,0:T(8,128)(2,1)}, bf16[2,256,1024]{2,1,0:T(8,128)(2,1)}, u32[]{:S(2)}, u32[]{:S(2)}) collective-permute-start(bf16[2,256,1024]{2,1,0:T(8,128)(2,1)} %pad_maximum_fusion), channel_id=1, source_target_pairs={{0,2},{1,3},{6,4},{7,5},{8,10},{9,11},{14,12},{15,13},{16,18},{17,... | collective-permute-start | bytes 3145736 | tf_op jit(solution)/shard_map/ppermute | solution.py:863
  42.0 22.8 %collective-permute-start.10 = (bf16[2,256,1024]{2,1,0:T(8,128)(2,1)S(1)}, bf16[2,256,1024]{2,1,0:T(8,128)(2,1)}, u32[]{:S(2)}, u32[]{:S(2)}) collective-permute-start(bf16[2,256,1024]{2,1,0:T(8,128)(2,1)S(1)} %broadcast_select_fusion.6.refs_10_.refs_24_), channel_id=1, source_target_pairs={{0,8},{1,9},{2,10},{3,11},{4,12},{5,13},{6,14},{7,15},{8,0},{9,1},... | collective-permute-start | bytes 3145736 | tf_op jit(solution)/shard_map/ppermute | solution.py:863
  44.0 21.3 %collective-permute-start.11 = (bf16[2,256,1024]{2,1,0:T(8,128)(2,1)S(1)}, bf16[2,256,1024]{2,1,0:T(8,128)(2,1)}, u32[]{:S(2)}, u32[]{:S(2)}) collective-permute-start(bf16[2,256,1024]{2,1,0:T(8,128)(2,1)S(1)} %broadcast_select_fusion.6.refs_10_.refs_24_), channel_id=1, source_target_pairs={{0,16},{1,17},{2,18},{3,19},{4,20},{5,21},{6,22},{7,23},{8,24},{9,... | collective-permute-start | bytes 3145736 | tf_op jit(solution)/shard_map/ppermute | solution.py:863
  65.3 20.5 %collective-permute-start.14 = (bf16[2,256,1024]{2,1,0:T(8,128)(2,1)S(1)}, bf16[2,256,1024]{2,1,0:T(8,128)(2,1)S(1)}, u32[]{:S(2)}, u32[]{:S(2)}) collective-permute-start(bf16[2,256,1024]{2,1,0:T(8,128)(2,1)S(1)} %broadcast_select_fusion.5.refs_6_.refs_20_), channel_id=1, source_target_pairs={{0,8},{1,9},{2,10},{3,11},{4,12},{5,13},{6,14},{7,15},{8,0},{9,1},... | collective-permute-start | bytes 3145736 | tf_op jit(solution)/shard_map/ppermute | solution.py:863
  66.1 21.8 %collective-permute-start.15 = (bf16[2,256,1024]{2,1,0:T(8,128)(2,1)}, bf16[2,256,1024]{2,1,0:T(8,128)(2,1)S(1)}, u32[]{:S(2)}, u32[]{:S(2)}) collective-permute-start(bf16[2,256,1024]{2,1,0:T(8,128)(2,1)} %collective-permute-done.10.refs_11_.refs_25_), channel_id=1, source_target_pairs={{0,16},{1,17},{2,18},{3,19},{4,20},{5,21},{6,22},{7,23},{8,24},{9,... | collective-permute-start | bytes 3145736 | tf_op jit(solution)/shard_map/ppermute | solution.py:863
  67.4 51.8 %collective-permute-start.12 = (bf16[256,2048]{1,0:T(8,128)(2,1)S(1)}, bf16[256,2048]{1,0:T(8,128)(2,1)S(1)}, u32[]{:S(2)}, u32[]{:S(2)}) collective-permute-start(bf16[256,2048]{1,0:T(8,128)(2,1)S(1)} %bitcast.139), channel_id=1, source_target_pairs={{2,4},{3,5},{4,2},{5,3},{10,12},{11,13},{12,10},{13,11},{18,20},{1... | collective-permute-start | bytes 3145736 | tf_op jit(solution)/shard_map/ppermute | solution.py:863
  69.3 51.3 %collective-permute-start.13 = (bf16[2,256,1024]{2,1,0:T(8,128)(2,1)S(1)}, bf16[2,256,1024]{2,1,0:T(8,128)(2,1)S(1)}, u32[]{:S(2)}, u32[]{:S(2)}) collective-permute-start(bf16[2,256,1024]{2,1,0:T(8,128)(2,1)S(1)} %copy-done.101), channel_id=1, source_target_pairs={{0,2},{1,3},{6,4},{7,5},{8,10},{9,11},{14,12},{15,13},{16,18},{17,... | collective-permute-start | bytes 3145736 | tf_op jit(solution)/shard_map/ppermute | solution.py:863
  87.9 35.0 %collective-permute-start.17 = (bf16[2,256,1024]{2,1,0:T(8,128)(2,1)S(1)}, bf16[2,256,1024]{2,1,0:T(8,128)(2,1)S(1)}, u32[]{:S(2)}, u32[]{:S(2)}) collective-permute-start(bf16[2,256,1024]{2,1,0:T(8,128)(2,1)S(1)} %broadcast_select_fusion.5.refs_6_.refs_20_), channel_id=1, source_target_pairs={{0,16},{1,17},{2,18},{3,19},{4,20},{5,21},{6,22},{7,23},{8,24},{9,... | collective-permute-start | bytes 3145736 | tf_op jit(solution)/shard_map/ppermute | solution.py:863
  89.2 33.8 %collective-permute-start.16 = (bf16[112,1024]{1,0:T(8,128)(2,1)S(1)}, bf16[112,1024]{1,0:T(8,128)(2,1)S(1)}, u32[]{:S(2)}, u32[]{:S(2)}) collective-permute-start(bf16[112,1024]{1,0:T(8,128)(2,1)S(1)} %get-tuple-element.235), channel_id=1, source_target_pairs={{0,2},{1,3},{6,4},{7,5},{8,10},{9,11},{14,12},{15,13},{16,18},{17,... | collective-permute-start | bytes 688136 | tf_op jit(solution)/shard_map/ppermute | solution.py:863
  125.1 45.7 %collective-permute-start.19 = (bf16[2,1024,256]{2,1,0:T(8,128)(2,1)}, bf16[2,1024,256]{2,1,0:T(8,128)(2,1)}, u32[]{:S(2)}, u32[]{:S(2)}) collective-permute-start(bf16[2,1024,256]{2,1,0:T(8,128)(2,1)} %pad_maximum_fusion.3), channel_id=1, source_target_pairs={{0,2},{1,3},{6,4},{7,5},{8,10},{9,11},{14,12},{15,13},{16,18},{17,... | collective-permute-start | bytes 3145736 | tf_op jit(solution)/shard_map/ppermute | solution.py:863
  126.4 46.1 %collective-permute-start.18 = (bf16[256,2048]{1,0:T(8,128)(2,1)}, bf16[256,2048]{1,0:T(8,128)(2,1)}, u32[]{:S(2)}, u32[]{:S(2)}) collective-permute-start(bf16[256,2048]{1,0:T(8,128)(2,1)} %norm_rows.1.refs_2_.refs_0_), channel_id=1, source_target_pairs={{0,1},{1,0},{2,3},{3,2},{4,5},{5,4},{6,7},{7,6},{8,9},{9,8},{10,11... | collective-permute-start | bytes 3145736 | tf_op jit(solution)/shard_map/ppermute | solution.py:863
  126.4 47.4 %collective-permute-start.23 = (bf16[256,2048]{1,0:T(8,128)(2,1)}, bf16[256,2048]{1,0:T(8,128)(2,1)}, u32[]{:S(2)}, u32[]{:S(2)}) collective-permute-start(bf16[256,2048]{1,0:T(8,128)(2,1)} %bitcast.140), channel_id=1, source_target_pairs={{2,4},{3,5},{4,2},{5,3},{10,12},{11,13},{12,10},{13,11},{18,20},{1... | collective-permute-start | bytes 3145736 | tf_op jit(solution)/shard_map/ppermute | solution.py:863
  140.3 33.6 %collective-permute-start.22 = (bf16[2,256,1024]{2,1,0:T(8,128)(2,1)}, bf16[2,256,1024]{2,1,0:T(8,128)(2,1)}, u32[]{:S(2)}, u32[]{:S(2)}) collective-permute-start(bf16[2,256,1024]{2,1,0:T(8,128)(2,1)} %copy-done.70), channel_id=1, source_target_pairs={{0,8},{1,9},{2,10},{3,11},{4,12},{5,13},{6,14},{7,15},{8,0},{9,1},... | collective-permute-start | bytes 3145736 | tf_op jit(solution)/shard_map/ppermute | solution.py:863
  141.5 32.4 %collective-permute-start.24 = (bf16[2,256,1024]{2,1,0:T(8,128)(2,1)}, bf16[2,256,1024]{2,1,0:T(8,128)(2,1)}, u32[]{:S(2)}, u32[]{:S(2)}) collective-permute-start(bf16[2,256,1024]{2,1,0:T(8,128)(2,1)} %collective-permute-done.20.refs_5_.refs_29_), channel_id=1, source_target_pairs={{0,16},{1,17},{2,18},{3,19},{4,20},{5,21},{6,22},{7,23},{8,24},{9,... | collective-permute-start | bytes 3145736 | tf_op jit(solution)/shard_map/ppermute | solution.py:863
  174.9 27.7 %collective-permute-start.25 = (bf16[2,1024,256]{2,1,0:T(8,128)(2,1)S(1)}, bf16[2,1024,256]{2,1,0:T(8,128)(2,1)S(1)}, u32[]{:S(2)}, u32[]{:S(2)}) collective-permute-start(bf16[2,1024,256]{2,1,0:T(8,128)(2,1)S(1)} %copy-done.99), channel_id=1, source_target_pairs={{0,2},{1,3},{6,4},{7,5},{8,10},{9,11},{14,12},{15,13},{16,18},{17,... | collective-permute-start | bytes 3145736 | tf_op jit(solution)/shard_map/ppermute | solution.py:863
  176.3 28.5 %collective-permute-start.26 = (bf16[2,1024,256]{2,1,0:T(8,128)(2,1)S(1)}, bf16[2,1024,256]{2,1,0:T(8,128)(2,1)}, u32[]{:S(2)}, u32[]{:S(2)}) collective-permute-start(bf16[2,1024,256]{2,1,0:T(8,128)(2,1)S(1)} %broadcast_select_fusion.1.refs_0_.refs_2_), channel_id=1, source_target_pairs={{0,8},{1,9},{2,10},{3,11},{4,12},{5,13},{6,14},{7,15},{8,0},{9,1},... | collective-permute-start | bytes 3145736 | tf_op jit(solution)/shard_map/ppermute | solution.py:863
  177.2 27.6 %collective-permute-start.29 = (bf16[2,1024,256]{2,1,0:T(8,128)(2,1)S(1)}, bf16[2,1024,256]{2,1,0:T(8,128)(2,1)S(1)}, u32[]{:S(2)}, u32[]{:S(2)}) collective-permute-start(bf16[2,1024,256]{2,1,0:T(8,128)(2,1)S(1)} %broadcast_select_fusion.1.refs_0_.refs_2_), channel_id=1, source_target_pairs={{0,16},{1,17},{2,18},{3,19},{4,20},{5,21},{6,22},{7,23},{8,24},{9,... | collective-permute-start | bytes 3145736 | tf_op jit(solution)/shard_map/ppermute | solution.py:863
  205.8 27.0 %collective-permute-start.30 = (bf16[2,256,1024]{2,1,0:T(8,128)(2,1)}, bf16[2,256,1024]{2,1,0:T(8,128)(2,1)}, u32[]{:S(2)}, u32[]{:S(2)}) collective-permute-start(bf16[2,256,1024]{2,1,0:T(8,128)(2,1)} %pad_maximum_fusion.5), channel_id=1, source_target_pairs={{0,2},{1,3},{6,4},{7,5},{8,10},{9,11},{14,12},{15,13},{16,18},{17,... | collective-permute-start | bytes 3145736 | tf_op jit(solution)/shard_map/ppermute | solution.py:863
  207.3 26.9 %collective-permute-start.31 = (bf16[2,1024,256]{2,1,0:T(8,128)(2,1)}, bf16[2,1024,256]{2,1,0:T(8,128)(2,1)}, u32[]{:S(2)}, u32[]{:S(2)}) collective-permute-start(bf16[2,1024,256]{2,1,0:T(8,128)(2,1)} %collective-permute-done.26.refs_1_.refs_3_), channel_id=1, source_target_pairs={{0,16},{1,17},{2,18},{3,19},{4,20},{5,21},{6,22},{7,23},{8,24},{9,... | collective-permute-start | bytes 3145736 | tf_op jit(solution)/shard_map/ppermute | solution.py:863
  208.2 26.0 %collective-permute-start.32 = (bf16[2,1024,256]{2,1,0:T(8,128)(2,1)}, bf16[2,1024,256]{2,1,0:T(8,128)(2,1)}, u32[]{:S(2)}, u32[]{:S(2)}) collective-permute-start(bf16[2,1024,256]{2,1,0:T(8,128)(2,1)} %broadcast_select_fusion.refs_4_.refs_0_), channel_id=1, source_target_pairs={{0,8},{1,9},{2,10},{3,11},{4,12},{5,13},{6,14},{7,15},{8,0},{9,1},... | collective-permute-start | bytes 3145736 | tf_op jit(solution)/shard_map/ppermute | solution.py:863
  209.5 24.7 %collective-permute-start.33 = (bf16[128,2048]{1,0:T(8,128)(2,1)}, bf16[128,2048]{1,0:T(8,128)(2,1)}, u32[]{:S(2)}, u32[]{:S(2)}) collective-permute-start(bf16[128,2048]{1,0:T(8,128)(2,1)} %get-tuple-element.277), channel_id=1, source_target_pairs={{0,1},{1,0},{2,3},{3,2},{4,5},{5,4},{6,7},{7,6},{8,9},{9,8},{10,11... | collective-permute-start | bytes 1572872 | tf_op jit(solution)/shard_map/ppermute | solution.py:863
  234.2 23.4 %collective-permute-start.34 = (bf16[2,1024,256]{2,1,0:T(8,128)(2,1)}, bf16[2,1024,256]{2,1,0:T(8,128)(2,1)S(1)}, u32[]{:S(2)}, u32[]{:S(2)}) collective-permute-start(bf16[2,1024,256]{2,1,0:T(8,128)(2,1)} %broadcast_select_fusion.refs_4_.refs_0_), channel_id=1, source_target_pairs={{0,16},{1,17},{2,18},{3,19},{4,20},{5,21},{6,22},{7,23},{8,24},{9,... | collective-permute-start | bytes 3145736 | tf_op jit(solution)/shard_map/ppermute | solution.py:863
  234.5 23.1 %collective-permute-start.35 = (bf16[2,256,1024]{2,1,0:T(8,128)(2,1)S(1)}, bf16[2,256,1024]{2,1,0:T(8,128)(2,1)S(1)}, u32[]{:S(2)}, u32[]{:S(2)}) collective-permute-start(bf16[2,256,1024]{2,1,0:T(8,128)(2,1)S(1)} %broadcast_select_fusion.3.refs_4_.refs_9_.refs_3_), channel_id=1, source_target_pairs={{0,8},{1,9},{2,10},{3,11},{4,12},{5,13},{6,14},{7,15},{8,0},{9,1},... | collective-permute-start | bytes 3145736 | tf_op jit(solution)/shard_map/ppermute | solution.py:863
  235.1 27.7 %collective-permute-start.36 = (bf16[2,256,1024]{2,1,0:T(8,128)(2,1)S(1)}, bf16[2,256,1024]{2,1,0:T(8,128)(2,1)S(1)}, u32[]{:S(2)}, u32[]{:S(2)}) collective-permute-start(bf16[2,256,1024]{2,1,0:T(8,128)(2,1)S(1)} %copy-done.98), channel_id=1, source_target_pairs={{0,2},{1,3},{6,4},{7,5},{8,10},{9,11},{14,12},{15,13},{16,18},{17,... | collective-permute-start | bytes 3145736 | tf_op jit(solution)/shard_map/ppermute | solution.py:863
  267.3 26.2 %collective-permute-start.40 = (bf16[256,2048]{1,0:T(8,128)(2,1)S(1)}, bf16[256,2048]{1,0:T(8,128)(2,1)S(1)}, u32[]{:S(2)}, u32[]{:S(2)}) collective-permute-start(bf16[256,2048]{1,0:T(8,128)(2,1)S(1)} %add_convert_fusion.4), channel_id=1, source_target_pairs={{0,1},{1,0},{2,3},{3,2},{4,5},{5,4},{6,7},{7,6},{8,9},{9,8},{10,11... | collective-permute-start | bytes 3145736 | tf_op jit(solution)/shard_map/ppermute | solution.py:863
  270.3 25.3 %collective-permute-start.41 = (bf16[2,1024,256]{2,1,0:T(8,128)(2,1)S(1)}, bf16[2,1024,256]{2,1,0:T(8,128)(2,1)S(1)}, u32[]{:S(2)}, u32[]{:S(2)}) collective-permute-start(bf16[2,1024,256]{2,1,0:T(8,128)(2,1)S(1)} %collective-permute-done.34.refs_6_.refs_2_), channel_id=1, source_target_pairs={{0,8},{1,9},{2,10},{3,11},{4,12},{5,13},{6,14},{7,15},{8,0},{9,1},... | collective-permute-start | bytes 3145736 | tf_op jit(solution)/shard_map/ppermute | solution.py:863
  270.9 24.7 %collective-permute-start.42 = (bf16[2,256,1024]{2,1,0:T(8,128)(2,1)S(1)}, bf16[2,256,1024]{2,1,0:T(8,128)(2,1)S(1)}, u32[]{:S(2)}, u32[]{:S(2)}) collective-permute-start(bf16[2,256,1024]{2,1,0:T(8,128)(2,1)S(1)} %broadcast_select_fusion.3.refs_4_.refs_9_.refs_3_), channel_id=1, source_target_pairs={{0,16},{1,17},{2,18},{3,19},{4,20},{5,21},{6,22},{7,23},{8,24},{9,... | collective-permute-start | bytes 3145736 | tf_op jit(solution)/shard_map/ppermute | solution.py:863
  295.6 23.9 %collective-permute-start.43 = (bf16[256,2048]{1,0:T(8,128)(2,1)S(1)}, bf16[256,2048]{1,0:T(8,128)(2,1)S(1)}, u32[]{:S(2)}, u32[]{:S(2)}) collective-permute-start(bf16[256,2048]{1,0:T(8,128)(2,1)S(1)} %get-tuple-element.307.refs_0_.refs_4_), channel_id=1, source_target_pairs={{0,1},{1,0},{2,3},{3,2},{4,5},{5,4},{6,7},{7,6},{8,9},{9,8},{10,11... | collective-permute-start | bytes 3145736 | tf_op jit(solution)/shard_map/ppermute | solution.py:863
  296.8 23.2 %collective-permute-start.44 = (bf16[2,256,1024]{2,1,0:T(8,128)(2,1)S(1)}, bf16[2,256,1024]{2,1,0:T(8,128)(2,1)S(1)}, u32[]{:S(2)}, u32[]{:S(2)}) collective-permute-start(bf16[2,256,1024]{2,1,0:T(8,128)(2,1)S(1)} %broadcast_select_fusion.2.refs_7_.refs_13_), channel_id=1, source_target_pairs={{0,8},{1,9},{2,10},{3,11},{4,12},{5,13},{6,14},{7,15},{8,0},{9,1},... | collective-permute-start | bytes 3145736 | tf_op jit(solution)/shard_map/ppermute | solution.py:863
  297.5 22.5 %collective-permute-start.45 = (bf16[256,2048]{1,0:T(8,128)(2,1)S(1)}, bf16[256,2048]{1,0:T(8,128)(2,1)S(1)}, u32[]{:S(2)}, u32[]{:S(2)}) collective-permute-start(bf16[256,2048]{1,0:T(8,128)(2,1)S(1)} %broadcast_select_fusion.7.refs_0_.grad_in), channel_id=1, source_target_pairs={{0,4},{1,5},{2,6},{3,7},{4,0},{5,1},{6,2},{7,3},{8,12},{9,13},{10,... | collective-permute-start | bytes 3145736 | tf_op jit(solution)/shard_map/ppermute | solution.py:863
  299.2 20.8 %collective-permute-start.46 = (bf16[256,2048]{1,0:T(8,128)(2,1)S(1)}, bf16[256,2048]{1,0:T(8,128)(2,1)S(1)}, u32[]{:S(2)}, u32[]{:S(2)}) collective-permute-start(bf16[256,2048]{1,0:T(8,128)(2,1)S(1)} %constant_dynamic-update-slice_fusion.14.refs_2_), channel_id=1, source_target_pairs={{0,4},{1,5},{2,6},{3,7},{4,0},{5,1},{6,2},{7,3},{8,12},{9,13},{10,... | collective-permute-start | bytes 3145736 | tf_op jit(solution)/shard_map/ppermute | solution.py:863
  299.2 24.2 %collective-permute-start.47 = (bf16[2,256,1024]{2,1,0:T(8,128)(2,1)S(1)}, bf16[2,256,1024]{2,1,0:T(8,128)(2,1)S(1)}, u32[]{:S(2)}, u32[]{:S(2)}) collective-permute-start(bf16[2,256,1024]{2,1,0:T(8,128)(2,1)S(1)} %broadcast_select_fusion.2.refs_7_.refs_13_), channel_id=1, source_target_pairs={{0,16},{1,17},{2,18},{3,19},{4,20},{5,21},{6,22},{7,23},{8,24},{9,... | collective-permute-start | bytes 3145736 | tf_op jit(solution)/shard_map/ppermute | solution.py:863
  324.8 24.8 %collective-permute-start.50 = (bf16[2,256,1024]{2,1,0:T(8,128)(2,1)S(1)}, bf16[2,256,1024]{2,1,0:T(8,128)(2,1)S(1)}, u32[]{:S(2)}, u32[]{:S(2)}) collective-permute-start(bf16[2,256,1024]{2,1,0:T(8,128)(2,1)S(1)} %collective-permute-done.42.refs_6_.refs_11_.refs_5_), channel_id=1, source_target_pairs={{0,8},{1,9},{2,10},{3,11},{4,12},{5,13},{6,14},{7,15},{8,0},{9,1},... | collective-permute-start | bytes 3145736 | tf_op jit(solution)/shard_map/ppermute | solution.py:863
  325.6 24.0 %collective-permute-start.51 = (bf16[2,256,1024]{2,1,0:T(8,128)(2,1)S(1)}, bf16[2,256,1024]{2,1,0:T(8,128)(2,1)S(1)}, u32[]{:S(2)}, u32[]{:S(2)}) collective-permute-start(bf16[2,256,1024]{2,1,0:T(8,128)(2,1)S(1)} %collective-permute-done.44.refs_8_.refs_14_), channel_id=1, source_target_pairs={{0,16},{1,17},{2,18},{3,19},{4,20},{5,21},{6,22},{7,23},{8,24},{9,... | collective-permute-start | bytes 3145736 | tf_op jit(solution)/shard_map/ppermute | solution.py:863
  381.6 23.7 %collective-permute-start.56 = (bf16[256,2048]{1,0:T(8,128)(2,1)}, bf16[256,2048]{1,0:T(8,128)(2,1)}, u32[]{:S(2)}, u32[]{:S(2)}) collective-permute-start(bf16[256,2048]{1,0:T(8,128)(2,1)} %add_convert_fusion.3), channel_id=1, source_target_pairs={{0,1},{1,0},{2,3},{3,2},{4,5},{5,4},{6,7},{7,6},{8,9},{9,8},{10,11... | collective-permute-start | bytes 3145736 | tf_op jit(solution)/shard_map/ppermute | solution.py:863
  411.0 24.4 %collective-permute-start.59 = (bf16[256,2048]{1,0:T(8,128)(2,1)}, bf16[256,2048]{1,0:T(8,128)(2,1)S(1)}, u32[]{:S(2)}, u32[]{:S(2)}) collective-permute-start(bf16[256,2048]{1,0:T(8,128)(2,1)} %rms_back.2.refs_0_.grad_in), channel_id=1, source_target_pairs={{0,1},{1,0},{2,3},{3,2},{4,5},{5,4},{6,7},{7,6},{8,9},{9,8},{10,11... | collective-permute-start | bytes 3145736 | tf_op jit(solution)/shard_map/ppermute | solution.py:863
  411.0 24.4 %collective-permute-start.60 = (bf16[256,2048]{1,0:T(8,128)(2,1)}, bf16[256,2048]{1,0:T(8,128)(2,1)S(1)}, u32[]{:S(2)}, u32[]{:S(2)}) collective-permute-start(bf16[256,2048]{1,0:T(8,128)(2,1)} %get-tuple-element.359), channel_id=1, source_target_pairs={{0,4},{1,5},{2,6},{3,7},{4,0},{5,1},{6,2},{7,3},{8,12},{9,13},{10,... | collective-permute-start | bytes 3145736 | tf_op jit(solution)/shard_map/ppermute | solution.py:863
  445.3 24.6 %collective-permute-start.63 = (bf16[256,2048]{1,0:T(8,128)(2,1)S(1)}, bf16[256,2048]{1,0:T(8,128)(2,1)}, u32[]{:S(2)}, u32[]{:S(2)}) collective-permute-start(bf16[256,2048]{1,0:T(8,128)(2,1)S(1)} %add_convert_fusion.2), channel_id=1, source_target_pairs={{0,1},{1,0},{2,3},{3,2},{4,5},{5,4},{6,7},{7,6},{8,9},{9,8},{10,11... | collective-permute-start | bytes 3145736 | tf_op jit(solution)/shard_map/ppermute | solution.py:863
  472.6 29.8 %collective-permute-start.67 = (bf16[256,2048]{1,0:T(8,128)(2,1)S(1)}, bf16[256,2048]{1,0:T(8,128)(2,1)S(1)}, u32[]{:S(2)}, u32[]{:S(2)}) collective-permute-start(bf16[256,2048]{1,0:T(8,128)(2,1)S(1)} %add_convert_fusion.1), channel_id=1, source_target_pairs={{2,4},{3,5},{4,2},{5,3},{10,12},{11,13},{12,10},{13,11},{18,20},{1... | collective-permute-start | bytes 3145736 | tf_op jit(solution)/shard_map/ppermute | solution.py:863
  477.7 24.8 %collective-permute-start.69 = (bf16[2,152,512]{2,1,0:T(8,128)(2,1)S(1)}, bf16[2,152,512]{2,1,0:T(8,128)(2,1)S(1)}, u32[]{:S(2)}, u32[]{:S(2)}) collective-permute-start(bf16[2,152,512]{2,1,0:T(8,128)(2,1)S(1)} %pad_maximum_fusion.10), channel_id=1, source_target_pairs={{0,16},{1,17},{2,18},{3,19},{4,20},{5,21},{6,22},{7,23},{8,24},{9,... | collective-permute-start | bytes 933896 | tf_op jit(solution)/shard_map/ppermute | solution.py:863
  478.4 24.0 %collective-permute-start.70 = (bf16[2,152,512]{2,1,0:T(8,128)(2,1)S(1)}, bf16[2,152,512]{2,1,0:T(8,128)(2,1)S(1)}, u32[]{:S(2)}, u32[]{:S(2)}) collective-permute-start(bf16[2,152,512]{2,1,0:T(8,128)(2,1)S(1)} %pad_maximum_fusion.11), channel_id=1, source_target_pairs={{0,8},{1,9},{2,10},{3,11},{4,12},{5,13},{6,14},{7,15},{8,0},{9,1},... | collective-permute-start | bytes 933896 | tf_op jit(solution)/shard_map/ppermute | solution.py:863
  479.5 22.9 %collective-permute-start.68 = (bf16[64,1024]{1,0:T(8,128)(2,1)S(1)}, bf16[64,1024]{1,0:T(8,128)(2,1)S(1)}, u32[]{:S(2)}, u32[]{:S(2)}) collective-permute-start(bf16[64,1024]{1,0:T(8,128)(2,1)S(1)} %fusion.3), channel_id=1, source_target_pairs={{0,1},{1,0},{2,3},{3,2},{4,5},{5,4},{6,7},{7,6},{8,9},{9,8},{10,11... | collective-permute-start | bytes 393224 | tf_op jit(solution)/shard_map/ppermute | solution.py:863
  547.3 16.9 %collective-permute-start.83 = (bf16[4,448,512]{2,1,0:T(8,128)(2,1)S(1)}, bf16[4,448,512]{2,1,0:T(8,128)(2,1)}, u32[]{:S(2)}, u32[]{:S(2)}) collective-permute-start(bf16[4,448,512]{2,1,0:T(8,128)(2,1)S(1)} %maximum_maximum_fusion.refs_0_), channel_id=1, source_target_pairs={{0,4},{1,5},{2,6},{3,7},{4,0},{5,1},{6,2},{7,3},{8,12},{9,13},{10,... | collective-permute-start | bytes 5505032 | tf_op jit(solution)/shard_map/ppermute | solution.py:863
  547.9 28.6 %collective-permute-start.81 = (bf16[256,2048]{1,0:T(8,128)(2,1)}, bf16[256,2048]{1,0:T(8,128)(2,1)}, u32[]{:S(2)}, u32[]{:S(2)}) collective-permute-start(bf16[256,2048]{1,0:T(8,128)(2,1)} %get-tuple-element.417), channel_id=1, source_target_pairs={{2,4},{3,5},{4,2},{5,3},{10,12},{11,13},{12,10},{13,11},{18,20},{1... | collective-permute-start | bytes 3145736 | tf_op jit(solution)/shard_map/ppermute | solution.py:863
  (152 other events, 2542.5 us)

commit v6 on v5

--- a/solution.py
+++ b/solution.py
@@ -808,16 +808,12 @@
         steps.mlp()
         dz = self.gather(steps.dz(self.scatter(steps.unfold_mlp(256, (0, 1, 2, 3)))))
         output = steps.output(self.scatter(steps.fold_down(steps.hid)))
-        lows = self.group_sum(steps.early_lows())
-        early = lax.all_gather(steps.early(lows), "dp")
+        early = lax.all_gather(steps.early(self.group_sum(steps.lows)), "dp")
         early = steps.place_early([early], jnp.arange(self.ndp, dtype=jnp.int32))
         steps.gate_back(dz, 0)
         steps.gate_back(dz, 1)
         steps.retention_back(*steps.dret)
-        late = jnp.concatenate(
-            [steps.late_shares(self.group_sum(steps.dlow)), steps.late_rest(lows, dz)]
-        )
-        late = lax.all_gather(late, "dp")
+        late = lax.all_gather(steps.late(self.group_sum(steps.late_lows()), dz), "dp")
         late = steps.place_late([late], jnp.arange(self.ndp, dtype=jnp.int32))
         parts = self.scatter(steps.unfold_attn(256, (0, 1, 2, 3)))
         dx, _ = steps.dx(parts)
@@ -1042,30 +1038,29 @@
         self.last_round = ()
         steps.mlp()
         (lows,), _, (near, far, beyond) = self.round(
-            [(steps.early_lows().astype(BF), core)],
+            [(steps.lows.astype(BF), core)],
             lambda dup: steps.unfold_mlp(256, (1, 2, 3), dup), (steps.dup,)
         )
-        lows = self.core_sum(steps.early_lows(), lows)
-        (beyond, near, other), _, _ = self.round([(beyond, core), (near, core), (lows, pair)])
+        lows = self.core_sum(steps.lows, lows)
+        (beyond, near), _, _ = self.round([(beyond, core), (near, core)])
         far = self.add(far, beyond)
         half = far.shape[0] // 2
-        lows = self.pair_sum(lows, other)
-        (far,), _, ((own,), folded, early) = self.round(
-            [(far, pair)],
-            lambda dup, hid, lows: (steps.unfold_mlp(256, (0,), dup), steps.fold_down(hid),
-                                    steps.early(lows)),
-            (steps.dup, steps.hid, lows)
+        (far, other), _, ((own,), folded) = self.round(
+            [(far, pair), (lows, pair)],
+            lambda dup, hid: (steps.unfold_mlp(256, (0,), dup), steps.fold_down(hid)),
+            (steps.dup, steps.hid)
         )
         own_out, near_out, far_out, beyond_out = folded
         dz = steps.dz((own, near, far))
 
 
-        def beside(beyond, dz_near, far, dz):
-            return self.add(far, beyond), steps.gate_back([dz, dz_near, dz, dz], 0)
-
-        (_, dz_near, across, near_out), _, (far_out, dret0) = self.round(
+        def beside(beyond, dz_near, far, dz, lows, other):
+            return (self.add(far, beyond), steps.gate_back([dz, dz_near, dz, dz], 0),
+                    steps.early(self.pair_sum(lows, other)))
+
+        (_, dz_near, across, near_out), _, (far_out, dret0, early) = self.round(
             [(beyond_out, core), (dz, core), (dz, pair), (near_out, core)],
-            beside, (far_out, dz), feed=2
+            beside, (far_out, dz, lows, other), feed=2
         )
         (dz_beyond,), _, _ = self.round([(across, core)])
         (moved, far_out), _, dret1 = self.round(
@@ -1083,27 +1078,26 @@
         dz = [dz, dz_near, across, dz_beyond]
 
         (dlow,), _, output = self.round(
-            [(steps.dlow.astype(BF), core)], lambda *parts: steps.output(parts),
+            [(steps.late_lows().astype(BF), core)], lambda *parts: steps.output(parts),
             (own_out, near_out, far_out)
         )
-        dlow = self.core_sum(steps.dlow, dlow)
-        (other, moved_out, one, two), _, ((own, near, far, beyond), rest) = self.round(
+        dlow = self.core_sum(steps.late_lows(), dlow)
+        (other, moved_out, one, two), _, (own, near, far, beyond) = self.round(
             [(dlow, pair), (output, swap), (early[0], by_two), (early[1], by_one)],
-            lambda dpv, lows: (steps.unfold_attn(256, (0, 1, 2, 3), dpv),
-                               steps.late_rest(lows, dz)),
-            (dpv, lows)
-        )
-        (beyond, near, moved), _, shares = self.round(
-            [(beyond, core), (near, core), (rest, swap)],
-            lambda dlow, other: steps.late_shares(self.pair_sum(dlow, other)), (dlow, other)
-        )
-        rest = self.mine(rest, moved)
+            lambda dpv: steps.unfold_attn(256, (0, 1, 2, 3), dpv), (dpv,)
+        )
+        (beyond, near), _, late = self.round(
+            [(beyond, core), (near, core)],
+            lambda dlow, other: steps.late(self.pair_sum(dlow, other), dz), (dlow, other)
+        )
         (moved,), _, (far, early) = self.round(
-            [(shares, swap)],
+            [(late, swap)],
             lambda far, beyond, *early: (self.add(far, beyond), self.both_halves(*early)),
             (far, beyond, early, one, two)
         )
-        late = [self.mine(shares, moved)[None], rest[None]]
+        late = self.mine(late, moved)
+        size = late.shape[0] // 2
+        late = [late[:size][None], late[size:][None]]
         (one, two, far0), _, _ = self.round(
             [(late[0], by_one), (late[1], by_two), (far[:half], pair)]
         )
@@ -1260,6 +1254,7 @@
 
     class Back:
         early_height = 3 * RANK
+        late_height = 5 * RANK
 
         def mlp(self):
             (self.hid, self.dgate, self.dup, self.lows, self.grad_hidden,
@@ -1284,13 +1279,10 @@
                 parts[0].astype(F32) + parts[1].astype(F32) + parts[2].astype(F32)
             )).astype(BF)
 
-        def early_lows(self):
-            return jnp.concatenate([self.lows, low_o])
-
         def early(self, lows):
             mark = jnp.full((RANK, span), work_id, F32).astype(BF)
             return jnp.concatenate(
-                [share(lows[:3 * RANK], span, ((RANK, dy), (2 * RANK, b))),
+                [share(lows, span, ((RANK, dy), (2 * RANK, b))),
                  halves(jnp.concatenate([self.grad_hidden, self.grad_down])), mark]
             )
 
@@ -1306,6 +1298,9 @@
             self.low_parts = self.low_parts + (dlow,)
             return dret
 
+        def late_lows(self):
+            return jnp.concatenate([self.dlow, low_o])
+
         def retention_back(self, *dret):
             (self.dpq, self.dpk, self.dpv, self.dlow, self.grad_q, self.grad_k,
              self.grad_v) = retention_back(
@@ -1314,12 +1309,9 @@
             )
             return self.dpv
 
-        def late_shares(self, lows):
-            return share(lows, span, ((4 * RANK, a),))
-
-        def late_rest(self, lows, dz):
+        def late(self, lows, dz):
             return jnp.concatenate(
-                [share(lows[3 * RANK:], span, ((RANK, dz),)),
+                [share(lows, span, ((4 * RANK, a), (RANK, dz))),
                  halves(jnp.concatenate(
                      [jnp.concatenate([self.grad_q, self.grad_k], axis=1), self.grad_v,
                       self.grad_gate.astype(BF), self.grad_out_in.astype(BF)]
@@ -1361,13 +1353,13 @@
         def place_late(self, arrays, at):
             if self.total is not None:
                 arrays, at = [self.total(arrays[0])], self.order
-            pitch = 4 * RANK
-            first, rest = nt * pitch, nt * (pitch + RANK)
+            pitch = self.late_height
+            shares = nt * pitch
             return place(
                 at[self.order], arrays,
-                ((0, pitch, "shares", pitch), (first, RANK, "shares", RANK),
-                 (rest, RANK, "two", 4 * RANK), (rest + RANK, 2 * RANK, "halves", 4 * RANK),
-                 (rest + 3 * RANK, RANK, "halves", 4 * RANK)), nt
+                ((0, 4 * RANK, "shares", pitch), (4 * RANK, RANK, "shares", pitch),
+                 (shares, RANK, "two", 4 * RANK), (shares + RANK, 2 * RANK, "halves", 4 * RANK),
+                 (shares + 3 * RANK, RANK, "halves", 4 * RANK)), nt
             )
 
     output, input_grad, early, late = links.backward(Back())

time: 589 us -> 598 us (1.015)
  Pallas kernels: 191 us -> 197 us
    pallas_call x3, Pallas kernels: 36.7 us -> 44.4 us  [unfold(): pl.pallas_call(partial(unfold_kernel, (count, len(acts), len(weights))),...]
    ppermute x76 -> x75, starting transfers between devices: 78.9 us -> 76.4 us  [send(): lax.ppermute(x, ('dp', 'tensor'), self.pairs(place))]
    unnamed x242 -> x270, local copies, waits for them, and re-layouts: 16.3 us -> 17.4 us
    ppermute x76 -> x75, waiting for transfers between devices: 219 us -> 220 us  [send(): lax.ppermute(x, ('dp', 'tensor'), self.pairs(place))]
    select_n x12 -> x13, other arithmetic: 12.2 us -> 12.3 us  [mine(): return jnp.where(self.home, own, other)]
  transfers between devices with their start and end apart: 84 -> 83, of which waited for: 33 -> 35; matrix products, arithmetic and copies ran while one was open for 10% -> 10% of each run, Pallas kernels for 30% -> 31%
where the time goes in v6:
time: 598 us; the launch traced here: 589 us
  waiting for transfers between devices  220 us (37%)
  Pallas kernels  197 us (33%)
  starting transfers between devices  83.9 us (14%)
  other arithmetic  46.5 us (8%)
  local copies, waits for them, and re-layouts  30.9 us (5%)
  between operations  10.3 us (2%)
    ppermute x75, waiting for transfers between devices, send(): lax.ppermute(x, ('dp', 'tensor'), self.pairs(place))  220 us
    ppermute x75, starting transfers between devices, send(): lax.ppermute(x, ('dp', 'tensor'), self.pairs(place))  76.4 us
    pallas_call x3, Pallas kernels, unfold(): pl.pallas_call(partial(unfold_kernel, (count, len(acts), len(weights))),...  44.4 us
    pallas_call x2, Pallas kernels, project(): pl.pallas_call(partial(project_kernel, (len(act), len(weights[0]), length...  27.2 us
    pallas_call x2, Pallas kernels, fold(): pl.pallas_call(fold_kernel, grid=(subs,), in_specs=[smem(), full(act.shap...  21 us
    pallas_call x2, Pallas kernels, gate_back(): pl.pallas_call(partial(gate_back_kernel, len(act)), grid=(width // block,...  18 us
    unnamed x270, local copies, waits for them, and re-layouts  17.4 us
    pallas_call x2, Pallas kernels, place(): pl.pallas_call(partial(place_kernel, layout, len(arrays)), grid_spec=pltp...  15.3 us
  transfers between devices with their start and end apart: 83, of which 35 were waited for; matrix products, arithmetic and copies ran while one was open for 10% of the time, Pallas kernels for 31%

profile of v6, /device:TPU:1, one launch (start us, length us, event | category | flops | bytes accessed | tf_op | source)
XLA Modules:
  0.0 588.5 jit_solution(1059229549930417622)
XLA Ops:
  11.8 5.7 collective-permute-start.7
  29.0 6.7 %collective-permute-done.2 = bf16[2,256,1024]{2,1,0:T(8,128)(2,1)} collective-permute-done((bf16[2,256,1024]{2,1,0:T(8,128)(2,1)}, bf16[2,256,1024]{2,1,0:T(8,128)(2,1)}, u32[]{:S(2)}, u32[]{:S(2)}) %collective-permute-start.2) | collective-permute-done | bytes 1048608 | tf_op jit(solution)/shard_map/ppermute | solution.py:859
  52.3 10.8 %collective-permute-done.9 = bf16[2,256,1024]{2,1,0:T(8,128)(2,1)} collective-permute-done((bf16[2,256,1024]{2,1,0:T(8,128)(2,1)}, bf16[2,256,1024]{2,1,0:T(8,128)(2,1)}, u32[]{:S(2)}, u32[]{:S(2)}) %collective-permute-start.9) | collective-permute-done | bytes 1048608 | tf_op jit(solution)/shard_map/ppermute | solution.py:859
  70.6 15.1 %collective-permute-done.14.refs_7_.refs_21_ = bf16[2,256,1024]{2,1,0:T(8,128)(2,1)S(1)} collective-permute-done((bf16[2,256,1024]{2,1,0:T(8,128)(2,1)S(1)}, bf16[2,256,1024]{2,1,0:T(8,128)(2,1)S(1)}, u32[]{:S(2)}, u32[]{:S(2)}) %collective-permute-start.14) | collective-permute-done | bytes 1048608 | tf_op jit(solution)/shard_map/ppermute | solution.py:859
  90.6 28.5 %collective-permute-done.12 = bf16[256,2048]{1,0:T(8,128)(2,1)S(1)} collective-permute-done((bf16[256,2048]{1,0:T(8,128)(2,1)S(1)}, bf16[256,2048]{1,0:T(8,128)(2,1)S(1)}, u32[]{:S(2)}, u32[]{:S(2)}) %collective-permute-start.12) | collective-permute-done | bytes 1048608 | tf_op jit(solution)/shard_map/ppermute | solution.py:859
  126.0 4.1 collective-permute-start.23
  130.2 9.7 %collective-permute-done.20.refs_5_.refs_29_ = bf16[2,256,1024]{2,1,0:T(8,128)(2,1)} collective-permute-done((bf16[2,256,1024]{2,1,0:T(8,128)(2,1)S(1)}, bf16[2,256,1024]{2,1,0:T(8,128)(2,1)}, u32[]{:S(2)}, u32[]{:S(2)}) %collective-permute-start.20) | collective-permute-done | bytes 1048608 | tf_op jit(solution)/shard_map/ppermute | solution.py:859
  145.4 25.0 %collective-permute-done.19 = bf16[2,1024,256]{2,1,0:T(8,128)(2,1)} collective-permute-done((bf16[2,1024,256]{2,1,0:T(8,128)(2,1)}, bf16[2,1024,256]{2,1,0:T(8,128)(2,1)}, u32[]{:S(2)}, u32[]{:S(2)}) %collective-permute-start.19) | collective-permute-done | bytes 1048608 | tf_op jit(solution)/shard_map/ppermute | solution.py:859
  182.6 17.7 %project.2 = (bf16[1024,1024]{1,0:T(8,128)(2,1)}, bf16[1024,1024]{1,0:T(8,128)(2,1)}, bf16[64,1024]{1,0:T(8,128)(2,1)S(1)}) custom-call(s32[8]{0:T(128)S(1)} %xor.51.ids, s32[4]{0:T(128)S(1)} %broadcast_xor_fusion.chunks, bf16[64,2048]{1,0:T(8,128)(2,1)S(1)} %dynamic-slice_bitcast_fusion.low_in, bf16[64,2048]{1,0:T(8,128)(2,1)S(1)} %maximum_maximum_fusion.3.low_out, ...), custom_call_target="tpu_custom_call" | custom-call | flops 1 | bytes 1 | tf_op jit(solution)/shard_map/project/pallas_call | solution.py:191
  210.8 9.5 %project.3.gate = bf16[1024,1024]{1,0:T(8,128)(2,1)} custom-call(s32[8]{0:T(128)S(1)} %xor.51.ids, s32[4]{0:T(128)S(1)} %broadcast_xor_fusion.chunks, bf16[64,1024]{1,0:T(8,128)(2,1)S(1)} %get-tuple-element.264.low_in.low_gate.low, bf16[64,1024]{1,0:T(8,128)(2,1)S(1)} %concatenate.124.low_out, bf16[256,2048]{1,0:T(8,128)(2,1)} %norm_rows.1.refs_2_.refs_0_, ...), custom_call_target="tpu_custom_call" | custom-call | flops 1 | bytes 1 | tf_op jit(solution)/shard_map/project/pallas_call | solution.py:191
  220.4 8.7 %retention.1 = (bf16[1024,1024]{1,0:T(8,128)(2,1)}, bf16[1024,1024]{1,0:T(8,128)(2,1)}, f32[2,1024,128]{2,1,0:T(8,128)}) custom-call(s32[4]{0:T(128)S(1)} %fusion.5.spots, f32[2]{0:T(128)S(1)} %copy-done.60, s32[1024,1]{1,0:T(8,128)S(1)} %copy-done.24, s32[1,1024]{1,0:T(1,128)S(1)} %get-tuple-element.493.seg_row, bf16[1024,1024]{1,0:T(8,128)(2,1)S(1)} %copy-done.2, ...), custom_call_target="tpu_custom_call" | custom-call | flops 1 | bytes 1 | tf_op jit(solution)/shard_map/retention/pallas_call | solution.py:243
  229.2 3.3 collective-permute-done.30
  237.1 10.5 %fold.2 = (bf16[256,2048]{1,0:T(8,128)(2,1)}, bf16[256,2048]{1,0:T(8,128)(2,1)}, bf16[256,2048]{1,0:T(8,128)(2,1)}, bf16[256,2048]{1,0:T(8,128)(2,1)}, f32[16,1024]{1,0:T(8,128)S(1)}) custom-call(s32[8]{0:T(128)S(1)} %xor.51.ids, bf16[1024,1024]{1,0:T(8,128)(2,1)} %get-tuple-element.279.act.hold, bf16[16,1024]{1,0:T(8,128)(2,1)S(1)} %copy-done.44, ...), custom_call_target="tpu_custom_call" | custom-call | flops 1 | bytes 1 | tf_op jit(solution)/shard_map/fold/pallas_call | solution.py:286
  247.6 3.5 collective-permute-done.37
  251.0 6.2 %collective-permute-done.34.refs_6_.refs_2_ = bf16[2,1024,256]{2,1,0:T(8,128)(2,1)S(1)} collective-permute-done((bf16[2,1024,256]{2,1,0:T(8,128)(2,1)}, bf16[2,1024,256]{2,1,0:T(8,128)(2,1)S(1)}, u32[]{:S(2)}, u32[]{:S(2)}) %collective-permute-start.34) | collective-permute-done | bytes 1048608 | tf_op jit(solution)/shard_map/ppermute | solution.py:859
  257.3 5.2 collective-permute-done.36
  267.0 2.9 collective-permute-start.40
  273.1 20.0 %collective-permute-done.40.part2 = bf16[256,2048]{1,0:T(8,128)(2,1)S(1)} collective-permute-done((bf16[256,2048]{1,0:T(8,128)(2,1)S(1)}, bf16[256,2048]{1,0:T(8,128)(2,1)S(1)}, u32[]{:S(2)}, u32[]{:S(2)}) %collective-permute-start.40) | collective-permute-done | bytes 1048608 | tf_op jit(solution)/shard_map/ppermute | solution.py:859
  300.1 19.0 %collective-permute-done.43.refs_2_.refs_6_ = bf16[256,2048]{1,0:T(8,128)(2,1)S(1)} collective-permute-done((bf16[256,2048]{1,0:T(8,128)(2,1)S(1)}, bf16[256,2048]{1,0:T(8,128)(2,1)S(1)}, u32[]{:S(2)}, u32[]{:S(2)}) %collective-permute-start.43) | collective-permute-done | bytes 1048608 | tf_op jit(solution)/shard_map/ppermute | solution.py:859
  319.6 3.4 collective-permute-done.47.refs_9_.refs_15_
  327.8 9.1 %hidden_grad.1 = (bf16[1024,1024]{1,0:T(8,128)(2,1)}, bf16[16,1024]{1,0:T(8,128)(2,1)S(1)}) custom-call(s32[8]{0:T(128)S(1)} %xor.51.ids, bf16[16,2048]{1,0:T(8,128)(2,1)S(1)} %dynamic-slice_bitcast_fusion.2.low_back.low_out, bf16[16,1024]{1,0:T(8,128)(2,1)S(1)} %copy-done.45, bf16[256,2048]{1,0:T(8,128)(2,1)S(1)} %broadcast_select_fusion.7.refs_0_.grad_in, ...), custom_call_target="tpu_custom_call" | custom-call | flops 1 | bytes 1 | tf_op jit(solution)/shard_map/hidden_grad/pallas_call | solution.py:361
  337.0 12.3 %mlp_begin.1 = (f32[1024,1024]{1,0:T(8,128)}, f32[1024,1024]{1,0:T(8,128)}, bf16[32,1024]{1,0:T(8,128)(2,1)S(1)}) custom-call(s32[8]{0:T(128)S(1)} %xor.51.ids, bf16[32,2048]{1,0:T(8,128)(2,1)S(1)} %dynamic-slice_bitcast_fusion.1.low_in, bf16[256,2048]{1,0:T(8,128)(2,1)S(1)} %get-tuple-element.306.refs_0_.refs_4_, ...), custom_call_target="tpu_custom_call" | custom-call | flops 1 | bytes 1 | tf_op jit(solution)/shard_map/mlp_begin/pallas_call | solution.py:397
  350.4 11.4 %mlp.1 = (bf16[1024,1024]{1,0:T(8,128)(2,1)}, bf16[1024,1024]{1,0:T(8,128)(2,1)}, bf16[1024,1024]{1,0:T(8,128)(2,1)}, f32[48,1024]{1,0:T(8,128)S(1)}, bf16[32,10...) custom-call(s32[8]{0:T(128)S(1)} %xor.51.ids, f32[1024,1024]{1,0:T(8,128)} %get-tuple-element.315.gate_in, ...), custom_call_target="tpu_custom_call" | custom-call | flops 1 | bytes 1 | tf_op jit(solution)/shard_map/mlp/pallas_call | solution.py:451
  363.2 19.0 %unfold.3 = (bf16[256,2048]{1,0:T(8,128)(2,1)S(1)}, bf16[256,2048]{1,0:T(8,128)(2,1)S(1)}, bf16[256,2048]{1,0:T(8,128)(2,1)S(1)}) custom-call(s32[8]{0:T(128)S(1)} %xor.51.ids, bf16[32,2048]{1,0:T(8,128)(2,1)S(1)} %dynamic-slice_bitcast_fusion.1.low_in, f32[32,1024]{1,0:T(8,128)S(1)} %slice.187.refs_0_.refs_1_.refs_2_, ...), custom_call_target="tpu_custom_call" | custom-call | flops 1 | bytes 1 | tf_op jit(solution)/shard_map/unfold/pallas_call | solution.py:506
  389.7 5.6 unfold.4.part0
  395.5 10.6 %fold.3 = (bf16[256,2048]{1,0:T(8,128)(2,1)}, bf16[256,2048]{1,0:T(8,128)(2,1)}, bf16[256,2048]{1,0:T(8,128)(2,1)}, bf16[256,2048]{1,0:T(8,128)(2,1)}, f32[16,1024]{1,0:T(8,128)}) custom-call(s32[8]{0:T(128)S(1)} %xor.51.ids, bf16[1024,1024]{1,0:T(8,128)(2,1)} %get-tuple-element.339.act, bf16[16,1024]{1,0:T(8,128)(2,1)S(1)} %copy-done.46, ...), custom_call_target="tpu_custom_call" | custom-call | flops 1 | bytes 1 | tf_op jit(solution)/shard_map/fold/pallas_call | solution.py:286
  406.0 6.4 %collective-permute-done.55.part2 = bf16[256,2048]{1,0:T(8,128)(2,1)} collective-permute-done((bf16[256,2048]{1,0:T(8,128)(2,1)}, bf16[256,2048]{1,0:T(8,128)(2,1)}, u32[]{:S(2)}, u32[]{:S(2)}) %collective-permute-start.55) | collective-permute-done | bytes 1048608 | tf_op jit(solution)/shard_map/ppermute | solution.py:859
  412.5 3.5 rms_back.2.refs_0_.refs_4_.grad_in
  420.3 4.7 share.2
  426.1 9.0 %gate_back.2 = (bf16[512,1024]{1,0:T(8,128)(2,1)}, bf16[512,1024]{1,0:T(8,128)(2,1)}, bf16[16,512]{1,0:T(8,128)(2,1)}, f32[64,512]{1,0:T(8,128)}, f32[16,1024]{1,0:T(8,128)}, /*index=5*/f32[16,1024]{1,0:T(8,128)}) custom-call(s32[8]{0:T(128)} %copy-done.47, bf16[16,2048]{1,0:T(8,128)(2,1)} %copy-done.37, bf16[16,1024]{1,0:T(8,128)(2,1)} %get-tuple-element.470.low_in, ...), custom_call_target="tpu_custom_call" | custom-call | flops 1 | bytes 1 | tf_op jit(solution)/shard_map/gate_back/pallas_call | solution.py:564
  437.8 4.4 collective-permute-done.59.refs_0_.refs_6_
  445.8 5.2 collective-permute-start.62
  451.3 9.1 %gate_back.3 = (bf16[512,1024]{1,0:T(8,128)(2,1)}, bf16[512,1024]{1,0:T(8,128)(2,1)}, bf16[16,512]{1,0:T(8,128)(2,1)}, f32[64,512]{1,0:T(8,128)}, f32[16,1024]{1,0:T(8,128)}, /*index=5*/f32[16,1024]{1,0:T(8,128)}) custom-call(s32[8]{0:T(128)} %copy-done.47, bf16[16,2048]{1,0:T(8,128)(2,1)} %copy-done.37, bf16[16,1024]{1,0:T(8,128)(2,1)} %get-tuple-element.470.low_in, ...), custom_call_target="tpu_custom_call" | custom-call | flops 1 | bytes 1 | tf_op jit(solution)/shard_map/gate_back/pallas_call | solution.py:564
  463.6 11.6 %retention_back.1 = (bf16[1024,512]{1,0:T(8,128)(2,1)S(1)}, bf16[1024,512]{1,0:T(8,128)(2,1)S(1)}, bf16[1024,1024]{1,0:T(8,128)(2,1)}, f32[64,1024]{1,0:T(8,128)...) custom-call(s32[4]{0:T(128)S(1)} %copy-done.59, f32[2]{0:T(128)S(1)} %copy-done.61, ...), custom_call_target="tpu_custom_call" | custom-call | flops 1 | bytes 1 | tf_op jit(solution)/shard_map/retention_back/pallas_call | solution.py:651
  479.3 3.4 collective-permute-start.67
  484.8 19.8 %unfold.5 = (bf16[256,2048]{1,0:T(8,128)(2,1)S(1)}, bf16[256,2048]{1,0:T(8,128)(2,1)S(1)}, bf16[256,2048]{1,0:T(8,128)(2,1)S(1)}, bf16[256,2048]{1,0:T(8,128)(2,1)S(1)}) custom-call(s32[8]{0:T(128)S(1)} %copy-done.48, bf16[64,2048]{1,0:T(8,128)(2,1)S(1)} %dynamic-slice_bitcast_fusion.low_in, ...), custom_call_target="tpu_custom_call" | custom-call | flops 1 | bytes 1 | tf_op jit(solution)/shard_map/unfold/pallas_call | solution.py:506
  504.6 3.0 collective-permute-done.67
  509.2 4.7 share.3
  516.6 12.7 %collective-permute-done.73 = bf16[448,512]{1,0:T(8,128)(2,1)S(1)} collective-permute-done((bf16[448,512]{1,0:T(8,128)(2,1)S(1)}, bf16[448,512]{1,0:T(8,128)(2,1)S(1)}, u32[]{:S(2)}, u32[]{:S(2)}) %collective-permute-start.73) | collective-permute-done | bytes 458784 | tf_op jit(solution)/shard_map/ppermute | solution.py:859
  530.8 5.8 collective-permute-done.76
  537.6 4.2 collective-permute-done.74
  542.3 6.8 %collective-permute-done.79 = bf16[2,224,512]{2,1,0:T(8,128)(2,1)S(1)} collective-permute-done((bf16[2,224,512]{2,1,0:T(8,128)(2,1)S(1)}, bf16[2,224,512]{2,1,0:T(8,128)(2,1)S(1)}, u32[]{:S(2)}, u32[]{:S(2)}) %collective-permute-start.79) | collective-permute-done | bytes 458784 | tf_op jit(solution)/shard_map/ppermute | solution.py:859
  550.9 2.8 rms_back.3
  554.2 6.8 %collective-permute-start.80 = (bf16[256,2048]{1,0:T(8,128)(2,1)}, bf16[256,2048]{1,0:T(8,128)(2,1)}, u32[]{:S(2)}, u32[]{:S(2)}) collective-permute-start(bf16[256,2048]{1,0:T(8,128)(2,1)} %get-tuple-element.415), channel_id=1, source_target_pairs={{2,4},{3,5},{4,2},{5,3},{10,12},{11,13},{12,10},{13,11},{18,20},{1... | collective-permute-start | bytes 3145736 | tf_op jit(solution)/shard_map/ppermute | solution.py:859
  566.4 7.0 %place.2 = (f32[8,16,2048]{2,1,0:T(8,128)}, f32[8,32,2048]{2,1,0:T(8,128)}, f32[8,32,1024]{2,1,0:T(8,128)}, f32[8,16,1024]{2,1,0:T(8,128)}) custom-call(s32[9]{0:T(128)S(1)} %pad_add_fusion.order, bf16[4,304,512]{2,1,0:T(8,128)(2,1)} %copy-done.74, bf16[4,304,512]{2,1,0:T(8,128)(2,1)} %copy-done.99), custom_call_target="tpu_custom_call" | custom-call | flops 1 | bytes 1 | tf_op jit(solution)/shard_map/place/pallas_call | solution.py:739
  573.4 8.3 %place.3 = (f32[8,64,2048]{2,1,0:T(8,128)}, f32[8,16,2048]{2,1,0:T(8,128)}, f32[8,2,16,512]{3,2,1,0:T(8,128)}, f32[8,32,1024]{2,1,0:T(8,128)}, f32[8,16,1024]{2,1,0:T(8,128)}) custom-call(s32[9]{0:T(128)S(1)} %pad_add_fusion.order, bf16[4,448,512]{2,1,0:T(8,128)(2,1)} %copy-done.73, bf16[4,448,512]{2,1,0:T(8,128)(2,1)} %collective-permute-done.82.refs_1_), custom_call_target="tpu_custom_call" | custom-call | flops 1 | bytes 1 | tf_op jit(solution)/shard_map/place/pallas_call | solution.py:739
  581.7 3.4 collective-permute-done.80
  585.1 3.0 select_bitcast_fusion
  (520 shorter events, 148.8 us)
Async XLA Ops:
  3.8 20.8 %collective-permute-start.6 = (bf16[1024,256]{1,0:T(8,128)(2,1)}, bf16[1024,256]{1,0:T(8,128)(2,1)}, u32[]{:S(2)}, u32[]{:S(2)}) collective-permute-start(bf16[1024,256]{1,0:T(8,128)(2,1)} %param.37), channel_id=1, source_target_pairs={{0,4},{1,5},{2,6},{3,7},{4,0},{5,1},{6,2},{7,3},{8,12},{9,13},{10,... | collective-permute-start | bytes 1572872 | tf_op jit(solution)/shard_map/ppermute | solution.py:853
  6.9 28.8 %collective-permute-start.2 = (bf16[2,256,1024]{2,1,0:T(8,128)(2,1)}, bf16[2,256,1024]{2,1,0:T(8,128)(2,1)}, u32[]{:S(2)}, u32[]{:S(2)}) collective-permute-start(bf16[2,256,1024]{2,1,0:T(8,128)(2,1)} %pad_maximum_fusion.1), channel_id=1, source_target_pairs={{0,2},{1,3},{6,4},{7,5},{8,10},{9,11},{14,12},{15,13},{16,18},{17,... | collective-permute-start | bytes 3145736 | tf_op jit(solution)/shard_map/ppermute | solution.py:859
  40.7 22.3 %collective-permute-start.9 = (bf16[2,256,1024]{2,1,0:T(8,128)(2,1)}, bf16[2,256,1024]{2,1,0:T(8,128)(2,1)}, u32[]{:S(2)}, u32[]{:S(2)}) collective-permute-start(bf16[2,256,1024]{2,1,0:T(8,128)(2,1)} %pad_maximum_fusion), channel_id=1, source_target_pairs={{0,2},{1,3},{6,4},{7,5},{8,10},{9,11},{14,12},{15,13},{16,18},{17,... | collective-permute-start | bytes 3145736 | tf_op jit(solution)/shard_map/ppermute | solution.py:859
  42.0 22.7 %collective-permute-start.10 = (bf16[2,256,1024]{2,1,0:T(8,128)(2,1)S(1)}, bf16[2,256,1024]{2,1,0:T(8,128)(2,1)}, u32[]{:S(2)}, u32[]{:S(2)}) collective-permute-start(bf16[2,256,1024]{2,1,0:T(8,128)(2,1)S(1)} %broadcast_select_fusion.6.refs_10_.refs_24_), channel_id=1, source_target_pairs={{0,8},{1,9},{2,10},{3,11},{4,12},{5,13},{6,14},{7,15},{8,0},{9,1},... | collective-permute-start | bytes 3145736 | tf_op jit(solution)/shard_map/ppermute | solution.py:859
  44.0 21.2 %collective-permute-start.11 = (bf16[2,256,1024]{2,1,0:T(8,128)(2,1)S(1)}, bf16[2,256,1024]{2,1,0:T(8,128)(2,1)}, u32[]{:S(2)}, u32[]{:S(2)}) collective-permute-start(bf16[2,256,1024]{2,1,0:T(8,128)(2,1)S(1)} %broadcast_select_fusion.6.refs_10_.refs_24_), channel_id=1, source_target_pairs={{0,16},{1,17},{2,18},{3,19},{4,20},{5,21},{6,22},{7,23},{8,24},{9,... | collective-permute-start | bytes 3145736 | tf_op jit(solution)/shard_map/ppermute | solution.py:859
  65.2 20.5 %collective-permute-start.14 = (bf16[2,256,1024]{2,1,0:T(8,128)(2,1)S(1)}, bf16[2,256,1024]{2,1,0:T(8,128)(2,1)S(1)}, u32[]{:S(2)}, u32[]{:S(2)}) collective-permute-start(bf16[2,256,1024]{2,1,0:T(8,128)(2,1)S(1)} %broadcast_select_fusion.5.refs_6_.refs_20_), channel_id=1, source_target_pairs={{0,8},{1,9},{2,10},{3,11},{4,12},{5,13},{6,14},{7,15},{8,0},{9,1},... | collective-permute-start | bytes 3145736 | tf_op jit(solution)/shard_map/ppermute | solution.py:859
  66.1 21.9 %collective-permute-start.15 = (bf16[2,256,1024]{2,1,0:T(8,128)(2,1)}, bf16[2,256,1024]{2,1,0:T(8,128)(2,1)S(1)}, u32[]{:S(2)}, u32[]{:S(2)}) collective-permute-start(bf16[2,256,1024]{2,1,0:T(8,128)(2,1)} %collective-permute-done.10.refs_11_.refs_25_), channel_id=1, source_target_pairs={{0,16},{1,17},{2,18},{3,19},{4,20},{5,21},{6,22},{7,23},{8,24},{9,... | collective-permute-start | bytes 3145736 | tf_op jit(solution)/shard_map/ppermute | solution.py:859
  67.3 51.8 %collective-permute-start.12 = (bf16[256,2048]{1,0:T(8,128)(2,1)S(1)}, bf16[256,2048]{1,0:T(8,128)(2,1)S(1)}, u32[]{:S(2)}, u32[]{:S(2)}) collective-permute-start(bf16[256,2048]{1,0:T(8,128)(2,1)S(1)} %bitcast.136), channel_id=1, source_target_pairs={{2,4},{3,5},{4,2},{5,3},{10,12},{11,13},{12,10},{13,11},{18,20},{1... | collective-permute-start | bytes 3145736 | tf_op jit(solution)/shard_map/ppermute | solution.py:859
  69.3 51.3 %collective-permute-start.13 = (bf16[2,256,1024]{2,1,0:T(8,128)(2,1)S(1)}, bf16[2,256,1024]{2,1,0:T(8,128)(2,1)S(1)}, u32[]{:S(2)}, u32[]{:S(2)}) collective-permute-start(bf16[2,256,1024]{2,1,0:T(8,128)(2,1)S(1)} %copy-done.107), channel_id=1, source_target_pairs={{0,2},{1,3},{6,4},{7,5},{8,10},{9,11},{14,12},{15,13},{16,18},{17,... | collective-permute-start | bytes 3145736 | tf_op jit(solution)/shard_map/ppermute | solution.py:859
  88.0 34.9 %collective-permute-start.17 = (bf16[2,256,1024]{2,1,0:T(8,128)(2,1)S(1)}, bf16[2,256,1024]{2,1,0:T(8,128)(2,1)}, u32[]{:S(2)}, u32[]{:S(2)}) collective-permute-start(bf16[2,256,1024]{2,1,0:T(8,128)(2,1)S(1)} %broadcast_select_fusion.5.refs_6_.refs_20_), channel_id=1, source_target_pairs={{0,16},{1,17},{2,18},{3,19},{4,20},{5,21},{6,22},{7,23},{8,24},{9,... | collective-permute-start | bytes 3145736 | tf_op jit(solution)/shard_map/ppermute | solution.py:859
  89.3 33.7 %collective-permute-start.16 = (bf16[112,1024]{1,0:T(8,128)(2,1)S(1)}, bf16[112,1024]{1,0:T(8,128)(2,1)S(1)}, u32[]{:S(2)}, u32[]{:S(2)}) collective-permute-start(bf16[112,1024]{1,0:T(8,128)(2,1)S(1)} %get-tuple-element.234), channel_id=1, source_target_pairs={{0,2},{1,3},{6,4},{7,5},{8,10},{9,11},{14,12},{15,13},{16,18},{17,... | collective-permute-start | bytes 688136 | tf_op jit(solution)/shard_map/ppermute | solution.py:859
  124.7 45.7 %collective-permute-start.19 = (bf16[2,1024,256]{2,1,0:T(8,128)(2,1)}, bf16[2,1024,256]{2,1,0:T(8,128)(2,1)}, u32[]{:S(2)}, u32[]{:S(2)}) collective-permute-start(bf16[2,1024,256]{2,1,0:T(8,128)(2,1)} %pad_maximum_fusion.3), channel_id=1, source_target_pairs={{0,2},{1,3},{6,4},{7,5},{8,10},{9,11},{14,12},{15,13},{16,18},{17,... | collective-permute-start | bytes 3145736 | tf_op jit(solution)/shard_map/ppermute | solution.py:859
  126.0 46.1 %collective-permute-start.18 = (bf16[256,2048]{1,0:T(8,128)(2,1)}, bf16[256,2048]{1,0:T(8,128)(2,1)}, u32[]{:S(2)}, u32[]{:S(2)}) collective-permute-start(bf16[256,2048]{1,0:T(8,128)(2,1)} %norm_rows.1.refs_2_.refs_0_), channel_id=1, source_target_pairs={{0,1},{1,0},{2,3},{3,2},{4,5},{5,4},{6,7},{7,6},{8,9},{9,8},{10,11... | collective-permute-start | bytes 3145736 | tf_op jit(solution)/shard_map/ppermute | solution.py:859
  126.0 47.4 %collective-permute-start.23 = (bf16[256,2048]{1,0:T(8,128)(2,1)}, bf16[256,2048]{1,0:T(8,128)(2,1)}, u32[]{:S(2)}, u32[]{:S(2)}) collective-permute-start(bf16[256,2048]{1,0:T(8,128)(2,1)} %bitcast.137), channel_id=1, source_target_pairs={{2,4},{3,5},{4,2},{5,3},{10,12},{11,13},{12,10},{13,11},{18,20},{1... | collective-permute-start | bytes 3145736 | tf_op jit(solution)/shard_map/ppermute | solution.py:859
  139.9 33.5 %collective-permute-start.22 = (bf16[2,256,1024]{2,1,0:T(8,128)(2,1)}, bf16[2,256,1024]{2,1,0:T(8,128)(2,1)}, u32[]{:S(2)}, u32[]{:S(2)}) collective-permute-start(bf16[2,256,1024]{2,1,0:T(8,128)(2,1)} %collective-permute-done.17.refs_8_.refs_22_), channel_id=1, source_target_pairs={{0,8},{1,9},{2,10},{3,11},{4,12},{5,13},{6,14},{7,15},{8,0},{9,1},... | collective-permute-start | bytes 3145736 | tf_op jit(solution)/shard_map/ppermute | solution.py:859
  141.1 32.3 %collective-permute-start.24 = (bf16[2,256,1024]{2,1,0:T(8,128)(2,1)}, bf16[2,256,1024]{2,1,0:T(8,128)(2,1)}, u32[]{:S(2)}, u32[]{:S(2)}) collective-permute-start(bf16[2,256,1024]{2,1,0:T(8,128)(2,1)} %collective-permute-done.20.refs_5_.refs_29_), channel_id=1, source_target_pairs={{0,16},{1,17},{2,18},{3,19},{4,20},{5,21},{6,22},{7,23},{8,24},{9,... | collective-permute-start | bytes 3145736 | tf_op jit(solution)/shard_map/ppermute | solution.py:859
  174.5 27.7 %collective-permute-start.25 = (bf16[2,1024,256]{2,1,0:T(8,128)(2,1)S(1)}, bf16[2,1024,256]{2,1,0:T(8,128)(2,1)S(1)}, u32[]{:S(2)}, u32[]{:S(2)}) collective-permute-start(bf16[2,1024,256]{2,1,0:T(8,128)(2,1)S(1)} %copy-done.105), channel_id=1, source_target_pairs={{0,2},{1,3},{6,4},{7,5},{8,10},{9,11},{14,12},{15,13},{16,18},{17,... | collective-permute-start | bytes 3145736 | tf_op jit(solution)/shard_map/ppermute | solution.py:859
  176.0 28.4 %collective-permute-start.26 = (bf16[2,1024,256]{2,1,0:T(8,128)(2,1)S(1)}, bf16[2,1024,256]{2,1,0:T(8,128)(2,1)}, u32[]{:S(2)}, u32[]{:S(2)}) collective-permute-start(bf16[2,1024,256]{2,1,0:T(8,128)(2,1)S(1)} %broadcast_select_fusion.1.refs_0_.refs_2_), channel_id=1, source_target_pairs={{0,8},{1,9},{2,10},{3,11},{4,12},{5,13},{6,14},{7,15},{8,0},{9,1},... | collective-permute-start | bytes 3145736 | tf_op jit(solution)/shard_map/ppermute | solution.py:859
  176.9 27.5 %collective-permute-start.29 = (bf16[2,1024,256]{2,1,0:T(8,128)(2,1)S(1)}, bf16[2,1024,256]{2,1,0:T(8,128)(2,1)S(1)}, u32[]{:S(2)}, u32[]{:S(2)}) collective-permute-start(bf16[2,1024,256]{2,1,0:T(8,128)(2,1)S(1)} %broadcast_select_fusion.1.refs_0_.refs_2_), channel_id=1, source_target_pairs={{0,16},{1,17},{2,18},{3,19},{4,20},{5,21},{6,22},{7,23},{8,24},{9,... | collective-permute-start | bytes 3145736 | tf_op jit(solution)/shard_map/ppermute | solution.py:859
  205.4 27.1 %collective-permute-start.30 = (bf16[2,256,1024]{2,1,0:T(8,128)(2,1)}, bf16[2,256,1024]{2,1,0:T(8,128)(2,1)}, u32[]{:S(2)}, u32[]{:S(2)}) collective-permute-start(bf16[2,256,1024]{2,1,0:T(8,128)(2,1)} %pad_maximum_fusion.5), channel_id=1, source_target_pairs={{0,2},{1,3},{6,4},{7,5},{8,10},{9,11},{14,12},{15,13},{16,18},{17,... | collective-permute-start | bytes 3145736 | tf_op jit(solution)/shard_map/ppermute | solution.py:859
  206.9 27.0 %collective-permute-start.31 = (bf16[2,1024,256]{2,1,0:T(8,128)(2,1)}, bf16[2,1024,256]{2,1,0:T(8,128)(2,1)}, u32[]{:S(2)}, u32[]{:S(2)}) collective-permute-start(bf16[2,1024,256]{2,1,0:T(8,128)(2,1)} %collective-permute-done.26.refs_1_.refs_3_), channel_id=1, source_target_pairs={{0,16},{1,17},{2,18},{3,19},{4,20},{5,21},{6,22},{7,23},{8,24},{9,... | collective-permute-start | bytes 3145736 | tf_op jit(solution)/shard_map/ppermute | solution.py:859
  207.9 26.0 %collective-permute-start.32 = (bf16[2,1024,256]{2,1,0:T(8,128)(2,1)}, bf16[2,1024,256]{2,1,0:T(8,128)(2,1)}, u32[]{:S(2)}, u32[]{:S(2)}) collective-permute-start(bf16[2,1024,256]{2,1,0:T(8,128)(2,1)} %broadcast_select_fusion.refs_4_.refs_0_), channel_id=1, source_target_pairs={{0,8},{1,9},{2,10},{3,11},{4,12},{5,13},{6,14},{7,15},{8,0},{9,1},... | collective-permute-start | bytes 3145736 | tf_op jit(solution)/shard_map/ppermute | solution.py:859
  209.1 24.7 %collective-permute-start.33 = (bf16[128,2048]{1,0:T(8,128)(2,1)}, bf16[128,2048]{1,0:T(8,128)(2,1)}, u32[]{:S(2)}, u32[]{:S(2)}) collective-permute-start(bf16[128,2048]{1,0:T(8,128)(2,1)} %get-tuple-element.276), channel_id=1, source_target_pairs={{0,1},{1,0},{2,3},{3,2},{4,5},{5,4},{6,7},{7,6},{8,9},{9,8},{10,11... | collective-permute-start | bytes 1572872 | tf_op jit(solution)/shard_map/ppermute | solution.py:859
  233.9 23.4 %collective-permute-start.34 = (bf16[2,1024,256]{2,1,0:T(8,128)(2,1)}, bf16[2,1024,256]{2,1,0:T(8,128)(2,1)S(1)}, u32[]{:S(2)}, u32[]{:S(2)}) collective-permute-start(bf16[2,1024,256]{2,1,0:T(8,128)(2,1)} %broadcast_select_fusion.refs_4_.refs_0_), channel_id=1, source_target_pairs={{0,16},{1,17},{2,18},{3,19},{4,20},{5,21},{6,22},{7,23},{8,24},{9,... | collective-permute-start | bytes 3145736 | tf_op jit(solution)/shard_map/ppermute | solution.py:859
  234.2 23.1 %collective-permute-start.35 = (bf16[2,256,1024]{2,1,0:T(8,128)(2,1)S(1)}, bf16[2,256,1024]{2,1,0:T(8,128)(2,1)S(1)}, u32[]{:S(2)}, u32[]{:S(2)}) collective-permute-start(bf16[2,256,1024]{2,1,0:T(8,128)(2,1)S(1)} %broadcast_select_fusion.3.refs_4_.refs_9_.refs_3_), channel_id=1, source_target_pairs={{0,8},{1,9},{2,10},{3,11},{4,12},{5,13},{6,14},{7,15},{8,0},{9,1},... | collective-permute-start | bytes 3145736 | tf_op jit(solution)/shard_map/ppermute | solution.py:859
  234.8 27.7 %collective-permute-start.36 = (bf16[2,256,1024]{2,1,0:T(8,128)(2,1)S(1)}, bf16[2,256,1024]{2,1,0:T(8,128)(2,1)S(1)}, u32[]{:S(2)}, u32[]{:S(2)}) collective-permute-start(bf16[2,256,1024]{2,1,0:T(8,128)(2,1)S(1)} %copy-done.104), channel_id=1, source_target_pairs={{0,2},{1,3},{6,4},{7,5},{8,10},{9,11},{14,12},{15,13},{16,18},{17,... | collective-permute-start | bytes 3145736 | tf_op jit(solution)/shard_map/ppermute | solution.py:859
  267.0 26.1 %collective-permute-start.40 = (bf16[256,2048]{1,0:T(8,128)(2,1)S(1)}, bf16[256,2048]{1,0:T(8,128)(2,1)S(1)}, u32[]{:S(2)}, u32[]{:S(2)}) collective-permute-start(bf16[256,2048]{1,0:T(8,128)(2,1)S(1)} %add_convert_fusion.4), channel_id=1, source_target_pairs={{0,1},{1,0},{2,3},{3,2},{4,5},{5,4},{6,7},{7,6},{8,9},{9,8},{10,11... | collective-permute-start | bytes 3145736 | tf_op jit(solution)/shard_map/ppermute | solution.py:859
  269.9 25.4 %collective-permute-start.41 = (bf16[2,1024,256]{2,1,0:T(8,128)(2,1)S(1)}, bf16[2,1024,256]{2,1,0:T(8,128)(2,1)S(1)}, u32[]{:S(2)}, u32[]{:S(2)}) collective-permute-start(bf16[2,1024,256]{2,1,0:T(8,128)(2,1)S(1)} %collective-permute-done.34.refs_6_.refs_2_), channel_id=1, source_target_pairs={{0,8},{1,9},{2,10},{3,11},{4,12},{5,13},{6,14},{7,15},{8,0},{9,1},... | collective-permute-start | bytes 3145736 | tf_op jit(solution)/shard_map/ppermute | solution.py:859
  270.5 24.7 %collective-permute-start.42 = (bf16[2,256,1024]{2,1,0:T(8,128)(2,1)S(1)}, bf16[2,256,1024]{2,1,0:T(8,128)(2,1)S(1)}, u32[]{:S(2)}, u32[]{:S(2)}) collective-permute-start(bf16[2,256,1024]{2,1,0:T(8,128)(2,1)S(1)} %broadcast_select_fusion.3.refs_4_.refs_9_.refs_3_), channel_id=1, source_target_pairs={{0,16},{1,17},{2,18},{3,19},{4,20},{5,21},{6,22},{7,23},{8,24},{9,... | collective-permute-start | bytes 3145736 | tf_op jit(solution)/shard_map/ppermute | solution.py:859
  295.2 23.9 %collective-permute-start.43 = (bf16[256,2048]{1,0:T(8,128)(2,1)S(1)}, bf16[256,2048]{1,0:T(8,128)(2,1)S(1)}, u32[]{:S(2)}, u32[]{:S(2)}) collective-permute-start(bf16[256,2048]{1,0:T(8,128)(2,1)S(1)} %get-tuple-element.306.refs_0_.refs_4_), channel_id=1, source_target_pairs={{0,1},{1,0},{2,3},{3,2},{4,5},{5,4},{6,7},{7,6},{8,9},{9,8},{10,11... | collective-permute-start | bytes 3145736 | tf_op jit(solution)/shard_map/ppermute | solution.py:859
  296.4 23.2 %collective-permute-start.44 = (bf16[2,256,1024]{2,1,0:T(8,128)(2,1)S(1)}, bf16[2,256,1024]{2,1,0:T(8,128)(2,1)S(1)}, u32[]{:S(2)}, u32[]{:S(2)}) collective-permute-start(bf16[2,256,1024]{2,1,0:T(8,128)(2,1)S(1)} %broadcast_select_fusion.2.refs_7_.refs_13_), channel_id=1, source_target_pairs={{0,8},{1,9},{2,10},{3,11},{4,12},{5,13},{6,14},{7,15},{8,0},{9,1},... | collective-permute-start | bytes 3145736 | tf_op jit(solution)/shard_map/ppermute | solution.py:859
  297.1 22.5 %collective-permute-start.45 = (bf16[256,2048]{1,0:T(8,128)(2,1)S(1)}, bf16[256,2048]{1,0:T(8,128)(2,1)S(1)}, u32[]{:S(2)}, u32[]{:S(2)}) collective-permute-start(bf16[256,2048]{1,0:T(8,128)(2,1)S(1)} %broadcast_select_fusion.7.refs_0_.grad_in), channel_id=1, source_target_pairs={{0,4},{1,5},{2,6},{3,7},{4,0},{5,1},{6,2},{7,3},{8,12},{9,13},{10,... | collective-permute-start | bytes 3145736 | tf_op jit(solution)/shard_map/ppermute | solution.py:859
  298.9 20.8 %collective-permute-start.46 = (bf16[256,2048]{1,0:T(8,128)(2,1)S(1)}, bf16[256,2048]{1,0:T(8,128)(2,1)S(1)}, u32[]{:S(2)}, u32[]{:S(2)}) collective-permute-start(bf16[256,2048]{1,0:T(8,128)(2,1)S(1)} %constant_dynamic-update-slice_fusion.14.refs_2_), channel_id=1, source_target_pairs={{0,4},{1,5},{2,6},{3,7},{4,0},{5,1},{6,2},{7,3},{8,12},{9,13},{10,... | collective-permute-start | bytes 3145736 | tf_op jit(solution)/shard_map/ppermute | solution.py:859
  298.9 24.2 %collective-permute-start.47 = (bf16[2,256,1024]{2,1,0:T(8,128)(2,1)S(1)}, bf16[2,256,1024]{2,1,0:T(8,128)(2,1)S(1)}, u32[]{:S(2)}, u32[]{:S(2)}) collective-permute-start(bf16[2,256,1024]{2,1,0:T(8,128)(2,1)S(1)} %broadcast_select_fusion.2.refs_7_.refs_13_), channel_id=1, source_target_pairs={{0,16},{1,17},{2,18},{3,19},{4,20},{5,21},{6,22},{7,23},{8,24},{9,... | collective-permute-start | bytes 3145736 | tf_op jit(solution)/shard_map/ppermute | solution.py:859
  324.4 24.8 %collective-permute-start.50 = (bf16[2,256,1024]{2,1,0:T(8,128)(2,1)S(1)}, bf16[2,256,1024]{2,1,0:T(8,128)(2,1)S(1)}, u32[]{:S(2)}, u32[]{:S(2)}) collective-permute-start(bf16[2,256,1024]{2,1,0:T(8,128)(2,1)S(1)} %collective-permute-done.42.refs_6_.refs_11_.refs_5_), channel_id=1, source_target_pairs={{0,8},{1,9},{2,10},{3,11},{4,12},{5,13},{6,14},{7,15},{8,0},{9,1},... | collective-permute-start | bytes 3145736 | tf_op jit(solution)/shard_map/ppermute | solution.py:859
  325.3 24.0 %collective-permute-start.51 = (bf16[2,256,1024]{2,1,0:T(8,128)(2,1)S(1)}, bf16[2,256,1024]{2,1,0:T(8,128)(2,1)S(1)}, u32[]{:S(2)}, u32[]{:S(2)}) collective-permute-start(bf16[2,256,1024]{2,1,0:T(8,128)(2,1)S(1)} %collective-permute-done.44.refs_8_.refs_14_), channel_id=1, source_target_pairs={{0,16},{1,17},{2,18},{3,19},{4,20},{5,21},{6,22},{7,23},{8,24},{9,... | collective-permute-start | bytes 3145736 | tf_op jit(solution)/shard_map/ppermute | solution.py:859
  361.8 20.6 %collective-permute-start.52 = (bf16[48,1024]{1,0:T(8,128)(2,1)S(1)}, bf16[48,1024]{1,0:T(8,128)(2,1)S(1)}, u32[]{:S(2)}, u32[]{:S(2)}) collective-permute-start(bf16[48,1024]{1,0:T(8,128)(2,1)S(1)} %convert_element_type.115), channel_id=1, source_target_pairs={{0,4},{1,5},{2,6},{3,7},{4,0},{5,1},{6,2},{7,3},{8,12},{9,13},{10,... | collective-permute-start | bytes 294920 | tf_op jit(solution)/shard_map/ppermute | solution.py:859
  387.5 24.9 %collective-permute-start.55 = (bf16[256,2048]{1,0:T(8,128)(2,1)}, bf16[256,2048]{1,0:T(8,128)(2,1)}, u32[]{:S(2)}, u32[]{:S(2)}) collective-permute-start(bf16[256,2048]{1,0:T(8,128)(2,1)} %add_convert_fusion.3), channel_id=1, source_target_pairs={{0,1},{1,0},{2,3},{3,2},{4,5},{5,4},{6,7},{7,6},{8,9},{9,8},{10,11... | collective-permute-start | bytes 3145736 | tf_op jit(solution)/shard_map/ppermute | solution.py:859
  387.6 28.4 %collective-permute-start.56 = (bf16[48,1024]{1,0:T(8,128)(2,1)}, bf16[48,1024]{1,0:T(8,128)(2,1)}, u32[]{:S(2)}, u32[]{:S(2)}) collective-permute-start(bf16[48,1024]{1,0:T(8,128)(2,1)} %fusion.3), channel_id=1, source_target_pairs={{0,1},{1,0},{2,3},{3,2},{4,5},{5,4},{6,7},{7,6},{8,9},{9,8},{10,11... | collective-permute-start | bytes 294920 | tf_op jit(solution)/shard_map/ppermute | solution.py:859
  417.6 24.6 %collective-permute-start.59 = (bf16[256,2048]{1,0:T(8,128)(2,1)}, bf16[256,2048]{1,0:T(8,128)(2,1)S(1)}, u32[]{:S(2)}, u32[]{:S(2)}) collective-permute-start(bf16[256,2048]{1,0:T(8,128)(2,1)} %rms_back.2.refs_0_.refs_4_.grad_in), channel_id=1, source_target_pairs={{0,1},{1,0},{2,3},{3,2},{4,5},{5,4},{6,7},{7,6},{8,9},{9,8},{10,11... | collective-permute-start | bytes 3145736 | tf_op jit(solution)/shard_map/ppermute | solution.py:859
  417.8 24.4 %collective-permute-start.60 = (bf16[256,2048]{1,0:T(8,128)(2,1)}, bf16[256,2048]{1,0:T(8,128)(2,1)S(1)}, u32[]{:S(2)}, u32[]{:S(2)}) collective-permute-start(bf16[256,2048]{1,0:T(8,128)(2,1)} %get-tuple-element.359), channel_id=1, source_target_pairs={{0,4},{1,5},{2,6},{3,7},{4,0},{5,1},{6,2},{7,3},{8,12},{9,13},{10,... | collective-permute-start | bytes 3145736 | tf_op jit(solution)/shard_map/ppermute | solution.py:859
  451.1 24.9 %collective-permute-start.63 = (bf16[256,2048]{1,0:T(8,128)(2,1)}, bf16[256,2048]{1,0:T(8,128)(2,1)}, u32[]{:S(2)}, u32[]{:S(2)}) collective-permute-start(bf16[256,2048]{1,0:T(8,128)(2,1)} %add_convert_fusion.2), channel_id=1, source_target_pairs={{0,1},{1,0},{2,3},{3,2},{4,5},{5,4},{6,7},{7,6},{8,9},{9,8},{10,11... | collective-permute-start | bytes 3145736 | tf_op jit(solution)/shard_map/ppermute | solution.py:859
  479.3 28.3 %collective-permute-start.67 = (bf16[256,2048]{1,0:T(8,128)(2,1)S(1)}, bf16[256,2048]{1,0:T(8,128)(2,1)S(1)}, u32[]{:S(2)}, u32[]{:S(2)}) collective-permute-start(bf16[256,2048]{1,0:T(8,128)(2,1)S(1)} %add_convert_fusion.1), channel_id=1, source_target_pairs={{2,4},{3,5},{4,2},{5,3},{10,12},{11,13},{12,10},{13,11},{18,20},{1... | collective-permute-start | bytes 3145736 | tf_op jit(solution)/shard_map/ppermute | solution.py:859
  482.8 21.8 %collective-permute-start.69 = (bf16[2,152,512]{2,1,0:T(8,128)(2,1)S(1)}, bf16[2,152,512]{2,1,0:T(8,128)(2,1)S(1)}, u32[]{:S(2)}, u32[]{:S(2)}) collective-permute-start(bf16[2,152,512]{2,1,0:T(8,128)(2,1)S(1)} %pad_maximum_fusion.11), channel_id=1, source_target_pairs={{0,16},{1,17},{2,18},{3,19},{4,20},{5,21},{6,22},{7,23},{8,24},{9,... | collective-permute-start | bytes 933896 | tf_op jit(solution)/shard_map/ppermute | solution.py:859
  483.6 20.9 %collective-permute-start.70 = (bf16[2,152,512]{2,1,0:T(8,128)(2,1)S(1)}, bf16[2,152,512]{2,1,0:T(8,128)(2,1)S(1)}, u32[]{:S(2)}, u32[]{:S(2)}) collective-permute-start(bf16[2,152,512]{2,1,0:T(8,128)(2,1)S(1)} %pad_maximum_fusion.12), channel_id=1, source_target_pairs={{0,8},{1,9},{2,10},{3,11},{4,12},{5,13},{6,14},{7,15},{8,0},{9,1},... | collective-permute-start | bytes 933896 | tf_op jit(solution)/shard_map/ppermute | solution.py:859
  484.7 19.8 %collective-permute-start.68 = (bf16[80,1024]{1,0:T(8,128)(2,1)S(1)}, bf16[80,1024]{1,0:T(8,128)(2,1)S(1)}, u32[]{:S(2)}, u32[]{:S(2)}) collective-permute-start(bf16[80,1024]{1,0:T(8,128)(2,1)S(1)} %fusion.2), channel_id=1, source_target_pairs={{0,1},{1,0},{2,3},{3,2},{4,5},{5,4},{6,7},{7,6},{8,9},{9,8},{10,11... | collective-permute-start | bytes 491528 | tf_op jit(solution)/shard_map/ppermute | solution.py:859
  553.7 19.7 %collective-permute-start.82 = (bf16[4,448,512]{2,1,0:T(8,128)(2,1)S(1)}, bf16[4,448,512]{2,1,0:T(8,128)(2,1)}, u32[]{:S(2)}, u32[]{:S(2)}) collective-permute-start(bf16[4,448,512]{2,1,0:T(8,128)(2,1)S(1)} %maximum_maximum_fusion.refs_0_), channel_id=1, source_target_pairs={{0,4},{1,5},{2,6},{3,7},{4,0},{5,1},{6,2},{7,3},{8,12},{9,13},{10,... | collective-permute-start | bytes 5505032 | tf_op jit(solution)/shard_map/ppermute | solution.py:859
  554.2 30.9 %collective-permute-start.80 = (bf16[256,2048]{1,0:T(8,128)(2,1)}, bf16[256,2048]{1,0:T(8,128)(2,1)}, u32[]{:S(2)}, u32[]{:S(2)}) collective-permute-start(bf16[256,2048]{1,0:T(8,128)(2,1)} %get-tuple-element.415), channel_id=1, source_target_pairs={{2,4},{3,5},{4,2},{5,3},{10,12},{11,13},{12,10},{13,11},{18,20},{1... | collective-permute-start | bytes 3145736 | tf_op jit(solution)/shard_map/ppermute | solution.py:859
  (165 other events, 2983.7 us)
